TPU v7x, 32 devices: a whole 2x2x4 slice. The times are simulated.
32 devices in a mesh: dom: 4 (over x, core), phase: 2 (over y), feat: 4 (over z).
Axes of the slice: x: 2, y: 2, z: 4, core: 2. Of those that a mesh axis runs over, the one named last changes fastest.
Arguments:
- node_in: bfloat16 [131072, 256], P(('dom', 'phase', 'feat')), may hold values from -6 to 6
- out_cot: bfloat16 [131072, 256], P(('dom', 'phase', 'feat')), may hold values from -6 to 6
- adjacency: bfloat16 [1024, 4, 128, 128], P(('dom', 'phase', 'feat')), may hold values from -0.25 to 0.25
- tile_nbrs: int32 [1024, 4], P(('dom', 'phase', 'feat')), may hold values from 0 to 47, as said below
- bound_tiles: int32 [32, 2, 8], P(('dom', 'phase', 'feat')), may hold values from 0 to 15, as said below
- live_tiles: int32 [32], P(('dom', 'phase', 'feat')), may hold values from 16 to 32, as said below
- w_self: bfloat16 [2, 256, 256], replicated, may hold values from -0.25 to 0.25
- w_nbr: bfloat16 [2, 256, 256], replicated, may hold values from -0.25 to 0.25
- pre_bias: float32 [2, 256], replicated, may hold values from -3 to 3
- w_out: bfloat16 [2, 256, 256], replicated, may hold values from -0.375 to 0.375
Outputs:
- section_out: bfloat16 [2, 131072, 256], P(None, ('dom', 'phase', 'feat'))
- section_in_grad: bfloat16 [2, 131072, 256], P(None, ('dom', 'phase', 'feat'))
- grad_self: float32 [2, 256, 256], replicated
- grad_nbr: float32 [2, 256, 256], replicated
- grad_bias: float32 [2, 256], replicated
- grad_out: float32 [2, 256, 256], replicated
Inputs may be any that keep to these rules, and one draw needn't show every extreme that they name: `live_tiles`: some partition has all 32 tiles live. `bound_tiles`: for each partition the 16 entries are the tiles 0 to 15, each once. `tile_nbrs`: slot 0 of local tile i is i; every entry of a live tile names a live own tile (below 32) or an extended tile (from 32 on); each extended tile is named by some live tile; all entries of a tile that is not live are i.
All inputs are finite; a program needn't handle non-finite values.
Results may differ from a plain program's by a relative error of at most 0.008.
Values may be sent and summed in bfloat16 or wider, within the bound.
No kernel may reach another device: no remote copies, remote signals or barrier semaphores. Data moves between devices by JAX's collectives and lax.ppermute only.
A program may use at most 192 MiB of HBM per device.

v0:
```python
import jax
import jax.numpy as jnp
from jax import lax
from jax.sharding import PartitionSpec as P


def passed_along(value, axis, steps):
    count = lax.axis_size(axis)
    pairs = [(source, (source + steps) % count) for source in range(count)]
    return lax.ppermute(value, axis, pairs)


def silu_slope(pre_act):
    sigma = jax.nn.sigmoid(pre_act)
    return sigma * (1.0 + pre_act * (1.0 - sigma))


def extend_tiles(node_tiles, bound_idx):
    west_send = node_tiles[bound_idx[0]]
    east_send = node_tiles[bound_idx[1]]
    from_west = passed_along(east_send, ("dom", "phase", "feat"), 1)
    from_east = passed_along(west_send, ("dom", "phase", "feat"), -1)
    return jnp.concatenate([node_tiles, from_west, from_east], axis=0)


def return_back(collected, bound_idx):
    edge_count = bound_idx.shape[1]
    tile_count = collected.shape[0] - 2 * edge_count
    west_part = collected[tile_count : tile_count + edge_count]
    east_part = collected[tile_count + edge_count :]
    from_east = passed_along(west_part.astype(jnp.bfloat16), ("dom", "phase", "feat"), -1).astype(
        west_part.dtype
    )
    from_west = passed_along(east_part.astype(jnp.bfloat16), ("dom", "phase", "feat"), 1).astype(
        east_part.dtype
    )
    local_part = collected[:tile_count].at[bound_idx[1]].add(from_east)
    return local_part.at[bound_idx[0]].add(from_west)


def forward(features, weights, graph_data):
    w_self, w_nbr, pre_bias, w_out = weights
    adjacency, neighbours, bound_idx, mask_rows = graph_data
    tile_count, tile_rows = (adjacency.shape[0], adjacency.shape[2])
    node_tiles = features.reshape(tile_count, tile_rows, -1)
    extended = extend_tiles(node_tiles, bound_idx)
    picked = extended[neighbours]
    summed = jnp.einsum("tkij,tkjc->tic", adjacency, picked, preferred_element_type=jnp.float32)
    gathered = summed.reshape(features.shape).astype(jnp.bfloat16)
    pre_act = (
        jnp.dot(features, w_self, preferred_element_type=jnp.float32)
        + jnp.dot(gathered, w_nbr, preferred_element_type=jnp.float32)
        + pre_bias
    )
    hidden = jax.nn.silu(pre_act).astype(jnp.bfloat16)
    result = (
        mask_rows
        * (
            features.astype(jnp.float32)
            + jnp.dot(hidden, w_out, preferred_element_type=jnp.float32)
        )
    ).astype(jnp.bfloat16)
    return (result, (features, gathered, pre_act, hidden))


def backward(upstream, saved_state, weights, graph_data):
    w_self, w_nbr, pre_bias, w_out = weights
    adjacency, neighbours, bound_idx, mask_rows = graph_data
    features, gathered, pre_act, hidden = saved_state
    tile_count, slot_count, tile_rows = (adjacency.shape[0], adjacency.shape[1], adjacency.shape[2])
    edge_count = bound_idx.shape[1]
    masked = upstream * mask_rows.astype(jnp.bfloat16)
    grad_out = jnp.dot(hidden.T, masked, preferred_element_type=jnp.float32)
    grad_hidden = jnp.dot(masked, w_out.T, preferred_element_type=jnp.float32)
    grad_pre = (grad_hidden * silu_slope(pre_act)).astype(jnp.bfloat16)
    grad_self = jnp.dot(features.T, grad_pre, preferred_element_type=jnp.float32)
    grad_nbr = jnp.dot(gathered.T, grad_pre, preferred_element_type=jnp.float32)
    grad_bias = jnp.sum(grad_pre, axis=0, dtype=jnp.float32)
    direct = masked.astype(jnp.float32) + jnp.dot(
        grad_pre, w_self.T, preferred_element_type=jnp.float32
    )
    grad_gathered = jnp.dot(grad_pre, w_nbr.T, preferred_element_type=jnp.float32).astype(
        jnp.bfloat16
    )
    contrib = jnp.einsum(
        "tkij,tic->tkjc",
        adjacency,
        grad_gathered.reshape(tile_count, tile_rows, -1),
        preferred_element_type=jnp.float32,
    )
    collected = jax.ops.segment_sum(
        contrib.reshape(tile_count * slot_count, tile_rows, -1),
        neighbours.reshape(-1),
        num_segments=tile_count + 2 * edge_count,
    )
    returned = return_back(collected, bound_idx)
    grad_in = (direct + returned.reshape(direct.shape)).astype(jnp.bfloat16)
    return (grad_in, (grad_self, grad_nbr, grad_bias, grad_out))


def per_device(
    node_in, out_cot, adjacency, tile_nbrs, bound_tiles, live_tiles, w_self, w_nbr, pre_bias, w_out
):
    tile_count, tile_rows = (adjacency.shape[0], adjacency.shape[2])
    alive_tiles = (jnp.arange(tile_count) < live_tiles[0]).astype(jnp.float32)
    mask_rows = jnp.repeat(alive_tiles, tile_rows)[:, None]
    graph_data = (adjacency, tile_nbrs, bound_tiles[0], mask_rows)
    first_weights = (w_self[0], w_nbr[0], pre_bias[0], w_out[0])
    second_weights = (w_self[1], w_nbr[1], pre_bias[1], w_out[1])
    first_out, first_saved = forward(node_in, first_weights, graph_data)
    second_out, second_saved = forward(first_out, second_weights, graph_data)
    grad_mid, later = backward(out_cot, second_saved, second_weights, graph_data)
    grad_first, early = backward(grad_mid, first_saved, first_weights, graph_data)
    summed_all = lax.psum(
        (early[0], early[1], early[2], early[3], later[0], later[1], later[2], later[3]),
        ("dom", "phase", "feat"),
    )
    early_sum = summed_all[:4]
    later_sum = summed_all[4:]
    section_out = jnp.stack([first_out, second_out])
    section_in_grad = jnp.stack([grad_first, grad_mid])
    grad_self = jnp.stack([early_sum[0], later_sum[0]])
    grad_nbr = jnp.stack([early_sum[1], later_sum[1]])
    grad_bias = jnp.stack([early_sum[2], later_sum[2]])
    grad_out = jnp.stack([early_sum[3], later_sum[3]])
    return (section_out, section_in_grad, grad_self, grad_nbr, grad_bias, grad_out)


def solution(mesh):
    in_specs = (
        P(("dom", "phase", "feat"), None),
        P(("dom", "phase", "feat"), None),
        P(("dom", "phase", "feat"), None, None, None),
        P(("dom", "phase", "feat"), None),
        P(("dom", "phase", "feat"), None, None),
        P(("dom", "phase", "feat")),
        P(),
        P(),
        P(),
        P(),
    )
    out_specs = (
        P(None, ("dom", "phase", "feat"), None),
        P(None, ("dom", "phase", "feat"), None),
        P(),
        P(),
        P(),
        P(),
    )
    return jax.shard_map(
        per_device, mesh=mesh, in_specs=in_specs, out_specs=out_specs, check_vma=False
    )
```

profile of v0, /device:TPU:0, one launch (start us, length us, event | category | flops | bytes accessed | tf_op | source)
XLA Modules:
  0.0 459.2 jit_solution(12905172138418600061)
XLA Ops:
  23.7 3.6 fusion.40
  29.9 10.5 %collective-permute-done.1 = bf16[8,128,256]{2,1,0:T(8,128)(2,1)S(1)} collective-permute-done((bf16[8,128,256]{2,1,0:T(8,128)(2,1)}, bf16[8,128,256]{2,1,0:T(8,128)(2,1)S(1)}, u32[]{:S(2)}, u32[]{:S(2)}) %collective-permute-start.1) | collective-permute-done | bytes 524320 | tf_op jit(solution)/shard_map/ppermute | solution.py:10
  42.2 8.5 %gather_fusion.2 = bf16[128,128,256]{2,1,0:T(8,128)(2,1)} fusion(bf16[48,128,256]{2,1,0:T(8,128)(2,1)} %pad_maximum_fusion.2, s32[1024]{0:T(1024)S(1)} %pad_clamp_fusion), kind=kCustom, calls=%fused_computation.2 | custom fusion | bytes 16777728 | tf_op jit(solution)/shard_map/gather | solution.py:47
  50.7 6.4 %bitcast_convert_fusion.1 = bf16[32,256,128]{1,2,0:T(8,128)(2,1)S(1)} fusion(bf16[32,4,128,128]{3,2,1,0:T(8,128)(2,1)} %param.12, bf16[32,4,128,256]{3,2,1,0:T(8,128)(2,1)} %bitcast.154), kind=kOutput, calls=%fused_computation.38 | convolution fusion | flops 1074790400 | bytes 14680064 | tf_op jit(solution)/shard_map/tkij,tkjc->tic/dot_general | solution.py:48
  63.5 4.8 %collective-permute-start.3 = (bf16[8,128,256]{2,1,0:T(8,128)(2,1)S(1)}, bf16[8,128,256]{2,1,0:T(8,128)(2,1)S(1)}, u32[]{:S(2)}, u32[]{:S(2)}) collective-permute-start(bf16[8,128,256]{2,1,0:T(8,128)(2,1)S(1)} %gather_fusion.4), channel_id=1, source_target_pairs={{0,31},{1,0},{2,1},{3,2},{4,3},{5,4},{6,5},{7,6},{8,7},{9,8},{10,9... | collective-permute-start | bytes 1572872 | tf_op jit(solution)/shard_map/ppermute | solution.py:10
  71.1 9.6 %collective-permute-done.2 = bf16[8,128,256]{2,1,0:T(8,128)(2,1)S(1)} collective-permute-done((bf16[8,128,256]{2,1,0:T(8,128)(2,1)S(1)}, bf16[8,128,256]{2,1,0:T(8,128)(2,1)S(1)}, u32[]{:S(2)}, u32[]{:S(2)}) %collective-permute-start.2) | collective-permute-done | bytes 524320 | tf_op jit(solution)/shard_map/ppermute | solution.py:10
  80.7 7.6 %collective-permute-done.3 = bf16[8,128,256]{2,1,0:T(8,128)(2,1)S(1)} collective-permute-done((bf16[8,128,256]{2,1,0:T(8,128)(2,1)S(1)}, bf16[8,128,256]{2,1,0:T(8,128)(2,1)S(1)}, u32[]{:S(2)}, u32[]{:S(2)}) %collective-permute-start.3) | collective-permute-done | bytes 524320 | tf_op jit(solution)/shard_map/ppermute | solution.py:10
  90.4 8.5 %gather_fusion.5 = bf16[128,128,256]{2,1,0:T(8,128)(2,1)} fusion(bf16[48,128,256]{2,1,0:T(8,128)(2,1)} %pad_maximum_fusion.3, s32[1024]{0:T(1024)S(1)} %pad_clamp_fusion), kind=kCustom, calls=%fused_computation.5 | custom fusion | bytes 16777728 | tf_op jit(solution)/shard_map/gather | solution.py:47
  98.9 6.4 %bitcast_convert_fusion = bf16[32,256,128]{1,2,0:T(8,128)(2,1)S(1)} fusion(bf16[32,4,128,128]{3,2,1,0:T(8,128)(2,1)} %param.12, bf16[32,4,128,256]{3,2,1,0:T(8,128)(2,1)} %bitcast.153), kind=kOutput, calls=%fused_computation.37 | convolution fusion | flops 1074790400 | bytes 14680064 | tf_op jit(solution)/shard_map/tkij,tkjc->tic/dot_general | solution.py:48
  114.9 8.1 %fusion.59 = f32[32,256,4,128]{3,1,2,0:T(8,128)} fusion(bf16[32,128,256,1]{2,1,3,0:T(8,128)(2,1)S(1)} %bitcast.159, bf16[32,4,128,128]{3,2,1,0:T(8,128)(2,1)S(1)} %copy-done.1), kind=kOutput, calls=%fused_computation.108 | convolution fusion | flops 1073741824 | bytes 23068672 | tf_op jit(solution)/shard_map/tkij,tic->tkjc/dot_general | solution.py:85
  123.0 17.4 %copy.27 = f32[128,128,256]{2,1,0:T(8,128)} copy(f32[128,128,256]{1,2,0:T(8,128)} %bitcast.151) | data formatting | bytes 33554432 | tf_op jit(solution)/shard_map/reshape | solution.py:92
  140.5 3.4 broadcast.51.clone
  143.9 38.0 %scatter_fusion = f32[48,128,256]{2,1,0:T(8,128)} fusion(f32[48,128,256]{2,1,0:T(8,128)} %broadcast.51.clone, s32[128]{0:T(128)S(1)} %reshape.168, f32[128,128,256]{2,1,0:T(8,128)} %copy.27), kind=kCustom, calls=%fused_computation.6 | custom fusion | flops 4194304 | bytes 50332160 | tf_op jit(solution)/shard_map/scatter-add | solution.py:91
  197.7 4.0 collective-permute-done.4
  205.1 8.1 %collective-permute-done.5 = bf16[8,128,256]{2,1,0:T(8,128)(2,1)} collective-permute-done((bf16[8,128,256]{2,1,0:T(8,128)(2,1)}, bf16[8,128,256]{2,1,0:T(8,128)(2,1)}, u32[]{:S(2)}, u32[]{:S(2)}) %collective-permute-start.5) | collective-permute-done | bytes 524320 | tf_op jit(solution)/shard_map/ppermute | solution.py:10
  217.7 4.6 fusion.10
  229.4 8.1 %fusion.60 = f32[32,256,4,128]{3,1,2,0:T(8,128)} fusion(bf16[32,128,256,1]{2,1,3,0:T(8,128)(2,1)S(1)} %bitcast.160, bf16[32,4,128,128]{3,2,1,0:T(8,128)(2,1)S(1)} %copy-done.2), kind=kOutput, calls=%fused_computation.109 | convolution fusion | flops 1073741824 | bytes 23068672 | tf_op jit(solution)/shard_map/tkij,tic->tkjc/dot_general | solution.py:85
  237.5 17.4 %copy.29 = f32[128,128,256]{2,1,0:T(8,128)} copy(f32[128,128,256]{1,2,0:T(8,128)} %bitcast.152) | data formatting | bytes 33554432 | tf_op jit(solution)/shard_map/reshape | solution.py:92
  255.0 3.4 broadcast.51
  258.4 38.3 %scatter_fusion.3 = f32[48,128,256]{2,1,0:T(8,128)} fusion(f32[48,128,256]{2,1,0:T(8,128)} %broadcast.51, s32[128]{0:T(128)S(1)} %reshape.168, f32[128,128,256]{2,1,0:T(8,128)} %copy.29), kind=kCustom, calls=%fused_computation.9 | custom fusion | flops 4194304 | bytes 50332160 | tf_op jit(solution)/shard_map/scatter-add | solution.py:91
  310.2 44.0 %all-reduce = (f32[1,256]{1,0:T(1,128)S(1)}, f32[1,256]{1,0:T(1,128)S(1)}) all-reduce(f32[1,256]{1,0:T(1,128)S(1)} %bitcast.165, f32[1,256]{1,0:T(1,128)S(1)} %bitcast.166), channel_id=1, replica_groups=mesh['dom'=4,'phase'=2,'feat'=4] {'dom','phase','feat'}, use_global_device_ids=true, to_apply=%region_13.14 | all-reduce | flops 512 | bytes 4096 | tf_op jit(solution)/shard_map/psum | solution.py:114
  363.7 4.6 %fusion.11 = bf16[1,4096,256]{2,1,0:T(8,128)(2,1)S(1)} fusion(f32[32,128,256]{2,1,0:T(8,128)} %scatter_fusion.5, bf16[4096,256]{1,0:T(8,128)(2,1)} %copy-done.9, bf16[4096,256]{1,0:T(8,128)(2,1)} %copy-done.6, bf16[4096]{0:T(1024)(128)(2,1)S(1)} %bitcast_convert_fusion.2, bf16[2,256,256]{2,1,0:T(8,128)(2,1)S(1)} %copy-done.23), kind=kOutput, calls=%fused_computation.41 | convolution fusion | flops 542113792 | bytes 10625024 | tf_op jit(solution)/shard_map/dot_general | solution.py:79
  368.5 3.7 pad_maximum_fusion
  372.1 75.5 %all-reduce.4.cloned.1.call-done = (f32[1,256,256]{1,2,0:T(8,128)}, f32[1,256,256]{1,2,0:T(8,128)}, f32[1,256,256]{2,1,0:T(8,128)}, f32[1,256,256]{2,1,0:T(8,128...) async-done(((f32[1,256,256]{1,2,0:T(8,128)}, f32[1,256,256]{1,2,0:T(8,128)}, f32[1,256,256]{2,1,0:T(8,128)}, f32[1,256,256]{2,1,0:T(8,128)}, f32[1,256,256]{2,1,0:T(8,128)}, ...) | async-done | bytes 1572880 | tf_op jit(solution)/shard_map/psum | solution.py:114
  (131 shorter events, 99.2 us)
Async XLA Ops:
  7.2 16.5 %copy-start.3 = (bf16[4096,256]{1,0:T(8,128)(2,1)S(1)}, bf16[4096,256]{1,0:T(8,128)(2,1)}, u32[]{:S(2)}) copy-start(bf16[4096,256]{1,0:T(8,128)(2,1)} %param.10) | copy-start | bytes 6291460
  7.2 440.4 %all-reduce.4.cloned.1.call-start = ((), (), s32[]{:S(2)}) async-start(), calls=%async_computation | async-start | bytes 3145728 | tf_op jit(solution)/shard_map/psum | solution.py:114
  11.0 18.8 %collective-permute-start = (bf16[8,128,256]{2,1,0:T(8,128)(2,1)}, bf16[8,128,256]{2,1,0:T(8,128)(2,1)S(1)}, u32[]{:S(2)}, u32[]{:S(2)}) collective-permute-start(bf16[8,128,256]{2,1,0:T(8,128)(2,1)} %gather_fusion), channel_id=1, source_target_pairs={{0,1},{1,2},{2,3},{3,4},{4,5},{5,6},{6,7},{7,8},{8,9},{9,10},{10,1... | collective-permute-start | bytes 1572872 | tf_op jit(solution)/shard_map/ppermute | solution.py:10
  17.0 23.3 %collective-permute-start.1 = (bf16[8,128,256]{2,1,0:T(8,128)(2,1)}, bf16[8,128,256]{2,1,0:T(8,128)(2,1)S(1)}, u32[]{:S(2)}, u32[]{:S(2)}) collective-permute-start(bf16[8,128,256]{2,1,0:T(8,128)(2,1)} %gather_fusion.1), channel_id=1, source_target_pairs={{0,31},{1,0},{2,1},{3,2},{4,3},{5,4},{6,5},{7,6},{8,7},{9,8},{10,9... | collective-permute-start | bytes 1572872 | tf_op jit(solution)/shard_map/ppermute | solution.py:10
  50.7 6.4 %copy-start.14 = (f32[4096,256]{1,0:T(8,128)S(1)}, f32[4096,256]{1,0:T(8,128)}, u32[]{:S(2)}) copy-start(f32[4096,256]{1,0:T(8,128)} %fusion.40) | copy-start | bytes 12582916
  50.7 6.4 %copy-start.24 = (bf16[2,256,256]{2,1,0:T(8,128)(2,1)S(1)}, bf16[2,256,256]{2,1,0:T(8,128)(2,1)}, u32[]{:S(2)}) copy-start(bf16[2,256,256]{2,1,0:T(8,128)(2,1)} %param.17) | copy-start | bytes 786436
  60.5 7.9 %copy-start.23 = (bf16[2,256,256]{2,1,0:T(8,128)(2,1)S(1)}, bf16[2,256,256]{2,1,0:T(8,128)(2,1)}, u32[]{:S(2)}) copy-start(bf16[2,256,256]{2,1,0:T(8,128)(2,1)} %param.16) | copy-start | bytes 786436
  62.9 17.8 %collective-permute-start.2 = (bf16[8,128,256]{2,1,0:T(8,128)(2,1)S(1)}, bf16[8,128,256]{2,1,0:T(8,128)(2,1)S(1)}, u32[]{:S(2)}, u32[]{:S(2)}) collective-permute-start(bf16[8,128,256]{2,1,0:T(8,128)(2,1)S(1)} %gather_fusion.3), channel_id=1, source_target_pairs={{0,1},{1,2},{2,3},{3,4},{4,5},{5,6},{6,7},{7,8},{8,9},{9,10},{10,1... | collective-permute-start | bytes 1572872 | tf_op jit(solution)/shard_map/ppermute | solution.py:10
  63.5 24.8 %collective-permute-start.3 = (bf16[8,128,256]{2,1,0:T(8,128)(2,1)S(1)}, bf16[8,128,256]{2,1,0:T(8,128)(2,1)S(1)}, u32[]{:S(2)}, u32[]{:S(2)}) collective-permute-start(bf16[8,128,256]{2,1,0:T(8,128)(2,1)S(1)} %gather_fusion.4), channel_id=1, source_target_pairs={{0,31},{1,0},{2,1},{3,2},{4,3},{5,4},{6,5},{7,6},{8,7},{9,8},{10,9... | collective-permute-start | bytes 1572872 | tf_op jit(solution)/shard_map/ppermute | solution.py:10
  98.9 6.4 %copy-start.13 = (f32[4096,256]{1,0:T(8,128)S(1)}, f32[4096,256]{1,0:T(8,128)}, u32[]{:S(2)}) copy-start(f32[4096,256]{1,0:T(8,128)} %fusion.33) | copy-start | bytes 12582916
  98.9 6.4 %copy-start.25 = (bf16[2,256,256]{2,1,0:T(8,128)(2,1)S(1)}, bf16[2,256,256]{2,1,0:T(8,128)(2,1)}, u32[]{:S(2)}) copy-start(bf16[2,256,256]{2,1,0:T(8,128)(2,1)} %param.17) | copy-start | bytes 786436
  181.9 7.4 %copy-start.20 = (bf16[4096,256]{1,0:T(8,128)(2,1)S(1)}, bf16[4096,256]{1,0:T(8,128)(2,1)}, u32[]{:S(2)}) copy-start(bf16[4096,256]{1,0:T(8,128)(2,1)} %get-tuple-element.36) | copy-start | bytes 6291460
  185.3 7.9 %slice-start = ((s8[6291456]{0:T(1024)(128)(4,1)}), s8[4194304]{0:T(1024)(128)(4,1)S(1)}, s32[]{:S(2)}) async-start(s8[6291456]{0:T(1024)(128)(4,1)} %bitcast.145), calls=%async_computation.1 | async-start | bytes 8388608
  186.1 15.6 %collective-permute-start.4 = (bf16[8,128,256]{2,1,0:T(8,128)(2,1)S(1)}, bf16[8,128,256]{2,1,0:T(8,128)(2,1)S(1)}, u32[]{:S(2)}, u32[]{:S(2)}) collective-permute-start(bf16[8,128,256]{2,1,0:T(8,128)(2,1)S(1)} %get-tuple-element.29), channel_id=1, source_target_pairs={{0,31},{1,0},{2,1},{3,2},{4,3},{5,4},{6,5},{7,6},{8,7},{9,8},{10,9... | collective-permute-start | bytes 1572872 | tf_op jit(solution)/shard_map/ppermute | solution.py:10
  189.3 23.9 %collective-permute-start.5 = (bf16[8,128,256]{2,1,0:T(8,128)(2,1)}, bf16[8,128,256]{2,1,0:T(8,128)(2,1)}, u32[]{:S(2)}, u32[]{:S(2)}) collective-permute-start(bf16[8,128,256]{2,1,0:T(8,128)(2,1)} %get-tuple-element.28), channel_id=1, source_target_pairs={{0,1},{1,2},{2,3},{3,4},{4,5},{5,6},{6,7},{7,8},{8,9},{9,10},{10,1... | collective-permute-start | bytes 1572872 | tf_op jit(solution)/shard_map/ppermute | solution.py:10
  217.6 4.6 copy-start.29
  217.7 4.7 %copy-start.30 = (f32[4096,256]{1,0:T(8,128)S(1)}, f32[4096,256]{1,0:T(8,128)}, u32[]{:S(2)}) copy-start(f32[4096,256]{1,0:T(8,128)} %get-tuple-element.35) | copy-start | bytes 12582916
  296.6 6.3 %copy-start.5 = (bf16[4096,256]{1,0:T(8,128)(2,1)S(1)}, bf16[4096,256]{1,0:T(8,128)(2,1)}, u32[]{:S(2)}) copy-start(bf16[4096,256]{1,0:T(8,128)(2,1)} %param.10) | copy-start | bytes 6291460
  296.7 6.3 %copy-start.10 = (bf16[4096,256]{1,0:T(8,128)(2,1)S(1)}, bf16[4096,256]{1,0:T(8,128)(2,1)}, u32[]{:S(2)}) copy-start(bf16[4096,256]{1,0:T(8,128)(2,1)} %copy-done.9) | copy-start | bytes 6291460
  300.1 4.4 copy-start
  300.9 53.9 %collective-permute-start.6 = (bf16[8,128,256]{2,1,0:T(8,128)(2,1)S(1)}, bf16[8,128,256]{2,1,0:T(8,128)(2,1)}, u32[]{:S(2)}, u32[]{:S(2)}) collective-permute-start(bf16[8,128,256]{2,1,0:T(8,128)(2,1)S(1)} %get-tuple-element.27), channel_id=1, source_target_pairs={{0,31},{1,0},{2,1},{3,2},{4,3},{5,4},{6,5},{7,6},{8,7},{9,8},{10,9... | collective-permute-start | bytes 1572872 | tf_op jit(solution)/shard_map/ppermute | solution.py:10
  302.3 56.9 %collective-permute-start.7 = (bf16[8,128,256]{2,1,0:T(8,128)(2,1)}, bf16[8,128,256]{2,1,0:T(8,128)(2,1)}, u32[]{:S(2)}, u32[]{:S(2)}) collective-permute-start(bf16[8,128,256]{2,1,0:T(8,128)(2,1)} %get-tuple-element.26), channel_id=1, source_target_pairs={{0,1},{1,2},{2,3},{3,4},{4,5},{5,6},{6,7},{7,8},{8,9},{9,10},{10,1... | collective-permute-start | bytes 1572872 | tf_op jit(solution)/shard_map/ppermute | solution.py:10
  363.7 4.6 %copy-start.8 = (bf16[4096,256]{1,0:T(8,128)(2,1)S(1)}, bf16[4096,256]{1,0:T(8,128)(2,1)}, u32[]{:S(2)}) copy-start(bf16[4096,256]{1,0:T(8,128)(2,1)} %copy-done.6) | copy-start | bytes 6291460
  363.7 4.7 %copy-start.15 = (bf16[1,4096,256]{2,1,0:T(8,128)(2,1)S(1)}, bf16[1,4096,256]{2,1,0:T(8,128)(2,1)}, u32[]{:S(2)}) copy-start(bf16[1,4096,256]{2,1,0:T(8,128)(2,1)} %fusion.8) | copy-start | bytes 6291460
  (18 other events, 47.8 us)
Sparse Core Ops, SparseCore 0:
  310.4 137.1 all-reduce.3
where the time goes:
time: 467 us; the launch traced here: 459 us
  waiting for transfers between devices  118 us (25%)
  other arithmetic  113 us (24%)
  local copies, waits for them, and re-layouts  80 us (17%)
  matrix products  72 us (15%)
  blocking collectives  44 us (9%)
  starting transfers between devices  17 us (4%)
  between operations  15.5 us (3%)
    scatter-add x2, other arithmetic, backward(): jax.ops.segment_sum(contrib.reshape(tile_count * slot_count, tile_rows, -...  76.3 us
    psum x1, waiting for transfers between devices, per_device(): lax.psum((early[0], early[1], early[2], early[3], later[0], later[1], lat...  75.5 us
    psum x1, blocking collectives, per_device(): lax.psum((early[0], early[1], early[2], early[3], later[0], later[1], lat...  44 us
    ppermute x8, waiting for transfers between devices, passed_along(): return lax.ppermute(value, axis, pairs)  42.4 us
    reshape x2, local copies, waits for them, and re-layouts, backward(): contrib.reshape(tile_count * slot_count, tile_rows, -1)  34.9 us
    gather x2, local copies, waits for them, and re-layouts, forward(): picked = extended[neighbours]  17 us
    ppermute x8, starting transfers between devices, passed_along(): return lax.ppermute(value, axis, pairs)  17 us
    dot_general x2, matrix products, backward(): jnp.einsum('tkij,tic->tkjc', adjacency, grad_gathered.reshape(tile_count,...  16.2 us
  transfers between devices with their start and end apart: 9, of which 7 were waited for; matrix products, arithmetic and copies ran while one was open for 10% of the time, Pallas kernels for 0%

commit v1 on v0

v1 whole, which is shorter than its diff:
```python
import functools

import jax
import jax.numpy as jnp
from jax import lax
from jax.experimental import pallas as pl
from jax.experimental.pallas import tpu as pltpu
from jax.sharding import PartitionSpec as P

AXES = ("dom", "phase", "feat")
PLANE = ("dom", "phase")
BF16 = jnp.bfloat16
F32 = jnp.float32
UNROLL = 8
ANY = pl.BlockSpec(memory_space=pl.ANY)
SMEM = pl.BlockSpec(memory_space=pltpu.SMEM)
VMEM_BYTES = 44 * 1024 * 1024


class Sizes:
    def __init__(self, adjacency, features, bound):
        self.tiles, self.slots, self.rows, _ = adjacency.shape
        self.cols = features.shape[-1]
        self.edge = bound.shape[-1]
        self.lent = 2 * self.edge
        self.ext = self.tiles + self.lent
        self.pairs = self.tiles * self.slots
        self.group = next(g for g in (4, 2, 1) if self.edge % g == 0 and self.tiles % g == 0)
        self.steps = self.tiles // self.group
        self.lent_steps = self.lent // self.group
        self.edge_steps = self.edge // self.group

    def nodes(self, count, dtype=BF16):
        return jax.ShapeDtypeStruct((count, self.rows, self.cols), dtype)

    def block(self, index):
        return pl.BlockSpec((self.group, self.rows, self.cols), lambda s, *_: (index(s), 0, 0))


def passed_along(value, steps):
    count = lax.axis_size(AXES)
    return lax.ppermute(value, AXES, [(i, (i + steps) % count) for i in range(count)])


def dot(a, b):
    return jnp.dot(a, b, preferred_element_type=F32)


def dot_rows(a, b):
    return lax.dot_general(a, b, (((0,), (0,)), ((), ())), preferred_element_type=F32)


def whole(shape):
    return pl.BlockSpec(shape, lambda *_: (0,) * len(shape))


def layer_of(cols, layer):
    return pl.BlockSpec((None, cols, cols), lambda *_: (layer, 0, 0))


def turned(cols, layer, which):
    return pl.BlockSpec((None, None, cols, cols), lambda *_: (layer, which, 0, 0))


def call(kernel, name, grid, prefetch, in_specs, out_specs, out_shape, scratch, flops, moved, args, aliases=None):
    return pl.pallas_call(
        kernel,
        grid_spec=pltpu.PrefetchScalarGridSpec(
            num_scalar_prefetch=prefetch,
            grid=grid,
            in_specs=in_specs,
            out_specs=out_specs,
            scratch_shapes=scratch,
        ),
        out_shape=out_shape,
        input_output_aliases=aliases or {},
        compiler_params=pltpu.CompilerParams(vmem_limit_bytes=VMEM_BYTES),
        cost_estimate=pl.CostEstimate(flops=int(flops), bytes_accessed=int(moved), transcendentals=0),
        name=name,
    )(*args)


def lend(z, bound, features):
    def kernel(bound, feats, west, east, sems):
        copies = []
        for i in range(z.edge):
            for side, target in ((0, west), (1, east)):
                copy = pltpu.make_async_copy(
                    feats.at[bound[0, side, i]], target.at[i], sems.at[side * z.edge + i]
                )
                copy.start()
                copies.append(copy)
        for copy in copies:
            copy.wait()

    return pl.pallas_call(
        kernel,
        in_specs=[SMEM, ANY],
        out_specs=[ANY, ANY],
        out_shape=[z.nodes(z.edge), z.nodes(z.edge)],
        scratch_shapes=[pltpu.SemaphoreType.DMA((z.lent,))],
        name="lend",
    )(bound, features)


def arrange(z, bound, nbrs, live, features, cot, adjacency, w_self, w_nbr, w_out):
    t, s4, r, c = z.tiles, z.slots, z.rows, z.cols

    def at_position(q, bound):
        clipped = jnp.minimum(q, z.lent - 1)
        return jnp.where(q < z.lent, bound[0, clipped // z.edge, clipped % z.edge], q)

    def kernel(bound, nbrs, live, feats, cot, adj, ws, wn, wo, f_out, m_out, ap, at, wt, meta, counts, place, inverse):
        q = pl.program_id(0)

        @pl.when(q == 0)
        def _():
            for layer in range(2):
                wt[layer, 0] = ws[layer].T
                wt[layer, 1] = wn[layer].T
                wt[layer, 2] = wo[layer].T
            for i in range(z.lent):
                inverse[bound[0, i // z.edge, i % z.edge]] = i

            def kind_of(position, target):
                return jnp.where(target < t, 0, jnp.where(position < z.lent, 2, 1))

            def count(position, carry):
                own, outer, lent = carry
                tile = at_position(position, bound)
                for k in range(s4):
                    target = nbrs[tile, k]
                    moved = jnp.where(
                        target < z.lent, inverse[jnp.minimum(target, z.lent - 1)], target
                    )
                    meta[position * s4 + k] = moved
                    kind = kind_of(position, moved)
                    own = own + jnp.where(kind == 0, 1, 0)
                    outer = outer + jnp.where(kind == 1, 1, 0)
                    lent = lent + jnp.where(kind == 2, 1, 0)
                return own, outer, lent

            zero = jnp.int32(0)
            own, outer, lent = lax.fori_loop(0, t, count, (zero, zero, zero))
            counts[0] = own
            counts[1] = outer
            counts[2] = lent

            def put(position, carry):
                own, outer, lent = carry
                for k in range(s4):
                    target = meta[position * s4 + k]
                    kind = kind_of(position, target)
                    slot = jnp.where(kind == 0, own, jnp.where(kind == 1, outer, lent))
                    place[position * s4 + k] = slot
                    meta[z.pairs + slot] = position
                    meta[2 * z.pairs + slot] = target
                    own = own + jnp.where(kind == 0, 1, 0)
                    outer = outer + jnp.where(kind == 1, 1, 0)
                    lent = lent + jnp.where(kind == 2, 1, 0)
                return own, outer, lent

            lax.fori_loop(0, t, put, (zero, own, own + outer))

        tile = at_position(q, bound)
        f_out[...] = feats[...]
        m_out[...] = jnp.where(tile < live[0], cot[...], jnp.zeros_like(cot))
        ap[0] = jnp.concatenate([adj[0, k] for k in range(s4)], axis=1)
        for k in range(s4):
            at[place[q * s4 + k]] = adj[0, k].T

    nodes_in = pl.BlockSpec((1, r, c), lambda q, bound, *_: (at_position(q, bound), 0, 0))
    nodes_out = pl.BlockSpec((1, r, c), lambda q, *_: (q, 0, 0))
    return call(
        kernel,
        "arrange",
        (t,),
        3,
        [
            nodes_in,
            nodes_in,
            pl.BlockSpec((1, s4, r, r), lambda q, bound, *_: (at_position(q, bound), 0, 0, 0)),
            whole((2, c, c)),
            whole((2, c, c)),
            whole((2, c, c)),
        ],
        [
            nodes_out,
            nodes_out,
            pl.BlockSpec((1, r, s4 * r), lambda q, *_: (q, 0, 0)),
            whole((z.pairs, r, r)),
            whole((2, 3, c, c)),
            SMEM,
            SMEM,
        ],
        [
            z.nodes(t),
            z.nodes(t),
            jax.ShapeDtypeStruct((t, r, s4 * r), BF16),
            jax.ShapeDtypeStruct((z.pairs, r, r), BF16),
            jax.ShapeDtypeStruct((2, 3, c, c), BF16),
            jax.ShapeDtypeStruct((3 * z.pairs,), jnp.int32),
            jax.ShapeDtypeStruct((8,), jnp.int32),
        ],
        [pltpu.SMEM((z.pairs,), jnp.int32), pltpu.SMEM((z.lent,), jnp.int32)],
        0,
        20 * 2**20,
        (bound, nbrs, live, features, cot, adjacency, w_self, w_nbr, w_out),
    )


def load_extended(z, own, fw, fe, ext, sems):
    copies = [
        pltpu.make_async_copy(own, ext.at[pl.ds(0, z.tiles)], sems.at[0]),
        pltpu.make_async_copy(fw, ext.at[pl.ds(z.tiles, z.edge)], sems.at[1]),
        pltpu.make_async_copy(fe, ext.at[pl.ds(z.tiles + z.edge, z.edge)], sems.at[2]),
    ]
    for copy in copies:
        copy.start()
    for copy in copies:
        copy.wait()


def aggregate(z, meta, first, ap, ext, agg):
    for g in range(z.group):
        base = (first + g) * z.slots
        picked = jnp.concatenate([ext[meta[base + k]] for k in range(z.slots)], axis=0)
        agg[g] = dot(ap[g], picked).astype(BF16)


def flat(z, value):
    return value.reshape(z.group * z.rows, z.cols)


def tiled(z, value):
    return value.reshape(z.group, z.rows, z.cols)


def live_rows(z, value, first, live):
    parts = []
    for g in range(z.group):
        part = value[g * z.rows : (g + 1) * z.rows]
        parts.append(jnp.where(first + g < live, part, jnp.zeros_like(part)))
    return jnp.concatenate(parts, axis=0)


def pre_activation(z, f, agg, ws, wn, bias, layer):
    return dot(f, ws[...]) + dot(agg, wn[...]) + bias[layer : layer + 1, :]


def sigmoid(v):
    return 1.0 / (1.0 + jnp.exp(-v))


def first_lent(z, meta, f0, fw, fe, ap, w_self, w_nbr, bias, w_out):
    def kernel(meta, own, fw, fe, ap, ws, wn, bias, wo, west, east, agg, ext, sems):
        s = pl.program_id(0)

        @pl.when(s == 0)
        def _():
            load_extended(z, own, fw, fe, ext, sems)

        first = s * z.group
        aggregate(z, meta, first, ap, ext, agg)
        f = flat(z, ext[pl.ds(first, z.group)])
        pre = pre_activation(z, f, flat(z, agg[...]), ws, wn, bias, 0)
        act = (pre * sigmoid(pre)).astype(BF16)
        out = tiled(z, (f.astype(F32) + dot(act, wo[...])).astype(BF16))

        @pl.when(s < z.edge_steps)
        def _():
            west[...] = out

        @pl.when(s >= z.edge_steps)
        def _():
            east[...] = out

    c = z.cols
    return call(
        kernel,
        "first_lent",
        (z.lent_steps,),
        1,
        [ANY, ANY, ANY, pl.BlockSpec((z.group, z.rows, z.slots * z.rows), lambda s, *_: (s, 0, 0)),
         layer_of(c, 0), layer_of(c, 0), whole((2, c)), layer_of(c, 0)],
        [
            z.block(lambda s: jnp.minimum(s, z.edge_steps - 1)),
            z.block(lambda s: jnp.maximum(s - z.edge_steps, 0)),
            z.block(lambda s: s),
        ],
        [z.nodes(z.edge), z.nodes(z.edge), z.nodes(z.tiles)],
        [pltpu.VMEM((z.ext, z.rows, z.cols), BF16), pltpu.SemaphoreType.DMA((3,))],
        2e9,
        8 * 2**20,
        (meta, f0, fw, fe, ap, w_self, w_nbr, bias, w_out),
    )


def first_rest(z, meta, bound, live, f0, fw, fe, ap, w_self, w_nbr, bias, w_out, west, east, agg0):
    rest = z.tiles - z.lent

    def kernel(meta, bound, live, own, fw, fe, ap, ws, wn, bias, wo, west, east, _agg, f1, out, agg, ext, keep, sems, more):
        s = pl.program_id(0)
        copies = [
            pltpu.make_async_copy(west, f1.at[pl.ds(0, z.edge)], more.at[0]),
            pltpu.make_async_copy(east, f1.at[pl.ds(z.edge, z.edge)], more.at[1]),
        ]
        for i in range(z.edge):
            for side, source in ((0, west), (1, east)):
                copies.append(
                    pltpu.make_async_copy(
                        source.at[i], out.at[0, bound[0, side, i]], more.at[2 + side * z.edge + i]
                    )
                )

        @pl.when(s == 0)
        def _():
            load_extended(z, own, fw, fe, ext, sems)
            for copy in copies:
                copy.start()

        first = z.lent + s * z.group
        aggregate(z, meta, first, ap, ext, agg)
        f = flat(z, ext[pl.ds(first, z.group)])
        pre = pre_activation(z, f, flat(z, agg[...]), ws, wn, bias, 0)
        act = (pre * sigmoid(pre)).astype(BF16)
        res = live_rows(z, f.astype(F32) + dot(act, wo[...]), first, live[0])
        keep[pl.ds(s * z.group, z.group)] = tiled(z, res.astype(BF16))

        @pl.when(s == pl.num_programs(0) - 1)
        def _():
            last = [
                pltpu.make_async_copy(keep, f1.at[pl.ds(z.lent, rest)], more.at[2 + z.lent]),
                pltpu.make_async_copy(keep, out.at[0, pl.ds(z.lent, rest)], more.at[3 + z.lent]),
            ]
            for copy in last:
                copy.start()
            for copy in copies + last:
                copy.wait()

    c = z.cols
    return call(
        kernel,
        "first_rest",
        (z.steps - z.lent_steps,),
        3,
        [ANY, ANY, ANY,
         pl.BlockSpec((z.group, z.rows, z.slots * z.rows), lambda s, *_: (s + z.lent_steps, 0, 0)),
         layer_of(c, 0), layer_of(c, 0), whole((2, c)), layer_of(c, 0), ANY, ANY, ANY],
        [ANY, ANY, z.block(lambda s: s + z.lent_steps)],
        [
            z.nodes(z.tiles),
            jax.ShapeDtypeStruct((2, z.tiles, z.rows, z.cols), BF16),
            z.nodes(z.tiles),
        ],
        [
            pltpu.VMEM((z.ext, z.rows, z.cols), BF16),
            pltpu.VMEM((rest, z.rows, z.cols), BF16),
            pltpu.SemaphoreType.DMA((3,)),
            pltpu.SemaphoreType.DMA((4 + z.lent,)),
        ],
        2e9,
        12 * 2**20,
        (meta, bound, live, f0, fw, fe, ap, w_self, w_nbr, bias, w_out, west, east, agg0),
        {13: 2},
    )


def spread(z, meta, start, stop, at, source, acc, shift, spare):
    def body(i, carry):
        for u in range(UNROLL):
            pair = start + i * UNROLL + u
            inside = pair < stop
            pair = jnp.minimum(pair, z.pairs - 1)
            target = jnp.where(inside, meta[2 * z.pairs + pair] - shift, spare)
            acc[target] += dot(at[pair], source[meta[z.pairs + pair]])
        return carry

    lax.fori_loop(0, (stop - start + UNROLL - 1) // UNROLL, body, 0)


def second(z, meta, counts, f1, fw, fe, ap, at, m1, w_self, w_nbr, bias, wt):
    def kernel(meta, counts, own, fw, fe, ap, at_hbm, m, ws, wn, bias, wnt, wot,
               agg, act, dpre, dagg, to_west, to_east, ext, at, kept, acc, sems, at_sem):
        s = pl.program_id(0)
        at_copy = pltpu.make_async_copy(at_hbm, at, at_sem)

        @pl.when(s == 0)
        def _():
            load_extended(z, own, fw, fe, ext, sems)
            at_copy.start()

        first = s * z.group
        aggregate(z, meta, first, ap, ext, agg)
        f = flat(z, ext[pl.ds(first, z.group)])
        pre = pre_activation(z, f, flat(z, agg[...]), ws, wn, bias, 1)
        sig = sigmoid(pre)
        act[...] = tiled(z, (pre * sig).astype(BF16))
        slope = sig * (1.0 + pre * (1.0 - sig))
        grad = (dot(flat(z, m[...]), wot[...]) * slope).astype(BF16)
        dpre[...] = tiled(z, grad)
        back = tiled(z, dot(grad, wnt[...]).astype(BF16))
        dagg[...] = back
        kept[pl.ds(first, z.group)] = back

        @pl.when(s == pl.num_programs(0) - 1)
        def _():
            at_copy.wait()
            acc[...] = jnp.zeros_like(acc)
            spread(z, meta, counts[0], z.pairs, at, kept, acc, z.tiles, z.lent)
            to_west[...] = acc[pl.ds(0, z.edge)].astype(BF16)
            to_east[...] = acc[pl.ds(z.edge, z.edge)].astype(BF16)

    c = z.cols
    edge_whole = whole((z.edge, z.rows, z.cols))
    return call(
        kernel,
        "second",
        (z.steps,),
        2,
        [ANY, ANY, ANY, pl.BlockSpec((z.group, z.rows, z.slots * z.rows), lambda s, *_: (s, 0, 0)),
         ANY, z.block(lambda s: s), layer_of(c, 1), layer_of(c, 1), whole((2, c)),
         turned(c, 1, 1), turned(c, 1, 2)],
        [z.block(lambda s: s)] * 4 + [edge_whole, edge_whole],
        [z.nodes(z.tiles)] * 4 + [z.nodes(z.edge)] * 2,
        [
            pltpu.VMEM((z.ext, z.rows, z.cols), BF16),
            pltpu.VMEM((z.pairs, z.rows, z.rows), BF16),
            pltpu.VMEM((z.tiles, z.rows, z.cols), BF16),
            pltpu.VMEM((z.lent + 1, z.rows, z.cols), F32),
            pltpu.SemaphoreType.DMA((3,)),
            pltpu.SemaphoreType.DMA,
        ],
        5e9,
        20 * 2**20,
        (meta, counts, f1, fw, fe, ap, at, m1, w_self, w_nbr, bias, wt, wt),
    )


def weight_grads(z, me, pieces, f, agg, act, m, dpre, name):
    c = z.cols
    piece = -(-(3 * c + 1) // (pieces * 16)) * 16
    height = piece * pieces

    def kernel(me, f, agg, act, m, dpre, *rest):
        outs, acc = rest[:-1], rest[-1]
        s = pl.program_id(0)

        @pl.when(s == 0)
        def _():
            acc[...] = jnp.zeros_like(acc)

        grad = flat(z, dpre[...])
        acc[pl.ds(0, c), :] += dot_rows(flat(z, f[...]), grad)
        acc[pl.ds(c, c), :] += dot_rows(flat(z, agg[...]), grad)
        acc[pl.ds(2 * c, c), :] += dot_rows(flat(z, act[...]), flat(z, m[...]))
        acc[pl.ds(3 * c, 1), :] += jnp.sum(grad.astype(F32), axis=0, keepdims=True)

        @pl.when(s == pl.num_programs(0) - 1)
        def _():
            for i in range(pieces):
                owner = lax.rem(me[0] + i, pieces)
                start = pl.multiple_of(owner * piece, 16)
                outs[i][...] = acc[pl.ds(start, piece), :].astype(BF16)

    return call(
        kernel,
        name,
        (z.steps,),
        1,
        [z.block(lambda s: s)] * 5,
        [whole((piece, c))] * pieces,
        [jax.ShapeDtypeStruct((piece, c), BF16)] * pieces,
        [pltpu.VMEM((height, c), F32)],
        4e9,
        10 * 2**20,
        (me, f, agg, act, m, dpre),
    )


def plane_pass(value, steps):
    count = lax.axis_size(PLANE)
    return lax.ppermute(value, PLANE, [(i, (i + steps) % count) for i in range(count)])


def added(parts):
    total = parts[0].astype(F32)
    for part in parts[1:]:
        total = total + part.astype(F32)
    return total.astype(BF16)


def summed_over_parts(pieces):
    count = len(pieces)
    share = added([pieces[0]] + [plane_pass(pieces[i], i) for i in range(1, count)])
    lines = lax.axis_size("feat")
    if lines & (lines - 1) == 0:
        step = 1
        while step < lines:
            other = lax.ppermute(share, "feat", [(i, i ^ step) for i in range(lines)])
            share = added([share, other])
            step *= 2
    else:
        share = lax.psum(share.astype(F32), "feat").astype(BF16)
    return [share] + [plane_pass(share, i) for i in range(1, count)]


def unpack(z, me, early, late):
    c = z.cols
    count = len(early)
    piece = early[0].shape[0]

    def kernel(me, *refs):
        ins, (g_self, g_nbr, g_bias, g_out, buf) = refs[: 2 * count], refs[2 * count :]
        for layer in range(2):
            for i in range(count):
                owner = lax.rem(me[0] + count - i, count)
                start = pl.multiple_of(owner * piece, 16)
                buf[pl.ds(start, piece), :] = ins[layer * count + i][...].astype(F32)
            g_self[layer] = buf[pl.ds(0, c), :]
            g_nbr[layer] = buf[pl.ds(c, c), :]
            g_out[layer] = buf[pl.ds(2 * c, c), :]
            g_bias[layer : layer + 1, :] = buf[pl.ds(3 * c, 1), :]

    square = jax.ShapeDtypeStruct((2, c, c), F32)
    return call(
        kernel,
        "unpack",
        (1,),
        1,
        [whole((piece, c))] * (2 * count),
        [whole((2, c, c)), whole((2, c, c)), whole((2, c)), whole((2, c, c))],
        [square, square, jax.ShapeDtypeStruct((2, c), F32), square],
        [pltpu.VMEM((piece * count, c), F32)],
        0,
        3 * 2**20,
        (me, *early, *late),
    )


def second_out(z, bound, live, f1, act, w_out, out):
    def kernel(bound, live, f, act, wo, _out, out, keep, sems):
        s = pl.program_id(0)
        first = s * z.group
        res = flat(z, f[...]).astype(F32) + dot(flat(z, act[...]), wo[...])
        keep[pl.ds(first, z.group)] = tiled(z, live_rows(z, res, first, live[0]).astype(BF16))

        @pl.when(s == pl.num_programs(0) - 1)
        def _():
            rest = z.tiles - z.lent
            copies = [
                pltpu.make_async_copy(
                    keep.at[i], out.at[1, bound[0, i // z.edge, i % z.edge]], sems.at[i]
                )
                for i in range(z.lent)
            ]
            copies.append(
                pltpu.make_async_copy(
                    keep.at[pl.ds(z.lent, rest)], out.at[1, pl.ds(z.lent, rest)], sems.at[z.lent]
                )
            )
            for copy in copies:
                copy.start()
            for copy in copies:
                copy.wait()

    return call(
        kernel,
        "second_out",
        (z.steps,),
        2,
        [z.block(lambda s: s), z.block(lambda s: s), layer_of(z.cols, 1), ANY],
        ANY,
        jax.ShapeDtypeStruct(out.shape, BF16),
        [pltpu.VMEM((z.tiles, z.rows, z.cols), BF16), pltpu.SemaphoreType.DMA((z.lent + 1,))],
        5e8,
        6 * 2**20,
        (bound, live, f1, act, w_out, out),
        {5: 0},
    )


def input_grad(z, layer, meta, counts, live, m, dpre, dagg, at, wt, grads):
    rest = z.tiles - z.lent
    fresh = grads is None

    def kernel(meta, counts, live, m, dpre, dagg_hbm, at_hbm, wst, *refs):
        if not fresh:
            refs = refs[1:]
        grads, part, masked, at, dagg, acc, keep, sems = refs
        s = pl.program_id(0)

        @pl.when(s == 0)
        def _():
            copies = [
                pltpu.make_async_copy(at_hbm, at, sems.at[0]),
                pltpu.make_async_copy(dagg_hbm, dagg, sems.at[1]),
            ]
            for copy in copies:
                copy.start()
            acc[...] = jnp.zeros_like(acc)
            for copy in copies:
                copy.wait()
            spread(z, meta, 0, counts[0], at, dagg, acc, 0, z.tiles)

        first = s * z.group
        res = flat(z, m[...]).astype(F32) + dot(flat(z, dpre[...]), wst[...])
        res = res + flat(z, acc[pl.ds(first, z.group)])

        @pl.when(s < z.lent_steps)
        def _():
            part[...] = tiled(z, res)

        @pl.when(s >= z.lent_steps)
        def _():
            keep[pl.ds(first - z.lent, z.group)] = tiled(z, res.astype(BF16))
            masked[...] = tiled(z, live_rows(z, res, first, live[0]).astype(BF16))

        @pl.when(s == pl.num_programs(0) - 1)
        def _():
            copy = pltpu.make_async_copy(keep, grads.at[layer, pl.ds(z.lent, rest)], sems.at[2])
            copy.start()
            copy.wait()

    args = [meta, counts, live, m, dpre, dagg, at, wt]
    in_specs = [z.block(lambda s: s), z.block(lambda s: s), ANY, ANY, turned(z.cols, layer, 0)]
    if not fresh:
        args.append(grads)
        in_specs.append(ANY)
    return call(
        kernel,
        "input_grad%d" % layer,
        (z.steps,),
        3,
        in_specs,
        [
            ANY,
            z.block(lambda s: jnp.minimum(s, z.lent_steps - 1)),
            z.block(lambda s: jnp.maximum(s, z.lent_steps)),
        ],
        [
            jax.ShapeDtypeStruct((2, z.tiles, z.rows, z.cols), BF16),
            z.nodes(z.lent, F32),
            z.nodes(z.tiles),
        ],
        [
            pltpu.VMEM((z.pairs, z.rows, z.rows), BF16),
            pltpu.VMEM((z.tiles, z.rows, z.cols), BF16),
            pltpu.VMEM((z.tiles + 1, z.rows, z.cols), F32),
            pltpu.VMEM((rest, z.rows, z.cols), BF16),
            pltpu.SemaphoreType.DMA((3,)),
        ],
        2e9,
        18 * 2**20,
        args,
        None if fresh else {8: 0},
    )


def early_rest(z, meta, counts, f0, agg0, m0, at, w_self, w_nbr, bias, wt):
    def kernel(meta, counts, f, agg, m, at_hbm, ws, wn, bias, wnt, wot,
               act, slope_out, dpre, dagg, part, at, kept, acc, sem):
        s = pl.program_id(0)
        copy = pltpu.make_async_copy(at_hbm, at, sem)

        @pl.when(s == 0)
        def _():
            copy.start()

        pre = pre_activation(z, flat(z, f[...]), flat(z, agg[...]), ws, wn, bias, 0)
        sig = sigmoid(pre)
        act[...] = tiled(z, (pre * sig).astype(BF16))
        slope = sig * (1.0 + pre * (1.0 - sig))

        @pl.when(s < z.lent_steps)
        def _():
            slope_out[...] = tiled(z, slope)

        @pl.when(s >= z.lent_steps)
        def _():
            grad = (dot(flat(z, m[...]), wot[...]) * slope).astype(BF16)
            dpre[...] = tiled(z, grad)
            back = tiled(z, dot(grad, wnt[...]).astype(BF16))
            dagg[...] = back
            kept[pl.ds(s * z.group, z.group)] = back

        @pl.when(s == pl.num_programs(0) - 1)
        def _():
            copy.wait()
            acc[...] = jnp.zeros_like(acc)
            spread(z, meta, counts[0], counts[0] + counts[1], at, kept, acc, z.tiles, z.lent)
            part[...] = acc[pl.ds(0, z.lent)]

    c = z.cols
    late = lambda s: jnp.maximum(s, z.lent_steps)
    return call(
        kernel,
        "early_rest",
        (z.steps,),
        2,
        [z.block(lambda s: s), z.block(lambda s: s), z.block(late), ANY,
         layer_of(c, 0), layer_of(c, 0), whole((2, c)), turned(c, 0, 1), turned(c, 0, 2)],
        [
            z.block(lambda s: s),
            z.block(lambda s: jnp.minimum(s, z.lent_steps - 1)),
            z.block(late),
            z.block(late),
            whole((z.lent, z.rows, z.cols)),
        ],
        [z.nodes(z.tiles), z.nodes(z.lent, F32), z.nodes(z.tiles), z.nodes(z.tiles), z.nodes(z.lent, F32)],
        [
            pltpu.VMEM((z.pairs, z.rows, z.rows), BF16),
            pltpu.VMEM((z.tiles, z.rows, z.cols), BF16),
            pltpu.VMEM((z.lent + 1, z.rows, z.cols), F32),
            pltpu.SemaphoreType.DMA,
        ],
        4e9,
        20 * 2**20,
        (meta, counts, f0, agg0, m0, at, w_self, w_nbr, bias, wt, wt),
    )


def early_lent(z, meta, counts, bound, part, fw, fe, slope, outer, at, wt, m0, dpre0, dagg0, grads):
    def kernel(meta, counts, bound, part, fw, fe, slope, outer, at_hbm, wnt, wot, _m, _d, _a, _g,
               m, dpre, dagg, grads, to_west, to_east, at, kept, acc, keep, sem, sems):
        s = pl.program_id(0)
        at_copy = pltpu.make_async_copy(at_hbm, at, sem)

        @pl.when(s == 0)
        def _():
            at_copy.start()

        got = jnp.where(s < z.edge_steps, fw[...], fe[...])
        g = flat(z, (part[...] + got.astype(F32)).astype(BF16))
        m[...] = tiled(z, g)
        keep[pl.ds(s * z.group, z.group)] = tiled(z, g)
        grad = (dot(g, wot[...]) * flat(z, slope[...])).astype(BF16)
        dpre[...] = tiled(z, grad)
        back = tiled(z, dot(grad, wnt[...]).astype(BF16))
        dagg[...] = back
        kept[pl.ds(s * z.group, z.group)] = back

        @pl.when(s == pl.num_programs(0) - 1)
        def _():
            copies = [
                pltpu.make_async_copy(
                    keep.at[i], grads.at[1, bound[0, i // z.edge, i % z.edge]], sems.at[i]
                )
                for i in range(z.lent)
            ]
            for copy in copies:
                copy.start()
            at_copy.wait()
            acc[pl.ds(0, z.lent)] = outer[...]
            spread(z, meta, counts[0] + counts[1], z.pairs, at, kept, acc, z.tiles, z.lent)
            to_west[...] = acc[pl.ds(0, z.edge)].astype(BF16)
            to_east[...] = acc[pl.ds(z.edge, z.edge)].astype(BF16)
            for copy in copies:
                copy.wait()

    c = z.cols
    edge_whole = whole((z.edge, z.rows, z.cols))
    return call(
        kernel,
        "early_lent",
        (z.lent_steps,),
        3,
        [
            z.block(lambda s: s),
            z.block(lambda s: jnp.minimum(s, z.edge_steps - 1)),
            z.block(lambda s: jnp.maximum(s - z.edge_steps, 0)),
            z.block(lambda s: s),
            whole((z.lent, z.rows, z.cols)),
            ANY,
            turned(c, 0, 1),
            turned(c, 0, 2),
            ANY,
            ANY,
            ANY,
            ANY,
        ],
        [z.block(lambda s: s)] * 3 + [ANY, edge_whole, edge_whole],
        [z.nodes(z.tiles)] * 3 + [jax.ShapeDtypeStruct(grads.shape, BF16)] + [z.nodes(z.edge)] * 2,
        [
            pltpu.VMEM((z.pairs, z.rows, z.rows), BF16),
            pltpu.VMEM((z.lent, z.rows, z.cols), BF16),
            pltpu.VMEM((z.lent + 1, z.rows, z.cols), F32),
            pltpu.VMEM((z.lent, z.rows, z.cols), BF16),
            pltpu.SemaphoreType.DMA,
            pltpu.SemaphoreType.DMA((z.lent,)),
        ],
        2e9,
        14 * 2**20,
        (meta, counts, bound, part, fw, fe, slope, outer, at, wt, wt, m0, dpre0, dagg0, grads),
        {11: 0, 12: 1, 13: 2, 14: 3},
    )


def finish(z, bound, part, fw, fe, grads):
    def kernel(bound, part, fw, fe, _g, grads, keep, sems):
        s = pl.program_id(0)
        got = jnp.where(s < z.edge_steps, fw[...], fe[...])
        keep[pl.ds(s * z.group, z.group)] = (part[...] + got.astype(F32)).astype(BF16)

        @pl.when(s == pl.num_programs(0) - 1)
        def _():
            copies = [
                pltpu.make_async_copy(
                    keep.at[i], grads.at[0, bound[0, i // z.edge, i % z.edge]], sems.at[i]
                )
                for i in range(z.lent)
            ]
            for copy in copies:
                copy.start()
            for copy in copies:
                copy.wait()

    return call(
        kernel,
        "finish",
        (z.lent_steps,),
        1,
        [
            z.block(lambda s: s),
            z.block(lambda s: jnp.minimum(s, z.edge_steps - 1)),
            z.block(lambda s: jnp.maximum(s - z.edge_steps, 0)),
            ANY,
        ],
        ANY,
        jax.ShapeDtypeStruct(grads.shape, BF16),
        [pltpu.VMEM((z.lent, z.rows, z.cols), BF16), pltpu.SemaphoreType.DMA((z.lent,))],
        0,
        4 * 2**20,
        (bound, part, fw, fe, grads),
        {4: 0},
    )


def per_device(
    node_in, out_cot, adjacency, tile_nbrs, bound_tiles, live_tiles, w_self, w_nbr, pre_bias, w_out
):
    z = Sizes(adjacency, node_in, bound_tiles)
    t, r, c = z.tiles, z.rows, z.cols
    features = node_in.reshape(t, r, c)
    cot = out_cot.reshape(t, r, c)
    pieces = lax.axis_size(PLANE)
    me = lax.axis_index(PLANE).astype(jnp.int32).reshape(1)

    west, east = lend(z, bound_tiles, features)
    from_west = passed_along(east, 1)
    from_east = passed_along(west, -1)
    f0, m1, ap, at, wt, meta, counts = arrange(
        z, bound_tiles, tile_nbrs, live_tiles, features, cot, adjacency, w_self, w_nbr, w_out
    )

    west, east, agg0 = first_lent(z, meta, f0, from_west, from_east, ap, w_self, w_nbr, pre_bias, w_out)
    next_west = passed_along(east, 1)
    next_east = passed_along(west, -1)
    f1, section_out, agg0 = first_rest(
        z, meta, bound_tiles, live_tiles, f0, from_west, from_east, ap, w_self, w_nbr, pre_bias, w_out,
        west, east, agg0,
    )

    agg1, act1, dpre1, dagg1, to_west, to_east = second(
        z, meta, counts, f1, next_west, next_east, ap, at, m1, w_self, w_nbr, pre_bias, wt
    )
    back_west = passed_along(to_east, 1)
    back_east = passed_along(to_west, -1)
    grads, part, m0 = input_grad(z, 1, meta, counts, live_tiles, m1, dpre1, dagg1, at, wt, None)
    late = summed_over_parts(weight_grads(z, me, pieces, f1, agg1, act1, m1, dpre1, "weight_grads1"))
    act0, slope, dpre0, dagg0, outer = early_rest(
        z, meta, counts, f0, agg0, m0, at, w_self, w_nbr, pre_bias, wt
    )
    section_out = second_out(z, bound_tiles, live_tiles, f1, act1, w_out, section_out)

    m0, dpre0, dagg0, grads, to_west, to_east = early_lent(
        z, meta, counts, bound_tiles, part, back_west, back_east, slope, outer, at, wt, m0, dpre0, dagg0, grads
    )
    back_west = passed_along(to_east, 1)
    back_east = passed_along(to_west, -1)
    early = summed_over_parts(weight_grads(z, me, pieces, f0, agg0, act0, m0, dpre0, "weight_grads0"))
    grads, part, _ = input_grad(z, 0, meta, counts, live_tiles, m0, dpre0, dagg0, at, wt, grads)
    grads = finish(z, bound_tiles, part, back_west, back_east, grads)

    grad_self, grad_nbr, grad_bias, grad_out = unpack(z, me, early, late)
    return (
        section_out.reshape(2, t * r, c),
        grads.reshape(2, t * r, c),
        grad_self,
        grad_nbr,
        grad_bias,
        grad_out,
    )


def solution(mesh):
    rows = P(AXES)
    in_specs = (rows, rows, rows, rows, rows, rows, P(), P(), P(), P())
    out_specs = (P(None, AXES), P(None, AXES), P(), P(), P(), P())
    return jax.shard_map(
        per_device, mesh=mesh, in_specs=in_specs, out_specs=out_specs, check_vma=False
    )
```

time: 467 us -> 252 us (0.54); the launches traced: 459 us -> 250 us
  Pallas kernels: 0 us -> 148 us
  other arithmetic: 113 us -> 0.21 us
  waiting for transfers between devices: 118 us -> 30 us
  matrix products: 72 us -> 0 us
  local copies, waits for them, and re-layouts: 80 us -> 19.7 us
  blocking collectives: 44 us -> 0 us
  starting transfers between devices: 17 us -> 50.9 us
  between operations: 15.5 us -> 1.73 us
    pallas_call x0 -> x14, Pallas kernels: none -> 148 us  [the longest x13 114 us: call(): pl.pallas_call(kernel, grid_spec=pltpu.PrefetchScalarGridSpec(num_scalar_...]
    scatter-add x6 -> x0, other arithmetic: 89.6 us -> none  [the longest x2 76.3 us: backward(): jax.ops.segment_sum(contrib.reshape(tile_count * slot_count, tile_rows, -...]
    psum x1 -> x0, waiting for transfers between devices: 75.5 us -> none  [per_device(): lax.psum((early[0], early[1], early[2], early[3], later[0], later[1], lat...]
    dot_general x22 -> x0, matrix products: 72 us -> none  [the longest x2 16.2 us: backward(): jnp.einsum('tkij,tic->tkjc', adjacency, grad_gathered.reshape(tile_count,...]
    psum x1 -> x0, blocking collectives: 44 us -> none  [per_device(): lax.psum((early[0], early[1], early[2], early[3], later[0], later[1], lat...]
    reshape x2 -> x0, local copies, waits for them, and re-layouts: 34.9 us -> none  [backward(): contrib.reshape(tile_count * slot_count, tile_rows, -1)]
    ppermute x8 -> x40, starting transfers between devices: 17 us -> 50.9 us  [the longest x28 27.7 us: plane_pass(): lax.ppermute(value, PLANE, [(i, (i + steps) % count) for i in range(count)])]
    gather x6 -> x0, local copies, waits for them, and re-layouts: 24.1 us -> none  [the longest x2 17 us: forward(): picked = extended[neighbours]]
  transfers between devices with their start and end apart: 9 -> 40, of which waited for: 7 -> 8; matrix products, arithmetic and copies ran while one was open for 10% -> 0% of each run, Pallas kernels for 0% -> 34%
where the time goes in v1:
time: 252 us; the launch traced here: 250 us
  Pallas kernels  148 us (59%)
  starting transfers between devices  50.9 us (20%)
  waiting for transfers between devices  30 us (12%)
  local copies, waits for them, and re-layouts  19.7 us (8%)
    pallas_call x13, Pallas kernels, call(): pl.pallas_call(kernel, grid_spec=pltpu.PrefetchScalarGridSpec(num_scalar_...  114 us
    pallas_call x1, Pallas kernels, lend(): pl.pallas_call(kernel, in_specs=[SMEM, ANY], out_specs=[ANY, ANY], out_sh...  33.8 us
    ppermute x28, starting transfers between devices, plane_pass(): lax.ppermute(value, PLANE, [(i, (i + steps) % count) for i in range(count)])  27.7 us
    unnamed x73, local copies, waits for them, and re-layouts  19.7 us
    ppermute x8, starting transfers between devices, passed_along(): lax.ppermute(value, AXES, [(i, (i + steps) % count) for i in range(count)])  19.2 us
    ppermute x8, waiting for transfers between devices, passed_along(): lax.ppermute(value, AXES, [(i, (i + steps) % count) for i in range(count)])  17.6 us
    ppermute x28, waiting for transfers between devices, plane_pass(): lax.ppermute(value, PLANE, [(i, (i + steps) % count) for i in range(count)])  9.89 us
  transfers between devices with their start and end apart: 40, of which 8 were waited for; matrix products, arithmetic and copies ran while one was open for 0% of the time, Pallas kernels for 34%

profile of v1, /device:TPU:0, one launch (start us, length us, event | category | flops | bytes accessed | tf_op | source)
XLA Modules:
  0.0 250.3 jit_solution(481794858399503367)
XLA Ops:
  0.7 33.8 %lend.1 = (bf16[8,128,256]{2,1,0:T(8,128)(2,1)}, bf16[8,128,256]{2,1,0:T(8,128)(2,1)}) custom-call(s32[1,2,8]{2,1,0:T(2,128)} %bound.11, bf16[32,128,256]{2,1,0:T(8,128)(2,1)} %bitcast.5), custom_call_target="tpu_custom_call" | custom-call | tf_op jit(solution)/shard_map/lend/pallas_call | solution.py:96
  34.5 3.1 %collective-permute-start = (bf16[8,128,256]{2,1,0:T(8,128)(2,1)}, bf16[8,128,256]{2,1,0:T(8,128)(2,1)}, u32[]{:S(2)}, u32[]{:S(2)}) collective-permute-start(bf16[8,128,256]{2,1,0:T(8,128)(2,1)} %get-tuple-element.65), channel_id=1, source_target_pairs={{0,1},{1,2},{2,3},{3,4},{4,5},{5,6},{6,7},{7,8},{8,9},{9,10},{10,1... | collective-permute-start | bytes 1572872 | tf_op jit(solution)/shard_map/ppermute | solution.py:42
  37.6 3.4 %collective-permute-start.1 = (bf16[8,128,256]{2,1,0:T(8,128)(2,1)}, bf16[8,128,256]{2,1,0:T(8,128)(2,1)}, u32[]{:S(2)}, u32[]{:S(2)}) collective-permute-start(bf16[8,128,256]{2,1,0:T(8,128)(2,1)} %get-tuple-element.66), channel_id=1, source_target_pairs={{0,31},{1,0},{2,1},{3,2},{4,3},{5,4},{6,5},{7,6},{8,7},{9,8},{10,9... | collective-permute-start | bytes 1572872 | tf_op jit(solution)/shard_map/ppermute | solution.py:42
  46.2 23.5 %arrange.1 = (bf16[32,128,256]{2,1,0:T(8,128)(2,1)S(1)}, bf16[32,128,256]{2,1,0:T(8,128)(2,1)S(1)}, bf16[32,128,512]{2,1,0:T(8,128)(2,1)}, bf16[128,128,128]{2,1...) custom-call(s32[1,2,8]{2,1,0:T(2,128)S(1)} %copy-done.33, ...), custom_call_target="tpu_custom_call" | custom-call | bytes 20971520 | tf_op jit(solution)/shard_map/arrange/pallas_call | solution.py:66
  71.0 6.5 %first_lent.1 = (bf16[8,128,256]{2,1,0:T(8,128)(2,1)S(1)}, bf16[8,128,256]{2,1,0:T(8,128)(2,1)S(1)}, bf16[32,128,256]{2,1,0:T(8,128)(2,1)S(1)}) custom-call(s32[384]{0:T(512)S(1)} %get-tuple-element.63.meta, bf16[32,128,256]{2,1,0:T(8,128)(2,1)S(1)} %get-tuple-element.64.own.f, bf16[8,128,256]{2,1,0:T(8,128)(2,1)} %collective-permute-done.fw, ...), custom_call_target="tpu_custom_call" | custom-call | flops 2000000000 | bytes 8388608 | tf_op jit(solution)/shard_map/first_lent/pallas_call | solution.py:66
  84.1 7.5 %first_rest.1 = (bf16[32,128,256]{2,1,0:T(8,128)(2,1)S(1)}, bf16[2,32,128,256]{3,2,1,0:T(8,128)(2,1)}, bf16[32,128,256]{2,1,0:T(8,128)(2,1)S(1)}) custom-call(s32[384]{0:T(512)S(1)} %get-tuple-element.63.meta, s32[1,2,8]{2,1,0:T(2,128)S(1)} %copy-done.33, s32[1]{0:T(128)S(6)} %copy.33.live, ...), custom_call_target="tpu_custom_call", output_to_operand_aliasing={{2}: (13, {})} | custom-call | flops 2000000000 | bytes 12582912 | tf_op jit(solution)/shard_map/first_rest/pallas_call | solution.py:66
  94.3 9.4 %collective-permute-done.3.fe = bf16[8,128,256]{2,1,0:T(8,128)(2,1)S(1)} collective-permute-done((bf16[8,128,256]{2,1,0:T(8,128)(2,1)S(1)}, bf16[8,128,256]{2,1,0:T(8,128)(2,1)S(1)}, u32[]{:S(2)}, u32[]{:S(2)}) %collective-permute-start.3) | collective-permute-done | bytes 524320 | tf_op jit(solution)/shard_map/ppermute | solution.py:42
  103.7 14.7 %second.1 = (bf16[32,128,256]{2,1,0:T(8,128)(2,1)S(1)}, bf16[32,128,256]{2,1,0:T(8,128)(2,1)S(1)}, bf16[32,128,256]{2,1,0:T(8,128)(2,1)S(1)}, bf16[32,128,256]{2...) custom-call(s32[384]{0:T(512)S(1)} %get-tuple-element.63.meta, ...), custom_call_target="tpu_custom_call" | custom-call | flops 5000000000 | bytes 20971520 | tf_op jit(solution)/shard_map/second/pallas_call | solution.py:66
  119.8 6.6 %weight_grads1.1 = (bf16[112,256]{1,0:T(8,128)(2,1)S(1)}, bf16[112,256]{1,0:T(8,128)(2,1)S(1)}, bf16[112,256]{1,0:T(8,128)(2,1)S(1)}, bf16[112,256]{1,0:T(8,128)...) custom-call(s32[1]{0:T(128)} %bitcast.4.me, ...), custom_call_target="tpu_custom_call" | custom-call | flops 4000000000 | bytes 10485760 | tf_op jit(solution)/shard_map/weight_grads1/pallas_call | solution.py:66
  127.0 2.2 collective-permute-start.26
  131.7 10.2 %input_grad1.1 = (bf16[2,32,128,256]{3,2,1,0:T(8,128)(2,1)}, f32[16,128,256]{2,1,0:T(8,128)S(1)}, bf16[32,128,256]{2,1,0:T(8,128)(2,1)S(1)}) custom-call(s32[384]{0:T(512)S(1)} %get-tuple-element.63.meta, s32[8]{0:T(128)S(1)} %get-tuple-element.72.counts, s32[1]{0:T(128)S(6)} %copy.33.live, bf16[32,128,256]{2,1,0:T(8,128)(2,1)S(1)} %copy-done.19, ...), custom_call_target="tpu_custom_call" | custom-call | flops 2000000000 | bytes 18874368 | tf_op jit(solution)/shard_map/input_grad1/pallas_call | solution.py:66
  147.6 4.3 %collective-permute-start.5 = (bf16[8,128,256]{2,1,0:T(8,128)(2,1)S(1)}, bf16[8,128,256]{2,1,0:T(8,128)(2,1)S(1)}, u32[]{:S(2)}, u32[]{:S(2)}) collective-permute-start(bf16[8,128,256]{2,1,0:T(8,128)(2,1)S(1)} %get-tuple-element.82), channel_id=1, source_target_pairs={{0,31},{1,0},{2,1},{3,2},{4,3},{5,4},{6,5},{7,6},{8,7},{9,8},{10,9... | collective-permute-start | bytes 1572872 | tf_op jit(solution)/shard_map/ppermute | solution.py:42
  152.0 11.5 %early_rest.1 = (bf16[32,128,256]{2,1,0:T(8,128)(2,1)S(1)}, f32[16,128,256]{2,1,0:T(8,128)S(1)}, bf16[32,128,256]{2,1,0:T(8,128)(2,1)S(1)}, bf16[32,128,256]{2,1,0:T(8,128)(2,1)S(1)}, f32[16,128,256]{2,1,0:T(8,128)}) custom-call(s32[384]{0:T(512)S(1)} %get-tuple-element.63.meta, s32[8]{0:T(128)S(1)} %get-tuple-element.72.counts, ...), custom_call_target="tpu_custom_call" | custom-call | flops 4000000000 | bytes 20971520 | tf_op jit(solution)/shard_map/early_rest/pallas_call | solution.py:66
  165.0 8.2 %collective-permute-done.5.fe = bf16[8,128,256]{2,1,0:T(8,128)(2,1)S(1)} collective-permute-done((bf16[8,128,256]{2,1,0:T(8,128)(2,1)S(1)}, bf16[8,128,256]{2,1,0:T(8,128)(2,1)S(1)}, u32[]{:S(2)}, u32[]{:S(2)}) %collective-permute-start.5) | collective-permute-done | bytes 524320 | tf_op jit(solution)/shard_map/ppermute | solution.py:42
  173.2 7.8 %early_lent.1 = (bf16[32,128,256]{2,1,0:T(8,128)(2,1)S(1)}, bf16[32,128,256]{2,1,0:T(8,128)(2,1)S(1)}, bf16[32,128,256]{2,1,0:T(8,128)(2,1)S(1)}, bf16[2,32,128,...) custom-call(s32[384]{0:T(512)S(1)} %get-tuple-element.63.meta, ...), custom_call_target="tpu_custom_call", output_to_operand_aliasing={{0}: (11, {}), {1}: (12, {}), {2}: (13, {}), {3}: (14, {})} | custom-call | flops 2000000000 | bytes 14680064 | tf_op jit(solution)/shard_map/early_lent/pallas_call | solution.py:66
  182.4 6.9 %weight_grads0.1 = (bf16[112,256]{1,0:T(8,128)(2,1)S(1)}, bf16[112,256]{1,0:T(8,128)(2,1)S(1)}, bf16[112,256]{1,0:T(8,128)(2,1)S(1)}, bf16[112,256]{1,0:T(8,128)...) custom-call(s32[1]{0:T(128)} %bitcast.4.me, ...), custom_call_target="tpu_custom_call" | custom-call | flops 4000000000 | bytes 10485760 | tf_op jit(solution)/shard_map/weight_grads0/pallas_call | solution.py:66
  199.7 2.3 collective-permute-done.32
  209.5 3.9 %collective-permute-start.7 = (bf16[8,128,256]{2,1,0:T(8,128)(2,1)S(1)}, bf16[8,128,256]{2,1,0:T(8,128)(2,1)S(1)}, u32[]{:S(2)}, u32[]{:S(2)}) collective-permute-start(bf16[8,128,256]{2,1,0:T(8,128)(2,1)S(1)} %get-tuple-element.96), channel_id=1, source_target_pairs={{0,31},{1,0},{2,1},{3,2},{4,3},{5,4},{6,5},{7,6},{8,7},{9,8},{10,9... | collective-permute-start | bytes 1572872 | tf_op jit(solution)/shard_map/ppermute | solution.py:42
  217.1 7.1 %collective-permute-done.33.refs_9_ = bf16[112,256]{1,0:T(8,128)(2,1)S(1)} collective-permute-done((bf16[112,256]{1,0:T(8,128)(2,1)S(1)}, bf16[112,256]{1,0:T(8,128)(2,1)S(1)}, u32[]{:S(2)}, u32[]{:S(2)}) %collective-permute-start.33) | collective-permute-done | bytes 57376 | tf_op jit(solution)/shard_map/ppermute | solution.py:483
  224.1 3.2 %collective-permute-start.21 = (bf16[112,256]{1,0:T(8,128)(2,1)S(1)}, bf16[112,256]{1,0:T(8,128)(2,1)S(1)}, u32[]{:S(2)}, u32[]{:S(2)}) collective-permute-start(bf16[112,256]{1,0:T(8,128)(2,1)S(1)} %add_convert_fusion.3.refs_0_), channel_id=1, source_target_pairs={{0,20},{4,24},{8,28},{12,0},{16,4},{20,8},{24,12},{28,16},{1,21},{... | collective-permute-start | bytes 172040 | tf_op jit(solution)/shard_map/ppermute | solution.py:483
  228.7 3.9 %second_out.1 = bf16[2,32,128,256]{3,2,1,0:T(8,128)(2,1)} custom-call(s32[1,2,8]{2,1,0:T(2,128)S(1)} %copy-done.33, s32[1]{0:T(128)S(6)} %copy.33.live, bf16[32,128,256]{2,1,0:T(8,128)(2,1)S(1)} %copy-done.24, bf16[32,128,256]{2,1,0:T(8,128)(2,1)S(1)} %copy-done.26, bf16[2,256,256]{2,1,0:T(8,128)(2,1)S(1)} %copy-done.10, ...), custom_call_target="tpu_custom_call", output_to_operand_aliasing={{}: (5, {})} | custom-call | flops 500000000 | bytes 6291456 | tf_op jit(solution)/shard_map/second_out/pallas_call | solution.py:66
  232.7 2.1 collective-permute-start.18
  235.5 11.3 %input_grad0.1 = (bf16[2,32,128,256]{3,2,1,0:T(8,128)(2,1)}, f32[16,128,256]{2,1,0:T(8,128)S(1)}, bf16[32,128,256]{2,1,0:T(8,128)(2,1)}) custom-call(s32[384]{0:T(512)S(1)} %get-tuple-element.63.meta, s32[8]{0:T(128)S(1)} %get-tuple-element.72.counts, s32[1]{0:T(128)S(6)} %copy.33.live, ...), custom_call_target="tpu_custom_call", output_to_operand_aliasing={{0}: (8, {})} | custom-call | flops 2000000000 | bytes 18874368 | tf_op jit(solution)/shard_map/input_grad0/pallas_call | solution.py:66
  248.3 2.1 finish.1
  (149 shorter events, 53.2 us)
Async XLA Ops:
  34.5 36.5 %collective-permute-start = (bf16[8,128,256]{2,1,0:T(8,128)(2,1)}, bf16[8,128,256]{2,1,0:T(8,128)(2,1)}, u32[]{:S(2)}, u32[]{:S(2)}) collective-permute-start(bf16[8,128,256]{2,1,0:T(8,128)(2,1)} %get-tuple-element.65), channel_id=1, source_target_pairs={{0,1},{1,2},{2,3},{3,4},{4,5},{5,6},{6,7},{7,8},{8,9},{9,10},{10,1... | collective-permute-start | bytes 1572872 | tf_op jit(solution)/shard_map/ppermute | solution.py:42
  37.6 33.4 %collective-permute-start.1 = (bf16[8,128,256]{2,1,0:T(8,128)(2,1)}, bf16[8,128,256]{2,1,0:T(8,128)(2,1)}, u32[]{:S(2)}, u32[]{:S(2)}) collective-permute-start(bf16[8,128,256]{2,1,0:T(8,128)(2,1)} %get-tuple-element.66), channel_id=1, source_target_pairs={{0,31},{1,0},{2,1},{3,2},{4,3},{5,4},{6,5},{7,6},{8,7},{9,8},{10,9... | collective-permute-start | bytes 1572872 | tf_op jit(solution)/shard_map/ppermute | solution.py:42
  78.9 24.8 %collective-permute-start.3 = (bf16[8,128,256]{2,1,0:T(8,128)(2,1)S(1)}, bf16[8,128,256]{2,1,0:T(8,128)(2,1)S(1)}, u32[]{:S(2)}, u32[]{:S(2)}) collective-permute-start(bf16[8,128,256]{2,1,0:T(8,128)(2,1)S(1)} %get-tuple-element.68.west), channel_id=1, source_target_pairs={{0,31},{1,0},{2,1},{3,2},{4,3},{5,4},{6,5},{7,6},{8,7},{9,8},{10,9... | collective-permute-start | bytes 1572872 | tf_op jit(solution)/shard_map/ppermute | solution.py:42
  80.3 23.4 %collective-permute-start.2 = (bf16[8,128,256]{2,1,0:T(8,128)(2,1)S(1)}, bf16[8,128,256]{2,1,0:T(8,128)(2,1)}, u32[]{:S(2)}, u32[]{:S(2)}) collective-permute-start(bf16[8,128,256]{2,1,0:T(8,128)(2,1)S(1)} %get-tuple-element.69.east), channel_id=1, source_target_pairs={{0,1},{1,2},{2,3},{3,4},{4,5},{5,6},{6,7},{7,8},{8,9},{9,10},{10,1... | collective-permute-start | bytes 1572872 | tf_op jit(solution)/shard_map/ppermute | solution.py:42
  126.4 18.1 %collective-permute-start.24 = (bf16[112,256]{1,0:T(8,128)(2,1)S(1)}, bf16[112,256]{1,0:T(8,128)(2,1)S(1)}, u32[]{:S(2)}, u32[]{:S(2)}) collective-permute-start(bf16[112,256]{1,0:T(8,128)(2,1)S(1)} %get-tuple-element.109), channel_id=1, source_target_pairs={{0,4},{4,8},{8,12},{12,16},{16,20},{20,24},{24,28},{28,0},{1,5},{5... | collective-permute-start | bytes 172040 | tf_op jit(solution)/shard_map/ppermute | solution.py:483
  127.0 18.8 %collective-permute-start.25 = (bf16[112,256]{1,0:T(8,128)(2,1)S(1)}, bf16[112,256]{1,0:T(8,128)(2,1)S(1)}, u32[]{:S(2)}, u32[]{:S(2)}) collective-permute-start(bf16[112,256]{1,0:T(8,128)(2,1)S(1)} %get-tuple-element.110), channel_id=1, source_target_pairs={{0,8},{4,12},{8,16},{12,20},{16,24},{20,28},{24,0},{28,4},{1,9},{5... | collective-permute-start | bytes 172040 | tf_op jit(solution)/shard_map/ppermute | solution.py:483
  127.0 19.7 %collective-permute-start.26 = (bf16[112,256]{1,0:T(8,128)(2,1)S(1)}, bf16[112,256]{1,0:T(8,128)(2,1)S(1)}, u32[]{:S(2)}, u32[]{:S(2)}) collective-permute-start(bf16[112,256]{1,0:T(8,128)(2,1)S(1)} %get-tuple-element.111), channel_id=1, source_target_pairs={{0,12},{4,16},{8,20},{12,24},{16,28},{20,0},{24,4},{28,8},{1,13},{... | collective-permute-start | bytes 172040 | tf_op jit(solution)/shard_map/ppermute | solution.py:483
  129.1 18.5 %collective-permute-start.27 = (bf16[112,256]{1,0:T(8,128)(2,1)S(1)}, bf16[112,256]{1,0:T(8,128)(2,1)S(1)}, u32[]{:S(2)}, u32[]{:S(2)}) collective-permute-start(bf16[112,256]{1,0:T(8,128)(2,1)S(1)} %get-tuple-element.112), channel_id=1, source_target_pairs={{0,16},{4,20},{8,24},{12,28},{16,0},{20,4},{24,8},{28,12},{1,17},{... | collective-permute-start | bytes 172040 | tf_op jit(solution)/shard_map/ppermute | solution.py:483
  130.2 34.7 %collective-permute-start.28 = (bf16[112,256]{1,0:T(8,128)(2,1)S(1)}, bf16[112,256]{1,0:T(8,128)(2,1)S(1)}, u32[]{:S(2)}, u32[]{:S(2)}) collective-permute-start(bf16[112,256]{1,0:T(8,128)(2,1)S(1)} %get-tuple-element.113), channel_id=1, source_target_pairs={{0,20},{4,24},{8,28},{12,0},{16,4},{20,8},{24,12},{28,16},{1,21},{... | collective-permute-start | bytes 172040 | tf_op jit(solution)/shard_map/ppermute | solution.py:483
  144.5 20.3 %collective-permute-start.29 = (bf16[112,256]{1,0:T(8,128)(2,1)S(1)}, bf16[112,256]{1,0:T(8,128)(2,1)S(1)}, u32[]{:S(2)}, u32[]{:S(2)}) collective-permute-start(bf16[112,256]{1,0:T(8,128)(2,1)S(1)} %get-tuple-element.114), channel_id=1, source_target_pairs={{0,24},{4,28},{8,0},{12,4},{16,8},{20,12},{24,16},{28,20},{1,25},{... | collective-permute-start | bytes 172040 | tf_op jit(solution)/shard_map/ppermute | solution.py:483
  145.7 19.1 %collective-permute-start.30 = (bf16[112,256]{1,0:T(8,128)(2,1)S(1)}, bf16[112,256]{1,0:T(8,128)(2,1)S(1)}, u32[]{:S(2)}, u32[]{:S(2)}) collective-permute-start(bf16[112,256]{1,0:T(8,128)(2,1)S(1)} %get-tuple-element.115), channel_id=1, source_target_pairs={{0,28},{4,0},{8,4},{12,8},{16,12},{20,16},{24,20},{28,24},{1,29},{... | collective-permute-start | bytes 172040 | tf_op jit(solution)/shard_map/ppermute | solution.py:483
  146.6 18.4 %collective-permute-start.4 = (bf16[8,128,256]{2,1,0:T(8,128)(2,1)S(1)}, bf16[8,128,256]{2,1,0:T(8,128)(2,1)S(1)}, u32[]{:S(2)}, u32[]{:S(2)}) collective-permute-start(bf16[8,128,256]{2,1,0:T(8,128)(2,1)S(1)} %get-tuple-element.81), channel_id=1, source_target_pairs={{0,1},{1,2},{2,3},{3,4},{4,5},{5,6},{6,7},{7,8},{8,9},{9,10},{10,1... | collective-permute-start | bytes 1572872 | tf_op jit(solution)/shard_map/ppermute | solution.py:42
  147.6 25.6 %collective-permute-start.5 = (bf16[8,128,256]{2,1,0:T(8,128)(2,1)S(1)}, bf16[8,128,256]{2,1,0:T(8,128)(2,1)S(1)}, u32[]{:S(2)}, u32[]{:S(2)}) collective-permute-start(bf16[8,128,256]{2,1,0:T(8,128)(2,1)S(1)} %get-tuple-element.82), channel_id=1, source_target_pairs={{0,31},{1,0},{2,1},{3,2},{4,3},{5,4},{6,5},{7,6},{8,7},{9,8},{10,9... | collective-permute-start | bytes 1572872 | tf_op jit(solution)/shard_map/ppermute | solution.py:42
  165.0 27.6 %collective-permute-start.31 = (bf16[112,256]{1,0:T(8,128)(2,1)S(1)}, bf16[112,256]{1,0:T(8,128)(2,1)S(1)}, u32[]{:S(2)}, u32[]{:S(2)}) collective-permute-start(bf16[112,256]{1,0:T(8,128)(2,1)S(1)} %add_convert_fusion.2), channel_id=1, source_target_pairs={{0,1},{1,0},{2,3},{3,2},{4,5},{5,4},{6,7},{7,6},{8,9},{9,8},{10,11... | collective-permute-start | bytes 172040 | tf_op jit(solution)/shard_map/ppermute | solution.py:500
  205.3 8.1 %collective-permute-start.37 = (bf16[112,256]{1,0:T(8,128)(2,1)S(1)}, bf16[112,256]{1,0:T(8,128)(2,1)S(1)}, u32[]{:S(2)}, u32[]{:S(2)}) collective-permute-start(bf16[112,256]{1,0:T(8,128)(2,1)S(1)} %add_convert_fusion.refs_8_), channel_id=1, source_target_pairs={{0,20},{4,24},{8,28},{12,0},{16,4},{20,8},{24,12},{28,16},{1,21},{... | collective-permute-start | bytes 172040 | tf_op jit(solution)/shard_map/ppermute | solution.py:483
  208.0 40.2 %collective-permute-start.6 = (bf16[8,128,256]{2,1,0:T(8,128)(2,1)S(1)}, bf16[8,128,256]{2,1,0:T(8,128)(2,1)S(1)}, u32[]{:S(2)}, u32[]{:S(2)}) collective-permute-start(bf16[8,128,256]{2,1,0:T(8,128)(2,1)S(1)} %get-tuple-element.95), channel_id=1, source_target_pairs={{0,1},{1,2},{2,3},{3,4},{4,5},{5,6},{6,7},{7,8},{8,9},{9,10},{10,1... | collective-permute-start | bytes 1572872 | tf_op jit(solution)/shard_map/ppermute | solution.py:42
  209.5 38.8 %collective-permute-start.7 = (bf16[8,128,256]{2,1,0:T(8,128)(2,1)S(1)}, bf16[8,128,256]{2,1,0:T(8,128)(2,1)S(1)}, u32[]{:S(2)}, u32[]{:S(2)}) collective-permute-start(bf16[8,128,256]{2,1,0:T(8,128)(2,1)S(1)} %get-tuple-element.96), channel_id=1, source_target_pairs={{0,31},{1,0},{2,1},{3,2},{4,3},{5,4},{6,5},{7,6},{8,7},{9,8},{10,9... | collective-permute-start | bytes 1572872 | tf_op jit(solution)/shard_map/ppermute | solution.py:42
  213.5 10.6 %collective-permute-start.33 = (bf16[112,256]{1,0:T(8,128)(2,1)S(1)}, bf16[112,256]{1,0:T(8,128)(2,1)S(1)}, u32[]{:S(2)}, u32[]{:S(2)}) collective-permute-start(bf16[112,256]{1,0:T(8,128)(2,1)S(1)} %add_convert_fusion.refs_8_), channel_id=1, source_target_pairs={{0,4},{4,8},{8,12},{12,16},{16,20},{20,24},{24,28},{28,0},{1,5},{5... | collective-permute-start | bytes 172040 | tf_op jit(solution)/shard_map/ppermute | solution.py:483
  215.1 12.9 %collective-permute-start.23 = (bf16[112,256]{1,0:T(8,128)(2,1)S(1)}, bf16[112,256]{1,0:T(8,128)(2,1)S(1)}, u32[]{:S(2)}, u32[]{:S(2)}) collective-permute-start(bf16[112,256]{1,0:T(8,128)(2,1)S(1)} %add_convert_fusion.3.refs_0_), channel_id=1, source_target_pairs={{0,28},{4,0},{8,4},{12,8},{16,12},{20,16},{24,20},{28,24},{1,29},{... | collective-permute-start | bytes 172040 | tf_op jit(solution)/shard_map/ppermute | solution.py:483
  217.1 15.6 %collective-permute-start.22 = (bf16[112,256]{1,0:T(8,128)(2,1)S(1)}, bf16[112,256]{1,0:T(8,128)(2,1)S(1)}, u32[]{:S(2)}, u32[]{:S(2)}) collective-permute-start(bf16[112,256]{1,0:T(8,128)(2,1)S(1)} %add_convert_fusion.3.refs_0_), channel_id=1, source_target_pairs={{0,24},{4,28},{8,0},{12,4},{16,8},{20,12},{24,16},{28,20},{1,25},{... | collective-permute-start | bytes 172040 | tf_op jit(solution)/shard_map/ppermute | solution.py:483
  224.1 8.6 %collective-permute-start.21 = (bf16[112,256]{1,0:T(8,128)(2,1)S(1)}, bf16[112,256]{1,0:T(8,128)(2,1)S(1)}, u32[]{:S(2)}, u32[]{:S(2)}) collective-permute-start(bf16[112,256]{1,0:T(8,128)(2,1)S(1)} %add_convert_fusion.3.refs_0_), channel_id=1, source_target_pairs={{0,20},{4,24},{8,28},{12,0},{16,4},{20,8},{24,12},{28,16},{1,21},{... | collective-permute-start | bytes 172040 | tf_op jit(solution)/shard_map/ppermute | solution.py:483
  232.7 14.2 %collective-permute-start.19 = (bf16[112,256]{1,0:T(8,128)(2,1)S(1)}, bf16[112,256]{1,0:T(8,128)(2,1)S(1)}, u32[]{:S(2)}, u32[]{:S(2)}) collective-permute-start(bf16[112,256]{1,0:T(8,128)(2,1)S(1)} %add_convert_fusion.3.refs_0_), channel_id=1, source_target_pairs={{0,12},{4,16},{8,20},{12,24},{16,28},{20,0},{24,4},{28,8},{1,13},{... | collective-permute-start | bytes 172040 | tf_op jit(solution)/shard_map/ppermute | solution.py:483
  232.7 14.1 %collective-permute-start.18 = (bf16[112,256]{1,0:T(8,128)(2,1)S(1)}, bf16[112,256]{1,0:T(8,128)(2,1)S(1)}, u32[]{:S(2)}, u32[]{:S(2)}) collective-permute-start(bf16[112,256]{1,0:T(8,128)(2,1)S(1)} %add_convert_fusion.3.refs_0_), channel_id=1, source_target_pairs={{0,8},{4,12},{8,16},{12,20},{16,24},{20,28},{24,0},{28,4},{1,9},{5... | collective-permute-start | bytes 172040 | tf_op jit(solution)/shard_map/ppermute | solution.py:483
  234.8 12.1 %collective-permute-start.17 = (bf16[112,256]{1,0:T(8,128)(2,1)S(1)}, bf16[112,256]{1,0:T(8,128)(2,1)S(1)}, u32[]{:S(2)}, u32[]{:S(2)}) collective-permute-start(bf16[112,256]{1,0:T(8,128)(2,1)S(1)} %add_convert_fusion.3.refs_0_), channel_id=1, source_target_pairs={{0,4},{4,8},{8,12},{12,16},{16,20},{20,24},{24,28},{28,0},{1,5},{5... | collective-permute-start | bytes 172040 | tf_op jit(solution)/shard_map/ppermute | solution.py:483
  (52 other events, 548.2 us)

commit v2 on v0

v2 whole, which is shorter than its diff:
```python
import jax
import jax.numpy as jnp
from jax import lax
from jax.experimental import pallas as pl
from jax.experimental.pallas import tpu as pltpu
from jax.sharding import PartitionSpec as P

AXES = ("dom", "phase", "feat")
PLANE = ("dom", "phase")
BF16 = jnp.bfloat16
F32 = jnp.float32
UNROLL = 8
ANY = pl.BlockSpec(memory_space=pl.ANY)
SMEM = pl.BlockSpec(memory_space=pltpu.SMEM)
VMEM = pl.BlockSpec(memory_space=pltpu.VMEM)
MIB = 1024 * 1024


class Sizes:
    def __init__(self, adjacency, features, bound):
        self.tiles, self.slots, self.rows, _ = adjacency.shape
        self.cols = features.shape[-1]
        self.edge = bound.shape[-1]
        self.lent = 2 * self.edge
        self.rest = self.tiles - self.lent
        self.ext = self.tiles + self.lent
        self.pairs = self.tiles * self.slots
        self.group = next(g for g in (4, 2, 1) if self.edge % g == 0 and self.rest % g == 0)
        self.parts = ((0, 0, self.lent), (1, self.lent, self.rest))

    def nodes(self, count, dtype=BF16):
        return jax.ShapeDtypeStruct((count, self.rows, self.cols), dtype)

    def held(self, count, dtype=BF16):
        return pltpu.VMEM((count, self.rows, self.cols), dtype)

    def flat(self, value):
        return value.reshape(self.group * self.rows, self.cols)

    def tiled(self, value):
        return value.reshape(self.group, self.rows, self.cols)


def group_of(z, array, part, first):
    if isinstance(array, tuple):
        base = z.lent if part else 0
        return array[part].at[pl.ds(first - base, z.group)]
    return array.at[pl.ds(first, z.group)]


def each_group(z, body, parts=(0, 1), unroll=1):
    for part, base, count in z.parts:
        if part in parts:

            @pl.loop(0, count // z.group, unroll=unroll)
            def _(s):
                body(part, base + s * z.group)


def passed_along(value, steps):
    count = lax.axis_size(AXES)
    return lax.ppermute(value, AXES, [(i, (i + steps) % count) for i in range(count)])


def dot(a, b):
    return jnp.dot(a, b, preferred_element_type=F32)


def dot_rows(a, b):
    return lax.dot_general(a, b, (((0,), (0,)), ((), ())), preferred_element_type=F32)


def call(kernel, name, in_specs, out_specs, out_shape, scratch, limit, args, aliases=None):
    return pl.pallas_call(
        kernel,
        in_specs=in_specs,
        out_specs=out_specs,
        out_shape=out_shape,
        scratch_shapes=scratch,
        input_output_aliases=aliases or {},
        compiler_params=pltpu.CompilerParams(vmem_limit_bytes=limit * MIB),
        cost_estimate=pl.CostEstimate(flops=1000, bytes_accessed=1000, transcendentals=0),
        name=name,
    )(*args)


def sigmoid(v):
    return 0.5 * jnp.tanh(0.5 * v) + 0.5


def lend(z, bound, features):
    def kernel(bound, feats, west, east, sems):
        copies = []
        for i in range(z.edge):
            for side, target in ((0, west), (1, east)):
                copy = pltpu.make_async_copy(
                    feats.at[bound[0, side, i]], target.at[i], sems.at[side * z.edge + i]
                )
                copy.start()
                copies.append(copy)
        for copy in copies:
            copy.wait()

    return call(
        kernel,
        "lend",
        [SMEM, ANY],
        [VMEM, VMEM],
        [z.nodes(z.edge), z.nodes(z.edge)],
        [pltpu.SemaphoreType.DMA((z.lent,))],
        4,
        (bound, features),
    )


def arrange(z, bound, nbrs, live, features, cot, adjacency):
    s4 = z.slots

    def kernel(bound, nbrs, live, feats, cot, adj, f_lent, f_rest, m_lent, m_rest, ap, meta, counts, inverse, sems):
        copies = []

        def start(source, target):
            copy = pltpu.make_async_copy(source, target, sems.at[len(copies)])
            copy.start()
            copies.append(copy)

        tail = pl.ds(z.lent, z.rest)
        start(adj.at[tail], ap.at[tail])
        start(feats.at[tail], f_rest)
        start(cot.at[tail], m_rest)
        for i in range(z.lent):
            tile = bound[0, i // z.edge, i % z.edge]
            inverse[tile] = i
            start(adj.at[tile], ap.at[i])
            start(feats.at[tile], f_lent.at[i])
            start(cot.at[tile], m_lent.at[i])

        def kind_of(position, target):
            return jnp.where(target < z.tiles, 0, jnp.where(position < z.lent, 2, 1))

        def step(kind, sums):
            return tuple(total + jnp.where(kind == i, 1, 0) for i, total in enumerate(sums))

        def count(position, sums):
            clipped = jnp.minimum(position, z.lent - 1)
            tile = jnp.where(position < z.lent, bound[0, clipped // z.edge, clipped % z.edge], position)
            for k in range(s4):
                target = nbrs[tile, k]
                moved = jnp.where(target < z.lent, inverse[jnp.minimum(target, z.lent - 1)], target)
                meta[position * s4 + k] = moved
                sums = step(kind_of(position, moved), sums)
            return sums

        zero = jnp.int32(0)
        own, outer, lent = lax.fori_loop(0, z.tiles, count, (zero, zero, zero))
        counts[0] = own
        counts[1] = outer
        counts[2] = lent

        def put(position, sums):
            for k in range(s4):
                target = meta[position * s4 + k]
                kind = kind_of(position, target)
                slot = jnp.where(kind == 0, sums[0], jnp.where(kind == 1, sums[1], sums[2]))
                meta[z.pairs + slot] = position * s4 + k
                meta[2 * z.pairs + slot] = target
                sums = step(kind, sums)
            return sums

        lax.fori_loop(0, z.tiles, put, (zero, own, own + outer))
        for copy in copies:
            copy.wait()

        @pl.loop(0, z.rest)
        def _(i):
            @pl.when(z.lent + i >= live[0])
            def _():
                m_rest[i] = jnp.zeros((z.rows, z.cols), BF16)

    return call(
        kernel,
        "arrange",
        [SMEM, SMEM, SMEM, ANY, ANY, ANY],
        [VMEM] * 5 + [SMEM, SMEM],
        [
            z.nodes(z.lent),
            z.nodes(z.rest),
            z.nodes(z.lent),
            z.nodes(z.rest),
            jax.ShapeDtypeStruct(adjacency.shape, BF16),
            jax.ShapeDtypeStruct((3 * z.pairs,), jnp.int32),
            jax.ShapeDtypeStruct((8,), jnp.int32),
        ],
        [pltpu.SMEM((z.lent,), jnp.int32), pltpu.SemaphoreType.DMA((3 * z.lent + 3,))],
        12,
        (bound, nbrs, live, features, cot, adjacency),
    )


def turn(z, ap, w_self, w_nbr, w_out):
    def kernel(ap, ws, wn, wo, at, wt):
        for layer in range(2):
            wt[layer, 0] = ws[layer].T
            wt[layer, 1] = wn[layer].T
            wt[layer, 2] = wo[layer].T

        @pl.loop(0, z.tiles)
        def _(q):
            for k in range(z.slots):
                at[q * z.slots + k] = ap[q, k].T

    return call(
        kernel,
        "turn",
        [VMEM] * 4,
        [VMEM, VMEM],
        [
            jax.ShapeDtypeStruct((z.pairs, z.rows, z.rows), BF16),
            jax.ShapeDtypeStruct((2, 3, z.cols, z.cols), BF16),
        ],
        [],
        12,
        (ap, w_self, w_nbr, w_out),
    )


def fill_extended(z, own, fw, fe, ext):
    ext[pl.ds(0, z.lent)] = own[0][...]
    ext[pl.ds(z.lent, z.rest)] = own[1][...]
    ext[pl.ds(z.tiles, z.edge)] = fw[...]
    ext[pl.ds(z.tiles + z.edge, z.edge)] = fe[...]


def aggregate(z, meta, first, ap, ext):
    rows = []
    for g in range(z.group):
        base = (first + g) * z.slots
        picked = jnp.concatenate([ext[meta[base + k]] for k in range(z.slots)], axis=0)
        blocks = jnp.concatenate([ap[first + g, k] for k in range(z.slots)], axis=1)
        rows.append(dot(blocks, picked).astype(BF16))
    return jnp.concatenate(rows, axis=0)


def live_rows(z, value, first, live):
    parts = []
    for g in range(z.group):
        part = value[g * z.rows : (g + 1) * z.rows]
        parts.append(jnp.where(first + g < live, part, jnp.zeros_like(part)))
    return jnp.concatenate(parts, axis=0)


def first_lent(z, meta, f0, fw, fe, ap, w_self, w_nbr, bias, w_out):
    def kernel(meta, f_lent, f_rest, fw, fe, ap, ws, wn, bias, wo, west, east, agg, ext):
        fill_extended(z, (f_lent, f_rest), fw, fe, ext)

        def work(first, target, offset):
            here = pl.ds(first, z.group)
            f = z.flat(ext[here])
            aggs = aggregate(z, meta, first, ap, ext)
            agg[here] = z.tiled(aggs)
            pre = dot(f, ws[0]) + dot(aggs, wn[0]) + bias[0:1, :]
            act = (pre * sigmoid(pre)).astype(BF16)
            target[pl.ds(offset, z.group)] = z.tiled((f.astype(F32) + dot(act, wo[0])).astype(BF16))

        @pl.loop(0, z.edge // z.group)
        def _(s):
            work(s * z.group, west, s * z.group)
            work(z.edge + s * z.group, east, s * z.group)

    return call(
        kernel,
        "first_lent",
        [SMEM] + [VMEM] * 9,
        [VMEM] * 3,
        [z.nodes(z.edge), z.nodes(z.edge), z.nodes(z.lent)],
        [z.held(z.ext)],
        12,
        (meta, *f0, fw, fe, ap, w_self, w_nbr, bias, w_out),
    )


def first_rest(z, meta, bound, live, f0, fw, fe, ap, w_self, w_nbr, bias, w_out, west, east):
    def kernel(meta, bound, live, f_lent, f_rest, fw, fe, ap, ws, wn, bias, wo, west, east,
               f1_lent, f1_rest, out, agg, ext, sems):
        copies = []
        for i in range(z.edge):
            for side, source in ((0, west), (1, east)):
                copy = pltpu.make_async_copy(
                    source.at[i], out.at[0, bound[0, side, i]], sems.at[side * z.edge + i]
                )
                copy.start()
                copies.append(copy)
        fill_extended(z, (f_lent, f_rest), fw, fe, ext)
        f1_lent[pl.ds(0, z.edge)] = west[...]
        f1_lent[pl.ds(z.edge, z.edge)] = east[...]

        def work(part, first):
            f = z.flat(ext[pl.ds(first, z.group)])
            aggs = aggregate(z, meta, first, ap, ext)
            here = pl.ds(first - z.lent, z.group)
            agg[here] = z.tiled(aggs)
            pre = dot(f, ws[0]) + dot(aggs, wn[0]) + bias[0:1, :]
            act = (pre * sigmoid(pre)).astype(BF16)
            res = live_rows(z, f.astype(F32) + dot(act, wo[0]), first, live[0])
            f1_rest[here] = z.tiled(res.astype(BF16))

        each_group(z, work, (1,))
        copy = pltpu.make_async_copy(f1_rest, out.at[0, pl.ds(z.lent, z.rest)], sems.at[z.lent])
        copy.start()
        for other in copies:
            other.wait()
        copy.wait()

    return call(
        kernel,
        "first_rest",
        [SMEM] * 3 + [VMEM] * 11,
        [VMEM, VMEM, ANY, VMEM],
        [
            z.nodes(z.lent),
            z.nodes(z.rest),
            jax.ShapeDtypeStruct((2, z.tiles, z.rows, z.cols), BF16),
            z.nodes(z.rest),
        ],
        [z.held(z.ext), pltpu.SemaphoreType.DMA((1 + z.lent,))],
        12,
        (meta, bound, live, *f0, fw, fe, ap, w_self, w_nbr, bias, w_out, west, east),
    )


def second_own(z, f1, m1, w_self, bias, wt):
    def kernel(f_lent, f_rest, m_lent, m_rest, ws, bias, wt, own, hidden):
        def work(part, first):
            f = z.flat(group_of(z, (f_lent, f_rest), part, first)[...])
            m = z.flat(group_of(z, (m_lent, m_rest), part, first)[...])
            here = pl.ds(first, z.group)
            own[here] = z.tiled(dot(f, ws[1]) + bias[1:2, :])
            hidden[here] = z.tiled(dot(m, wt[1, 2]))

        each_group(z, work)

    return call(
        kernel,
        "second_own",
        [VMEM] * 7,
        [VMEM] * 2,
        [z.nodes(z.tiles, F32)] * 2,
        [],
        12,
        (*f1, *m1, w_self, bias, wt),
    )


def saved(z, f0, agg0, w_self, w_nbr, bias):
    def kernel(f_lent, f_rest, a_lent, a_rest, ws, wn, bias, act, slope):
        def work(part, first):
            f = z.flat(group_of(z, (f_lent, f_rest), part, first)[...])
            aggs = z.flat(group_of(z, (a_lent, a_rest), part, first)[...])
            pre = dot(f, ws[0]) + dot(aggs, wn[0]) + bias[0:1, :]
            sig = sigmoid(pre)
            here = pl.ds(first, z.group)
            act[here] = z.tiled((pre * sig).astype(BF16))
            slope[here] = z.tiled(sig * (1.0 + pre * (1.0 - sig)))

        each_group(z, work)

    return call(
        kernel,
        "saved",
        [VMEM] * 7,
        [VMEM] * 2,
        [z.nodes(z.tiles), z.nodes(z.tiles, F32)],
        [],
        12,
        (*f0, *agg0, w_self, w_nbr, bias),
    )


def spread(z, meta, start, stop, at, source, acc, shift, spare):
    def body(i, carry):
        for u in range(UNROLL):
            entry = start + i * UNROLL + u
            inside = entry < stop
            entry = jnp.minimum(entry, z.pairs - 1)
            target = jnp.where(inside, meta[2 * z.pairs + entry] - shift, spare)
            pair = meta[z.pairs + entry]
            acc[target] += dot(at[pair], source(pair // z.slots))
        return carry

    lax.fori_loop(0, (stop - start + UNROLL - 1) // UNROLL, body, 0)


def second(z, meta, counts, f1, fw, fe, ap, at, own, hidden, w_nbr, wt):
    def kernel(meta, counts, f_lent, f_rest, fw, fe, ap, at, own, hidden, wn, wt,
               agg, act, dpre, dagg, to_west, to_east, ext, acc):
        fill_extended(z, (f_lent, f_rest), fw, fe, ext)
        acc[...] = jnp.zeros_like(acc)

        def work(part, first):
            here = pl.ds(first, z.group)
            aggs = aggregate(z, meta, first, ap, ext)
            agg[here] = z.tiled(aggs)
            pre = z.flat(own[here]) + dot(aggs, wn[1])
            sig = sigmoid(pre)
            act[here] = z.tiled((pre * sig).astype(BF16))
            grad = (z.flat(hidden[here]) * (sig * (1.0 + pre * (1.0 - sig)))).astype(BF16)
            dpre[here] = z.tiled(grad)
            dagg[here] = z.tiled(dot(grad, wt[1, 1]).astype(BF16))

        each_group(z, work)
        spread(z, meta, counts[0], z.pairs, at, lambda q: dagg[q], acc, z.tiles, z.lent)
        to_west[...] = acc[pl.ds(0, z.edge)].astype(BF16)
        to_east[...] = acc[pl.ds(z.edge, z.edge)].astype(BF16)

    return call(
        kernel,
        "second",
        [SMEM] * 2 + [VMEM] * 10,
        [VMEM] * 6,
        [z.nodes(z.tiles)] * 4 + [z.nodes(z.edge)] * 2,
        [z.held(z.ext), z.held(z.lent + 1, F32)],
        16,
        (meta, counts, *f1, fw, fe, ap, at, own, hidden, w_nbr, wt),
    )


def weight_grads(z, me, pieces, f, agg, act, m, dpre, name):
    c = z.cols
    piece = -(-(3 * c + 1) // (pieces * 16)) * 16
    height = piece * pieces
    arrays = (f, agg, act, m, dpre)
    flat_args = [x for a in arrays for x in (a if isinstance(a, tuple) else (a,))]

    def kernel(me, *refs):
        refs = list(refs)
        f, agg, act, m, dpre = [
            (refs.pop(0), refs.pop(0)) if isinstance(a, tuple) else refs.pop(0) for a in arrays
        ]
        outs, acc = refs[:-1], refs[-1]
        acc[...] = jnp.zeros_like(acc)

        def work(part, first):
            def rows(array):
                return z.flat(group_of(z, array, part, first)[...])

            grad = rows(dpre)
            acc[pl.ds(0, c), :] += dot_rows(rows(f), grad)
            acc[pl.ds(c, c), :] += dot_rows(rows(agg), grad)
            acc[pl.ds(2 * c, c), :] += dot_rows(rows(act), rows(m))
            acc[pl.ds(3 * c, 1), :] += jnp.sum(grad.astype(F32), axis=0, keepdims=True)

        each_group(z, work)
        for i in range(pieces):
            owner = lax.rem(me[0] + i, pieces)
            outs[i][...] = acc[pl.ds(pl.multiple_of(owner * piece, 16), piece), :]

    return call(
        kernel,
        name,
        [SMEM] + [VMEM] * len(flat_args),
        [VMEM] * pieces,
        [jax.ShapeDtypeStruct((piece, c), F32)] * pieces,
        [pltpu.VMEM((height, c), F32)],
        12,
        (me, *flat_args),
    )


def plane_pass(value, steps):
    count = lax.axis_size(PLANE)
    return lax.ppermute(value, PLANE, [(i, (i + steps) % count) for i in range(count)])


def added(parts):
    total = parts[0].astype(F32)
    for part in parts[1:]:
        total = total + part.astype(F32)
    return total.astype(BF16)


def summed_over_parts(pieces):
    count = len(pieces)
    share = added([pieces[0]] + [plane_pass(pieces[i], i) for i in range(1, count)])
    lines = lax.axis_size("feat")
    if lines & (lines - 1) == 0:
        step = 1
        while step < lines:
            other = lax.ppermute(share, "feat", [(i, i ^ step) for i in range(lines)])
            share = added([share, other])
            step *= 2
    else:
        share = lax.psum(share.astype(F32), "feat").astype(BF16)
    return lax.all_gather(share, PLANE, axis=0, tiled=True)


def unpack(z, early, late):
    c = z.cols

    def kernel(early, late, g_self, g_nbr, g_bias, g_out):
        for layer, packed in ((0, early), (1, late)):
            g_self[layer] = packed[pl.ds(0, c), :].astype(F32)
            g_nbr[layer] = packed[pl.ds(c, c), :].astype(F32)
            g_out[layer] = packed[pl.ds(2 * c, c), :].astype(F32)
            g_bias[layer : layer + 1, :] = packed[pl.ds(3 * c, 16), :].astype(F32)[0:1]

    square = jax.ShapeDtypeStruct((2, c, c), F32)
    return call(
        kernel,
        "unpack",
        [VMEM] * 2,
        [VMEM] * 4,
        [square, square, jax.ShapeDtypeStruct((2, c), F32), square],
        [],
        12,
        (early, late),
    )


def second_out(z, bound, live, f1, act, w_out, out):
    def kernel(bound, live, f_lent, f_rest, act, wo, _out, out, keep, sems):
        copies = []

        def work(part, first):
            f = z.flat(group_of(z, (f_lent, f_rest), part, first)[...])
            res = f.astype(F32) + dot(z.flat(act[pl.ds(first, z.group)]), wo[1])
            keep[pl.ds(first, z.group)] = z.tiled(live_rows(z, res, first, live[0]).astype(BF16))

        each_group(z, work, (0,))
        for i in range(z.lent):
            copy = pltpu.make_async_copy(
                keep.at[i], out.at[1, bound[0, i // z.edge, i % z.edge]], sems.at[i]
            )
            copy.start()
            copies.append(copy)
        each_group(z, work, (1,))
        tail = pl.ds(z.lent, z.rest)
        copy = pltpu.make_async_copy(keep.at[tail], out.at[1, tail], sems.at[z.lent])
        copy.start()
        copies.append(copy)
        for copy in copies:
            copy.wait()

    return call(
        kernel,
        "second_out",
        [SMEM] * 2 + [VMEM] * 4 + [ANY],
        ANY,
        jax.ShapeDtypeStruct(out.shape, BF16),
        [z.held(z.tiles), pltpu.SemaphoreType.DMA((z.lent + 1,))],
        12,
        (bound, live, *f1, act, w_out, out),
        {6: 0},
    )


def input_grad(z, layer, meta, counts, live, m, dpre, dagg, at, wt, grads):
    fresh = grads is None
    arrays = (m, dpre, dagg)
    flat_args = [x for a in arrays for x in (a if isinstance(a, tuple) else (a,))]

    def kernel(meta, counts, live, *refs):
        refs = list(refs)
        m, dpre, dagg = [
            (refs.pop(0), refs.pop(0)) if isinstance(a, tuple) else refs.pop(0) for a in arrays
        ]
        at, wt = refs[:2]
        grads, part_out, masked, acc, keep, sem = refs[2 if fresh else 3 :]

        def direct(part, first):
            mine = z.flat(group_of(z, m, part, first)[...]).astype(F32)
            res = mine + dot(z.flat(group_of(z, dpre, part, first)[...]), wt[layer, 0])
            acc[pl.ds(first, z.group)] = z.tiled(res)

        each_group(z, direct)

        def source(q):
            if not isinstance(dagg, tuple):
                return dagg[q]
            lent = dagg[0][jnp.minimum(q, z.lent - 1)]
            rest = dagg[1][jnp.maximum(q - z.lent, 0)]
            return jnp.where(q < z.lent, lent, rest)

        spread(z, meta, 0, counts[0], at, source, acc, 0, z.tiles)
        tail = pl.ds(z.lent, z.rest)
        keep[...] = acc[tail].astype(BF16)
        copy = pltpu.make_async_copy(keep, grads.at[layer, tail], sem)
        copy.start()
        part_out[...] = acc[pl.ds(0, z.lent)]

        @pl.loop(0, z.rest)
        def _(i):
            value = keep[i]
            masked[i] = jnp.where(z.lent + i < live[0], value, jnp.zeros_like(value))

        copy.wait()

    args = [meta, counts, live, *flat_args, at, wt]
    if not fresh:
        args.append(grads)
    return call(
        kernel,
        "input_grad%d" % layer,
        [SMEM] * 3 + [VMEM] * (len(flat_args) + 2) + ([] if fresh else [ANY]),
        [ANY, VMEM, VMEM],
        [
            jax.ShapeDtypeStruct((2, z.tiles, z.rows, z.cols), BF16),
            z.nodes(z.lent, F32),
            z.nodes(z.rest),
        ],
        [z.held(z.tiles + 1, F32), z.held(z.rest), pltpu.SemaphoreType.DMA],
        16,
        args,
        None if fresh else {len(args) - 1: 0},
    )


def early_rest(z, meta, counts, m0, slope, at, wt):
    def kernel(meta, counts, m, slope, at, wt, dpre, dagg, outer, acc):
        def work(part, first):
            here = pl.ds(first - z.lent, z.group)
            grad = dot(z.flat(m[here]), wt[0, 2]) * z.flat(slope[pl.ds(first, z.group)])
            grad = grad.astype(BF16)
            dpre[here] = z.tiled(grad)
            dagg[here] = z.tiled(dot(grad, wt[0, 1]).astype(BF16))

        each_group(z, work, (1,))
        acc[...] = jnp.zeros_like(acc)

        def source(q):
            return dagg[jnp.maximum(q - z.lent, 0)]

        spread(z, meta, counts[0], counts[0] + counts[1], at, source, acc, z.tiles, z.lent)
        outer[...] = acc[pl.ds(0, z.lent)]

    return call(
        kernel,
        "early_rest",
        [SMEM] * 2 + [VMEM] * 4,
        [VMEM] * 3,
        [z.nodes(z.rest), z.nodes(z.rest), z.nodes(z.lent, F32)],
        [z.held(z.lent + 1, F32)],
        12,
        (meta, counts, m0, slope, at, wt),
    )


def early_lent(z, meta, counts, bound, part, fw, fe, slope, outer, at, wt, grads):
    def kernel(meta, counts, bound, part, fw, fe, slope, outer, at, wt, _g,
               m, dpre, dagg, grads, to_west, to_east, acc, sems):
        def work(first, got):
            here = pl.ds(first, z.group)
            g = z.flat((part[here] + got.astype(F32)).astype(BF16))
            m[here] = z.tiled(g)
            grad = (dot(g, wt[0, 2]) * z.flat(slope[here])).astype(BF16)
            dpre[here] = z.tiled(grad)
            dagg[here] = z.tiled(dot(grad, wt[0, 1]).astype(BF16))

        @pl.loop(0, z.edge // z.group)
        def _(s):
            here = pl.ds(s * z.group, z.group)
            work(s * z.group, fw[here])
            work(z.edge + s * z.group, fe[here])

        copies = [
            pltpu.make_async_copy(m.at[i], grads.at[1, bound[0, i // z.edge, i % z.edge]], sems.at[i])
            for i in range(z.lent)
        ]
        for copy in copies:
            copy.start()
        acc[pl.ds(0, z.lent)] = outer[...]
        acc[z.lent] = jnp.zeros((z.rows, z.cols), F32)

        def source(q):
            return dagg[jnp.minimum(q, z.lent - 1)]

        spread(z, meta, counts[0] + counts[1], z.pairs, at, source, acc, z.tiles, z.lent)
        to_west[...] = acc[pl.ds(0, z.edge)].astype(BF16)
        to_east[...] = acc[pl.ds(z.edge, z.edge)].astype(BF16)
        for copy in copies:
            copy.wait()

    return call(
        kernel,
        "early_lent",
        [SMEM] * 3 + [VMEM] * 7 + [ANY],
        [VMEM] * 3 + [ANY] + [VMEM] * 2,
        [z.nodes(z.lent)] * 3 + [jax.ShapeDtypeStruct(grads.shape, BF16)] + [z.nodes(z.edge)] * 2,
        [z.held(z.lent + 1, F32), pltpu.SemaphoreType.DMA((z.lent,))],
        12,
        (meta, counts, bound, part, fw, fe, slope, outer, at, wt, grads),
        {10: 3},
    )


def finish(z, bound, part, fw, fe, grads):
    def kernel(bound, part, fw, fe, _g, grads, keep, sems):
        copies = []
        for i in range(z.lent):
            got = fw[i] if i < z.edge else fe[i - z.edge]
            keep[i] = (part[i] + got.astype(F32)).astype(BF16)
            copy = pltpu.make_async_copy(
                keep.at[i], grads.at[0, bound[0, i // z.edge, i % z.edge]], sems.at[i]
            )
            copy.start()
            copies.append(copy)
        for copy in copies:
            copy.wait()

    return call(
        kernel,
        "finish",
        [SMEM] + [VMEM] * 3 + [ANY],
        ANY,
        jax.ShapeDtypeStruct(grads.shape, BF16),
        [z.held(z.lent), pltpu.SemaphoreType.DMA((z.lent,))],
        12,
        (bound, part, fw, fe, grads),
        {4: 0},
    )


def per_device(
    node_in, out_cot, adjacency, tile_nbrs, bound_tiles, live_tiles, w_self, w_nbr, pre_bias, w_out
):
    z = Sizes(adjacency, node_in, bound_tiles)
    t, r, c = z.tiles, z.rows, z.cols
    features = node_in.reshape(t, r, c)
    cot = out_cot.reshape(t, r, c)
    pieces = lax.axis_size(PLANE)
    me = lax.axis_index(PLANE).astype(jnp.int32).reshape(1)

    west, east = lend(z, bound_tiles, features)
    from_west = passed_along(east, 1)
    from_east = passed_along(west, -1)
    *nodes, ap, meta, counts = arrange(z, bound_tiles, tile_nbrs, live_tiles, features, cot, adjacency)
    f0, m1 = tuple(nodes[:2]), tuple(nodes[2:])
    at, wt = turn(z, ap, w_self, w_nbr, w_out)

    west, east, agg_lent = first_lent(z, meta, f0, from_west, from_east, ap, w_self, w_nbr, pre_bias, w_out)
    next_west = passed_along(east, 1)
    next_east = passed_along(west, -1)
    f1_lent, f1_rest, section_out, agg_rest = first_rest(
        z, meta, bound_tiles, live_tiles, f0, from_west, from_east, ap, w_self, w_nbr, pre_bias, w_out,
        west, east,
    )
    f1, agg0 = (f1_lent, f1_rest), (agg_lent, agg_rest)
    own, hidden = second_own(z, f1, m1, w_self, pre_bias, wt)
    act0, slope = saved(z, f0, agg0, w_self, w_nbr, pre_bias)

    agg1, act1, dpre1, dagg1, to_west, to_east = second(
        z, meta, counts, f1, next_west, next_east, ap, at, own, hidden, w_nbr, wt
    )
    back_west = passed_along(to_east, 1)
    back_east = passed_along(to_west, -1)
    grads, part, m0_rest = input_grad(z, 1, meta, counts, live_tiles, m1, dpre1, dagg1, at, wt, None)
    dpre_rest, dagg_rest, outer = early_rest(z, meta, counts, m0_rest, slope, at, wt)
    late = summed_over_parts(weight_grads(z, me, pieces, f1, agg1, act1, m1, dpre1, "weight_grads1"))
    section_out = second_out(z, bound_tiles, live_tiles, f1, act1, w_out, section_out)

    m0_lent, dpre_lent, dagg_lent, grads, to_west, to_east = early_lent(
        z, meta, counts, bound_tiles, part, back_west, back_east, slope, outer, at, wt, grads
    )
    back_west = passed_along(to_east, 1)
    back_east = passed_along(to_west, -1)
    m0, dpre0, dagg0 = (m0_lent, m0_rest), (dpre_lent, dpre_rest), (dagg_lent, dagg_rest)
    early = summed_over_parts(weight_grads(z, me, pieces, f0, agg0, act0, m0, dpre0, "weight_grads0"))
    grads, part, _ = input_grad(z, 0, meta, counts, live_tiles, m0, dpre0, dagg0, at, wt, grads)
    grads = finish(z, bound_tiles, part, back_west, back_east, grads)

    grad_self, grad_nbr, grad_bias, grad_out = unpack(z, early, late)
    return (
        section_out.reshape(2, t * r, c),
        grads.reshape(2, t * r, c),
        grad_self,
        grad_nbr,
        grad_bias,
        grad_out,
    )


def solution(mesh):
    rows = P(AXES)
    in_specs = (rows, rows, rows, rows, rows, rows, P(), P(), P(), P())
    out_specs = (P(None, AXES), P(None, AXES), P(), P(), P(), P())
    return jax.shard_map(
        per_device, mesh=mesh, in_specs=in_specs, out_specs=out_specs, check_vma=False
    )
```

time: 467 us -> 211 us (0.45); the launches traced: 459 us -> 210 us
  other arithmetic: 113 us -> 0.2 us
  waiting for transfers between devices: 118 us -> 18.7 us
  Pallas kernels: 0 us -> 76.5 us
  matrix products: 72 us -> 0 us
  local copies, waits for them, and re-layouts: 80 us -> 25.2 us
  starting transfers between devices: 17 us -> 46.1 us
  between operations: 15.5 us -> 1.89 us
    scatter-add x6 -> x0, other arithmetic: 89.6 us -> none  [the longest x2 76.3 us: backward(): jax.ops.segment_sum(contrib.reshape(tile_count * slot_count, tile_rows, -...]
    pallas_call x0 -> x17, Pallas kernels: none -> 76.5 us  [call(): pl.pallas_call(kernel, in_specs=in_specs, out_specs=out_specs, out_shape=...]
    psum x1 -> x0, waiting for transfers between devices: 75.5 us -> none  [per_device(): lax.psum((early[0], early[1], early[2], early[3], later[0], later[1], lat...]
    dot_general x22 -> x0, matrix products: 72 us -> none  [the longest x2 16.2 us: backward(): jnp.einsum('tkij,tic->tkjc', adjacency, grad_gathered.reshape(tile_count,...]
    psum x1 -> x0, blocking collectives: 44 us -> none  [per_device(): lax.psum((early[0], early[1], early[2], early[3], later[0], later[1], lat...]
    all_gather x0 -> x2, blocking collectives: none -> 41.2 us  [summed_over_parts(): return lax.all_gather(share, PLANE, axis=0, tiled=True)]
    reshape x2 -> x0, local copies, waits for them, and re-layouts: 34.9 us -> none  [backward(): contrib.reshape(tile_count * slot_count, tile_rows, -1)]
    ppermute x8 -> x26, starting transfers between devices: 17 us -> 46.1 us  [the longest x8 22.6 us: passed_along(): lax.ppermute(value, AXES, [(i, (i + steps) % count) for i in range(count)])]
  transfers between devices with their start and end apart: 9 -> 26, of which waited for: 7 -> 6; matrix products, arithmetic and copies ran while one was open for 10% -> 0% of each run, Pallas kernels for 0% -> 28%
where the time goes in v2:
time: 211 us; the launch traced here: 210 us
  Pallas kernels  76.5 us (36%)
  starting transfers between devices  46.1 us (22%)
  blocking collectives  41.2 us (20%)
  local copies, waits for them, and re-layouts  25.2 us (12%)
  waiting for transfers between devices  18.7 us (9%)
    pallas_call x17, Pallas kernels, call(): pl.pallas_call(kernel, in_specs=in_specs, out_specs=out_specs, out_shape=...  76.5 us
    all_gather x2, blocking collectives, summed_over_parts(): return lax.all_gather(share, PLANE, axis=0, tiled=True)  41.2 us
    unnamed x83, local copies, waits for them, and re-layouts  25.2 us
    ppermute x8, starting transfers between devices, passed_along(): lax.ppermute(value, AXES, [(i, (i + steps) % count) for i in range(count)])  22.6 us
    ppermute x14, starting transfers between devices, plane_pass(): lax.ppermute(value, PLANE, [(i, (i + steps) % count) for i in range(count)])  13.4 us
    ppermute x8, waiting for transfers between devices, passed_along(): lax.ppermute(value, AXES, [(i, (i + steps) % count) for i in range(count)])  12.7 us
    ppermute x4, starting transfers between devices, summed_over_parts(): other = lax.ppermute(share, 'feat', [(i, i ^ step) for i in range(lines)])  10.1 us
  transfers between devices with their start and end apart: 26, of which 6 were waited for; matrix products, arithmetic and copies ran while one was open for 0% of the time, Pallas kernels for 28%

profile of v2, /device:TPU:0, one launch (start us, length us, event | category | flops | bytes accessed | tf_op | source)
XLA Modules:
  0.0 209.8 jit_solution(5191217097224960945)
XLA Ops:
  2.9 3.1 %lend.1 = (bf16[8,128,256]{2,1,0:T(8,128)(2,1)}, bf16[8,128,256]{2,1,0:T(8,128)(2,1)}) custom-call(s32[1,2,8]{2,1,0:T(2,128)S(1)} %copy-done.37, bf16[32,128,256]{2,1,0:T(8,128)(2,1)S(1)} %bitcast.5), custom_call_target="tpu_custom_call" | custom-call | flops 1000 | bytes 1000 | tf_op jit(solution)/shard_map/lend/pallas_call | solution.py:74
  6.0 3.1 %collective-permute-start = (bf16[8,128,256]{2,1,0:T(8,128)(2,1)}, bf16[8,128,256]{2,1,0:T(8,128)(2,1)S(1)}, u32[]{:S(2)}, u32[]{:S(2)}) collective-permute-start(bf16[8,128,256]{2,1,0:T(8,128)(2,1)} %get-tuple-element.71), channel_id=1, source_target_pairs={{0,1},{1,2},{2,3},{3,4},{4,5},{5,6},{6,7},{7,8},{8,9},{9,10},{10,1... | collective-permute-start | bytes 1572872 | tf_op jit(solution)/shard_map/ppermute | solution.py:62
  9.1 3.4 %collective-permute-start.1 = (bf16[8,128,256]{2,1,0:T(8,128)(2,1)}, bf16[8,128,256]{2,1,0:T(8,128)(2,1)}, u32[]{:S(2)}, u32[]{:S(2)}) collective-permute-start(bf16[8,128,256]{2,1,0:T(8,128)(2,1)} %get-tuple-element.72), channel_id=1, source_target_pairs={{0,31},{1,0},{2,1},{3,2},{4,3},{5,4},{6,5},{7,6},{8,7},{9,8},{10,9... | collective-permute-start | bytes 1572872 | tf_op jit(solution)/shard_map/ppermute | solution.py:62
  20.0 10.7 %arrange.1 = (bf16[16,128,256]{2,1,0:T(8,128)(2,1)S(1)}, bf16[16,128,256]{2,1,0:T(8,128)(2,1)S(1)}, bf16[16,128,256]{2,1,0:T(8,128)(2,1)S(1)}, bf16[16,128,256]{...) custom-call(s32[1,2,8]{2,1,0:T(2,128)S(1)} %copy-done.38, ...), custom_call_target="tpu_custom_call" | custom-call | flops 1000 | bytes 1000 | tf_op jit(solution)/shard_map/arrange/pallas_call | solution.py:74
  30.7 3.3 %collective-permute-done.1.fe = bf16[8,128,256]{2,1,0:T(8,128)(2,1)} collective-permute-done((bf16[8,128,256]{2,1,0:T(8,128)(2,1)}, bf16[8,128,256]{2,1,0:T(8,128)(2,1)}, u32[]{:S(2)}, u32[]{:S(2)}) %collective-permute-start.1) | collective-permute-done | bytes 524320 | tf_op jit(solution)/shard_map/ppermute | solution.py:62
  34.0 3.9 %first_lent.1 = (bf16[8,128,256]{2,1,0:T(8,128)(2,1)S(1)}, bf16[8,128,256]{2,1,0:T(8,128)(2,1)S(1)}, bf16[16,128,256]{2,1,0:T(8,128)(2,1)S(1)}) custom-call(s32[384]{0:T(512)S(1)} %get-tuple-element.68.meta, bf16[16,128,256]{2,1,0:T(8,128)(2,1)S(1)} %get-tuple-element.69.f_lent.refs_0_, bf16[16,128,256]{2,1,0:T(8,128)(2,1)S(1)} %get-tuple-element.70.f_rest.refs_1_, ...), custom_call_target="tpu_custom_call" | custom-call | flops 1000 | bytes 1000 | tf_op jit(solution)/shard_map/first_lent/pallas_call | solution.py:74
  40.4 3.8 %collective-permute-start.3 = (bf16[8,128,256]{2,1,0:T(8,128)(2,1)S(1)}, bf16[8,128,256]{2,1,0:T(8,128)(2,1)S(1)}, u32[]{:S(2)}, u32[]{:S(2)}) collective-permute-start(bf16[8,128,256]{2,1,0:T(8,128)(2,1)S(1)} %get-tuple-element.74.west), channel_id=1, source_target_pairs={{0,31},{1,0},{2,1},{3,2},{4,3},{5,4},{6,5},{7,6},{8,7},{9,8},{10,9... | collective-permute-start | bytes 1572872 | tf_op jit(solution)/shard_map/ppermute | solution.py:62
  44.2 3.1 %turn.1 = (bf16[128,128,128]{2,1,0:T(8,128)(2,1)S(1)}, bf16[2,3,256,256]{3,2,1,0:T(8,128)(2,1)S(1)}) custom-call(bf16[32,4,128,128]{3,2,1,0:T(8,128)(2,1)S(1)} %get-tuple-element.73.ap, bf16[2,256,256]{2,1,0:T(8,128)(2,1)S(1)} %copy-done.22, bf16[2,256,256]{2,1,0:T(8,128)(2,1)S(1)} %copy-done.21, bf16[2,256,256]{2,1,0:T(8,128)(2,1)S(1)} %copy-done.28), custom_call_target="tpu_custom_call" | custom-call | flops 1000 | bytes 1000 | tf_op jit(solution)/shard_map/turn/pallas_call | solution.py:74
  47.3 5.6 %first_rest.1 = (bf16[16,128,256]{2,1,0:T(8,128)(2,1)S(1)}, bf16[16,128,256]{2,1,0:T(8,128)(2,1)S(1)}, bf16[2,32,128,256]{3,2,1,0:T(8,128)(2,1)}, bf16[16,128,256]{2,1,0:T(8,128)(2,1)S(1)}) custom-call(s32[384]{0:T(512)S(1)} %get-tuple-element.68.meta, s32[1,2,8]{2,1,0:T(2,128)S(1)} %copy-done.38, s32[1]{0:T(128)S(6)} %copy.25.live, ...), custom_call_target="tpu_custom_call" | custom-call | flops 1000 | bytes 1000 | tf_op jit(solution)/shard_map/first_rest/pallas_call | solution.py:74
  56.7 8.0 %collective-permute-done.3.fe = bf16[8,128,256]{2,1,0:T(8,128)(2,1)S(1)} collective-permute-done((bf16[8,128,256]{2,1,0:T(8,128)(2,1)S(1)}, bf16[8,128,256]{2,1,0:T(8,128)(2,1)S(1)}, u32[]{:S(2)}, u32[]{:S(2)}) %collective-permute-start.3) | collective-permute-done | bytes 524320 | tf_op jit(solution)/shard_map/ppermute | solution.py:62
  64.7 8.7 %second.1 = (bf16[32,128,256]{2,1,0:T(8,128)(2,1)S(1)}, bf16[32,128,256]{2,1,0:T(8,128)(2,1)S(1)}, bf16[32,128,256]{2,1,0:T(8,128)(2,1)S(1)}, bf16[32,128,256]{2...) custom-call(s32[384]{0:T(512)S(1)} %get-tuple-element.68.meta, ...), custom_call_target="tpu_custom_call" | custom-call | flops 1000 | bytes 1000 | tf_op jit(solution)/shard_map/second/pallas_call | solution.py:74
  79.4 4.8 %collective-permute-start.5 = (bf16[8,128,256]{2,1,0:T(8,128)(2,1)}, bf16[8,128,256]{2,1,0:T(8,128)(2,1)}, u32[]{:S(2)}, u32[]{:S(2)}) collective-permute-start(bf16[8,128,256]{2,1,0:T(8,128)(2,1)} %get-tuple-element.91), channel_id=1, source_target_pairs={{0,31},{1,0},{2,1},{3,2},{4,3},{5,4},{6,5},{7,6},{8,7},{9,8},{10,9... | collective-permute-start | bytes 1572872 | tf_op jit(solution)/shard_map/ppermute | solution.py:62
  93.9 3.5 %weight_grads1.1 = (f32[112,256]{1,0:T(8,128)S(1)}, f32[112,256]{1,0:T(8,128)S(1)}, f32[112,256]{1,0:T(8,128)S(1)}, f32[112,256]{1,0:T(8,128)S(1)}, f32[112,256]...) custom-call(s32[1]{0:T(128)} %bitcast.4.me, ...), custom_call_target="tpu_custom_call" | custom-call | flops 1000 | bytes 1000 | tf_op jit(solution)/shard_map/weight_grads1/pallas_call | solution.py:74
  106.5 3.0 %saved.1 = (bf16[32,128,256]{2,1,0:T(8,128)(2,1)S(1)}, f32[32,128,256]{2,1,0:T(8,128)S(1)}) custom-call(bf16[16,128,256]{2,1,0:T(8,128)(2,1)S(1)} %get-tuple-element.69.f_lent.refs_0_, bf16[16,128,256]{2,1,0:T(8,128)(2,1)S(1)} %get-tuple-element.70.f_rest.refs_1_, bf16[16,128,256]{2,1,0:T(8,128)(2,1)S(1)} %copy-done.25, ...), custom_call_target="tpu_custom_call" | custom-call | flops 1000 | bytes 1000 | tf_op jit(solution)/shard_map/saved/pallas_call | solution.py:74
  109.6 7.2 %input_grad1.1 = (bf16[2,32,128,256]{3,2,1,0:T(8,128)(2,1)}, f32[16,128,256]{2,1,0:T(8,128)S(1)}, bf16[16,128,256]{2,1,0:T(8,128)(2,1)S(1)}) custom-call(s32[384]{0:T(512)S(1)} %get-tuple-element.68.meta, s32[8]{0:T(128)S(1)} %get-tuple-element.78.counts, s32[1]{0:T(128)S(6)} %copy.25.live, bf16[16,128,256]{2,1,0:T(8,128)(2,1)S(1)} %copy-done.10, ...), custom_call_target="tpu_custom_call" | custom-call | flops 1000 | bytes 1000 | tf_op jit(solution)/shard_map/input_grad1/pallas_call | solution.py:74
  119.6 4.1 %early_lent.1 = (bf16[16,128,256]{2,1,0:T(8,128)(2,1)S(1)}, bf16[16,128,256]{2,1,0:T(8,128)(2,1)S(1)}, bf16[16,128,256]{2,1,0:T(8,128)(2,1)S(1)}, bf16[2,32,128,...) custom-call(s32[384]{0:T(512)S(1)} %get-tuple-element.68.meta, ...), custom_call_target="tpu_custom_call", output_to_operand_aliasing={{3}: (10, {})} | custom-call | flops 1000 | bytes 1000 | tf_op jit(solution)/shard_map/early_lent/pallas_call | solution.py:74
  123.8 3.5 %weight_grads0.1 = (f32[112,256]{1,0:T(8,128)S(1)}, f32[112,256]{1,0:T(8,128)S(1)}, f32[112,256]{1,0:T(8,128)S(1)}, f32[112,256]{1,0:T(8,128)S(1)}, f32[112,256]...) custom-call(s32[1]{0:T(128)} %bitcast.4.me, ...), custom_call_target="tpu_custom_call" | custom-call | flops 1000 | bytes 1000 | tf_op jit(solution)/shard_map/weight_grads0/pallas_call | solution.py:74
  129.8 3.6 %second_out.1 = bf16[2,32,128,256]{3,2,1,0:T(8,128)(2,1)} custom-call(s32[1,2,8]{2,1,0:T(2,128)S(1)} %copy-done.39, s32[1]{0:T(128)S(6)} %copy.25.live, bf16[16,128,256]{2,1,0:T(8,128)(2,1)S(1)} %copy-done.4, bf16[16,128,256]{2,1,0:T(8,128)(2,1)S(1)} %copy-done.7, bf16[32,128,256]{2,1,0:T(8,128)(2,1)S(1)} %copy-done.20, ...), custom_call_target="tpu_custom_call", output_to_operand_aliasing={{}: (6, {})} | custom-call | flops 1000 | bytes 1000 | tf_op jit(solution)/shard_map/second_out/pallas_call | solution.py:74
  133.4 2.9 %collective-permute-start.12 = (f32[112,256]{1,0:T(8,128)S(1)}, f32[112,256]{1,0:T(8,128)S(1)}, u32[]{:S(2)}, u32[]{:S(2)}) collective-permute-start(f32[112,256]{1,0:T(8,128)S(1)} %get-tuple-element.114), channel_id=1, source_target_pairs={{0,20},{4,24},{8,28},{12,0},{16,4},{20,8},{24,12},{28,16},{1,21},{... | collective-permute-start | bytes 344072 | tf_op jit(solution)/shard_map/ppermute | solution.py:471
  138.6 9.0 %collective-permute-start.25 = (bf16[112,256]{1,0:T(8,128)(2,1)S(1)}, bf16[112,256]{1,0:T(8,128)(2,1)S(1)}, u32[]{:S(2)}, u32[]{:S(2)}) collective-permute-start(bf16[112,256]{1,0:T(8,128)(2,1)S(1)} %add_convert_fusion.1), channel_id=1, source_target_pairs={{0,2},{1,3},{2,0},{3,1},{4,6},{5,7},{6,4},{7,5},{8,10},{9,11},{10,... | collective-permute-start | bytes 172040 | tf_op jit(solution)/shard_map/ppermute | solution.py:488
  150.9 5.3 %collective-permute-start.7 = (bf16[8,128,256]{2,1,0:T(8,128)(2,1)S(1)}, bf16[8,128,256]{2,1,0:T(8,128)(2,1)S(1)}, u32[]{:S(2)}, u32[]{:S(2)}) collective-permute-start(bf16[8,128,256]{2,1,0:T(8,128)(2,1)S(1)} %get-tuple-element.106), channel_id=1, source_target_pairs={{0,31},{1,0},{2,1},{3,2},{4,3},{5,4},{6,5},{7,6},{8,7},{9,8},{10,9... | collective-permute-start | bytes 1572872 | tf_op jit(solution)/shard_map/ppermute | solution.py:62
  157.0 24.2 %all_gather.7.late = bf16[896,256]{1,0:T(8,128)(2,1)S(1)} all-gather(bf16[112,256]{1,0:T(8,128)(2,1)S(1)} %add_convert_fusion), channel_id=1, replica_groups=mesh['dom'=4,'phase'=2,'feat'=4] {'dom','phase'}, dimensions={0}, use_global_device_ids=true | all-gather | bytes 516096 | tf_op jit(solution)/shard_map/all_gather | solution.py:493
  181.2 17.0 %all_gather.6.early = bf16[896,256]{1,0:T(8,128)(2,1)S(1)} all-gather(bf16[112,256]{1,0:T(8,128)(2,1)S(1)} %add_convert_fusion.3), channel_id=1, replica_groups=mesh['dom'=4,'phase'=2,'feat'=4] {'dom','phase'}, dimensions={0}, use_global_device_ids=true | all-gather | bytes 516096 | tf_op jit(solution)/shard_map/all_gather | solution.py:493
  198.2 8.5 %input_grad0.1 = (bf16[2,32,128,256]{3,2,1,0:T(8,128)(2,1)}, f32[16,128,256]{2,1,0:T(8,128)S(1)}, bf16[16,128,256]{2,1,0:T(8,128)(2,1)}) custom-call(s32[384]{0:T(512)S(1)} %get-tuple-element.68.meta, s32[8]{0:T(128)S(1)} %get-tuple-element.78.counts, s32[1]{0:T(128)S(6)} %copy.25.live, ...), custom_call_target="tpu_custom_call", output_to_operand_aliasing={{0}: (11, {})} | custom-call | flops 1000 | bytes 1000 | tf_op jit(solution)/shard_map/input_grad0/pallas_call | solution.py:74
  (136 shorter events, 54.5 us)
Async XLA Ops:
  6.0 24.7 %collective-permute-start = (bf16[8,128,256]{2,1,0:T(8,128)(2,1)}, bf16[8,128,256]{2,1,0:T(8,128)(2,1)S(1)}, u32[]{:S(2)}, u32[]{:S(2)}) collective-permute-start(bf16[8,128,256]{2,1,0:T(8,128)(2,1)} %get-tuple-element.71), channel_id=1, source_target_pairs={{0,1},{1,2},{2,3},{3,4},{4,5},{5,6},{6,7},{7,8},{8,9},{9,10},{10,1... | collective-permute-start | bytes 1572872 | tf_op jit(solution)/shard_map/ppermute | solution.py:62
  9.1 24.9 %collective-permute-start.1 = (bf16[8,128,256]{2,1,0:T(8,128)(2,1)}, bf16[8,128,256]{2,1,0:T(8,128)(2,1)}, u32[]{:S(2)}, u32[]{:S(2)}) collective-permute-start(bf16[8,128,256]{2,1,0:T(8,128)(2,1)} %get-tuple-element.72), channel_id=1, source_target_pairs={{0,31},{1,0},{2,1},{3,2},{4,3},{5,4},{6,5},{7,6},{8,7},{9,8},{10,9... | collective-permute-start | bytes 1572872 | tf_op jit(solution)/shard_map/ppermute | solution.py:62
  38.9 17.8 %collective-permute-start.2 = (bf16[8,128,256]{2,1,0:T(8,128)(2,1)S(1)}, bf16[8,128,256]{2,1,0:T(8,128)(2,1)S(1)}, u32[]{:S(2)}, u32[]{:S(2)}) collective-permute-start(bf16[8,128,256]{2,1,0:T(8,128)(2,1)S(1)} %get-tuple-element.75.east), channel_id=1, source_target_pairs={{0,1},{1,2},{2,3},{3,4},{4,5},{5,6},{6,7},{7,8},{8,9},{9,10},{10,1... | collective-permute-start | bytes 1572872 | tf_op jit(solution)/shard_map/ppermute | solution.py:62
  40.4 24.3 %collective-permute-start.3 = (bf16[8,128,256]{2,1,0:T(8,128)(2,1)S(1)}, bf16[8,128,256]{2,1,0:T(8,128)(2,1)S(1)}, u32[]{:S(2)}, u32[]{:S(2)}) collective-permute-start(bf16[8,128,256]{2,1,0:T(8,128)(2,1)S(1)} %get-tuple-element.74.west), channel_id=1, source_target_pairs={{0,31},{1,0},{2,1},{3,2},{4,3},{5,4},{6,5},{7,6},{8,7},{9,8},{10,9... | collective-permute-start | bytes 1572872 | tf_op jit(solution)/shard_map/ppermute | solution.py:62
  78.9 26.7 %collective-permute-start.4 = (bf16[8,128,256]{2,1,0:T(8,128)(2,1)}, bf16[8,128,256]{2,1,0:T(8,128)(2,1)}, u32[]{:S(2)}, u32[]{:S(2)}) collective-permute-start(bf16[8,128,256]{2,1,0:T(8,128)(2,1)} %get-tuple-element.90), channel_id=1, source_target_pairs={{0,1},{1,2},{2,3},{3,4},{4,5},{5,6},{6,7},{7,8},{8,9},{9,10},{10,1... | collective-permute-start | bytes 1572872 | tf_op jit(solution)/shard_map/ppermute | solution.py:62
  79.4 26.2 %collective-permute-start.5 = (bf16[8,128,256]{2,1,0:T(8,128)(2,1)}, bf16[8,128,256]{2,1,0:T(8,128)(2,1)}, u32[]{:S(2)}, u32[]{:S(2)}) collective-permute-start(bf16[8,128,256]{2,1,0:T(8,128)(2,1)} %get-tuple-element.91), channel_id=1, source_target_pairs={{0,31},{1,0},{2,1},{3,2},{4,3},{5,4},{6,5},{7,6},{8,7},{9,8},{10,9... | collective-permute-start | bytes 1572872 | tf_op jit(solution)/shard_map/ppermute | solution.py:62
  98.4 5.5 %collective-permute-start.18 = (f32[112,256]{1,0:T(8,128)S(1)}, f32[112,256]{1,0:T(8,128)S(1)}, u32[]{:S(2)}, u32[]{:S(2)}) collective-permute-start(f32[112,256]{1,0:T(8,128)S(1)} %get-tuple-element.120), channel_id=1, source_target_pairs={{0,8},{4,12},{8,16},{12,20},{16,24},{20,28},{24,0},{28,4},{1,9},{5... | collective-permute-start | bytes 344072 | tf_op jit(solution)/shard_map/ppermute | solution.py:471
  98.4 28.9 %collective-permute-start.19 = (f32[112,256]{1,0:T(8,128)S(1)}, f32[112,256]{1,0:T(8,128)S(1)}, u32[]{:S(2)}, u32[]{:S(2)}) collective-permute-start(f32[112,256]{1,0:T(8,128)S(1)} %get-tuple-element.121), channel_id=1, source_target_pairs={{0,12},{4,16},{8,20},{12,24},{16,28},{20,0},{24,4},{28,8},{1,13},{... | collective-permute-start | bytes 344072 | tf_op jit(solution)/shard_map/ppermute | solution.py:471
  102.6 25.8 %collective-permute-start.20 = (f32[112,256]{1,0:T(8,128)S(1)}, f32[112,256]{1,0:T(8,128)S(1)}, u32[]{:S(2)}, u32[]{:S(2)}) collective-permute-start(f32[112,256]{1,0:T(8,128)S(1)} %get-tuple-element.122), channel_id=1, source_target_pairs={{0,16},{4,20},{8,24},{12,28},{16,0},{20,4},{24,8},{28,12},{1,17},{... | collective-permute-start | bytes 344072 | tf_op jit(solution)/shard_map/ppermute | solution.py:471
  103.9 25.6 %collective-permute-start.21 = (f32[112,256]{1,0:T(8,128)S(1)}, f32[112,256]{1,0:T(8,128)S(1)}, u32[]{:S(2)}, u32[]{:S(2)}) collective-permute-start(f32[112,256]{1,0:T(8,128)S(1)} %get-tuple-element.123), channel_id=1, source_target_pairs={{0,20},{4,24},{8,28},{12,0},{16,4},{20,8},{24,12},{28,16},{1,21},{... | collective-permute-start | bytes 344072 | tf_op jit(solution)/shard_map/ppermute | solution.py:471
  105.6 23.8 %collective-permute-start.22 = (f32[112,256]{1,0:T(8,128)S(1)}, f32[112,256]{1,0:T(8,128)S(1)}, u32[]{:S(2)}, u32[]{:S(2)}) collective-permute-start(f32[112,256]{1,0:T(8,128)S(1)} %get-tuple-element.124), channel_id=1, source_target_pairs={{0,24},{4,28},{8,0},{12,4},{16,8},{20,12},{24,16},{28,20},{1,25},{... | collective-permute-start | bytes 344072 | tf_op jit(solution)/shard_map/ppermute | solution.py:471
  105.6 23.8 %collective-permute-start.23 = (f32[112,256]{1,0:T(8,128)S(1)}, f32[112,256]{1,0:T(8,128)S(1)}, u32[]{:S(2)}, u32[]{:S(2)}) collective-permute-start(f32[112,256]{1,0:T(8,128)S(1)} %get-tuple-element.125), channel_id=1, source_target_pairs={{0,28},{4,0},{8,4},{12,8},{16,12},{20,16},{24,20},{28,24},{1,29},{... | collective-permute-start | bytes 344072 | tf_op jit(solution)/shard_map/ppermute | solution.py:471
  127.3 9.1 %collective-permute-start.10 = (f32[112,256]{1,0:T(8,128)S(1)}, f32[112,256]{1,0:T(8,128)S(1)}, u32[]{:S(2)}, u32[]{:S(2)}) collective-permute-start(f32[112,256]{1,0:T(8,128)S(1)} %get-tuple-element.112), channel_id=1, source_target_pairs={{0,12},{4,16},{8,20},{12,24},{16,28},{20,0},{24,4},{28,8},{1,13},{... | collective-permute-start | bytes 344072 | tf_op jit(solution)/shard_map/ppermute | solution.py:471
  128.4 9.9 %collective-permute-start.11 = (f32[112,256]{1,0:T(8,128)S(1)}, f32[112,256]{1,0:T(8,128)S(1)}, u32[]{:S(2)}, u32[]{:S(2)}) collective-permute-start(f32[112,256]{1,0:T(8,128)S(1)} %get-tuple-element.113), channel_id=1, source_target_pairs={{0,16},{4,20},{8,24},{12,28},{16,0},{20,4},{24,8},{28,12},{1,17},{... | collective-permute-start | bytes 344072 | tf_op jit(solution)/shard_map/ppermute | solution.py:471
  129.5 6.7 %collective-permute-start.24 = (bf16[112,256]{1,0:T(8,128)(2,1)S(1)}, bf16[112,256]{1,0:T(8,128)(2,1)S(1)}, u32[]{:S(2)}, u32[]{:S(2)}) collective-permute-start(bf16[112,256]{1,0:T(8,128)(2,1)S(1)} %add_convert_fusion.2), channel_id=1, source_target_pairs={{0,1},{1,0},{2,3},{3,2},{4,5},{5,4},{6,7},{7,6},{8,9},{9,8},{10,11... | collective-permute-start | bytes 172040 | tf_op jit(solution)/shard_map/ppermute | solution.py:488
  136.3 11.4 %collective-permute-start.13 = (f32[112,256]{1,0:T(8,128)S(1)}, f32[112,256]{1,0:T(8,128)S(1)}, u32[]{:S(2)}, u32[]{:S(2)}) collective-permute-start(f32[112,256]{1,0:T(8,128)S(1)} %get-tuple-element.115), channel_id=1, source_target_pairs={{0,24},{4,28},{8,0},{12,4},{16,8},{20,12},{24,16},{28,20},{1,25},{... | collective-permute-start | bytes 344072 | tf_op jit(solution)/shard_map/ppermute | solution.py:471
  136.3 11.4 %collective-permute-start.14 = (f32[112,256]{1,0:T(8,128)S(1)}, f32[112,256]{1,0:T(8,128)S(1)}, u32[]{:S(2)}, u32[]{:S(2)}) collective-permute-start(f32[112,256]{1,0:T(8,128)S(1)} %get-tuple-element.116), channel_id=1, source_target_pairs={{0,28},{4,0},{8,4},{12,8},{16,12},{20,16},{24,20},{28,24},{1,29},{... | collective-permute-start | bytes 344072 | tf_op jit(solution)/shard_map/ppermute | solution.py:471
  136.5 11.2 %collective-permute-start.8 = (f32[112,256]{1,0:T(8,128)S(1)}, f32[112,256]{1,0:T(8,128)S(1)}, u32[]{:S(2)}, u32[]{:S(2)}) collective-permute-start(f32[112,256]{1,0:T(8,128)S(1)} %get-tuple-element.110), channel_id=1, source_target_pairs={{0,4},{4,8},{8,12},{12,16},{16,20},{20,24},{24,28},{28,0},{1,5},{5... | collective-permute-start | bytes 344072 | tf_op jit(solution)/shard_map/ppermute | solution.py:471
  138.3 9.4 %collective-permute-start.9 = (f32[112,256]{1,0:T(8,128)S(1)}, f32[112,256]{1,0:T(8,128)S(1)}, u32[]{:S(2)}, u32[]{:S(2)}) collective-permute-start(f32[112,256]{1,0:T(8,128)S(1)} %get-tuple-element.111), channel_id=1, source_target_pairs={{0,8},{4,12},{8,16},{12,20},{16,24},{20,28},{24,0},{28,4},{1,9},{5... | collective-permute-start | bytes 344072 | tf_op jit(solution)/shard_map/ppermute | solution.py:471
  138.6 12.1 %collective-permute-start.25 = (bf16[112,256]{1,0:T(8,128)(2,1)S(1)}, bf16[112,256]{1,0:T(8,128)(2,1)S(1)}, u32[]{:S(2)}, u32[]{:S(2)}) collective-permute-start(bf16[112,256]{1,0:T(8,128)(2,1)S(1)} %add_convert_fusion.1), channel_id=1, source_target_pairs={{0,2},{1,3},{2,0},{3,1},{4,6},{5,7},{6,4},{7,5},{8,10},{9,11},{10,... | collective-permute-start | bytes 172040 | tf_op jit(solution)/shard_map/ppermute | solution.py:488
  147.8 8.4 %collective-permute-start.15 = (bf16[112,256]{1,0:T(8,128)(2,1)S(1)}, bf16[112,256]{1,0:T(8,128)(2,1)S(1)}, u32[]{:S(2)}, u32[]{:S(2)}) collective-permute-start(bf16[112,256]{1,0:T(8,128)(2,1)S(1)} %add_convert_fusion.5), channel_id=1, source_target_pairs={{0,1},{1,0},{2,3},{3,2},{4,5},{5,4},{6,7},{7,6},{8,9},{9,8},{10,11... | collective-permute-start | bytes 172040 | tf_op jit(solution)/shard_map/ppermute | solution.py:488
  150.8 57.2 %collective-permute-start.6 = (bf16[8,128,256]{2,1,0:T(8,128)(2,1)S(1)}, bf16[8,128,256]{2,1,0:T(8,128)(2,1)S(1)}, u32[]{:S(2)}, u32[]{:S(2)}) collective-permute-start(bf16[8,128,256]{2,1,0:T(8,128)(2,1)S(1)} %get-tuple-element.105), channel_id=1, source_target_pairs={{0,1},{1,2},{2,3},{3,4},{4,5},{5,6},{6,7},{7,8},{8,9},{9,10},{10,1... | collective-permute-start | bytes 1572872 | tf_op jit(solution)/shard_map/ppermute | solution.py:62
  150.9 57.1 %collective-permute-start.7 = (bf16[8,128,256]{2,1,0:T(8,128)(2,1)S(1)}, bf16[8,128,256]{2,1,0:T(8,128)(2,1)S(1)}, u32[]{:S(2)}, u32[]{:S(2)}) collective-permute-start(bf16[8,128,256]{2,1,0:T(8,128)(2,1)S(1)} %get-tuple-element.106), channel_id=1, source_target_pairs={{0,31},{1,0},{2,1},{3,2},{4,3},{5,4},{6,5},{7,6},{8,7},{9,8},{10,9... | collective-permute-start | bytes 1572872 | tf_op jit(solution)/shard_map/ppermute | solution.py:62
  156.2 25.0 %collective-permute-start.16 = (bf16[112,256]{1,0:T(8,128)(2,1)S(1)}, bf16[112,256]{1,0:T(8,128)(2,1)S(1)}, u32[]{:S(2)}, u32[]{:S(2)}) collective-permute-start(bf16[112,256]{1,0:T(8,128)(2,1)S(1)} %add_convert_fusion.4), channel_id=1, source_target_pairs={{0,2},{1,3},{2,0},{3,1},{4,6},{5,7},{6,4},{7,5},{8,10},{9,11},{10,... | collective-permute-start | bytes 172040 | tf_op jit(solution)/shard_map/ppermute | solution.py:488
  (43 other events, 338.8 us)

commit v3 on v2

--- a/solution.py
+++ b/solution.py
@@ -10,7 +10,7 @@
 BF16 = jnp.bfloat16
 F32 = jnp.float32
 UNROLL = 8
-ANY = pl.BlockSpec(memory_space=pl.ANY)
+ANY = pl.BlockSpec(memory_space=pltpu.HBM)
 SMEM = pl.BlockSpec(memory_space=pltpu.SMEM)
 VMEM = pl.BlockSpec(memory_space=pltpu.VMEM)
 MIB = 1024 * 1024
@@ -108,7 +108,7 @@
         [VMEM, VMEM],
         [z.nodes(z.edge), z.nodes(z.edge)],
         [pltpu.SemaphoreType.DMA((z.lent,))],
-        4,
+        2,
         (bound, features),
     )
 
@@ -192,7 +192,7 @@
             jax.ShapeDtypeStruct((8,), jnp.int32),
         ],
         [pltpu.SMEM((z.lent,), jnp.int32), pltpu.SemaphoreType.DMA((3 * z.lent + 3,))],
-        12,
+        6,
         (bound, nbrs, live, features, cot, adjacency),
     )
 
@@ -219,7 +219,7 @@
             jax.ShapeDtypeStruct((2, 3, z.cols, z.cols), BF16),
         ],
         [],
-        12,
+        6,
         (ap, w_self, w_nbr, w_out),
     )
 
@@ -274,7 +274,7 @@
         [VMEM] * 3,
         [z.nodes(z.edge), z.nodes(z.edge), z.nodes(z.lent)],
         [z.held(z.ext)],
-        12,
+        6,
         (meta, *f0, fw, fe, ap, w_self, w_nbr, bias, w_out),
     )
 
@@ -323,7 +323,7 @@
             z.nodes(z.rest),
         ],
         [z.held(z.ext), pltpu.SemaphoreType.DMA((1 + z.lent,))],
-        12,
+        6,
         (meta, bound, live, *f0, fw, fe, ap, w_self, w_nbr, bias, w_out, west, east),
     )
 
@@ -346,7 +346,7 @@
         [VMEM] * 2,
         [z.nodes(z.tiles, F32)] * 2,
         [],
-        12,
+        6,
         (*f1, *m1, w_self, bias, wt),
     )
 
@@ -371,7 +371,7 @@
         [VMEM] * 2,
         [z.nodes(z.tiles), z.nodes(z.tiles, F32)],
         [],
-        12,
+        6,
         (*f0, *agg0, w_self, w_nbr, bias),
     )
 
@@ -407,7 +407,7 @@
             dpre[here] = z.tiled(grad)
             dagg[here] = z.tiled(dot(grad, wt[1, 1]).astype(BF16))
 
-        each_group(z, work)
+        each_group(z, work, unroll=2)
         spread(z, meta, counts[0], z.pairs, at, lambda q: dagg[q], acc, z.tiles, z.lent)
         to_west[...] = acc[pl.ds(0, z.edge)].astype(BF16)
         to_east[...] = acc[pl.ds(z.edge, z.edge)].astype(BF16)
@@ -419,24 +419,24 @@
         [VMEM] * 6,
         [z.nodes(z.tiles)] * 4 + [z.nodes(z.edge)] * 2,
         [z.held(z.ext), z.held(z.lent + 1, F32)],
-        16,
+        8,
         (meta, counts, *f1, fw, fe, ap, at, own, hidden, w_nbr, wt),
     )
 
 
-def weight_grads(z, me, pieces, f, agg, act, m, dpre, name):
+def weight_grads(z, pieces, f, agg, act, m, dpre, name):
     c = z.cols
     piece = -(-(3 * c + 1) // (pieces * 16)) * 16
     height = piece * pieces
     arrays = (f, agg, act, m, dpre)
     flat_args = [x for a in arrays for x in (a if isinstance(a, tuple) else (a,))]
 
-    def kernel(me, *refs):
+    def kernel(*refs):
         refs = list(refs)
         f, agg, act, m, dpre = [
             (refs.pop(0), refs.pop(0)) if isinstance(a, tuple) else refs.pop(0) for a in arrays
         ]
-        outs, acc = refs[:-1], refs[-1]
+        out, acc = refs
         acc[...] = jnp.zeros_like(acc)
 
         def work(part, first):
@@ -451,68 +451,64 @@
 
         each_group(z, work)
         for i in range(pieces):
-            owner = lax.rem(me[0] + i, pieces)
-            outs[i][...] = acc[pl.ds(pl.multiple_of(owner * piece, 16), piece), :]
+            out[i] = acc[pl.ds(i * piece, piece), :].astype(BF16)
 
     return call(
         kernel,
         name,
-        [SMEM] + [VMEM] * len(flat_args),
-        [VMEM] * pieces,
-        [jax.ShapeDtypeStruct((piece, c), F32)] * pieces,
+        [VMEM] * len(flat_args),
+        VMEM,
+        jax.ShapeDtypeStruct((pieces, piece, c), BF16),
         [pltpu.VMEM((height, c), F32)],
-        12,
-        (me, *flat_args),
-    )
-
-
-def plane_pass(value, steps):
-    count = lax.axis_size(PLANE)
-    return lax.ppermute(value, PLANE, [(i, (i + steps) % count) for i in range(count)])
-
-
-def added(parts):
-    total = parts[0].astype(F32)
-    for part in parts[1:]:
-        total = total + part.astype(F32)
-    return total.astype(BF16)
-
-
-def summed_over_parts(pieces):
-    count = len(pieces)
-    share = added([pieces[0]] + [plane_pass(pieces[i], i) for i in range(1, count)])
-    lines = lax.axis_size("feat")
-    if lines & (lines - 1) == 0:
-        step = 1
-        while step < lines:
-            other = lax.ppermute(share, "feat", [(i, i ^ step) for i in range(lines)])
-            share = added([share, other])
-            step *= 2
-    else:
-        share = lax.psum(share.astype(F32), "feat").astype(BF16)
-    return lax.all_gather(share, PLANE, axis=0, tiled=True)
-
-
-def unpack(z, early, late):
+        6,
+        flat_args,
+    )
+
+
+def exchanged(value, axes):
+    return lax.all_to_all(value, axes, 0, 0, tiled=True)
+
+
+def to_all(value, axes):
+    return exchanged(jnp.broadcast_to(value, (lax.axis_size(axes),) + value.shape), axes)
+
+
+def added(values):
+    return jnp.sum(values.astype(F32), axis=0).astype(BF16)
+
+
+def plane_share(pieces):
+    return added(exchanged(pieces, PLANE))
+
+
+def summed_over_parts(shares):
+    shares = added(to_all(jnp.stack(shares), "feat"))
+    return to_all(shares, PLANE)
+
+
+def unpack(z, packed):
     c = z.cols
-
-    def kernel(early, late, g_self, g_nbr, g_bias, g_out):
-        for layer, packed in ((0, early), (1, late)):
-            g_self[layer] = packed[pl.ds(0, c), :].astype(F32)
-            g_nbr[layer] = packed[pl.ds(c, c), :].astype(F32)
-            g_out[layer] = packed[pl.ds(2 * c, c), :].astype(F32)
-            g_bias[layer : layer + 1, :] = packed[pl.ds(3 * c, 16), :].astype(F32)[0:1]
+    pieces, _, piece, _ = packed.shape
+
+    def kernel(packed, g_self, g_nbr, g_bias, g_out, buf):
+        for layer in range(2):
+            for i in range(pieces):
+                buf[pl.ds(i * piece, piece), :] = packed[i, layer].astype(F32)
+            g_self[layer] = buf[pl.ds(0, c), :]
+            g_nbr[layer] = buf[pl.ds(c, c), :]
+            g_out[layer] = buf[pl.ds(2 * c, c), :]
+            g_bias[layer : layer + 1, :] = buf[pl.ds(3 * c, 1), :]
 
     square = jax.ShapeDtypeStruct((2, c, c), F32)
     return call(
         kernel,
         "unpack",
-        [VMEM] * 2,
+        [VMEM],
         [VMEM] * 4,
         [square, square, jax.ShapeDtypeStruct((2, c), F32), square],
-        [],
-        12,
-        (early, late),
+        [pltpu.VMEM((pieces * piece, c), F32)],
+        6,
+        (packed,),
     )
 
 
@@ -547,7 +543,7 @@
         ANY,
         jax.ShapeDtypeStruct(out.shape, BF16),
         [z.held(z.tiles), pltpu.SemaphoreType.DMA((z.lent + 1,))],
-        12,
+        6,
         (bound, live, *f1, act, w_out, out),
         {6: 0},
     )
@@ -608,7 +604,7 @@
             z.nodes(z.rest),
         ],
         [z.held(z.tiles + 1, F32), z.held(z.rest), pltpu.SemaphoreType.DMA],
-        16,
+        10,
         args,
         None if fresh else {len(args) - 1: 0},
     )
@@ -639,7 +635,7 @@
         [VMEM] * 3,
         [z.nodes(z.rest), z.nodes(z.rest), z.nodes(z.lent, F32)],
         [z.held(z.lent + 1, F32)],
-        12,
+        6,
         (meta, counts, m0, slope, at, wt),
     )
 
@@ -686,7 +682,7 @@
         [VMEM] * 3 + [ANY] + [VMEM] * 2,
         [z.nodes(z.lent)] * 3 + [jax.ShapeDtypeStruct(grads.shape, BF16)] + [z.nodes(z.edge)] * 2,
         [z.held(z.lent + 1, F32), pltpu.SemaphoreType.DMA((z.lent,))],
-        12,
+        6,
         (meta, counts, bound, part, fw, fe, slope, outer, at, wt, grads),
         {10: 3},
     )
@@ -713,7 +709,7 @@
         ANY,
         jax.ShapeDtypeStruct(grads.shape, BF16),
         [z.held(z.lent), pltpu.SemaphoreType.DMA((z.lent,))],
-        12,
+        4,
         (bound, part, fw, fe, grads),
         {4: 0},
     )
@@ -727,7 +723,6 @@
     features = node_in.reshape(t, r, c)
     cot = out_cot.reshape(t, r, c)
     pieces = lax.axis_size(PLANE)
-    me = lax.axis_index(PLANE).astype(jnp.int32).reshape(1)
 
     west, east = lend(z, bound_tiles, features)
     from_west = passed_along(east, 1)
@@ -754,7 +749,7 @@
     back_east = passed_along(to_west, -1)
     grads, part, m0_rest = input_grad(z, 1, meta, counts, live_tiles, m1, dpre1, dagg1, at, wt, None)
     dpre_rest, dagg_rest, outer = early_rest(z, meta, counts, m0_rest, slope, at, wt)
-    late = summed_over_parts(weight_grads(z, me, pieces, f1, agg1, act1, m1, dpre1, "weight_grads1"))
+    late = plane_share(weight_grads(z, pieces, f1, agg1, act1, m1, dpre1, "weight_grads1"))
     section_out = second_out(z, bound_tiles, live_tiles, f1, act1, w_out, section_out)
 
     m0_lent, dpre_lent, dagg_lent, grads, to_west, to_east = early_lent(
@@ -763,11 +758,11 @@
     back_west = passed_along(to_east, 1)
     back_east = passed_along(to_west, -1)
     m0, dpre0, dagg0 = (m0_lent, m0_rest), (dpre_lent, dpre_rest), (dagg_lent, dagg_rest)
-    early = summed_over_parts(weight_grads(z, me, pieces, f0, agg0, act0, m0, dpre0, "weight_grads0"))
+    early = plane_share(weight_grads(z, pieces, f0, agg0, act0, m0, dpre0, "weight_grads0"))
     grads, part, _ = input_grad(z, 0, meta, counts, live_tiles, m0, dpre0, dagg0, at, wt, grads)
     grads = finish(z, bound_tiles, part, back_west, back_east, grads)
 
-    grad_self, grad_nbr, grad_bias, grad_out = unpack(z, early, late)
+    grad_self, grad_nbr, grad_bias, grad_out = unpack(z, summed_over_parts([early, late]))
     return (
         section_out.reshape(2, t * r, c),
         grads.reshape(2, t * r, c),

time: 211 us -> 196 us (0.929)
  blocking collectives: 41.2 us -> 16.6 us
  starting transfers between devices: 46.1 us -> 33.3 us
  waiting for transfers between devices: 18.7 us -> 27.6 us
  local copies, waits for them, and re-layouts: 25.2 us -> 33.4 us
  other arithmetic: 0.2 us -> 3.27 us
    all_gather x2 -> x0, blocking collectives: 41.2 us -> none  [summed_over_parts(): return lax.all_gather(share, PLANE, axis=0, tiled=True)]
    ppermute x18 -> x0, starting transfers between devices: 23.5 us -> none  [the longest x14 13.4 us: plane_pass(): lax.ppermute(value, PLANE, [(i, (i + steps) % count) for i in range(count)])]
    all_to_all x0 -> x1, blocking collectives: none -> 16.6 us  [exchanged(): return lax.all_to_all(value, axes, 0, 0, tiled=True)]
    all_to_all x0 -> x3, starting transfers between devices: none -> 12.6 us  [exchanged(): return lax.all_to_all(value, axes, 0, 0, tiled=True)]
    ppermute x8, waiting for transfers between devices: 12.7 us -> 20.5 us  [passed_along(): lax.ppermute(value, AXES, [(i, (i + steps) % count) for i in range(count)])]
    unnamed x83 -> x107, local copies, waits for them, and re-layouts: 25.2 us -> 32.4 us
    all_to_all x0 -> x3, waiting for transfers between devices: none -> 7.06 us  [exchanged(): return lax.all_to_all(value, axes, 0, 0, tiled=True)]
    ppermute x18 -> x0, waiting for transfers between devices: 5.99 us -> none  [the longest x14 3.09 us: plane_pass(): lax.ppermute(value, PLANE, [(i, (i + steps) % count) for i in range(count)])]
  transfers between devices with their start and end apart: 26 -> 11, of which waited for: 6 -> 5; matrix products, arithmetic and copies ran while one was open for 0% -> 1% of each run, Pallas kernels for 28% -> 31%
where the time goes in v3:
time: 196 us; the launch traced here: 193 us
  Pallas kernels  77.5 us (40%)
  local copies, waits for them, and re-layouts  33.4 us (17%)
  starting transfers between devices  33.3 us (17%)
  waiting for transfers between devices  27.6 us (14%)
  blocking collectives  16.6 us (8%)
  other arithmetic  3.27 us (2%)
    pallas_call x17, Pallas kernels, call(): pl.pallas_call(kernel, in_specs=in_specs, out_specs=out_specs, out_shape=...  77.5 us
    unnamed x107, local copies, waits for them, and re-layouts  32.4 us
    ppermute x8, starting transfers between devices, passed_along(): lax.ppermute(value, AXES, [(i, (i + steps) % count) for i in range(count)])  20.7 us
    ppermute x8, waiting for transfers between devices, passed_along(): lax.ppermute(value, AXES, [(i, (i + steps) % count) for i in range(count)])  20.5 us
    all_to_all x1, blocking collectives, exchanged(): return lax.all_to_all(value, axes, 0, 0, tiled=True)  16.6 us
    all_to_all x3, starting transfers between devices, exchanged(): return lax.all_to_all(value, axes, 0, 0, tiled=True)  12.6 us
    all_to_all x3, waiting for transfers between devices, exchanged(): return lax.all_to_all(value, axes, 0, 0, tiled=True)  7.06 us
  transfers between devices with their start and end apart: 11, of which 5 were waited for; matrix products, arithmetic and copies ran while one was open for 1% of the time, Pallas kernels for 31%

profile of v3, /device:TPU:0, one launch (start us, length us, event | category | flops | bytes accessed | tf_op | source)
XLA Modules:
  0.0 193.5 jit_solution(5750822708483987914)
XLA Ops:
  2.9 3.1 %lend.1 = (bf16[8,128,256]{2,1,0:T(8,128)(2,1)}, bf16[8,128,256]{2,1,0:T(8,128)(2,1)}) custom-call(s32[1,2,8]{2,1,0:T(2,128)S(1)} %copy-done.47, bf16[32,128,256]{2,1,0:T(8,128)(2,1)S(1)} %bitcast.6), custom_call_target="tpu_custom_call" | custom-call | flops 1000 | bytes 1000 | tf_op jit(solution)/shard_map/lend/pallas_call | solution.py:74
  6.0 3.1 %collective-permute-start = (bf16[8,128,256]{2,1,0:T(8,128)(2,1)}, bf16[8,128,256]{2,1,0:T(8,128)(2,1)S(1)}, u32[]{:S(2)}, u32[]{:S(2)}) collective-permute-start(bf16[8,128,256]{2,1,0:T(8,128)(2,1)} %get-tuple-element.55), channel_id=1, source_target_pairs={{0,1},{1,2},{2,3},{3,4},{4,5},{5,6},{6,7},{7,8},{8,9},{9,10},{10,1... | collective-permute-start | bytes 1572872 | tf_op jit(solution)/shard_map/ppermute | solution.py:62
  9.1 3.4 %collective-permute-start.1 = (bf16[8,128,256]{2,1,0:T(8,128)(2,1)}, bf16[8,128,256]{2,1,0:T(8,128)(2,1)}, u32[]{:S(2)}, u32[]{:S(2)}) collective-permute-start(bf16[8,128,256]{2,1,0:T(8,128)(2,1)} %get-tuple-element.56), channel_id=1, source_target_pairs={{0,31},{1,0},{2,1},{3,2},{4,3},{5,4},{6,5},{7,6},{8,7},{9,8},{10,9... | collective-permute-start | bytes 1572872 | tf_op jit(solution)/shard_map/ppermute | solution.py:62
  20.0 10.7 %arrange.1 = (bf16[16,128,256]{2,1,0:T(8,128)(2,1)S(1)}, bf16[16,128,256]{2,1,0:T(8,128)(2,1)S(1)}, bf16[16,128,256]{2,1,0:T(8,128)(2,1)S(1)}, bf16[16,128,256]{...) custom-call(s32[1,2,8]{2,1,0:T(2,128)S(1)} %copy-done.48, ...), custom_call_target="tpu_custom_call" | custom-call | flops 1000 | bytes 1000 | tf_op jit(solution)/shard_map/arrange/pallas_call | solution.py:74
  30.7 3.3 %collective-permute-done.1.fe = bf16[8,128,256]{2,1,0:T(8,128)(2,1)} collective-permute-done((bf16[8,128,256]{2,1,0:T(8,128)(2,1)}, bf16[8,128,256]{2,1,0:T(8,128)(2,1)}, u32[]{:S(2)}, u32[]{:S(2)}) %collective-permute-start.1) | collective-permute-done | bytes 524320 | tf_op jit(solution)/shard_map/ppermute | solution.py:62
  34.0 3.8 %first_lent.1 = (bf16[8,128,256]{2,1,0:T(8,128)(2,1)S(1)}, bf16[8,128,256]{2,1,0:T(8,128)(2,1)S(1)}, bf16[16,128,256]{2,1,0:T(8,128)(2,1)S(1)}) custom-call(s32[384]{0:T(512)S(1)} %get-tuple-element.52.meta, bf16[16,128,256]{2,1,0:T(8,128)(2,1)S(1)} %get-tuple-element.53.f_lent.refs_0_, bf16[16,128,256]{2,1,0:T(8,128)(2,1)S(1)} %get-tuple-element.54.f_rest.refs_1_, ...), custom_call_target="tpu_custom_call" | custom-call | flops 1000 | bytes 1000 | tf_op jit(solution)/shard_map/first_lent/pallas_call | solution.py:74
  38.8 3.5 %collective-permute-start.3 = (bf16[8,128,256]{2,1,0:T(8,128)(2,1)S(1)}, bf16[8,128,256]{2,1,0:T(8,128)(2,1)S(1)}, u32[]{:S(2)}, u32[]{:S(2)}) collective-permute-start(bf16[8,128,256]{2,1,0:T(8,128)(2,1)S(1)} %get-tuple-element.58.west), channel_id=1, source_target_pairs={{0,31},{1,0},{2,1},{3,2},{4,3},{5,4},{6,5},{7,6},{8,7},{9,8},{10,9... | collective-permute-start | bytes 1572872 | tf_op jit(solution)/shard_map/ppermute | solution.py:62
  45.4 5.5 %first_rest.1 = (bf16[16,128,256]{2,1,0:T(8,128)(2,1)S(1)}, bf16[16,128,256]{2,1,0:T(8,128)(2,1)S(1)}, bf16[2,32,128,256]{3,2,1,0:T(8,128)(2,1)}, bf16[16,128,256]{2,1,0:T(8,128)(2,1)S(1)}) custom-call(s32[384]{0:T(512)S(1)} %get-tuple-element.52.meta, s32[1,2,8]{2,1,0:T(2,128)S(1)} %copy-done.49, s32[1]{0:T(128)S(6)} %copy.26.live, ...), custom_call_target="tpu_custom_call" | custom-call | flops 1000 | bytes 1000 | tf_op jit(solution)/shard_map/first_rest/pallas_call | solution.py:74
  54.6 10.6 %collective-permute-done.2.fw = bf16[8,128,256]{2,1,0:T(8,128)(2,1)S(1)} collective-permute-done((bf16[8,128,256]{2,1,0:T(8,128)(2,1)S(1)}, bf16[8,128,256]{2,1,0:T(8,128)(2,1)S(1)}, u32[]{:S(2)}, u32[]{:S(2)}) %collective-permute-start.2) | collective-permute-done | bytes 524320 | tf_op jit(solution)/shard_map/ppermute | solution.py:62
  65.2 7.8 %second.1 = (bf16[32,128,256]{2,1,0:T(8,128)(2,1)S(1)}, bf16[32,128,256]{2,1,0:T(8,128)(2,1)S(1)}, bf16[32,128,256]{2,1,0:T(8,128)(2,1)S(1)}, bf16[32,128,256]{2...) custom-call(s32[384]{0:T(512)S(1)} %get-tuple-element.52.meta, ...), custom_call_target="tpu_custom_call" | custom-call | flops 1000 | bytes 1000 | tf_op jit(solution)/shard_map/second/pallas_call | solution.py:74
  74.3 3.1 %collective-permute-start.4 = (bf16[8,128,256]{2,1,0:T(8,128)(2,1)}, bf16[8,128,256]{2,1,0:T(8,128)(2,1)}, u32[]{:S(2)}, u32[]{:S(2)}) collective-permute-start(bf16[8,128,256]{2,1,0:T(8,128)(2,1)} %get-tuple-element.74), channel_id=1, source_target_pairs={{0,1},{1,2},{2,3},{3,4},{4,5},{5,6},{6,7},{7,8},{8,9},{9,10},{10,1... | collective-permute-start | bytes 1572872 | tf_op jit(solution)/shard_map/ppermute | solution.py:62
  79.7 3.5 %weight_grads1.1 = bf16[8,112,256]{2,1,0:T(8,128)(2,1)S(1)} custom-call(bf16[16,128,256]{2,1,0:T(8,128)(2,1)S(1)} %get-tuple-element.60.f_lent.refs_0_, bf16[16,128,256]{2,1,0:T(8,128)(2,1)S(1)} %get-tuple-element.61.f_rest.refs_1_, bf16[32,128,256]{2,1,0:T(8,128)(2,1)S(1)} %get-tuple-element.93.refs_2_, ...), custom_call_target="tpu_custom_call" | custom-call | flops 1000 | bytes 1000 | tf_op jit(solution)/shard_map/weight_grads1/pallas_call | solution.py:74
  86.7 4.1 %all-to-all-start.1 = ((bf16[8,112,256]{2,1,0:T(8,128)(2,1)}), bf16[8,112,256]{2,1,0:T(8,128)(2,1)}, u32[]{:S(2)}, u32[]{:S(2)}) async-start(bf16[8,112,256]{2,1,0:T(8,128)(2,1)} %copy-done.41), calls=%async_computation.1 | async-start | bytes 917504 | tf_op jit(solution)/shard_map/all_to_all | solution.py:469
  102.3 7.5 %input_grad1.1 = (bf16[2,32,128,256]{3,2,1,0:T(8,128)(2,1)}, f32[16,128,256]{2,1,0:T(8,128)S(1)}, bf16[16,128,256]{2,1,0:T(8,128)(2,1)S(1)}) custom-call(s32[384]{0:T(512)S(1)} %get-tuple-element.52.meta, s32[8]{0:T(128)S(1)} %get-tuple-element.62.counts, s32[1]{0:T(128)S(6)} %copy.26.live, bf16[16,128,256]{2,1,0:T(8,128)(2,1)S(1)} %copy-done.10, ...), custom_call_target="tpu_custom_call" | custom-call | flops 1000 | bytes 1000 | tf_op jit(solution)/shard_map/input_grad1/pallas_call | solution.py:74
  113.7 4.6 %early_lent.1 = (bf16[16,128,256]{2,1,0:T(8,128)(2,1)S(1)}, bf16[16,128,256]{2,1,0:T(8,128)(2,1)S(1)}, bf16[16,128,256]{2,1,0:T(8,128)(2,1)S(1)}, bf16[2,32,128,...) custom-call(s32[384]{0:T(512)S(1)} %get-tuple-element.52.meta, ...), custom_call_target="tpu_custom_call", output_to_operand_aliasing={{3}: (10, {})} | custom-call | flops 1000 | bytes 1000 | tf_op jit(solution)/shard_map/early_lent/pallas_call | solution.py:74
  120.8 3.6 %weight_grads0.1 = bf16[8,112,256]{2,1,0:T(8,128)(2,1)S(1)} custom-call(bf16[16,128,256]{2,1,0:T(8,128)(2,1)S(1)} %get-tuple-element.53.f_lent.refs_0_, bf16[16,128,256]{2,1,0:T(8,128)(2,1)S(1)} %get-tuple-element.54.f_rest.refs_1_, bf16[16,128,256]{2,1,0:T(8,128)(2,1)S(1)} %copy-done.30, bf16[16,128,256]{2,1,0:T(8,128)(2,1)S(1)} %copy-done.33, ...), custom_call_target="tpu_custom_call" | custom-call | flops 1000 | bytes 1000 | tf_op jit(solution)/shard_map/weight_grads0/pallas_call | solution.py:74
  127.2 4.3 %all-to-all-start = ((bf16[8,112,256]{2,1,0:T(8,128)(2,1)}), bf16[8,112,256]{2,1,0:T(8,128)(2,1)}, u32[]{:S(2)}, u32[]{:S(2)}) async-start(bf16[8,112,256]{2,1,0:T(8,128)(2,1)} %copy-done.42), calls=%async_computation | async-start | bytes 917504 | tf_op jit(solution)/shard_map/all_to_all | solution.py:469
  132.6 7.1 %all-to-all-done = bf16[8,112,256]{2,1,0:T(8,128)(2,1)} async-done(((bf16[8,112,256]{2,1,0:T(8,128)(2,1)}), bf16[8,112,256]{2,1,0:T(8,128)(2,1)}, u32[]{:S(2)}, u32[]{:S(2)}) %all-to-all-start) | async-done | bytes 458784 | tf_op jit(solution)/shard_map/all_to_all | solution.py:469
  140.8 16.6 %all_to_all.20 = bf16[4,2,112,256]{3,2,1,0:T(8,128)(2,1)} all-to-all(bf16[4,2,112,256]{3,2,1,0:T(8,128)(2,1)S(1)} %broadcast_in_dim.6), channel_id=1, replica_groups=mesh['dom'=4,'phase'=2,'feat'=4] {'feat'}, dimensions={0} | all-to-all | bytes 917504 | tf_op jit(solution)/shard_map/all_to_all | solution.py:469
  159.4 4.2 %all-to-all-start.3 = ((bf16[8,2,112,256]{3,2,1,0:T(8,128)(2,1)}), bf16[8,2,112,256]{3,2,1,0:T(8,128)(2,1)}, u32[]{:S(2)}, u32[]{:S(2)}) async-start(bf16[8,2,112,256]{3,2,1,0:T(8,128)(2,1)} %broadcast_in_dim.7), calls=%async_computation.3 | async-start | bytes 1835008 | tf_op jit(solution)/shard_map/all_to_all | solution.py:469
  164.1 5.0 %collective-permute-start.7 = (bf16[8,128,256]{2,1,0:T(8,128)(2,1)}, bf16[8,128,256]{2,1,0:T(8,128)(2,1)S(1)}, u32[]{:S(2)}, u32[]{:S(2)}) collective-permute-start(bf16[8,128,256]{2,1,0:T(8,128)(2,1)} %copy-done.51), channel_id=1, source_target_pairs={{0,31},{1,0},{2,1},{3,2},{4,3},{5,4},{6,5},{7,6},{8,7},{9,8},{10,9... | collective-permute-start | bytes 1572872 | tf_op jit(solution)/shard_map/ppermute | solution.py:62
  170.7 3.6 %second_out.1 = bf16[2,32,128,256]{3,2,1,0:T(8,128)(2,1)} custom-call(s32[1,2,8]{2,1,0:T(2,128)S(1)} %copy-done.49, s32[1]{0:T(128)S(6)} %copy.26.live, bf16[16,128,256]{2,1,0:T(8,128)(2,1)S(1)} %copy-done.4, bf16[16,128,256]{2,1,0:T(8,128)(2,1)S(1)} %copy-done.6, bf16[32,128,256]{2,1,0:T(8,128)(2,1)S(1)} %copy-done.18, ...), custom_call_target="tpu_custom_call", output_to_operand_aliasing={{}: (6, {})} | custom-call | flops 1000 | bytes 1000 | tf_op jit(solution)/shard_map/second_out/pallas_call | solution.py:74
  175.4 8.7 %input_grad0.1 = (bf16[2,32,128,256]{3,2,1,0:T(8,128)(2,1)}, f32[16,128,256]{2,1,0:T(8,128)S(1)}, bf16[16,128,256]{2,1,0:T(8,128)(2,1)}) custom-call(s32[384]{0:T(512)S(1)} %get-tuple-element.52.meta, s32[8]{0:T(128)S(1)} %get-tuple-element.62.counts, s32[1]{0:T(128)S(6)} %copy.26.live, ...), custom_call_target="tpu_custom_call", output_to_operand_aliasing={{0}: (11, {})} | custom-call | flops 1000 | bytes 1000 | tf_op jit(solution)/shard_map/input_grad0/pallas_call | solution.py:74
  184.1 5.3 %collective-permute-done.7.fe = bf16[8,128,256]{2,1,0:T(8,128)(2,1)S(1)} collective-permute-done((bf16[8,128,256]{2,1,0:T(8,128)(2,1)}, bf16[8,128,256]{2,1,0:T(8,128)(2,1)S(1)}, u32[]{:S(2)}, u32[]{:S(2)}) %collective-permute-start.7) | collective-permute-done | bytes 524320 | tf_op jit(solution)/shard_map/ppermute | solution.py:62
  (129 shorter events, 55.9 us)
Async XLA Ops:
  6.0 24.7 %collective-permute-start = (bf16[8,128,256]{2,1,0:T(8,128)(2,1)}, bf16[8,128,256]{2,1,0:T(8,128)(2,1)S(1)}, u32[]{:S(2)}, u32[]{:S(2)}) collective-permute-start(bf16[8,128,256]{2,1,0:T(8,128)(2,1)} %get-tuple-element.55), channel_id=1, source_target_pairs={{0,1},{1,2},{2,3},{3,4},{4,5},{5,6},{6,7},{7,8},{8,9},{9,10},{10,1... | collective-permute-start | bytes 1572872 | tf_op jit(solution)/shard_map/ppermute | solution.py:62
  9.1 24.9 %collective-permute-start.1 = (bf16[8,128,256]{2,1,0:T(8,128)(2,1)}, bf16[8,128,256]{2,1,0:T(8,128)(2,1)}, u32[]{:S(2)}, u32[]{:S(2)}) collective-permute-start(bf16[8,128,256]{2,1,0:T(8,128)(2,1)} %get-tuple-element.56), channel_id=1, source_target_pairs={{0,31},{1,0},{2,1},{3,2},{4,3},{5,4},{6,5},{7,6},{8,7},{9,8},{10,9... | collective-permute-start | bytes 1572872 | tf_op jit(solution)/shard_map/ppermute | solution.py:62
  20.0 14.1 %copy-start.19 = (bf16[2,256,256]{2,1,0:T(8,128)(2,1)S(1)}, bf16[2,256,256]{2,1,0:T(8,128)(2,1)}, u32[]{:S(2)}) copy-start(bf16[2,256,256]{2,1,0:T(8,128)(2,1)} %wn.9) | copy-start | bytes 786436
  20.0 14.1 %copy-start.20 = (bf16[2,256,256]{2,1,0:T(8,128)(2,1)S(1)}, bf16[2,256,256]{2,1,0:T(8,128)(2,1)}, u32[]{:S(2)}) copy-start(bf16[2,256,256]{2,1,0:T(8,128)(2,1)} %ws.9) | copy-start | bytes 786436
  20.0 14.1 %copy-start.34 = (bf16[2,256,256]{2,1,0:T(8,128)(2,1)S(1)}, bf16[2,256,256]{2,1,0:T(8,128)(2,1)}, u32[]{:S(2)}) copy-start(bf16[2,256,256]{2,1,0:T(8,128)(2,1)} %wo.7) | copy-start | bytes 786436
  20.0 14.1 %copy-start.50 = (f32[2,256]{1,0:T(2,128)S(1)}, f32[2,256]{1,0:T(2,128)}, u32[]{:S(2)}) copy-start(f32[2,256]{1,0:T(2,128)} %bias.7) | copy-start | bytes 6148
  30.6 49.1 %copy-start.9 = (bf16[16,128,256]{2,1,0:T(8,128)(2,1)}, bf16[16,128,256]{2,1,0:T(8,128)(2,1)S(1)}, u32[]{:S(2)}) copy-start(bf16[16,128,256]{2,1,0:T(8,128)(2,1)S(1)} %get-tuple-element.64.m_lent.refs_0_.refs_4_) | copy-start | bytes 3145732
  30.6 49.0 %copy-start.11 = (bf16[16,128,256]{2,1,0:T(8,128)(2,1)}, bf16[16,128,256]{2,1,0:T(8,128)(2,1)S(1)}, u32[]{:S(2)}) copy-start(bf16[16,128,256]{2,1,0:T(8,128)(2,1)S(1)} %get-tuple-element.65.m_rest.refs_1_.refs_5_) | copy-start | bytes 3145732
  38.8 15.8 %collective-permute-start.3 = (bf16[8,128,256]{2,1,0:T(8,128)(2,1)S(1)}, bf16[8,128,256]{2,1,0:T(8,128)(2,1)S(1)}, u32[]{:S(2)}, u32[]{:S(2)}) collective-permute-start(bf16[8,128,256]{2,1,0:T(8,128)(2,1)S(1)} %get-tuple-element.58.west), channel_id=1, source_target_pairs={{0,31},{1,0},{2,1},{3,2},{4,3},{5,4},{6,5},{7,6},{8,7},{9,8},{10,9... | collective-permute-start | bytes 1572872 | tf_op jit(solution)/shard_map/ppermute | solution.py:62
  42.3 22.9 %collective-permute-start.2 = (bf16[8,128,256]{2,1,0:T(8,128)(2,1)S(1)}, bf16[8,128,256]{2,1,0:T(8,128)(2,1)S(1)}, u32[]{:S(2)}, u32[]{:S(2)}) collective-permute-start(bf16[8,128,256]{2,1,0:T(8,128)(2,1)S(1)} %get-tuple-element.59.east), channel_id=1, source_target_pairs={{0,1},{1,2},{2,3},{3,4},{4,5},{5,6},{6,7},{7,8},{8,9},{9,10},{10,1... | collective-permute-start | bytes 1572872 | tf_op jit(solution)/shard_map/ppermute | solution.py:62
  45.4 19.8 %copy-start = (bf16[128,128,128]{2,1,0:T(8,128)(2,1)}, bf16[128,128,128]{2,1,0:T(8,128)(2,1)S(1)}, u32[]{:S(2)}) copy-start(bf16[128,128,128]{2,1,0:T(8,128)(2,1)S(1)} %get-tuple-element.63.at.refs_4_.refs_6_) | copy-start | bytes 12582916
  51.0 14.2 %copy-start.31 = (bf16[16,128,256]{2,1,0:T(8,128)(2,1)}, bf16[16,128,256]{2,1,0:T(8,128)(2,1)S(1)}, u32[]{:S(2)}) copy-start(bf16[16,128,256]{2,1,0:T(8,128)(2,1)S(1)} %get-tuple-element.77.a_rest.refs_3_) | copy-start | bytes 3145732
  51.0 28.7 %copy-start.3 = (bf16[16,128,256]{2,1,0:T(8,128)(2,1)}, bf16[16,128,256]{2,1,0:T(8,128)(2,1)S(1)}, u32[]{:S(2)}) copy-start(bf16[16,128,256]{2,1,0:T(8,128)(2,1)S(1)} %get-tuple-element.60.f_lent.refs_0_) | copy-start | bytes 3145732
  51.0 28.7 %copy-start.5 = (bf16[16,128,256]{2,1,0:T(8,128)(2,1)}, bf16[16,128,256]{2,1,0:T(8,128)(2,1)S(1)}, u32[]{:S(2)}) copy-start(bf16[16,128,256]{2,1,0:T(8,128)(2,1)S(1)} %get-tuple-element.61.f_rest.refs_1_) | copy-start | bytes 3145732
  74.3 39.3 %collective-permute-start.4 = (bf16[8,128,256]{2,1,0:T(8,128)(2,1)}, bf16[8,128,256]{2,1,0:T(8,128)(2,1)}, u32[]{:S(2)}, u32[]{:S(2)}) collective-permute-start(bf16[8,128,256]{2,1,0:T(8,128)(2,1)} %get-tuple-element.74), channel_id=1, source_target_pairs={{0,1},{1,2},{2,3},{3,4},{4,5},{5,6},{6,7},{7,8},{8,9},{9,10},{10,1... | collective-permute-start | bytes 1572872 | tf_op jit(solution)/shard_map/ppermute | solution.py:62
  77.5 36.2 %collective-permute-start.5 = (bf16[8,128,256]{2,1,0:T(8,128)(2,1)}, bf16[8,128,256]{2,1,0:T(8,128)(2,1)}, u32[]{:S(2)}, u32[]{:S(2)}) collective-permute-start(bf16[8,128,256]{2,1,0:T(8,128)(2,1)} %get-tuple-element.75), channel_id=1, source_target_pairs={{0,31},{1,0},{2,1},{3,2},{4,3},{5,4},{6,5},{7,6},{8,7},{9,8},{10,9... | collective-permute-start | bytes 1572872 | tf_op jit(solution)/shard_map/ppermute | solution.py:62
  86.7 40.5 %all-to-all-start.1 = ((bf16[8,112,256]{2,1,0:T(8,128)(2,1)}), bf16[8,112,256]{2,1,0:T(8,128)(2,1)}, u32[]{:S(2)}, u32[]{:S(2)}) async-start(bf16[8,112,256]{2,1,0:T(8,128)(2,1)} %copy-done.41), calls=%async_computation.1 | async-start | bytes 917504 | tf_op jit(solution)/shard_map/all_to_all | solution.py:469
  127.2 41.9 %copy-start.4 = (bf16[16,128,256]{2,1,0:T(8,128)(2,1)S(1)}, bf16[16,128,256]{2,1,0:T(8,128)(2,1)}, u32[]{:S(2)}) copy-start(bf16[16,128,256]{2,1,0:T(8,128)(2,1)} %copy-done.3) | copy-start | bytes 3145732
  127.2 41.9 %copy-start.6 = (bf16[16,128,256]{2,1,0:T(8,128)(2,1)S(1)}, bf16[16,128,256]{2,1,0:T(8,128)(2,1)}, u32[]{:S(2)}) copy-start(bf16[16,128,256]{2,1,0:T(8,128)(2,1)} %copy-done.5) | copy-start | bytes 3145732
  127.2 41.9 %copy-start.35 = (bf16[2,256,256]{2,1,0:T(8,128)(2,1)S(1)}, bf16[2,256,256]{2,1,0:T(8,128)(2,1)}, u32[]{:S(2)}) copy-start(bf16[2,256,256]{2,1,0:T(8,128)(2,1)} %wo.7) | copy-start | bytes 786436
  127.2 12.4 %all-to-all-start = ((bf16[8,112,256]{2,1,0:T(8,128)(2,1)}), bf16[8,112,256]{2,1,0:T(8,128)(2,1)}, u32[]{:S(2)}, u32[]{:S(2)}) async-start(bf16[8,112,256]{2,1,0:T(8,128)(2,1)} %copy-done.42), calls=%async_computation | async-start | bytes 917504 | tf_op jit(solution)/shard_map/all_to_all | solution.py:469
  159.4 31.7 %all-to-all-start.3 = ((bf16[8,2,112,256]{3,2,1,0:T(8,128)(2,1)}), bf16[8,2,112,256]{3,2,1,0:T(8,128)(2,1)}, u32[]{:S(2)}, u32[]{:S(2)}) async-start(bf16[8,2,112,256]{3,2,1,0:T(8,128)(2,1)} %broadcast_in_dim.7), calls=%async_computation.3 | async-start | bytes 1835008 | tf_op jit(solution)/shard_map/all_to_all | solution.py:469
  163.7 20.4 %collective-permute-start.6 = (bf16[8,128,256]{2,1,0:T(8,128)(2,1)}, bf16[8,128,256]{2,1,0:T(8,128)(2,1)S(1)}, u32[]{:S(2)}, u32[]{:S(2)}) collective-permute-start(bf16[8,128,256]{2,1,0:T(8,128)(2,1)} %copy-done.52), channel_id=1, source_target_pairs={{0,1},{1,2},{2,3},{3,4},{4,5},{5,6},{6,7},{7,8},{8,9},{9,10},{10,1... | collective-permute-start | bytes 1572872 | tf_op jit(solution)/shard_map/ppermute | solution.py:62
  164.1 25.3 %collective-permute-start.7 = (bf16[8,128,256]{2,1,0:T(8,128)(2,1)}, bf16[8,128,256]{2,1,0:T(8,128)(2,1)S(1)}, u32[]{:S(2)}, u32[]{:S(2)}) collective-permute-start(bf16[8,128,256]{2,1,0:T(8,128)(2,1)} %copy-done.51), channel_id=1, source_target_pairs={{0,31},{1,0},{2,1},{3,2},{4,3},{5,4},{6,5},{7,6},{8,7},{9,8},{10,9... | collective-permute-start | bytes 1572872 | tf_op jit(solution)/shard_map/ppermute | solution.py:62
  (40 other events, 117.9 us)

commit v4 on v2

--- a/solution.py
+++ b/solution.py
@@ -14,6 +14,7 @@
 SMEM = pl.BlockSpec(memory_space=pltpu.SMEM)
 VMEM = pl.BlockSpec(memory_space=pltpu.VMEM)
 MIB = 1024 * 1024
+TOKEN = jax.ShapeDtypeStruct((8, 128), F32)
 
 
 class Sizes:
@@ -108,7 +109,7 @@
         [VMEM, VMEM],
         [z.nodes(z.edge), z.nodes(z.edge)],
         [pltpu.SemaphoreType.DMA((z.lent,))],
-        4,
+        2,
         (bound, features),
     )
 
@@ -192,7 +193,7 @@
             jax.ShapeDtypeStruct((8,), jnp.int32),
         ],
         [pltpu.SMEM((z.lent,), jnp.int32), pltpu.SemaphoreType.DMA((3 * z.lent + 3,))],
-        12,
+        6,
         (bound, nbrs, live, features, cot, adjacency),
     )
 
@@ -219,7 +220,7 @@
             jax.ShapeDtypeStruct((2, 3, z.cols, z.cols), BF16),
         ],
         [],
-        12,
+        6,
         (ap, w_self, w_nbr, w_out),
     )
 
@@ -274,7 +275,7 @@
         [VMEM] * 3,
         [z.nodes(z.edge), z.nodes(z.edge), z.nodes(z.lent)],
         [z.held(z.ext)],
-        12,
+        8,
         (meta, *f0, fw, fe, ap, w_self, w_nbr, bias, w_out),
     )
 
@@ -323,36 +324,35 @@
             z.nodes(z.rest),
         ],
         [z.held(z.ext), pltpu.SemaphoreType.DMA((1 + z.lent,))],
-        12,
+        10,
         (meta, bound, live, *f0, fw, fe, ap, w_self, w_nbr, bias, w_out, west, east),
     )
 
 
-def second_own(z, f1, m1, w_self, bias, wt):
-    def kernel(f_lent, f_rest, m_lent, m_rest, ws, bias, wt, own, hidden):
+def second_own(z, m1, wt):
+    def kernel(m_lent, m_rest, wt, hidden):
         def work(part, first):
-            f = z.flat(group_of(z, (f_lent, f_rest), part, first)[...])
             m = z.flat(group_of(z, (m_lent, m_rest), part, first)[...])
-            here = pl.ds(first, z.group)
-            own[here] = z.tiled(dot(f, ws[1]) + bias[1:2, :])
-            hidden[here] = z.tiled(dot(m, wt[1, 2]))
+            hidden[pl.ds(first, z.group)] = z.tiled(dot(m, wt[1, 2]))
 
         each_group(z, work)
 
     return call(
         kernel,
         "second_own",
-        [VMEM] * 7,
-        [VMEM] * 2,
-        [z.nodes(z.tiles, F32)] * 2,
+        [VMEM] * 3,
+        VMEM,
+        z.nodes(z.tiles, F32),
         [],
-        12,
-        (*f1, *m1, w_self, bias, wt),
+        8,
+        (*m1, wt),
     )
 
 
 def saved(z, f0, agg0, w_self, w_nbr, bias):
-    def kernel(f_lent, f_rest, a_lent, a_rest, ws, wn, bias, act, slope):
+    def kernel(f_lent, f_rest, a_lent, a_rest, ws, wn, bias, act, slope, token):
+        token[...] = jnp.zeros_like(token)
+
         def work(part, first):
             f = z.flat(group_of(z, (f_lent, f_rest), part, first)[...])
             aggs = z.flat(group_of(z, (a_lent, a_rest), part, first)[...])
@@ -368,10 +368,10 @@
         kernel,
         "saved",
         [VMEM] * 7,
-        [VMEM] * 2,
-        [z.nodes(z.tiles), z.nodes(z.tiles, F32)],
+        [VMEM] * 3,
+        [z.nodes(z.tiles), z.nodes(z.tiles, F32), TOKEN],
         [],
-        12,
+        10,
         (*f0, *agg0, w_self, w_nbr, bias),
     )
 
@@ -390,8 +390,8 @@
     lax.fori_loop(0, (stop - start + UNROLL - 1) // UNROLL, body, 0)
 
 
-def second(z, meta, counts, f1, fw, fe, ap, at, own, hidden, w_nbr, wt):
-    def kernel(meta, counts, f_lent, f_rest, fw, fe, ap, at, own, hidden, wn, wt,
+def second(z, meta, counts, f1, fw, fe, ap, at, hidden, w_self, w_nbr, bias, wt, after):
+    def kernel(meta, counts, f_lent, f_rest, fw, fe, ap, at, hidden, ws, wn, bias, wt, _after,
                agg, act, dpre, dagg, to_west, to_east, ext, acc):
         fill_extended(z, (f_lent, f_rest), fw, fe, ext)
         acc[...] = jnp.zeros_like(acc)
@@ -400,14 +400,14 @@
             here = pl.ds(first, z.group)
             aggs = aggregate(z, meta, first, ap, ext)
             agg[here] = z.tiled(aggs)
-            pre = z.flat(own[here]) + dot(aggs, wn[1])
+            pre = dot(z.flat(ext[here]), ws[1]) + dot(aggs, wn[1]) + bias[1:2, :]
             sig = sigmoid(pre)
             act[here] = z.tiled((pre * sig).astype(BF16))
             grad = (z.flat(hidden[here]) * (sig * (1.0 + pre * (1.0 - sig)))).astype(BF16)
             dpre[here] = z.tiled(grad)
             dagg[here] = z.tiled(dot(grad, wt[1, 1]).astype(BF16))
 
-        each_group(z, work)
+        each_group(z, work, unroll=2)
         spread(z, meta, counts[0], z.pairs, at, lambda q: dagg[q], acc, z.tiles, z.lent)
         to_west[...] = acc[pl.ds(0, z.edge)].astype(BF16)
         to_east[...] = acc[pl.ds(z.edge, z.edge)].astype(BF16)
@@ -415,19 +415,50 @@
     return call(
         kernel,
         "second",
-        [SMEM] * 2 + [VMEM] * 10,
+        [SMEM] * 2 + [VMEM] * 12,
         [VMEM] * 6,
         [z.nodes(z.tiles)] * 4 + [z.nodes(z.edge)] * 2,
         [z.held(z.ext), z.held(z.lent + 1, F32)],
-        16,
-        (meta, counts, *f1, fw, fe, ap, at, own, hidden, w_nbr, wt),
-    )
-
-
-def weight_grads(z, me, pieces, f, agg, act, m, dpre, name):
+        12,
+        (meta, counts, *f1, fw, fe, ap, at, hidden, w_self, w_nbr, bias, wt, after),
+    )
+
+
+class Plane:
+    def __init__(self):
+        dom, phase = lax.axis_size("dom"), lax.axis_size("phase")
+        self.pair = 2 if dom % 2 == 0 else 1
+        self.phase = phase
+        self.groups = dom // self.pair * phase
+        self.count = dom * phase
+        place = lax.axis_index("dom")
+        half = lax.rem(place, self.pair)
+        group = place // self.pair * phase + lax.axis_index("phase")
+        self.me = jnp.stack([half, group]).astype(jnp.int32)
+
+    def index(self, half, group):
+        return (group // self.phase * self.pair + half) * self.phase + group % self.phase
+
+    def across(self, value):
+        pairs = [
+            (self.index(h, g), self.index((h + 1) % self.pair, g))
+            for h in range(self.pair)
+            for g in range(self.groups)
+        ]
+        return lax.ppermute(value, PLANE, pairs)
+
+    def along(self, value, steps):
+        pairs = [
+            (self.index(h, g), self.index(h, (g + steps) % self.groups))
+            for h in range(self.pair)
+            for g in range(self.groups)
+        ]
+        return lax.ppermute(value, PLANE, pairs)
+
+
+def weight_grads(z, plane, f, agg, act, m, dpre, name):
     c = z.cols
-    piece = -(-(3 * c + 1) // (pieces * 16)) * 16
-    height = piece * pieces
+    piece = -(-(3 * c + 1) // (plane.count * 16)) * 16
     arrays = (f, agg, act, m, dpre)
     flat_args = [x for a in arrays for x in (a if isinstance(a, tuple) else (a,))]
 
@@ -450,75 +481,58 @@
             acc[pl.ds(3 * c, 1), :] += jnp.sum(grad.astype(F32), axis=0, keepdims=True)
 
         each_group(z, work)
-        for i in range(pieces):
-            owner = lax.rem(me[0] + i, pieces)
-            outs[i][...] = acc[pl.ds(pl.multiple_of(owner * piece, 16), piece), :]
+        for h, out in enumerate(outs):
+            half = lax.rem(me[0] + h, plane.pair)
+            for g in range(plane.groups):
+                owner = half * plane.groups + lax.rem(me[1] + g, plane.groups)
+                out[g] = acc[pl.ds(pl.multiple_of(owner * piece, 16), piece), :].astype(BF16)
 
     return call(
         kernel,
         name,
         [SMEM] + [VMEM] * len(flat_args),
-        [VMEM] * pieces,
-        [jax.ShapeDtypeStruct((piece, c), F32)] * pieces,
-        [pltpu.VMEM((height, c), F32)],
-        12,
-        (me, *flat_args),
-    )
-
-
-def plane_pass(value, steps):
-    count = lax.axis_size(PLANE)
-    return lax.ppermute(value, PLANE, [(i, (i + steps) % count) for i in range(count)])
-
-
-def added(parts):
-    total = parts[0].astype(F32)
-    for part in parts[1:]:
-        total = total + part.astype(F32)
+        [VMEM] * plane.pair,
+        [jax.ShapeDtypeStruct((plane.groups, piece, c), BF16)] * plane.pair,
+        [pltpu.VMEM((piece * plane.count, c), F32)],
+        14,
+        (plane.me, *flat_args),
+    )
+
+
+def added(*values):
+    total = values[0].astype(F32)
+    for value in values[1:]:
+        total = total + value.astype(F32)
     return total.astype(BF16)
 
 
-def summed_over_parts(pieces):
-    count = len(pieces)
-    share = added([pieces[0]] + [plane_pass(pieces[i], i) for i in range(1, count)])
+def pair_sums(plane, halves):
+    if plane.pair == 1:
+        return halves[0]
+    return added(halves[0], plane.across(halves[1]))
+
+
+def share_totals(plane, late, halves):
+    both = jnp.stack([pair_sums(plane, halves), late], axis=1)
+    share = added(both[0], *[plane.along(both[g], g) for g in range(1, plane.groups)])
     lines = lax.axis_size("feat")
     if lines & (lines - 1) == 0:
         step = 1
         while step < lines:
-            other = lax.ppermute(share, "feat", [(i, i ^ step) for i in range(lines)])
-            share = added([share, other])
+            share = added(share, lax.ppermute(share, "feat", [(i, i ^ step) for i in range(lines)]))
             step *= 2
     else:
         share = lax.psum(share.astype(F32), "feat").astype(BF16)
-    return lax.all_gather(share, PLANE, axis=0, tiled=True)
-
-
-def unpack(z, early, late):
-    c = z.cols
-
-    def kernel(early, late, g_self, g_nbr, g_bias, g_out):
-        for layer, packed in ((0, early), (1, late)):
-            g_self[layer] = packed[pl.ds(0, c), :].astype(F32)
-            g_nbr[layer] = packed[pl.ds(c, c), :].astype(F32)
-            g_out[layer] = packed[pl.ds(2 * c, c), :].astype(F32)
-            g_bias[layer : layer + 1, :] = packed[pl.ds(3 * c, 16), :].astype(F32)[0:1]
-
-    square = jax.ShapeDtypeStruct((2, c, c), F32)
-    return call(
-        kernel,
-        "unpack",
-        [VMEM] * 2,
-        [VMEM] * 4,
-        [square, square, jax.ShapeDtypeStruct((2, c), F32), square],
-        [],
-        12,
-        (early, late),
-    )
+    gathered = jnp.stack([share] + [plane.along(share, g) for g in range(1, plane.groups)])
+    if plane.pair == 1:
+        return gathered[None]
+    return jnp.stack([gathered, plane.across(gathered)])
 
 
 def second_out(z, bound, live, f1, act, w_out, out):
-    def kernel(bound, live, f_lent, f_rest, act, wo, _out, out, keep, sems):
+    def kernel(bound, live, f_lent, f_rest, act, wo, _out, out, token, keep, sems):
         copies = []
+        token[...] = jnp.zeros_like(token)
 
         def work(part, first):
             f = z.flat(group_of(z, (f_lent, f_rest), part, first)[...])
@@ -544,8 +558,8 @@
         kernel,
         "second_out",
         [SMEM] * 2 + [VMEM] * 4 + [ANY],
-        ANY,
-        jax.ShapeDtypeStruct(out.shape, BF16),
+        [ANY, VMEM],
+        [jax.ShapeDtypeStruct(out.shape, BF16), TOKEN],
         [z.held(z.tiles), pltpu.SemaphoreType.DMA((z.lent + 1,))],
         12,
         (bound, live, *f1, act, w_out, out),
@@ -553,18 +567,16 @@
     )
 
 
-def input_grad(z, layer, meta, counts, live, m, dpre, dagg, at, wt, grads):
-    fresh = grads is None
+def input_grad(z, layer, meta, counts, m, dpre, dagg, at, wt):
     arrays = (m, dpre, dagg)
     flat_args = [x for a in arrays for x in (a if isinstance(a, tuple) else (a,))]
 
-    def kernel(meta, counts, live, *refs):
+    def kernel(meta, counts, *refs):
         refs = list(refs)
         m, dpre, dagg = [
             (refs.pop(0), refs.pop(0)) if isinstance(a, tuple) else refs.pop(0) for a in arrays
         ]
-        at, wt = refs[:2]
-        grads, part_out, masked, acc, keep, sem = refs[2 if fresh else 3 :]
+        at, wt, part_out, rest_out, acc = refs
 
         def direct(part, first):
             mine = z.flat(group_of(z, m, part, first)[...]).astype(F32)
@@ -581,44 +593,31 @@
             return jnp.where(q < z.lent, lent, rest)
 
         spread(z, meta, 0, counts[0], at, source, acc, 0, z.tiles)
-        tail = pl.ds(z.lent, z.rest)
-        keep[...] = acc[tail].astype(BF16)
-        copy = pltpu.make_async_copy(keep, grads.at[layer, tail], sem)
+        part_out[...] = acc[pl.ds(0, z.lent)]
+        rest_out[...] = acc[pl.ds(z.lent, z.rest)].astype(BF16)
+
+    return call(
+        kernel,
+        "input_grad%d" % layer,
+        [SMEM] * 2 + [VMEM] * (len(flat_args) + 2),
+        [VMEM, VMEM],
+        [z.nodes(z.lent, F32), z.nodes(z.rest)],
+        [z.held(z.tiles + 1, F32)],
+        28,
+        [meta, counts, *flat_args, at, wt],
+    )
+
+
+def early_rest(z, meta, counts, live, upstream, slope, at, wt):
+    def kernel(meta, counts, live, g, slope, at, wt, grads, m, dpre, dagg, outer, acc, sem):
+        copy = pltpu.make_async_copy(g, grads.at[1, pl.ds(z.lent, z.rest)], sem)
         copy.start()
-        part_out[...] = acc[pl.ds(0, z.lent)]
-
-        @pl.loop(0, z.rest)
-        def _(i):
-            value = keep[i]
-            masked[i] = jnp.where(z.lent + i < live[0], value, jnp.zeros_like(value))
-
-        copy.wait()
-
-    args = [meta, counts, live, *flat_args, at, wt]
-    if not fresh:
-        args.append(grads)
-    return call(
-        kernel,
-        "input_grad%d" % layer,
-        [SMEM] * 3 + [VMEM] * (len(flat_args) + 2) + ([] if fresh else [ANY]),
-        [ANY, VMEM, VMEM],
-        [
-            jax.ShapeDtypeStruct((2, z.tiles, z.rows, z.cols), BF16),
-            z.nodes(z.lent, F32),
-            z.nodes(z.rest),
-        ],
-        [z.held(z.tiles + 1, F32), z.held(z.rest), pltpu.SemaphoreType.DMA],
-        16,
-        args,
-        None if fresh else {len(args) - 1: 0},
-    )
-
-
-def early_rest(z, meta, counts, m0, slope, at, wt):
-    def kernel(meta, counts, m, slope, at, wt, dpre, dagg, outer, acc):
+
         def work(part, first):
             here = pl.ds(first - z.lent, z.group)
-            grad = dot(z.flat(m[here]), wt[0, 2]) * z.flat(slope[pl.ds(first, z.group)])
+            masked = live_rows(z, z.flat(g[here]), first, live[0])
+            m[here] = z.tiled(masked)
+            grad = dot(masked, wt[0, 2]) * z.flat(slope[pl.ds(first, z.group)])
             grad = grad.astype(BF16)
             dpre[here] = z.tiled(grad)
             dagg[here] = z.tiled(dot(grad, wt[0, 1]).astype(BF16))
@@ -631,21 +630,24 @@
 
         spread(z, meta, counts[0], counts[0] + counts[1], at, source, acc, z.tiles, z.lent)
         outer[...] = acc[pl.ds(0, z.lent)]
+        copy.wait()
 
     return call(
         kernel,
         "early_rest",
-        [SMEM] * 2 + [VMEM] * 4,
-        [VMEM] * 3,
-        [z.nodes(z.rest), z.nodes(z.rest), z.nodes(z.lent, F32)],
-        [z.held(z.lent + 1, F32)],
-        12,
-        (meta, counts, m0, slope, at, wt),
-    )
-
-
-def early_lent(z, meta, counts, bound, part, fw, fe, slope, outer, at, wt, grads):
-    def kernel(meta, counts, bound, part, fw, fe, slope, outer, at, wt, _g,
+        [SMEM] * 3 + [VMEM] * 4,
+        [ANY] + [VMEM] * 4,
+        [jax.ShapeDtypeStruct((2, z.tiles, z.rows, z.cols), BF16)]
+        + [z.nodes(z.rest)] * 3
+        + [z.nodes(z.lent, F32)],
+        [z.held(z.lent + 1, F32), pltpu.SemaphoreType.DMA],
+        14,
+        (meta, counts, live, upstream, slope, at, wt),
+    )
+
+
+def early_lent(z, meta, counts, bound, part, fw, fe, slope, outer, at, wt, grads, after):
+    def kernel(meta, counts, bound, part, fw, fe, slope, outer, at, wt, _g, _ready, _late,
                m, dpre, dagg, grads, to_west, to_east, acc, sems):
         def work(first, got):
             here = pl.ds(first, z.group)
@@ -682,19 +684,23 @@
     return call(
         kernel,
         "early_lent",
-        [SMEM] * 3 + [VMEM] * 7 + [ANY],
+        [SMEM] * 3 + [VMEM] * 7 + [ANY, VMEM, VMEM],
         [VMEM] * 3 + [ANY] + [VMEM] * 2,
         [z.nodes(z.lent)] * 3 + [jax.ShapeDtypeStruct(grads.shape, BF16)] + [z.nodes(z.edge)] * 2,
         [z.held(z.lent + 1, F32), pltpu.SemaphoreType.DMA((z.lent,))],
-        12,
-        (meta, counts, bound, part, fw, fe, slope, outer, at, wt, grads),
+        16,
+        (meta, counts, bound, part, fw, fe, slope, outer, at, wt, grads, *after),
         {10: 3},
     )
 
 
-def finish(z, bound, part, fw, fe, grads):
-    def kernel(bound, part, fw, fe, _g, grads, keep, sems):
-        copies = []
+def finish(z, plane, bound, part, rest, fw, fe, totals, grads):
+    c = z.cols
+    piece = totals.shape[3]
+
+    def kernel(me, bound, part, rest, fw, fe, totals, _g, grads, g_self, g_nbr, g_bias, g_out, keep, buf, sems):
+        copies = [pltpu.make_async_copy(rest, grads.at[0, pl.ds(z.lent, z.rest)], sems.at[z.lent])]
+        copies[0].start()
         for i in range(z.lent):
             got = fw[i] if i < z.edge else fe[i - z.edge]
             keep[i] = (part[i] + got.astype(F32)).astype(BF16)
@@ -703,19 +709,35 @@
             )
             copy.start()
             copies.append(copy)
+        for layer in range(2):
+            for h in range(plane.pair):
+                half = lax.rem(me[0] + h, plane.pair)
+                for g in range(plane.groups):
+                    owner = half * plane.groups + lax.rem(me[1] + plane.groups - g, plane.groups)
+                    start = pl.multiple_of(owner * piece, 16)
+                    buf[pl.ds(start, piece), :] = totals[h, g, layer].astype(F32)
+            g_self[layer] = buf[pl.ds(0, c), :]
+            g_nbr[layer] = buf[pl.ds(c, c), :]
+            g_out[layer] = buf[pl.ds(2 * c, c), :]
+            g_bias[layer : layer + 1, :] = buf[pl.ds(3 * c, 1), :]
         for copy in copies:
             copy.wait()
 
+    square = jax.ShapeDtypeStruct((2, c, c), F32)
     return call(
         kernel,
         "finish",
-        [SMEM] + [VMEM] * 3 + [ANY],
-        ANY,
-        jax.ShapeDtypeStruct(grads.shape, BF16),
-        [z.held(z.lent), pltpu.SemaphoreType.DMA((z.lent,))],
-        12,
-        (bound, part, fw, fe, grads),
-        {4: 0},
+        [SMEM] * 2 + [VMEM] * 5 + [ANY],
+        [ANY] + [VMEM] * 4,
+        [jax.ShapeDtypeStruct(grads.shape, BF16), square, square, jax.ShapeDtypeStruct((2, c), F32), square],
+        [
+            z.held(z.lent),
+            pltpu.VMEM((piece * plane.count, c), F32),
+            pltpu.SemaphoreType.DMA((z.lent + 1,)),
+        ],
+        14,
+        (plane.me, bound, part, rest, fw, fe, totals, grads),
+        {7: 0},
     )
 
 
@@ -726,8 +748,7 @@
     t, r, c = z.tiles, z.rows, z.cols
     features = node_in.reshape(t, r, c)
     cot = out_cot.reshape(t, r, c)
-    pieces = lax.axis_size(PLANE)
-    me = lax.axis_index(PLANE).astype(jnp.int32).reshape(1)
+    plane = Plane()
 
     west, east = lend(z, bound_tiles, features)
     from_west = passed_along(east, 1)
@@ -744,30 +765,42 @@
         west, east,
     )
     f1, agg0 = (f1_lent, f1_rest), (agg_lent, agg_rest)
-    own, hidden = second_own(z, f1, m1, w_self, pre_bias, wt)
-    act0, slope = saved(z, f0, agg0, w_self, w_nbr, pre_bias)
+    hidden = second_own(z, m1, wt)
+    act0, slope, ready = saved(z, f0, agg0, w_self, w_nbr, pre_bias)
 
     agg1, act1, dpre1, dagg1, to_west, to_east = second(
-        z, meta, counts, f1, next_west, next_east, ap, at, own, hidden, w_nbr, wt
+        z, meta, counts, f1, next_west, next_east, ap, at, hidden, w_self, w_nbr, pre_bias, wt, ready
     )
     back_west = passed_along(to_east, 1)
     back_east = passed_along(to_west, -1)
-    grads, part, m0_rest = input_grad(z, 1, meta, counts, live_tiles, m1, dpre1, dagg1, at, wt, None)
-    dpre_rest, dagg_rest, outer = early_rest(z, meta, counts, m0_rest, slope, at, wt)
-    late = summed_over_parts(weight_grads(z, me, pieces, f1, agg1, act1, m1, dpre1, "weight_grads1"))
-    section_out = second_out(z, bound_tiles, live_tiles, f1, act1, w_out, section_out)
+    part, upstream = input_grad(z, 1, meta, counts, m1, dpre1, dagg1, at, wt)
+    grads, m0_rest, dpre_rest, dagg_rest, outer = early_rest(
+        z, meta, counts, live_tiles, upstream, slope, at, wt
+    )
+    late = pair_sums(plane, weight_grads(z, plane, f1, agg1, act1, m1, dpre1, "weight_grads1"))
+    section_out, ready = second_out(z, bound_tiles, live_tiles, f1, act1, w_out, section_out)
 
     m0_lent, dpre_lent, dagg_lent, grads, to_west, to_east = early_lent(
-        z, meta, counts, bound_tiles, part, back_west, back_east, slope, outer, at, wt, grads
+        z, meta, counts, bound_tiles, part, back_west, back_east, slope, outer, at, wt, grads,
+        (ready, late),
     )
     back_west = passed_along(to_east, 1)
     back_east = passed_along(to_west, -1)
     m0, dpre0, dagg0 = (m0_lent, m0_rest), (dpre_lent, dpre_rest), (dagg_lent, dagg_rest)
-    early = summed_over_parts(weight_grads(z, me, pieces, f0, agg0, act0, m0, dpre0, "weight_grads0"))
-    grads, part, _ = input_grad(z, 0, meta, counts, live_tiles, m0, dpre0, dagg0, at, wt, grads)
-    grads = finish(z, bound_tiles, part, back_west, back_east, grads)
-
-    grad_self, grad_nbr, grad_bias, grad_out = unpack(z, early, late)
+    halves = weight_grads(z, plane, f0, agg0, act0, m0, dpre0, "weight_grads0")
+
+    def last(late, halves, m0, dpre0, dagg0, meta, counts, at, wt):
+        sums = share_totals(plane, late, halves)
+        return (sums, *input_grad(z, 0, meta, counts, m0, dpre0, dagg0, at, wt))
+
+    args = (late, halves, m0, dpre0, dagg0, meta, counts, at, wt)
+    shapes = jax.eval_shape(last, *args)
+    totals, part, rest = lax.cond(
+        live_tiles[0] > 0, last, lambda *_: tuple(jnp.zeros(a.shape, a.dtype) for a in shapes), *args
+    )
+    grads, grad_self, grad_nbr, grad_bias, grad_out = finish(
+        z, plane, bound_tiles, part, rest, back_west, back_east, totals, grads
+    )
     return (
         section_out.reshape(2, t * r, c),
         grads.reshape(2, t * r, c),

time: 211 us -> 163 us (0.77)
  blocking collectives: 41.2 us -> 0 us
  local copies, waits for them, and re-layouts: 25.2 us -> 13.9 us
  waiting for transfers between devices: 18.7 us -> 29.3 us
  starting transfers between devices: 46.1 us -> 38.2 us
  Pallas kernels: 76.5 us -> 79.1 us
    all_gather x2 -> x0, blocking collectives: 41.2 us -> none  [summed_over_parts(): return lax.all_gather(share, PLANE, axis=0, tiled=True)]
    ppermute x18 -> x11, waiting for transfers between devices: 5.99 us -> 23.7 us  [the longest x6 11.4 us: along(): return lax.ppermute(value, PLANE, pairs)]
    unnamed x83 -> x53, local copies, waits for them, and re-layouts: 25.2 us -> 13.9 us
    ppermute x18 -> x11, starting transfers between devices: 23.5 us -> 15.5 us  [the longest x2 8.18 us: share_totals(): lax.ppermute(share, 'feat', [(i, i ^ step) for i in range(lines)])]
    ppermute x8, waiting for transfers between devices: 12.7 us -> 5.6 us  [passed_along(): lax.ppermute(value, AXES, [(i, (i + steps) % count) for i in range(count)])]
    pallas_call x17 -> x16, Pallas kernels: 76.5 us -> 79.1 us  [call(): pl.pallas_call(kernel, in_specs=in_specs, out_specs=out_specs, out_shape=...]
  transfers between devices with their start and end apart: 26 -> 19, of which waited for: 6 -> 9; matrix products, arithmetic and copies ran while one was open for 0% -> 0% of each run, Pallas kernels for 28% -> 33%
where the time goes in v4:
time: 163 us
  Pallas kernels  79.1 us (49%)
  starting transfers between devices  38.2 us (23%)
  waiting for transfers between devices  29.3 us (18%)
  local copies, waits for them, and re-layouts  13.9 us (9%)
  between operations  1.79 us (1%)
    pallas_call x16, Pallas kernels, call(): pl.pallas_call(kernel, in_specs=in_specs, out_specs=out_specs, out_shape=...  79.1 us
    ppermute x8, starting transfers between devices, passed_along(): lax.ppermute(value, AXES, [(i, (i + steps) % count) for i in range(count)])  22.6 us
    unnamed x53, local copies, waits for them, and re-layouts  13.9 us
    ppermute x6, waiting for transfers between devices, along(): return lax.ppermute(value, PLANE, pairs)  11.4 us
    ppermute x2, waiting for transfers between devices, share_totals(): lax.ppermute(share, 'feat', [(i, i ^ step) for i in range(lines)])  10.8 us
    ppermute x2, starting transfers between devices, share_totals(): lax.ppermute(share, 'feat', [(i, i ^ step) for i in range(lines)])  8.18 us
    ppermute x6, starting transfers between devices, along(): return lax.ppermute(value, PLANE, pairs)  7.15 us
    ppermute x8, waiting for transfers between devices, passed_along(): lax.ppermute(value, AXES, [(i, (i + steps) % count) for i in range(count)])  5.6 us
  transfers between devices with their start and end apart: 19, of which 9 were waited for; matrix products, arithmetic and copies ran while one was open for 0% of the time, Pallas kernels for 33%

profile of v4, /device:TPU:0, one launch (start us, length us, event | category | flops | bytes accessed | tf_op | source)
XLA Modules:
  0.0 162.8 jit_solution(5454163569005809152)
XLA Ops:
  2.9 3.1 %lend.1 = (bf16[8,128,256]{2,1,0:T(8,128)(2,1)}, bf16[8,128,256]{2,1,0:T(8,128)(2,1)}) custom-call(s32[1,2,8]{2,1,0:T(2,128)S(1)} %copy-done.19, bf16[32,128,256]{2,1,0:T(8,128)(2,1)S(1)} %bitcast.28), custom_call_target="tpu_custom_call" | custom-call | flops 1000 | bytes 1000 | tf_op jit(solution)/shard_map/lend/pallas_call | solution.py:75
  9.1 3.4 %collective-permute-start.11 = (bf16[8,128,256]{2,1,0:T(8,128)(2,1)}, bf16[8,128,256]{2,1,0:T(8,128)(2,1)}, u32[]{:S(2)}, u32[]{:S(2)}) collective-permute-start(bf16[8,128,256]{2,1,0:T(8,128)(2,1)} %get-tuple-element.105), channel_id=1, source_target_pairs={{0,31},{1,0},{2,1},{3,2},{4,3},{5,4},{6,5},{7,6},{8,7},{9,8},{10,9... | collective-permute-start | bytes 1572872 | tf_op jit(solution)/shard_map/ppermute | solution.py:63
  18.6 10.6 %arrange.1 = (bf16[16,128,256]{2,1,0:T(8,128)(2,1)S(1)}, bf16[16,128,256]{2,1,0:T(8,128)(2,1)S(1)}, bf16[16,128,256]{2,1,0:T(8,128)(2,1)S(1)}, bf16[16,128,256]{...) custom-call(s32[1,2,8]{2,1,0:T(2,128)S(1)} %copy-done.20, ...), custom_call_target="tpu_custom_call" | custom-call | flops 1000 | bytes 1000 | tf_op jit(solution)/shard_map/arrange/pallas_call | solution.py:75
  29.3 4.7 %collective-permute-done.11.fe = bf16[8,128,256]{2,1,0:T(8,128)(2,1)} collective-permute-done((bf16[8,128,256]{2,1,0:T(8,128)(2,1)}, bf16[8,128,256]{2,1,0:T(8,128)(2,1)}, u32[]{:S(2)}, u32[]{:S(2)}) %collective-permute-start.11) | collective-permute-done | bytes 524320 | tf_op jit(solution)/shard_map/ppermute | solution.py:63
  34.1 4.9 %first_lent.1 = (bf16[8,128,256]{2,1,0:T(8,128)(2,1)}, bf16[8,128,256]{2,1,0:T(8,128)(2,1)}, bf16[16,128,256]{2,1,0:T(8,128)(2,1)S(1)}) custom-call(s32[384]{0:T(512)S(1)} %get-tuple-element.101.meta, bf16[16,128,256]{2,1,0:T(8,128)(2,1)S(1)} %get-tuple-element.102.f_lent.refs_0_, bf16[16,128,256]{2,1,0:T(8,128)(2,1)S(1)} %get-tuple-element.103.f_rest.refs_1_, ...), custom_call_target="tpu_custom_call" | custom-call | flops 1000 | bytes 1000 | tf_op jit(solution)/shard_map/first_lent/pallas_call | solution.py:75
  40.6 3.8 %collective-permute-start.13 = (bf16[8,128,256]{2,1,0:T(8,128)(2,1)}, bf16[8,128,256]{2,1,0:T(8,128)(2,1)}, u32[]{:S(2)}, u32[]{:S(2)}) collective-permute-start(bf16[8,128,256]{2,1,0:T(8,128)(2,1)} %get-tuple-element.107.west), channel_id=1, source_target_pairs={{0,31},{1,0},{2,1},{3,2},{4,3},{5,4},{6,5},{7,6},{8,7},{9,8},{10,9... | collective-permute-start | bytes 1572872 | tf_op jit(solution)/shard_map/ppermute | solution.py:63
  44.3 5.1 %turn.1 = (bf16[128,128,128]{2,1,0:T(8,128)(2,1)}, bf16[2,3,256,256]{3,2,1,0:T(8,128)(2,1)S(1)}) custom-call(bf16[32,4,128,128]{3,2,1,0:T(8,128)(2,1)S(1)} %get-tuple-element.106.ap, bf16[2,256,256]{2,1,0:T(8,128)(2,1)S(1)} %copy-done.9, bf16[2,256,256]{2,1,0:T(8,128)(2,1)S(1)} %copy-done.10, bf16[2,256,256]{2,1,0:T(8,128)(2,1)S(1)} %copy-done.12), custom_call_target="tpu_custom_call" | custom-call | flops 1000 | bytes 1000 | tf_op jit(solution)/shard_map/turn/pallas_call | solution.py:75
  57.3 5.8 %first_rest.1 = (bf16[16,128,256]{2,1,0:T(8,128)(2,1)S(1)}, bf16[16,128,256]{2,1,0:T(8,128)(2,1)S(1)}, bf16[2,32,128,256]{3,2,1,0:T(8,128)(2,1)}, bf16[16,128,256]{2,1,0:T(8,128)(2,1)S(1)}) custom-call(s32[384]{0:T(512)S(1)} %get-tuple-element.101.meta, s32[1,2,8]{2,1,0:T(2,128)S(1)} %copy-done.20, s32[1]{0:T(128)S(6)} %copy.29.live, ...), custom_call_target="tpu_custom_call" | custom-call | flops 1000 | bytes 1000 | tf_op jit(solution)/shard_map/first_rest/pallas_call | solution.py:75
  66.3 9.5 %second.1 = (bf16[32,128,256]{2,1,0:T(8,128)(2,1)S(1)}, bf16[32,128,256]{2,1,0:T(8,128)(2,1)S(1)}, bf16[32,128,256]{2,1,0:T(8,128)(2,1)S(1)}, bf16[32,128,256]{2...) custom-call(s32[384]{0:T(512)S(1)} %get-tuple-element.101.meta, ...), custom_call_target="tpu_custom_call" | custom-call | flops 1000 | bytes 1000 | tf_op jit(solution)/shard_map/second/pallas_call | solution.py:75
  75.8 5.3 %collective-permute-start.15 = (bf16[8,128,256]{2,1,0:T(8,128)(2,1)S(1)}, bf16[8,128,256]{2,1,0:T(8,128)(2,1)S(1)}, u32[]{:S(2)}, u32[]{:S(2)}) collective-permute-start(bf16[8,128,256]{2,1,0:T(8,128)(2,1)S(1)} %get-tuple-element.127), channel_id=1, source_target_pairs={{0,31},{1,0},{2,1},{3,2},{4,3},{5,4},{6,5},{7,6},{8,7},{9,8},{10,9... | collective-permute-start | bytes 1572872 | tf_op jit(solution)/shard_map/ppermute | solution.py:63
  81.2 4.1 %weight_grads1.1 = (bf16[4,112,256]{2,1,0:T(8,128)(2,1)S(1)}, bf16[4,112,256]{2,1,0:T(8,128)(2,1)S(1)}) custom-call(s32[2]{0:T(128)S(1)} %pad_add_fusion.me, bf16[16,128,256]{2,1,0:T(8,128)(2,1)S(1)} %get-tuple-element.109.f_lent.refs_0_, bf16[16,128,256]{2,1,0:T(8,128)(2,1)S(1)} %get-tuple-element.110.f_rest.refs_1_, ...), custom_call_target="tpu_custom_call" | custom-call | flops 1000 | bytes 1000 | tf_op jit(solution)/shard_map/weight_grads1/pallas_call | solution.py:75
  85.4 6.4 %input_grad1.1 = (f32[16,128,256]{2,1,0:T(8,128)S(1)}, bf16[16,128,256]{2,1,0:T(8,128)(2,1)S(1)}) custom-call(s32[384]{0:T(512)S(1)} %get-tuple-element.101.meta, s32[8]{0:T(128)S(1)} %get-tuple-element.111.counts, bf16[16,128,256]{2,1,0:T(8,128)(2,1)S(1)} %get-tuple-element.113.m_lent.refs_0_.refs_4_, bf16[16,128,256]{2,1,0:T(8,128)(2,1)S(1)} %copy-done.6, ...), custom_call_target="tpu_custom_call" | custom-call | flops 1000 | bytes 1000 | tf_op jit(solution)/shard_map/input_grad1/pallas_call | solution.py:75
  91.8 3.5 %second_out.1 = (bf16[2,32,128,256]{3,2,1,0:T(8,128)(2,1)}, f32[8,128]{1,0:T(8,128)S(1)}) custom-call(s32[1,2,8]{2,1,0:T(2,128)S(1)} %copy-done.20, s32[1]{0:T(128)S(6)} %copy.29.live, bf16[16,128,256]{2,1,0:T(8,128)(2,1)S(1)} %get-tuple-element.109.f_lent.refs_0_, ...), custom_call_target="tpu_custom_call", output_to_operand_aliasing={{0}: (6, {})} | custom-call | flops 1000 | bytes 1000 | tf_op jit(solution)/shard_map/second_out/pallas_call | solution.py:75
  95.3 3.1 %early_rest.1 = (bf16[2,32,128,256]{3,2,1,0:T(8,128)(2,1)}, bf16[16,128,256]{2,1,0:T(8,128)(2,1)S(1)}, bf16[16,128,256]{2,1,0:T(8,128)(2,1)S(1)}, bf16[16,128,256]{2,1,0:T(8,128)(2,1)S(1)}, f32[16,128,256]{2,1,0:T(8,128)S(1)}) custom-call(s32[384]{0:T(512)S(1)} %get-tuple-element.101.meta, s32[8]{0:T(128)S(1)} %get-tuple-element.111.counts, ...), custom_call_target="tpu_custom_call" | custom-call | flops 1000 | bytes 1000 | tf_op jit(solution)/shard_map/early_rest/pallas_call | solution.py:75
  99.4 4.5 %early_lent.1 = (bf16[16,128,256]{2,1,0:T(8,128)(2,1)S(1)}, bf16[16,128,256]{2,1,0:T(8,128)(2,1)S(1)}, bf16[16,128,256]{2,1,0:T(8,128)(2,1)S(1)}, bf16[2,32,128,...) custom-call(s32[384]{0:T(512)S(1)} %get-tuple-element.101.meta, ...), custom_call_target="tpu_custom_call", output_to_operand_aliasing={{3}: (10, {})} | custom-call | flops 1000 | bytes 1000 | tf_op jit(solution)/shard_map/early_lent/pallas_call | solution.py:75
  104.9 4.5 %collective-permute-start.18 = (bf16[8,128,256]{2,1,0:T(8,128)(2,1)}, bf16[8,128,256]{2,1,0:T(8,128)(2,1)S(1)}, u32[]{:S(2)}, u32[]{:S(2)}) collective-permute-start(bf16[8,128,256]{2,1,0:T(8,128)(2,1)} %get-tuple-element.147), channel_id=1, source_target_pairs={{0,31},{1,0},{2,1},{3,2},{4,3},{5,4},{6,5},{7,6},{8,7},{9,8},{10,9... | collective-permute-start | bytes 1572872 | tf_op jit(solution)/shard_map/ppermute | solution.py:63
  109.3 4.1 %weight_grads0.1 = (bf16[4,112,256]{2,1,0:T(8,128)(2,1)S(1)}, bf16[4,112,256]{2,1,0:T(8,128)(2,1)S(1)}) custom-call(s32[2]{0:T(128)S(1)} %pad_add_fusion.me, bf16[16,128,256]{2,1,0:T(8,128)(2,1)S(1)} %get-tuple-element.102.f_lent.refs_0_, bf16[16,128,256]{2,1,0:T(8,128)(2,1)S(1)} %get-tuple-element.103.f_rest.refs_1_, bf16[16,128,256]{2,1,0:T(8,128)(2,1)S(1)} %copy-done.17, ...), custom_call_target="tpu_custom_call" | custom-call | flops 1000 | bytes 1000 | tf_op jit(solution)/shard_map/weight_grads0/pallas_call | solution.py:75
  113.4 46.1 %conditional.1 = (bf16[2,4,2,112,256]{4,3,2,1,0:T(8,128)(2,1)S(1)}, f32[16,128,256]{2,1,0:T(8,128)S(1)}, bf16[16,128,256]{2,1,0:T(8,128)(2,1)S(1)}) conditional(s32[]{:T(128)} %bitcast.18, () %tuple.16, (bf16[4,112,256]{2,1,0:T(8,128)(2,1)S(1)}, bf16[4,112,256]{2,1,0:T(8,128)(2,1)S(1)}, bf16[4,112,256]{2,1,0:T(8,128)(2,1)S(1)}, s32[384]{0:T(512)S(1)}, ...), branch_computations={%region_0.1_spmd, %region_1.2_spmd} | conditional | flops 2753512 | bytes 12731792 | solution.py:798
  118.8 5.9 %collective-permute-done.1 = bf16[2,112,256]{2,1,0:T(8,128)(2,1)S(1)} collective-permute-done((bf16[2,112,256]{2,1,0:T(8,128)(2,1)S(1)}, bf16[2,112,256]{2,1,0:T(8,128)(2,1)S(1)}, u32[]{:S(2)}, u32[]{:S(2)}) %collective-permute-start.1) | collective-permute-done | bytes 114720 | tf_op jit(solution)/shard_map/cond/branch_1_fun/ppermute | solution.py:456
  126.2 5.6 %collective-permute-done.4 = bf16[2,112,256]{2,1,0:T(8,128)(2,1)S(1)} collective-permute-done((bf16[2,112,256]{2,1,0:T(8,128)(2,1)S(1)}, bf16[2,112,256]{2,1,0:T(8,128)(2,1)S(1)}, u32[]{:S(2)}, u32[]{:S(2)}) %collective-permute-start.4) | collective-permute-done | bytes 114720 | tf_op jit(solution)/shard_map/cond/branch_1_fun/ppermute | solution.py:522
  131.8 8.1 %collective-permute-start.5 = (bf16[2,112,256]{2,1,0:T(8,128)(2,1)S(1)}, bf16[2,112,256]{2,1,0:T(8,128)(2,1)S(1)}, u32[]{:S(2)}, u32[]{:S(2)}) collective-permute-start(bf16[2,112,256]{2,1,0:T(8,128)(2,1)S(1)} %add_convert_fusion.2), channel_id=1, source_target_pairs={{0,2},{1,3},{2,0},{3,1},{4,6},{5,7},{6,4},{7,5},{8,10},{9,11},{10,... | collective-permute-start | bytes 344072 | tf_op jit(solution)/shard_map/cond/branch_1_fun/ppermute | solution.py:522
  139.9 5.3 %collective-permute-done.5 = bf16[2,112,256]{2,1,0:T(8,128)(2,1)S(1)} collective-permute-done((bf16[2,112,256]{2,1,0:T(8,128)(2,1)S(1)}, bf16[2,112,256]{2,1,0:T(8,128)(2,1)S(1)}, u32[]{:S(2)}, u32[]{:S(2)}) %collective-permute-start.5) | collective-permute-done | bytes 114720 | tf_op jit(solution)/shard_map/cond/branch_1_fun/ppermute | solution.py:522
  152.9 6.5 %input_grad0.1 = (f32[16,128,256]{2,1,0:T(8,128)S(1)}, bf16[16,128,256]{2,1,0:T(8,128)(2,1)S(1)}) custom-call(s32[384]{0:T(512)S(1)} %get-tuple-element.29.meta, s32[8]{0:T(128)S(1)} %get-tuple-element.30.counts, bf16[16,128,256]{2,1,0:T(8,128)(2,1)S(1)} %get-tuple-element.31.refs_0_, bf16[16,128,256]{2,1,0:T(8,128)(2,1)S(1)} %get-tuple-element.32.refs_1_, ...), custom_call_target="tpu_custom_call" | custom-call | flops 1000 | bytes 1000 | tf_op jit(solution)/shard_map/cond/branch_1_fun/input_grad0/pallas_call | solution.py:75
  159.5 3.1 %finish.1 = (bf16[2,32,128,256]{3,2,1,0:T(8,128)(2,1)}, f32[2,256,256]{2,1,0:T(8,128)}, f32[2,256,256]{2,1,0:T(8,128)}, f32[2,256]{1,0:T(2,128)}, f32[2,256,256]{2,1,0:T(8,128)}) custom-call(s32[2]{0:T(128)S(1)} %pad_add_fusion.me, s32[1,2,8]{2,1,0:T(2,128)S(1)} %copy-done.20, ...), custom_call_target="tpu_custom_call", output_to_operand_aliasing={{0}: (7, {})} | custom-call | flops 1000 | bytes 1000 | tf_op jit(solution)/shard_map/finish/pallas_call | solution.py:75
  (93 shorter events, 40.2 us)
Async XLA Ops:
  6.0 23.3 %collective-permute-start.10 = (bf16[8,128,256]{2,1,0:T(8,128)(2,1)}, bf16[8,128,256]{2,1,0:T(8,128)(2,1)}, u32[]{:S(2)}, u32[]{:S(2)}) collective-permute-start(bf16[8,128,256]{2,1,0:T(8,128)(2,1)} %get-tuple-element.104), channel_id=1, source_target_pairs={{0,1},{1,2},{2,3},{3,4},{4,5},{5,6},{6,7},{7,8},{8,9},{9,10},{10,1... | collective-permute-start | bytes 1572872 | tf_op jit(solution)/shard_map/ppermute | solution.py:63
  9.1 24.9 %collective-permute-start.11 = (bf16[8,128,256]{2,1,0:T(8,128)(2,1)}, bf16[8,128,256]{2,1,0:T(8,128)(2,1)}, u32[]{:S(2)}, u32[]{:S(2)}) collective-permute-start(bf16[8,128,256]{2,1,0:T(8,128)(2,1)} %get-tuple-element.105), channel_id=1, source_target_pairs={{0,31},{1,0},{2,1},{3,2},{4,3},{5,4},{6,5},{7,6},{8,7},{9,8},{10,9... | collective-permute-start | bytes 1572872 | tf_op jit(solution)/shard_map/ppermute | solution.py:63
  18.6 15.4 %copy-start.9 = (bf16[2,256,256]{2,1,0:T(8,128)(2,1)S(1)}, bf16[2,256,256]{2,1,0:T(8,128)(2,1)}, u32[]{:S(2)}) copy-start(bf16[2,256,256]{2,1,0:T(8,128)(2,1)} %ws.9) | copy-start | bytes 786436
  18.6 15.4 %copy-start.10 = (bf16[2,256,256]{2,1,0:T(8,128)(2,1)S(1)}, bf16[2,256,256]{2,1,0:T(8,128)(2,1)}, u32[]{:S(2)}) copy-start(bf16[2,256,256]{2,1,0:T(8,128)(2,1)} %wn.9) | copy-start | bytes 786436
  18.6 15.4 %copy-start.12 = (bf16[2,256,256]{2,1,0:T(8,128)(2,1)S(1)}, bf16[2,256,256]{2,1,0:T(8,128)(2,1)}, u32[]{:S(2)}) copy-start(bf16[2,256,256]{2,1,0:T(8,128)(2,1)} %wo.7) | copy-start | bytes 786436
  18.6 15.4 %copy-start.21 = (f32[2,256]{1,0:T(2,128)S(1)}, f32[2,256]{1,0:T(2,128)}, u32[]{:S(2)}) copy-start(f32[2,256]{1,0:T(2,128)} %bias.7) | copy-start | bytes 6148
  29.3 20.1 %copy-start.5 = (bf16[16,128,256]{2,1,0:T(8,128)(2,1)}, bf16[16,128,256]{2,1,0:T(8,128)(2,1)S(1)}, u32[]{:S(2)}) copy-start(bf16[16,128,256]{2,1,0:T(8,128)(2,1)S(1)} %get-tuple-element.114.m_rest.refs_1_.refs_5_) | copy-start | bytes 3145732
  39.0 27.2 %collective-permute-start.12 = (bf16[8,128,256]{2,1,0:T(8,128)(2,1)}, bf16[8,128,256]{2,1,0:T(8,128)(2,1)}, u32[]{:S(2)}, u32[]{:S(2)}) collective-permute-start(bf16[8,128,256]{2,1,0:T(8,128)(2,1)} %get-tuple-element.108.east), channel_id=1, source_target_pairs={{0,1},{1,2},{2,3},{3,4},{4,5},{5,6},{6,7},{7,8},{8,9},{9,10},{10,1... | collective-permute-start | bytes 1572872 | tf_op jit(solution)/shard_map/ppermute | solution.py:63
  40.6 25.6 %collective-permute-start.13 = (bf16[8,128,256]{2,1,0:T(8,128)(2,1)}, bf16[8,128,256]{2,1,0:T(8,128)(2,1)}, u32[]{:S(2)}, u32[]{:S(2)}) collective-permute-start(bf16[8,128,256]{2,1,0:T(8,128)(2,1)} %get-tuple-element.107.west), channel_id=1, source_target_pairs={{0,31},{1,0},{2,1},{3,2},{4,3},{5,4},{6,5},{7,6},{8,7},{9,8},{10,9... | collective-permute-start | bytes 1572872 | tf_op jit(solution)/shard_map/ppermute | solution.py:63
  75.7 22.8 %collective-permute-start.14 = (bf16[8,128,256]{2,1,0:T(8,128)(2,1)S(1)}, bf16[8,128,256]{2,1,0:T(8,128)(2,1)S(1)}, u32[]{:S(2)}, u32[]{:S(2)}) collective-permute-start(bf16[8,128,256]{2,1,0:T(8,128)(2,1)S(1)} %get-tuple-element.126), channel_id=1, source_target_pairs={{0,1},{1,2},{2,3},{3,4},{4,5},{5,6},{6,7},{7,8},{8,9},{9,10},{10,1... | collective-permute-start | bytes 1572872 | tf_op jit(solution)/shard_map/ppermute | solution.py:63
  75.8 23.6 %collective-permute-start.15 = (bf16[8,128,256]{2,1,0:T(8,128)(2,1)S(1)}, bf16[8,128,256]{2,1,0:T(8,128)(2,1)S(1)}, u32[]{:S(2)}, u32[]{:S(2)}) collective-permute-start(bf16[8,128,256]{2,1,0:T(8,128)(2,1)S(1)} %get-tuple-element.127), channel_id=1, source_target_pairs={{0,31},{1,0},{2,1},{3,2},{4,3},{5,4},{6,5},{7,6},{8,7},{9,8},{10,9... | collective-permute-start | bytes 1572872 | tf_op jit(solution)/shard_map/ppermute | solution.py:63
  85.3 13.1 %collective-permute-start.16 = (bf16[4,112,256]{2,1,0:T(8,128)(2,1)S(1)}, bf16[4,112,256]{2,1,0:T(8,128)(2,1)S(1)}, u32[]{:S(2)}, u32[]{:S(2)}) collective-permute-start(bf16[4,112,256]{2,1,0:T(8,128)(2,1)S(1)} %get-tuple-element.135), channel_id=1, source_target_pairs={{0,8},{4,12},{16,24},{20,28},{8,0},{12,4},{24,16},{28,20},{1,9},{5... | collective-permute-start | bytes 688136 | tf_op jit(solution)/shard_map/ppermute | solution.py:448
  103.9 55.6 %collective-permute-start.17 = (bf16[8,128,256]{2,1,0:T(8,128)(2,1)}, bf16[8,128,256]{2,1,0:T(8,128)(2,1)S(1)}, u32[]{:S(2)}, u32[]{:S(2)}) collective-permute-start(bf16[8,128,256]{2,1,0:T(8,128)(2,1)} %get-tuple-element.146), channel_id=1, source_target_pairs={{0,1},{1,2},{2,3},{3,4},{4,5},{5,6},{6,7},{7,8},{8,9},{9,10},{10,1... | collective-permute-start | bytes 1572872 | tf_op jit(solution)/shard_map/ppermute | solution.py:63
  104.9 54.7 %collective-permute-start.18 = (bf16[8,128,256]{2,1,0:T(8,128)(2,1)}, bf16[8,128,256]{2,1,0:T(8,128)(2,1)S(1)}, u32[]{:S(2)}, u32[]{:S(2)}) collective-permute-start(bf16[8,128,256]{2,1,0:T(8,128)(2,1)} %get-tuple-element.147), channel_id=1, source_target_pairs={{0,31},{1,0},{2,1},{3,2},{4,3},{5,4},{6,5},{7,6},{8,7},{9,8},{10,9... | collective-permute-start | bytes 1572872 | tf_op jit(solution)/shard_map/ppermute | solution.py:63
  113.4 1.6 collective-permute-start
  115.1 9.6 %collective-permute-start.1 = (bf16[2,112,256]{2,1,0:T(8,128)(2,1)S(1)}, bf16[2,112,256]{2,1,0:T(8,128)(2,1)S(1)}, u32[]{:S(2)}, u32[]{:S(2)}) collective-permute-start(bf16[2,112,256]{2,1,0:T(8,128)(2,1)S(1)} %get-tuple-element.157), channel_id=1, source_target_pairs={{0,4},{4,16},{16,20},{20,0},{8,12},{12,24},{24,28},{28,8},{1,5},{5... | collective-permute-start | bytes 344072 | tf_op jit(solution)/shard_map/cond/branch_1_fun/ppermute | solution.py:456
  117.2 7.5 %collective-permute-start.2 = (bf16[2,112,256]{2,1,0:T(8,128)(2,1)S(1)}, bf16[2,112,256]{2,1,0:T(8,128)(2,1)S(1)}, u32[]{:S(2)}, u32[]{:S(2)}) collective-permute-start(bf16[2,112,256]{2,1,0:T(8,128)(2,1)S(1)} %get-tuple-element.159), channel_id=1, source_target_pairs={{0,16},{4,20},{16,0},{20,4},{8,24},{12,28},{24,8},{28,12},{1,17},{... | collective-permute-start | bytes 344072 | tf_op jit(solution)/shard_map/cond/branch_1_fun/ppermute | solution.py:456
  117.6 8.5 %collective-permute-start.3 = (bf16[2,112,256]{2,1,0:T(8,128)(2,1)S(1)}, bf16[2,112,256]{2,1,0:T(8,128)(2,1)S(1)}, u32[]{:S(2)}, u32[]{:S(2)}) collective-permute-start(bf16[2,112,256]{2,1,0:T(8,128)(2,1)S(1)} %get-tuple-element.158), channel_id=1, source_target_pairs={{0,20},{4,0},{16,4},{20,16},{8,28},{12,8},{24,12},{28,24},{1,21},{... | collective-permute-start | bytes 344072 | tf_op jit(solution)/shard_map/cond/branch_1_fun/ppermute | solution.py:456
  126.1 5.7 %collective-permute-start.4 = (bf16[2,112,256]{2,1,0:T(8,128)(2,1)S(1)}, bf16[2,112,256]{2,1,0:T(8,128)(2,1)S(1)}, u32[]{:S(2)}, u32[]{:S(2)}) collective-permute-start(bf16[2,112,256]{2,1,0:T(8,128)(2,1)S(1)} %fusion.3), channel_id=1, source_target_pairs={{0,1},{1,0},{2,3},{3,2},{4,5},{5,4},{6,7},{7,6},{8,9},{9,8},{10,11... | collective-permute-start | bytes 344072 | tf_op jit(solution)/shard_map/cond/branch_1_fun/ppermute | solution.py:522
  131.8 13.4 %collective-permute-start.5 = (bf16[2,112,256]{2,1,0:T(8,128)(2,1)S(1)}, bf16[2,112,256]{2,1,0:T(8,128)(2,1)S(1)}, u32[]{:S(2)}, u32[]{:S(2)}) collective-permute-start(bf16[2,112,256]{2,1,0:T(8,128)(2,1)S(1)} %add_convert_fusion.2), channel_id=1, source_target_pairs={{0,2},{1,3},{2,0},{3,1},{4,6},{5,7},{6,4},{7,5},{8,10},{9,11},{10,... | collective-permute-start | bytes 344072 | tf_op jit(solution)/shard_map/cond/branch_1_fun/ppermute | solution.py:522
  145.2 6.5 %collective-permute-start.6 = (bf16[2,112,256]{2,1,0:T(8,128)(2,1)S(1)}, bf16[2,112,256]{2,1,0:T(8,128)(2,1)S(1)}, u32[]{:S(2)}, u32[]{:S(2)}) collective-permute-start(bf16[2,112,256]{2,1,0:T(8,128)(2,1)S(1)} %add_convert_fusion.1), channel_id=1, source_target_pairs={{0,4},{4,16},{16,20},{20,0},{8,12},{12,24},{24,28},{28,8},{1,5},{5... | collective-permute-start | bytes 344072 | tf_op jit(solution)/shard_map/cond/branch_1_fun/ppermute | solution.py:456
  145.2 6.4 %collective-permute-start.7 = (bf16[2,112,256]{2,1,0:T(8,128)(2,1)S(1)}, bf16[2,112,256]{2,1,0:T(8,128)(2,1)S(1)}, u32[]{:S(2)}, u32[]{:S(2)}) collective-permute-start(bf16[2,112,256]{2,1,0:T(8,128)(2,1)S(1)} %add_convert_fusion.1), channel_id=1, source_target_pairs={{0,16},{4,20},{16,0},{20,4},{8,24},{12,28},{24,8},{28,12},{1,17},{... | collective-permute-start | bytes 344072 | tf_op jit(solution)/shard_map/cond/branch_1_fun/ppermute | solution.py:456
  145.8 7.0 %collective-permute-start.8 = (bf16[2,112,256]{2,1,0:T(8,128)(2,1)S(1)}, bf16[2,112,256]{2,1,0:T(8,128)(2,1)S(1)}, u32[]{:S(2)}, u32[]{:S(2)}) collective-permute-start(bf16[2,112,256]{2,1,0:T(8,128)(2,1)S(1)} %add_convert_fusion.1), channel_id=1, source_target_pairs={{0,20},{4,0},{16,4},{20,16},{8,28},{12,8},{24,12},{28,24},{1,21},{... | collective-permute-start | bytes 344072 | tf_op jit(solution)/shard_map/cond/branch_1_fun/ppermute | solution.py:456
  152.8 6.6 %collective-permute-start.9 = (bf16[4,2,112,256]{3,2,1,0:T(8,128)(2,1)S(1)}, bf16[4,2,112,256]{3,2,1,0:T(8,128)(2,1)S(1)}, u32[]{:S(2)}, u32[]{:S(2)}) collective-permute-start(bf16[4,2,112,256]{3,2,1,0:T(8,128)(2,1)S(1)} %get-tuple-element.156), channel_id=1, source_target_pairs={{0,8},{4,12},{16,24},{20,28},{8,0},{12,4},{24,16},{28,20},{1,9},{5... | collective-permute-start | bytes 1376264 | tf_op jit(solution)/shard_map/cond/branch_1_fun/ppermute | solution.py:448
  (21 other events, 116.0 us)

commit v5 on v4

--- a/solution.py
+++ b/solution.py
@@ -109,7 +109,7 @@
         [VMEM, VMEM],
         [z.nodes(z.edge), z.nodes(z.edge)],
         [pltpu.SemaphoreType.DMA((z.lent,))],
-        2,
+        56,
         (bound, features),
     )
 
@@ -427,38 +427,36 @@
 class Plane:
     def __init__(self):
         dom, phase = lax.axis_size("dom"), lax.axis_size("phase")
-        self.pair = 2 if dom % 2 == 0 else 1
-        self.phase = phase
-        self.groups = dom // self.pair * phase
+        core = 2 if dom % 2 == 0 else 1
+        self.sizes = (core, dom // core, phase)
         self.count = dom * phase
         place = lax.axis_index("dom")
-        half = lax.rem(place, self.pair)
-        group = place // self.pair * phase + lax.axis_index("phase")
-        self.me = jnp.stack([half, group]).astype(jnp.int32)
-
-    def index(self, half, group):
-        return (group // self.phase * self.pair + half) * self.phase + group % self.phase
-
-    def across(self, value):
-        pairs = [
-            (self.index(h, g), self.index((h + 1) % self.pair, g))
-            for h in range(self.pair)
-            for g in range(self.groups)
-        ]
+        self.me = jnp.stack([lax.rem(place, core), place // core, lax.axis_index("phase")]).astype(jnp.int32)
+
+    def piece_of(self, me, steps):
+        at = [lax.rem(me[i] + (steps[i] + n) % n, n) for i, n in enumerate(self.sizes)]
+        return (at[0] * self.sizes[1] + at[1]) * self.sizes[2] + at[2]
+
+    def passed(self, value, dim, steps):
+        pairs = []
+        for c in range(self.sizes[0]):
+            for d in range(self.sizes[1]):
+                for p in range(self.sizes[2]):
+                    to = [c, d, p]
+                    to[dim] = (to[dim] + steps) % self.sizes[dim]
+                    source = (d * self.sizes[0] + c) * self.sizes[2] + p
+                    target = (to[1] * self.sizes[0] + to[0]) * self.sizes[2] + to[2]
+                    pairs.append((source, target))
         return lax.ppermute(value, PLANE, pairs)
 
-    def along(self, value, steps):
-        pairs = [
-            (self.index(h, g), self.index(h, (g + steps) % self.groups))
-            for h in range(self.pair)
-            for g in range(self.groups)
-        ]
-        return lax.ppermute(value, PLANE, pairs)
+    def received(self, parts, dim):
+        return [parts[0]] + [self.passed(parts[i], dim, i) for i in range(1, self.sizes[dim])]
 
 
 def weight_grads(z, plane, f, agg, act, m, dpre, name):
     c = z.cols
     piece = -(-(3 * c + 1) // (plane.count * 16)) * 16
+    core, ahead, side = plane.sizes
     arrays = (f, agg, act, m, dpre)
     flat_args = [x for a in arrays for x in (a if isinstance(a, tuple) else (a,))]
 
@@ -481,52 +479,71 @@
             acc[pl.ds(3 * c, 1), :] += jnp.sum(grad.astype(F32), axis=0, keepdims=True)
 
         each_group(z, work)
-        for h, out in enumerate(outs):
-            half = lax.rem(me[0] + h, plane.pair)
-            for g in range(plane.groups):
-                owner = half * plane.groups + lax.rem(me[1] + g, plane.groups)
-                out[g] = acc[pl.ds(pl.multiple_of(owner * piece, 16), piece), :].astype(BF16)
+        for i, out in enumerate(outs):
+            for j in range(ahead):
+                for k in range(side):
+                    owner = pl.multiple_of(plane.piece_of(me, (i, j, k)) * piece, 16)
+                    out[j, k] = acc[pl.ds(owner, piece), :].astype(BF16)
 
     return call(
         kernel,
         name,
         [SMEM] + [VMEM] * len(flat_args),
-        [VMEM] * plane.pair,
-        [jax.ShapeDtypeStruct((plane.groups, piece, c), BF16)] * plane.pair,
+        [VMEM] * core,
+        [jax.ShapeDtypeStruct((ahead, side, piece, c), BF16)] * core,
         [pltpu.VMEM((piece * plane.count, c), F32)],
         14,
         (plane.me, *flat_args),
     )
 
 
-def added(*values):
-    total = values[0].astype(F32)
-    for value in values[1:]:
-        total = total + value.astype(F32)
-    return total.astype(BF16)
-
-
-def pair_sums(plane, halves):
-    if plane.pair == 1:
-        return halves[0]
-    return added(halves[0], plane.across(halves[1]))
-
-
-def share_totals(plane, late, halves):
-    both = jnp.stack([pair_sums(plane, halves), late], axis=1)
-    share = added(both[0], *[plane.along(both[g], g) for g in range(1, plane.groups)])
+def added(values, split=False, after=None):
+    shape = values[0].shape
+    count = shape[0] if split else 1
+
+    def kernel(*refs):
+        outs = refs[-count:]
+        for i, out in enumerate(outs):
+            parts = [ref[i] if split else ref[...] for ref in refs[: len(values)]]
+            total = parts[0].astype(F32)
+            for part in parts[1:]:
+                total = total + part.astype(F32)
+            out[...] = total.astype(BF16)
+
+    args = list(values) if after is None else [*values, after]
+    outs = call(
+        kernel,
+        "added",
+        [VMEM] * len(args),
+        [VMEM] * count,
+        [jax.ShapeDtypeStruct(shape[1:] if split else shape, BF16)] * count,
+        [],
+        8,
+        args,
+    )
+    return outs if split else outs[0]
+
+
+def plane_share(plane, pieces, after=None):
+    parts = added(plane.received(pieces, 0), split=True)
+    parts = added(plane.received(parts, 1), split=True)
+    return added(plane.received(parts, 2), after=after)
+
+
+def share_totals(plane, share):
     lines = lax.axis_size("feat")
     if lines & (lines - 1) == 0:
         step = 1
         while step < lines:
-            share = added(share, lax.ppermute(share, "feat", [(i, i ^ step) for i in range(lines)]))
+            other = lax.ppermute(share, "feat", [(i, i ^ step) for i in range(lines)])
+            share = added([share, other])
             step *= 2
     else:
         share = lax.psum(share.astype(F32), "feat").astype(BF16)
-    gathered = jnp.stack([share] + [plane.along(share, g) for g in range(1, plane.groups)])
-    if plane.pair == 1:
-        return gathered[None]
-    return jnp.stack([gathered, plane.across(gathered)])
+    for dim in (2, 1):
+        size = plane.sizes[dim]
+        share = jnp.stack([share] + [plane.passed(share, dim, i) for i in range(1, size)])
+    return [share] + [plane.passed(share, 0, i) for i in range(1, plane.sizes[0])]
 
 
 def second_out(z, bound, live, f1, act, w_out, out):
@@ -576,7 +593,8 @@
         m, dpre, dagg = [
             (refs.pop(0), refs.pop(0)) if isinstance(a, tuple) else refs.pop(0) for a in arrays
         ]
-        at, wt, part_out, rest_out, acc = refs
+        at, wt, part_out, rest_out, token, acc = refs
+        token[...] = jnp.zeros_like(token)
 
         def direct(part, first):
             mine = z.flat(group_of(z, m, part, first)[...]).astype(F32)
@@ -600,8 +618,8 @@
         kernel,
         "input_grad%d" % layer,
         [SMEM] * 2 + [VMEM] * (len(flat_args) + 2),
-        [VMEM, VMEM],
-        [z.nodes(z.lent, F32), z.nodes(z.rest)],
+        [VMEM] * 3,
+        [z.nodes(z.lent, F32), z.nodes(z.rest), TOKEN],
         [z.held(z.tiles + 1, F32)],
         28,
         [meta, counts, *flat_args, at, wt],
@@ -694,11 +712,14 @@
     )
 
 
-def finish(z, plane, bound, part, rest, fw, fe, totals, grads):
+def finish(z, plane, bound, part, rest, fw, fe, early, late, grads):
     c = z.cols
-    piece = totals.shape[3]
-
-    def kernel(me, bound, part, rest, fw, fe, totals, _g, grads, g_self, g_nbr, g_bias, g_out, keep, buf, sems):
+    piece = early[0].shape[2]
+    core, ahead, side = plane.sizes
+
+    def kernel(me, bound, part, rest, fw, fe, *refs):
+        totals = refs[: 2 * core]
+        _g, grads, g_self, g_nbr, g_bias, g_out, keep, buf, sems = refs[2 * core :]
         copies = [pltpu.make_async_copy(rest, grads.at[0, pl.ds(z.lent, z.rest)], sems.at[z.lent])]
         copies[0].start()
         for i in range(z.lent):
@@ -710,12 +731,11 @@
             copy.start()
             copies.append(copy)
         for layer in range(2):
-            for h in range(plane.pair):
-                half = lax.rem(me[0] + h, plane.pair)
-                for g in range(plane.groups):
-                    owner = half * plane.groups + lax.rem(me[1] + plane.groups - g, plane.groups)
-                    start = pl.multiple_of(owner * piece, 16)
-                    buf[pl.ds(start, piece), :] = totals[h, g, layer].astype(F32)
+            for i in range(core):
+                for j in range(ahead):
+                    for k in range(side):
+                        start = pl.multiple_of(plane.piece_of(me, (-i, -j, -k)) * piece, 16)
+                        buf[pl.ds(start, piece), :] = totals[layer * core + i][j, k].astype(F32)
             g_self[layer] = buf[pl.ds(0, c), :]
             g_nbr[layer] = buf[pl.ds(c, c), :]
             g_out[layer] = buf[pl.ds(2 * c, c), :]
@@ -727,7 +747,7 @@
     return call(
         kernel,
         "finish",
-        [SMEM] * 2 + [VMEM] * 5 + [ANY],
+        [SMEM] * 2 + [VMEM] * (4 + 2 * core) + [ANY],
         [ANY] + [VMEM] * 4,
         [jax.ShapeDtypeStruct(grads.shape, BF16), square, square, jax.ShapeDtypeStruct((2, c), F32), square],
         [
@@ -736,8 +756,8 @@
             pltpu.SemaphoreType.DMA((z.lent + 1,)),
         ],
         14,
-        (plane.me, bound, part, rest, fw, fe, totals, grads),
-        {7: 0},
+        (plane.me, bound, part, rest, fw, fe, *early, *late, grads),
+        {6 + 2 * core: 0},
     )
 
 
@@ -773,11 +793,11 @@
     )
     back_west = passed_along(to_east, 1)
     back_east = passed_along(to_west, -1)
-    part, upstream = input_grad(z, 1, meta, counts, m1, dpre1, dagg1, at, wt)
+    part, upstream, _ = input_grad(z, 1, meta, counts, m1, dpre1, dagg1, at, wt)
     grads, m0_rest, dpre_rest, dagg_rest, outer = early_rest(
         z, meta, counts, live_tiles, upstream, slope, at, wt
     )
-    late = pair_sums(plane, weight_grads(z, plane, f1, agg1, act1, m1, dpre1, "weight_grads1"))
+    late = plane_share(plane, weight_grads(z, plane, f1, agg1, act1, m1, dpre1, "weight_grads1"))
     section_out, ready = second_out(z, bound_tiles, live_tiles, f1, act1, w_out, section_out)
 
     m0_lent, dpre_lent, dagg_lent, grads, to_west, to_east = early_lent(
@@ -790,16 +810,20 @@
     halves = weight_grads(z, plane, f0, agg0, act0, m0, dpre0, "weight_grads0")
 
     def last(late, halves, m0, dpre0, dagg0, meta, counts, at, wt):
-        sums = share_totals(plane, late, halves)
-        return (sums, *input_grad(z, 0, meta, counts, m0, dpre0, dagg0, at, wt))
+        part, rest, done = input_grad(z, 0, meta, counts, m0, dpre0, dagg0, at, wt)
+        early = plane_share(plane, halves, done)
+        return share_totals(plane, early), share_totals(plane, late), part, rest
 
     args = (late, halves, m0, dpre0, dagg0, meta, counts, at, wt)
     shapes = jax.eval_shape(last, *args)
-    totals, part, rest = lax.cond(
-        live_tiles[0] > 0, last, lambda *_: tuple(jnp.zeros(a.shape, a.dtype) for a in shapes), *args
+    early, late, part, rest = lax.cond(
+        live_tiles[0] > 0,
+        last,
+        lambda *_: jax.tree.map(lambda a: jnp.zeros(a.shape, a.dtype), shapes),
+        *args,
     )
     grads, grad_self, grad_nbr, grad_bias, grad_out = finish(
-        z, plane, bound_tiles, part, rest, back_west, back_east, totals, grads
+        z, plane, bound_tiles, part, rest, back_west, back_east, early, late, grads
     )
     return (
         section_out.reshape(2, t * r, c),

time: 163 us -> 174 us (1.067)
  local copies, waits for them, and re-layouts: 13.9 us -> 22.8 us
    unnamed x53 -> x81, local copies, waits for them, and re-layouts: 13.9 us -> 22.8 us
    ppermute x8, waiting for transfers between devices: 5.6 us -> 8.47 us  [passed_along(): lax.ppermute(value, AXES, [(i, (i + steps) % count) for i in range(count)])]
    ppermute x11 -> x16, waiting for transfers between devices: 23.7 us -> 22.4 us  [the longest x12 17.3 us: passed(): return lax.ppermute(value, PLANE, pairs)]
    pallas_call x16 -> x26, Pallas kernels: 79.1 us -> 77.8 us  [call(): pl.pallas_call(kernel, in_specs=in_specs, out_specs=out_specs, out_shape=...]
    ppermute x11 -> x16, starting transfers between devices: 15.5 us -> 15.2 us  [the longest x12 10.7 us: passed(): return lax.ppermute(value, PLANE, pairs)]
  transfers between devices with their start and end apart: 19 -> 24, of which waited for: 9 -> 14; matrix products, arithmetic and copies ran while one was open for 0% -> 1% of each run, Pallas kernels for 33% -> 30%
where the time goes in v5:
time: 174 us; the launch traced here: 173 us
  Pallas kernels  77.8 us (45%)
  starting transfers between devices  37.8 us (22%)
  waiting for transfers between devices  30.9 us (18%)
  local copies, waits for them, and re-layouts  22.8 us (13%)
  between operations  1.86 us (1%)
    pallas_call x26, Pallas kernels, call(): pl.pallas_call(kernel, in_specs=in_specs, out_specs=out_specs, out_shape=...  77.8 us
    unnamed x81, local copies, waits for them, and re-layouts  22.8 us
    ppermute x8, starting transfers between devices, passed_along(): lax.ppermute(value, AXES, [(i, (i + steps) % count) for i in range(count)])  22.6 us
    ppermute x12, waiting for transfers between devices, passed(): return lax.ppermute(value, PLANE, pairs)  17.3 us
    ppermute x12, starting transfers between devices, passed(): return lax.ppermute(value, PLANE, pairs)  10.7 us
    ppermute x8, waiting for transfers between devices, passed_along(): lax.ppermute(value, AXES, [(i, (i + steps) % count) for i in range(count)])  8.47 us
    ppermute x4, waiting for transfers between devices, share_totals(): other = lax.ppermute(share, 'feat', [(i, i ^ step) for i in range(lines)])  5.14 us
    ppermute x4, starting transfers between devices, share_totals(): other = lax.ppermute(share, 'feat', [(i, i ^ step) for i in range(lines)])  4.45 us
  transfers between devices with their start and end apart: 24, of which 14 were waited for; matrix products, arithmetic and copies ran while one was open for 1% of the time, Pallas kernels for 30%

profile of v5, /device:TPU:0, one launch (start us, length us, event | category | flops | bytes accessed | tf_op | source)
XLA Modules:
  0.0 172.9 jit_solution(4395414406656305155)
XLA Ops:
  0.7 3.2 %lend.1 = (bf16[8,128,256]{2,1,0:T(8,128)(2,1)}, bf16[8,128,256]{2,1,0:T(8,128)(2,1)}) custom-call(s32[1,2,8]{2,1,0:T(2,128)} %bound.11, bf16[32,128,256]{2,1,0:T(8,128)(2,1)} %bitcast.18), custom_call_target="tpu_custom_call" | custom-call | flops 1000 | bytes 1000 | tf_op jit(solution)/shard_map/lend/pallas_call | solution.py:75
  3.8 3.1 %collective-permute-start.13 = (bf16[8,128,256]{2,1,0:T(8,128)(2,1)}, bf16[8,128,256]{2,1,0:T(8,128)(2,1)}, u32[]{:S(2)}, u32[]{:S(2)}) collective-permute-start(bf16[8,128,256]{2,1,0:T(8,128)(2,1)} %get-tuple-element.116), channel_id=1, source_target_pairs={{0,1},{1,2},{2,3},{3,4},{4,5},{5,6},{6,7},{7,8},{8,9},{9,10},{10,1... | collective-permute-start | bytes 1572872 | tf_op jit(solution)/shard_map/ppermute | solution.py:63
  6.9 3.4 %collective-permute-start.14 = (bf16[8,128,256]{2,1,0:T(8,128)(2,1)}, bf16[8,128,256]{2,1,0:T(8,128)(2,1)}, u32[]{:S(2)}, u32[]{:S(2)}) collective-permute-start(bf16[8,128,256]{2,1,0:T(8,128)(2,1)} %get-tuple-element.117), channel_id=1, source_target_pairs={{0,31},{1,0},{2,1},{3,2},{4,3},{5,4},{6,5},{7,6},{8,7},{9,8},{10,9... | collective-permute-start | bytes 1572872 | tf_op jit(solution)/shard_map/ppermute | solution.py:63
  16.5 10.7 %arrange.1 = (bf16[16,128,256]{2,1,0:T(8,128)(2,1)S(1)}, bf16[16,128,256]{2,1,0:T(8,128)(2,1)S(1)}, bf16[16,128,256]{2,1,0:T(8,128)(2,1)S(1)}, bf16[16,128,256]{...) custom-call(s32[1,2,8]{2,1,0:T(2,128)S(1)} %copy-done.33, ...), custom_call_target="tpu_custom_call" | custom-call | flops 1000 | bytes 1000 | tf_op jit(solution)/shard_map/arrange/pallas_call | solution.py:75
  27.1 4.7 %collective-permute-done.14.fe = bf16[8,128,256]{2,1,0:T(8,128)(2,1)} collective-permute-done((bf16[8,128,256]{2,1,0:T(8,128)(2,1)}, bf16[8,128,256]{2,1,0:T(8,128)(2,1)}, u32[]{:S(2)}, u32[]{:S(2)}) %collective-permute-start.14) | collective-permute-done | bytes 524320 | tf_op jit(solution)/shard_map/ppermute | solution.py:63
  31.9 4.0 %first_lent.1 = (bf16[8,128,256]{2,1,0:T(8,128)(2,1)S(1)}, bf16[8,128,256]{2,1,0:T(8,128)(2,1)S(1)}, bf16[16,128,256]{2,1,0:T(8,128)(2,1)S(1)}) custom-call(s32[384]{0:T(512)S(1)} %get-tuple-element.113.meta, bf16[16,128,256]{2,1,0:T(8,128)(2,1)S(1)} %get-tuple-element.114.f_lent.refs_0_, bf16[16,128,256]{2,1,0:T(8,128)(2,1)S(1)} %get-tuple-element.115.f_rest.refs_1_, ...), custom_call_target="tpu_custom_call" | custom-call | flops 1000 | bytes 1000 | tf_op jit(solution)/shard_map/first_lent/pallas_call | solution.py:75
  37.5 3.8 %collective-permute-start.16 = (bf16[8,128,256]{2,1,0:T(8,128)(2,1)S(1)}, bf16[8,128,256]{2,1,0:T(8,128)(2,1)S(1)}, u32[]{:S(2)}, u32[]{:S(2)}) collective-permute-start(bf16[8,128,256]{2,1,0:T(8,128)(2,1)S(1)} %get-tuple-element.119.west), channel_id=1, source_target_pairs={{0,31},{1,0},{2,1},{3,2},{4,3},{5,4},{6,5},{7,6},{8,7},{9,8},{10,9... | collective-permute-start | bytes 1572872 | tf_op jit(solution)/shard_map/ppermute | solution.py:63
  41.3 3.1 %turn.1 = (bf16[128,128,128]{2,1,0:T(8,128)(2,1)S(1)}, bf16[2,3,256,256]{3,2,1,0:T(8,128)(2,1)S(1)}) custom-call(bf16[32,4,128,128]{3,2,1,0:T(8,128)(2,1)S(1)} %get-tuple-element.118.ap, bf16[2,256,256]{2,1,0:T(8,128)(2,1)S(1)} %copy-done.18, bf16[2,256,256]{2,1,0:T(8,128)(2,1)S(1)} %copy-done.19, bf16[2,256,256]{2,1,0:T(8,128)(2,1)S(1)} %copy-done.20), custom_call_target="tpu_custom_call" | custom-call | flops 1000 | bytes 1000 | tf_op jit(solution)/shard_map/turn/pallas_call | solution.py:75
  46.2 5.4 %first_rest.1 = (bf16[16,128,256]{2,1,0:T(8,128)(2,1)S(1)}, bf16[16,128,256]{2,1,0:T(8,128)(2,1)S(1)}, bf16[2,32,128,256]{3,2,1,0:T(8,128)(2,1)}, bf16[16,128,256]{2,1,0:T(8,128)(2,1)S(1)}) custom-call(s32[384]{0:T(512)S(1)} %get-tuple-element.113.meta, s32[1,2,8]{2,1,0:T(2,128)S(1)} %copy-done.33, s32[1]{0:T(128)S(6)} %copy.35.live, ...), custom_call_target="tpu_custom_call" | custom-call | flops 1000 | bytes 1000 | tf_op jit(solution)/shard_map/first_rest/pallas_call | solution.py:75
  58.1 3.8 %collective-permute-done.16.fe = bf16[8,128,256]{2,1,0:T(8,128)(2,1)S(1)} collective-permute-done((bf16[8,128,256]{2,1,0:T(8,128)(2,1)S(1)}, bf16[8,128,256]{2,1,0:T(8,128)(2,1)S(1)}, u32[]{:S(2)}, u32[]{:S(2)}) %collective-permute-start.16) | collective-permute-done | bytes 524320 | tf_op jit(solution)/shard_map/ppermute | solution.py:63
  61.8 9.4 %second.1 = (bf16[32,128,256]{2,1,0:T(8,128)(2,1)S(1)}, bf16[32,128,256]{2,1,0:T(8,128)(2,1)S(1)}, bf16[32,128,256]{2,1,0:T(8,128)(2,1)S(1)}, bf16[32,128,256]{2...) custom-call(s32[384]{0:T(512)S(1)} %get-tuple-element.113.meta, ...), custom_call_target="tpu_custom_call" | custom-call | flops 1000 | bytes 1000 | tf_op jit(solution)/shard_map/second/pallas_call | solution.py:75
  76.9 5.1 %collective-permute-start.18 = (bf16[8,128,256]{2,1,0:T(8,128)(2,1)}, bf16[8,128,256]{2,1,0:T(8,128)(2,1)}, u32[]{:S(2)}, u32[]{:S(2)}) collective-permute-start(bf16[8,128,256]{2,1,0:T(8,128)(2,1)} %get-tuple-element.139), channel_id=1, source_target_pairs={{0,31},{1,0},{2,1},{3,2},{4,3},{5,4},{6,5},{7,6},{8,7},{9,8},{10,9... | collective-permute-start | bytes 1572872 | tf_op jit(solution)/shard_map/ppermute | solution.py:63
  90.6 4.0 %weight_grads1.1 = (bf16[2,2,112,256]{3,2,1,0:T(8,128)(2,1)S(1)}, bf16[2,2,112,256]{3,2,1,0:T(8,128)(2,1)S(1)}) custom-call(s32[3]{0:T(128)S(1)} %pad_add_fusion.me, bf16[16,128,256]{2,1,0:T(8,128)(2,1)S(1)} %copy-done.6, bf16[16,128,256]{2,1,0:T(8,128)(2,1)S(1)} %copy-done.9, bf16[32,128,256]{2,1,0:T(8,128)(2,1)S(1)} %copy-done.32, ...), custom_call_target="tpu_custom_call" | custom-call | flops 1000 | bytes 1000 | tf_op jit(solution)/shard_map/weight_grads1/pallas_call | solution.py:75
  97.4 4.0 %collective-permute-done.20.refs_1_ = bf16[2,112,256]{2,1,0:T(8,128)(2,1)S(1)} collective-permute-done((bf16[2,112,256]{2,1,0:T(8,128)(2,1)S(1)}, bf16[2,112,256]{2,1,0:T(8,128)(2,1)S(1)}, u32[]{:S(2)}, u32[]{:S(2)}) %collective-permute-start.20) | collective-permute-done | bytes 114720 | tf_op jit(solution)/shard_map/ppermute | solution.py:450
  102.5 6.9 %input_grad1.1 = (f32[16,128,256]{2,1,0:T(8,128)S(1)}, bf16[16,128,256]{2,1,0:T(8,128)(2,1)S(1)}, f32[8,128]{1,0:T(8,128)}) custom-call(s32[384]{0:T(512)S(1)} %get-tuple-element.113.meta, s32[8]{0:T(128)S(1)} %get-tuple-element.123.counts, bf16[16,128,256]{2,1,0:T(8,128)(2,1)S(1)} %get-tuple-element.125.m_lent.refs_0_.refs_4_, ...), custom_call_target="tpu_custom_call" | custom-call | flops 1000 | bytes 1000 | tf_op jit(solution)/shard_map/input_grad1/pallas_call | solution.py:75
  109.4 3.5 %second_out.1 = (bf16[2,32,128,256]{3,2,1,0:T(8,128)(2,1)}, f32[8,128]{1,0:T(8,128)S(1)}) custom-call(s32[1,2,8]{2,1,0:T(2,128)S(1)} %copy-done.33, s32[1]{0:T(128)S(6)} %copy.35.live, bf16[16,128,256]{2,1,0:T(8,128)(2,1)S(1)} %copy-done.7, bf16[16,128,256]{2,1,0:T(8,128)(2,1)S(1)} %copy-done.10, ...), custom_call_target="tpu_custom_call", output_to_operand_aliasing={{0}: (6, {})} | custom-call | flops 1000 | bytes 1000 | tf_op jit(solution)/shard_map/second_out/pallas_call | solution.py:75
  116.0 5.1 %early_lent.1 = (bf16[16,128,256]{2,1,0:T(8,128)(2,1)S(1)}, bf16[16,128,256]{2,1,0:T(8,128)(2,1)S(1)}, bf16[16,128,256]{2,1,0:T(8,128)(2,1)S(1)}, bf16[2,32,128,...) custom-call(s32[384]{0:T(512)S(1)} %get-tuple-element.113.meta, ...), custom_call_target="tpu_custom_call", output_to_operand_aliasing={{3}: (10, {})} | custom-call | flops 1000 | bytes 1000 | tf_op jit(solution)/shard_map/early_lent/pallas_call | solution.py:75
  121.2 5.3 %collective-permute-start.23 = (bf16[8,128,256]{2,1,0:T(8,128)(2,1)}, bf16[8,128,256]{2,1,0:T(8,128)(2,1)S(1)}, u32[]{:S(2)}, u32[]{:S(2)}) collective-permute-start(bf16[8,128,256]{2,1,0:T(8,128)(2,1)} %get-tuple-element.163), channel_id=1, source_target_pairs={{0,31},{1,0},{2,1},{3,2},{4,3},{5,4},{6,5},{7,6},{8,7},{9,8},{10,9... | collective-permute-start | bytes 1572872 | tf_op jit(solution)/shard_map/ppermute | solution.py:63
  126.6 4.1 %weight_grads0.1 = (bf16[2,2,112,256]{3,2,1,0:T(8,128)(2,1)S(1)}, bf16[2,2,112,256]{3,2,1,0:T(8,128)(2,1)S(1)}) custom-call(s32[3]{0:T(128)S(1)} %pad_add_fusion.me, bf16[16,128,256]{2,1,0:T(8,128)(2,1)S(1)} %get-tuple-element.114.f_lent.refs_0_, bf16[16,128,256]{2,1,0:T(8,128)(2,1)S(1)} %get-tuple-element.115.f_rest.refs_1_, ...), custom_call_target="tpu_custom_call" | custom-call | flops 1000 | bytes 1000 | tf_op jit(solution)/shard_map/weight_grads0/pallas_call | solution.py:75
  130.7 38.1 %conditional.1 = (bf16[2,2,112,256]{3,2,1,0:T(8,128)(2,1)}, bf16[2,2,112,256]{3,2,1,0:T(8,128)(2,1)}, bf16[2,2,112,256]{3,2,1,0:T(8,128)(2,1)}, bf16[2,2,112,256...) conditional(s32[]{:T(128)} %bitcast.14, () %tuple.16, ...), branch_computations={%region_0.1_spmd, %region_1.2_spmd} | conditional | flops 352064 | bytes 7348600 | solution.py:819
  134.2 3.4 %collective-permute-done.1.refs_1_ = bf16[2,112,256]{2,1,0:T(8,128)(2,1)S(1)} collective-permute-done((bf16[2,112,256]{2,1,0:T(8,128)(2,1)S(1)}, bf16[2,112,256]{2,1,0:T(8,128)(2,1)S(1)}, u32[]{:S(2)}, u32[]{:S(2)}) %collective-permute-start.1) | collective-permute-done | bytes 114720 | tf_op jit(solution)/shard_map/cond/branch_1_fun/ppermute | solution.py:450
  140.3 6.6 %input_grad0.1 = (f32[16,128,256]{2,1,0:T(8,128)S(1)}, bf16[16,128,256]{2,1,0:T(8,128)(2,1)S(1)}, f32[8,128]{1,0:T(8,128)S(1)}) custom-call(s32[384]{0:T(512)S(1)} %get-tuple-element.32.meta, s32[8]{0:T(128)S(1)} %get-tuple-element.33.counts, bf16[16,128,256]{2,1,0:T(8,128)(2,1)S(1)} %get-tuple-element.34.refs_0_, ...), custom_call_target="tpu_custom_call" | custom-call | flops 1000 | bytes 1000 | tf_op jit(solution)/shard_map/cond/branch_1_fun/input_grad0/pallas_call | solution.py:75
  152.7 3.0 %collective-permute-done.9.refs_1_ = bf16[112,256]{1,0:T(8,128)(2,1)S(1)} collective-permute-done((bf16[112,256]{1,0:T(8,128)(2,1)S(1)}, bf16[112,256]{1,0:T(8,128)(2,1)S(1)}, u32[]{:S(2)}, u32[]{:S(2)}) %collective-permute-start.9) | collective-permute-done | bytes 57376 | tf_op jit(solution)/shard_map/cond/branch_1_fun/ppermute | solution.py:538
  168.8 3.9 %finish.1 = (bf16[2,32,128,256]{3,2,1,0:T(8,128)(2,1)}, f32[2,256,256]{2,1,0:T(8,128)}, f32[2,256,256]{2,1,0:T(8,128)}, f32[2,256]{1,0:T(2,128)}, f32[2,256,256]{2,1,0:T(8,128)}) custom-call(s32[3]{0:T(128)S(1)} %pad_add_fusion.me, s32[1,2,8]{2,1,0:T(2,128)S(1)} %copy-done.33, ...), custom_call_target="tpu_custom_call", output_to_operand_aliasing={{0}: (10, {})} | custom-call | flops 1000 | bytes 1000 | tf_op jit(solution)/shard_map/finish/pallas_call | solution.py:75
  (137 shorter events, 61.5 us)
Async XLA Ops:
  3.8 23.3 %collective-permute-start.13 = (bf16[8,128,256]{2,1,0:T(8,128)(2,1)}, bf16[8,128,256]{2,1,0:T(8,128)(2,1)}, u32[]{:S(2)}, u32[]{:S(2)}) collective-permute-start(bf16[8,128,256]{2,1,0:T(8,128)(2,1)} %get-tuple-element.116), channel_id=1, source_target_pairs={{0,1},{1,2},{2,3},{3,4},{4,5},{5,6},{6,7},{7,8},{8,9},{9,10},{10,1... | collective-permute-start | bytes 1572872 | tf_op jit(solution)/shard_map/ppermute | solution.py:63
  6.9 24.9 %collective-permute-start.14 = (bf16[8,128,256]{2,1,0:T(8,128)(2,1)}, bf16[8,128,256]{2,1,0:T(8,128)(2,1)}, u32[]{:S(2)}, u32[]{:S(2)}) collective-permute-start(bf16[8,128,256]{2,1,0:T(8,128)(2,1)} %get-tuple-element.117), channel_id=1, source_target_pairs={{0,31},{1,0},{2,1},{3,2},{4,3},{5,4},{6,5},{7,6},{8,7},{9,8},{10,9... | collective-permute-start | bytes 1572872 | tf_op jit(solution)/shard_map/ppermute | solution.py:63
  35.9 22.2 %collective-permute-start.15 = (bf16[8,128,256]{2,1,0:T(8,128)(2,1)S(1)}, bf16[8,128,256]{2,1,0:T(8,128)(2,1)S(1)}, u32[]{:S(2)}, u32[]{:S(2)}) collective-permute-start(bf16[8,128,256]{2,1,0:T(8,128)(2,1)S(1)} %get-tuple-element.120.east), channel_id=1, source_target_pairs={{0,1},{1,2},{2,3},{3,4},{4,5},{5,6},{6,7},{7,8},{8,9},{9,10},{10,1... | collective-permute-start | bytes 1572872 | tf_op jit(solution)/shard_map/ppermute | solution.py:63
  37.5 24.3 %collective-permute-start.16 = (bf16[8,128,256]{2,1,0:T(8,128)(2,1)S(1)}, bf16[8,128,256]{2,1,0:T(8,128)(2,1)S(1)}, u32[]{:S(2)}, u32[]{:S(2)}) collective-permute-start(bf16[8,128,256]{2,1,0:T(8,128)(2,1)S(1)} %get-tuple-element.119.west), channel_id=1, source_target_pairs={{0,31},{1,0},{2,1},{3,2},{4,3},{5,4},{6,5},{7,6},{8,7},{9,8},{10,9... | collective-permute-start | bytes 1572872 | tf_op jit(solution)/shard_map/ppermute | solution.py:63
  76.7 39.3 %collective-permute-start.17 = (bf16[8,128,256]{2,1,0:T(8,128)(2,1)}, bf16[8,128,256]{2,1,0:T(8,128)(2,1)}, u32[]{:S(2)}, u32[]{:S(2)}) collective-permute-start(bf16[8,128,256]{2,1,0:T(8,128)(2,1)} %get-tuple-element.138), channel_id=1, source_target_pairs={{0,1},{1,2},{2,3},{3,4},{4,5},{5,6},{6,7},{7,8},{8,9},{9,10},{10,1... | collective-permute-start | bytes 1572872 | tf_op jit(solution)/shard_map/ppermute | solution.py:63
  76.9 39.1 %collective-permute-start.18 = (bf16[8,128,256]{2,1,0:T(8,128)(2,1)}, bf16[8,128,256]{2,1,0:T(8,128)(2,1)}, u32[]{:S(2)}, u32[]{:S(2)}) collective-permute-start(bf16[8,128,256]{2,1,0:T(8,128)(2,1)} %get-tuple-element.139), channel_id=1, source_target_pairs={{0,31},{1,0},{2,1},{3,2},{4,3},{5,4},{6,5},{7,6},{8,7},{9,8},{10,9... | collective-permute-start | bytes 1572872 | tf_op jit(solution)/shard_map/ppermute | solution.py:63
  94.5 1.6 collective-permute-start.19
  96.2 5.3 %collective-permute-start.20 = (bf16[2,112,256]{2,1,0:T(8,128)(2,1)S(1)}, bf16[2,112,256]{2,1,0:T(8,128)(2,1)S(1)}, u32[]{:S(2)}, u32[]{:S(2)}) collective-permute-start(bf16[2,112,256]{2,1,0:T(8,128)(2,1)S(1)} %get-tuple-element.149), channel_id=1, source_target_pairs={{0,16},{4,20},{16,0},{20,4},{8,24},{12,28},{24,8},{28,12},{1,17},{... | collective-permute-start | bytes 344072 | tf_op jit(solution)/shard_map/ppermute | solution.py:450
  101.4 14.5 %collective-permute-start.21 = (bf16[112,256]{1,0:T(8,128)(2,1)S(1)}, bf16[112,256]{1,0:T(8,128)(2,1)S(1)}, u32[]{:S(2)}, u32[]{:S(2)}) collective-permute-start(bf16[112,256]{1,0:T(8,128)(2,1)S(1)} %get-tuple-element.151), channel_id=1, source_target_pairs={{0,4},{4,0},{16,20},{20,16},{8,12},{12,8},{24,28},{28,24},{1,5},{5... | collective-permute-start | bytes 172040 | tf_op jit(solution)/shard_map/ppermute | solution.py:450
  121.2 47.7 %collective-permute-start.22 = (bf16[8,128,256]{2,1,0:T(8,128)(2,1)}, bf16[8,128,256]{2,1,0:T(8,128)(2,1)S(1)}, u32[]{:S(2)}, u32[]{:S(2)}) collective-permute-start(bf16[8,128,256]{2,1,0:T(8,128)(2,1)} %get-tuple-element.162), channel_id=1, source_target_pairs={{0,1},{1,2},{2,3},{3,4},{4,5},{5,6},{6,7},{7,8},{8,9},{9,10},{10,1... | collective-permute-start | bytes 1572872 | tf_op jit(solution)/shard_map/ppermute | solution.py:63
  121.2 47.6 %collective-permute-start.23 = (bf16[8,128,256]{2,1,0:T(8,128)(2,1)}, bf16[8,128,256]{2,1,0:T(8,128)(2,1)S(1)}, u32[]{:S(2)}, u32[]{:S(2)}) collective-permute-start(bf16[8,128,256]{2,1,0:T(8,128)(2,1)} %get-tuple-element.163), channel_id=1, source_target_pairs={{0,31},{1,0},{2,1},{3,2},{4,3},{5,4},{6,5},{7,6},{8,7},{9,8},{10,9... | collective-permute-start | bytes 1572872 | tf_op jit(solution)/shard_map/ppermute | solution.py:63
  130.7 1.6 collective-permute-start
  132.3 5.3 %collective-permute-start.1 = (bf16[2,112,256]{2,1,0:T(8,128)(2,1)S(1)}, bf16[2,112,256]{2,1,0:T(8,128)(2,1)S(1)}, u32[]{:S(2)}, u32[]{:S(2)}) collective-permute-start(bf16[2,112,256]{2,1,0:T(8,128)(2,1)S(1)} %get-tuple-element.29), channel_id=1, source_target_pairs={{0,16},{4,20},{16,0},{20,4},{8,24},{12,28},{24,8},{28,12},{1,17},{... | collective-permute-start | bytes 344072 | tf_op jit(solution)/shard_map/cond/branch_1_fun/ppermute | solution.py:450
  137.7 9.3 %collective-permute-start.2 = (bf16[112,256]{1,0:T(8,128)(2,1)S(1)}, bf16[112,256]{1,0:T(8,128)(2,1)S(1)}, u32[]{:S(2)}, u32[]{:S(2)}) collective-permute-start(bf16[112,256]{1,0:T(8,128)(2,1)S(1)} %get-tuple-element.31), channel_id=1, source_target_pairs={{0,4},{4,0},{16,20},{20,16},{8,12},{12,8},{24,28},{28,24},{1,5},{5... | collective-permute-start | bytes 172040 | tf_op jit(solution)/shard_map/cond/branch_1_fun/ppermute | solution.py:450
  140.3 9.1 %collective-permute-start.8 = (bf16[112,256]{1,0:T(8,128)(2,1)S(1)}, bf16[112,256]{1,0:T(8,128)(2,1)S(1)}, u32[]{:S(2)}, u32[]{:S(2)}) collective-permute-start(bf16[112,256]{1,0:T(8,128)(2,1)S(1)} %get-tuple-element.43.refs_0_), channel_id=1, source_target_pairs={{0,1},{1,0},{2,3},{3,2},{4,5},{5,4},{6,7},{7,6},{8,9},{9,8},{10,11... | collective-permute-start | bytes 172040 | tf_op jit(solution)/shard_map/cond/branch_1_fun/ppermute | solution.py:538
  147.0 4.6 %collective-permute-start.3 = (bf16[112,256]{1,0:T(8,128)(2,1)S(1)}, bf16[112,256]{1,0:T(8,128)(2,1)S(1)}, u32[]{:S(2)}, u32[]{:S(2)}) collective-permute-start(bf16[112,256]{1,0:T(8,128)(2,1)S(1)} %added.12.refs_0_), channel_id=1, source_target_pairs={{0,1},{1,0},{2,3},{3,2},{4,5},{5,4},{6,7},{7,6},{8,9},{9,8},{10,11... | collective-permute-start | bytes 172040 | tf_op jit(solution)/shard_map/cond/branch_1_fun/ppermute | solution.py:538
  149.4 6.4 %collective-permute-start.9 = (bf16[112,256]{1,0:T(8,128)(2,1)S(1)}, bf16[112,256]{1,0:T(8,128)(2,1)S(1)}, u32[]{:S(2)}, u32[]{:S(2)}) collective-permute-start(bf16[112,256]{1,0:T(8,128)(2,1)S(1)} %added.15.refs_0_), channel_id=1, source_target_pairs={{0,2},{1,3},{2,0},{3,1},{4,6},{5,7},{6,4},{7,5},{8,10},{9,11},{10,... | collective-permute-start | bytes 172040 | tf_op jit(solution)/shard_map/cond/branch_1_fun/ppermute | solution.py:538
  151.6 5.1 %collective-permute-start.4 = (bf16[112,256]{1,0:T(8,128)(2,1)S(1)}, bf16[112,256]{1,0:T(8,128)(2,1)S(1)}, u32[]{:S(2)}, u32[]{:S(2)}) collective-permute-start(bf16[112,256]{1,0:T(8,128)(2,1)S(1)} %added.13.refs_0_), channel_id=1, source_target_pairs={{0,2},{1,3},{2,0},{3,1},{4,6},{5,7},{6,4},{7,5},{8,10},{9,11},{10,... | collective-permute-start | bytes 172040 | tf_op jit(solution)/shard_map/cond/branch_1_fun/ppermute | solution.py:538
  155.8 4.2 %collective-permute-start.10 = (bf16[112,256]{1,0:T(8,128)(2,1)S(1)}, bf16[112,256]{1,0:T(8,128)(2,1)S(1)}, u32[]{:S(2)}, u32[]{:S(2)}) collective-permute-start(bf16[112,256]{1,0:T(8,128)(2,1)S(1)} %added.16), channel_id=1, source_target_pairs={{0,4},{4,0},{16,20},{20,16},{8,12},{12,8},{24,28},{28,24},{1,5},{5... | collective-permute-start | bytes 172040 | tf_op jit(solution)/shard_map/cond/branch_1_fun/ppermute | solution.py:450
  156.7 4.6 %collective-permute-start.5 = (bf16[112,256]{1,0:T(8,128)(2,1)S(1)}, bf16[112,256]{1,0:T(8,128)(2,1)S(1)}, u32[]{:S(2)}, u32[]{:S(2)}) collective-permute-start(bf16[112,256]{1,0:T(8,128)(2,1)S(1)} %added.14), channel_id=1, source_target_pairs={{0,4},{4,0},{16,20},{20,16},{8,12},{12,8},{24,28},{28,24},{1,5},{5... | collective-permute-start | bytes 172040 | tf_op jit(solution)/shard_map/cond/branch_1_fun/ppermute | solution.py:450
  160.1 4.9 %collective-permute-start.11 = (bf16[2,112,256]{2,1,0:T(8,128)(2,1)S(1)}, bf16[2,112,256]{2,1,0:T(8,128)(2,1)S(1)}, u32[]{:S(2)}, u32[]{:S(2)}) collective-permute-start(bf16[2,112,256]{2,1,0:T(8,128)(2,1)S(1)} %get-tuple-element.175), channel_id=1, source_target_pairs={{0,16},{4,20},{16,0},{20,4},{8,24},{12,28},{24,8},{28,12},{1,17},{... | collective-permute-start | bytes 344072 | tf_op jit(solution)/shard_map/cond/branch_1_fun/ppermute | solution.py:450
  161.4 4.9 %collective-permute-start.6 = (bf16[2,112,256]{2,1,0:T(8,128)(2,1)S(1)}, bf16[2,112,256]{2,1,0:T(8,128)(2,1)S(1)}, u32[]{:S(2)}, u32[]{:S(2)}) collective-permute-start(bf16[2,112,256]{2,1,0:T(8,128)(2,1)S(1)} %get-tuple-element.177), channel_id=1, source_target_pairs={{0,16},{4,20},{16,0},{20,4},{8,24},{12,28},{24,8},{28,12},{1,17},{... | collective-permute-start | bytes 344072 | tf_op jit(solution)/shard_map/cond/branch_1_fun/ppermute | solution.py:450
  165.6 1.8 %collective-permute-start.12 = (bf16[2,2,112,256]{3,2,1,0:T(8,128)(2,1)}, bf16[2,2,112,256]{3,2,1,0:T(8,128)(2,1)}, u32[]{:S(2)}, u32[]{:S(2)}) collective-permute-start(bf16[2,2,112,256]{3,2,1,0:T(8,128)(2,1)} %pad_maximum_fusion.1), channel_id=1, source_target_pairs={{0,8},{4,12},{16,24},{20,28},{8,0},{12,4},{24,16},{28,20},{1,9},{5... | collective-permute-start | bytes 688136 | tf_op jit(solution)/shard_map/cond/branch_1_fun/ppermute | solution.py:450
  167.0 1.8 %collective-permute-start.7 = (bf16[2,2,112,256]{3,2,1,0:T(8,128)(2,1)}, bf16[2,2,112,256]{3,2,1,0:T(8,128)(2,1)}, u32[]{:S(2)}, u32[]{:S(2)}) collective-permute-start(bf16[2,2,112,256]{3,2,1,0:T(8,128)(2,1)} %pad_maximum_fusion), channel_id=1, source_target_pairs={{0,8},{4,12},{16,24},{20,28},{8,0},{12,4},{24,16},{28,20},{1,9},{5... | collective-permute-start | bytes 688136 | tf_op jit(solution)/shard_map/cond/branch_1_fun/ppermute | solution.py:450
  (40 other events, 312.0 us)

commit v6 on v5

--- a/solution.py
+++ b/solution.py
@@ -9,7 +9,6 @@
 PLANE = ("dom", "phase")
 BF16 = jnp.bfloat16
 F32 = jnp.float32
-UNROLL = 8
 ANY = pl.BlockSpec(memory_space=pl.ANY)
 SMEM = pl.BlockSpec(memory_space=pltpu.SMEM)
 VMEM = pl.BlockSpec(memory_space=pltpu.VMEM)
@@ -28,6 +27,7 @@
         self.pairs = self.tiles * self.slots
         self.group = next(g for g in (4, 2, 1) if self.edge % g == 0 and self.rest % g == 0)
         self.parts = ((0, 0, self.lent), (1, self.lent, self.rest))
+        self.index = Index(self)
 
     def nodes(self, count, dtype=BF16):
         return jax.ShapeDtypeStruct((count, self.rows, self.cols), dtype)
@@ -114,11 +114,26 @@
     )
 
 
-def arrange(z, bound, nbrs, live, features, cot, adjacency):
+class Index:
+    QUAD = 4
+
+    def __init__(self, z):
+        self.first = (0, z.tiles, z.tiles + z.lent, z.tiles + 2 * z.lent, z.tiles + 3 * z.lent)
+        self.targets = z.tiles + 3 * z.lent + 1
+        self.more = tuple(self.QUAD * self.targets + i * z.pairs for i in range(5))
+        self.size = self.QUAD * self.targets + 5 * z.pairs
+        self.size = -(-self.size // 8) * 8
+
+
+def arrange(z, bound, nbrs, live, place, features, cot, adjacency):
     s4 = z.slots
-
-    def kernel(bound, nbrs, live, feats, cot, adj, f_lent, f_rest, m_lent, m_rest, ap, meta, counts, inverse, sems):
+    x = z.index
+
+    def kernel(bound, nbrs, live, place, feats, cot, adj, f_lent, f_rest, m_lent, m_rest, adj_out,
+               tiles, reads, blocks, sources, targets, counts, me, inverse, used, sems):
         copies = []
+        for i in range(8):
+            me[i] = place[i]
 
         def start(source, target):
             copy = pltpu.make_async_copy(source, target, sems.at[len(copies)])
@@ -126,49 +141,55 @@
             copies.append(copy)
 
         tail = pl.ds(z.lent, z.rest)
-        start(adj.at[tail], ap.at[tail])
         start(feats.at[tail], f_rest)
         start(cot.at[tail], m_rest)
+        start(adj, adj_out)
         for i in range(z.lent):
             tile = bound[0, i // z.edge, i % z.edge]
             inverse[tile] = i
-            start(adj.at[tile], ap.at[i])
             start(feats.at[tile], f_lent.at[i])
             start(cot.at[tile], m_lent.at[i])
 
-        def kind_of(position, target):
-            return jnp.where(target < z.tiles, 0, jnp.where(position < z.lent, 2, 1))
-
-        def step(kind, sums):
-            return tuple(total + jnp.where(kind == i, 1, 0) for i, total in enumerate(sums))
-
-        def count(position, sums):
+        @pl.loop(0, x.targets)
+        def _(i):
+            used[i] = 0
+            for k in range(x.QUAD):
+                blocks[i * x.QUAD + k] = -1
+                sources[i * x.QUAD + k] = 0
+
+        for i in range(8):
+            counts[i] = 0
+
+        def put(table, target, block, position):
+            place = used[target]
+            used[target] = place + 1
+            fits = place < x.QUAD
+            listed = counts[table]
+            counts[table] = listed + jnp.where(fits, 0, 1)
+            at = jnp.where(fits, target * x.QUAD + place, x.more[0] + table * z.pairs + listed)
+            blocks[at] = block
+            sources[at] = position
+            return at
+
+        @pl.loop(0, z.tiles)
+        def _(position):
             clipped = jnp.minimum(position, z.lent - 1)
             tile = jnp.where(position < z.lent, bound[0, clipped // z.edge, clipped % z.edge], position)
+            tiles[position] = tile
             for k in range(s4):
                 target = nbrs[tile, k]
                 moved = jnp.where(target < z.lent, inverse[jnp.minimum(target, z.lent - 1)], target)
-                meta[position * s4 + k] = moved
-                sums = step(kind_of(position, moved), sums)
-            return sums
-
-        zero = jnp.int32(0)
-        own, outer, lent = lax.fori_loop(0, z.tiles, count, (zero, zero, zero))
-        counts[0] = own
-        counts[1] = outer
-        counts[2] = lent
-
-        def put(position, sums):
-            for k in range(s4):
-                target = meta[position * s4 + k]
-                kind = kind_of(position, target)
-                slot = jnp.where(kind == 0, sums[0], jnp.where(kind == 1, sums[1], sums[2]))
-                meta[z.pairs + slot] = position * s4 + k
-                meta[2 * z.pairs + slot] = target
-                sums = step(kind, sums)
-            return sums
-
-        lax.fori_loop(0, z.tiles, put, (zero, own, own + outer))
+                reads[position * s4 + k] = moved
+                block = tile * s4 + k
+                own = moved < z.tiles
+                at = put(jnp.where(own, 0, 1), moved, block, position)
+                targets[at] = jnp.where(own, moved, moved - z.tiles)
+                lent = position < z.lent
+                table = jnp.where(own, 4, jnp.where(lent, 2, 3))
+                shift = jnp.where(lent, z.lent, 2 * z.lent)
+                at = put(table, jnp.where(own, x.first[4], moved + shift), block, position)
+                targets[at] = moved - z.tiles
+
         for copy in copies:
             copy.wait()
 
@@ -181,47 +202,37 @@
     return call(
         kernel,
         "arrange",
-        [SMEM, SMEM, SMEM, ANY, ANY, ANY],
-        [VMEM] * 5 + [SMEM, SMEM],
+        [SMEM] * 4 + [ANY] * 3,
+        [VMEM] * 5 + [SMEM] * 7,
+        [z.nodes(z.lent), z.nodes(z.rest), z.nodes(z.lent), z.nodes(z.rest)]
+        + [jax.ShapeDtypeStruct(adjacency.shape, BF16)]
+        + [jax.ShapeDtypeStruct((n,), jnp.int32) for n in (z.tiles, z.pairs, x.size, x.size, x.size, 8, 8)],
         [
-            z.nodes(z.lent),
-            z.nodes(z.rest),
-            z.nodes(z.lent),
-            z.nodes(z.rest),
-            jax.ShapeDtypeStruct(adjacency.shape, BF16),
-            jax.ShapeDtypeStruct((3 * z.pairs,), jnp.int32),
-            jax.ShapeDtypeStruct((8,), jnp.int32),
+            pltpu.SMEM((z.lent,), jnp.int32),
+            pltpu.SMEM((x.targets,), jnp.int32),
+            pltpu.SemaphoreType.DMA((2 * z.lent + 3,)),
         ],
-        [pltpu.SMEM((z.lent,), jnp.int32), pltpu.SemaphoreType.DMA((3 * z.lent + 3,))],
-        6,
-        (bound, nbrs, live, features, cot, adjacency),
-    )
-
-
-def turn(z, ap, w_self, w_nbr, w_out):
-    def kernel(ap, ws, wn, wo, at, wt):
+        12,
+        (bound, nbrs, live, place, features, cot, adjacency),
+    )
+
+
+def turn(z, w_self, w_nbr, w_out):
+    def kernel(ws, wn, wo, wt):
         for layer in range(2):
             wt[layer, 0] = ws[layer].T
             wt[layer, 1] = wn[layer].T
             wt[layer, 2] = wo[layer].T
 
-        @pl.loop(0, z.tiles)
-        def _(q):
-            for k in range(z.slots):
-                at[q * z.slots + k] = ap[q, k].T
-
     return call(
         kernel,
         "turn",
-        [VMEM] * 4,
-        [VMEM, VMEM],
-        [
-            jax.ShapeDtypeStruct((z.pairs, z.rows, z.rows), BF16),
-            jax.ShapeDtypeStruct((2, 3, z.cols, z.cols), BF16),
-        ],
+        [VMEM] * 3,
+        VMEM,
+        jax.ShapeDtypeStruct((2, 3, z.cols, z.cols), BF16),
         [],
         6,
-        (ap, w_self, w_nbr, w_out),
+        (w_self, w_nbr, w_out),
     )
 
 
@@ -232,12 +243,13 @@
     ext[pl.ds(z.tiles + z.edge, z.edge)] = fe[...]
 
 
-def aggregate(z, meta, first, ap, ext):
+def aggregate(z, tiles, reads, first, adj, ext):
     rows = []
     for g in range(z.group):
         base = (first + g) * z.slots
-        picked = jnp.concatenate([ext[meta[base + k]] for k in range(z.slots)], axis=0)
-        blocks = jnp.concatenate([ap[first + g, k] for k in range(z.slots)], axis=1)
+        block = tiles[first + g] * z.slots
+        picked = jnp.concatenate([ext[reads[base + k]] for k in range(z.slots)], axis=0)
+        blocks = jnp.concatenate([adj[block + k] for k in range(z.slots)], axis=1)
         rows.append(dot(blocks, picked).astype(BF16))
     return jnp.concatenate(rows, axis=0)
 
@@ -250,14 +262,14 @@
     return jnp.concatenate(parts, axis=0)
 
 
-def first_lent(z, meta, f0, fw, fe, ap, w_self, w_nbr, bias, w_out):
-    def kernel(meta, f_lent, f_rest, fw, fe, ap, ws, wn, bias, wo, west, east, agg, ext):
+def first_lent(z, tiles, reads, f0, fw, fe, adj, w_self, w_nbr, bias, w_out):
+    def kernel(tiles, reads, f_lent, f_rest, fw, fe, adj, ws, wn, bias, wo, west, east, agg, ext):
         fill_extended(z, (f_lent, f_rest), fw, fe, ext)
 
         def work(first, target, offset):
             here = pl.ds(first, z.group)
             f = z.flat(ext[here])
-            aggs = aggregate(z, meta, first, ap, ext)
+            aggs = aggregate(z, tiles, reads, first, adj, ext)
             agg[here] = z.tiled(aggs)
             pre = dot(f, ws[0]) + dot(aggs, wn[0]) + bias[0:1, :]
             act = (pre * sigmoid(pre)).astype(BF16)
@@ -271,17 +283,17 @@
     return call(
         kernel,
         "first_lent",
-        [SMEM] + [VMEM] * 9,
+        [SMEM] * 2 + [VMEM] * 9,
         [VMEM] * 3,
         [z.nodes(z.edge), z.nodes(z.edge), z.nodes(z.lent)],
         [z.held(z.ext)],
-        8,
-        (meta, *f0, fw, fe, ap, w_self, w_nbr, bias, w_out),
-    )
-
-
-def first_rest(z, meta, bound, live, f0, fw, fe, ap, w_self, w_nbr, bias, w_out, west, east):
-    def kernel(meta, bound, live, f_lent, f_rest, fw, fe, ap, ws, wn, bias, wo, west, east,
+        12,
+        (tiles, reads, *f0, fw, fe, adj, w_self, w_nbr, bias, w_out),
+    )
+
+
+def first_rest(z, tiles, reads, bound, live, f0, fw, fe, adj, w_self, w_nbr, bias, w_out, west, east):
+    def kernel(tiles, reads, bound, live, f_lent, f_rest, fw, fe, adj, ws, wn, bias, wo, west, east,
                f1_lent, f1_rest, out, agg, ext, sems):
         copies = []
         for i in range(z.edge):
@@ -297,7 +309,7 @@
 
         def work(part, first):
             f = z.flat(ext[pl.ds(first, z.group)])
-            aggs = aggregate(z, meta, first, ap, ext)
+            aggs = aggregate(z, tiles, reads, first, adj, ext)
             here = pl.ds(first - z.lent, z.group)
             agg[here] = z.tiled(aggs)
             pre = dot(f, ws[0]) + dot(aggs, wn[0]) + bias[0:1, :]
@@ -315,7 +327,7 @@
     return call(
         kernel,
         "first_rest",
-        [SMEM] * 3 + [VMEM] * 11,
+        [SMEM] * 4 + [VMEM] * 11,
         [VMEM, VMEM, ANY, VMEM],
         [
             z.nodes(z.lent),
@@ -325,7 +337,7 @@
         ],
         [z.held(z.ext), pltpu.SemaphoreType.DMA((1 + z.lent,))],
         10,
-        (meta, bound, live, *f0, fw, fe, ap, w_self, w_nbr, bias, w_out, west, east),
+        (tiles, reads, bound, live, *f0, fw, fe, adj, w_self, w_nbr, bias, w_out, west, east),
     )
 
 
@@ -350,9 +362,7 @@
 
 
 def saved(z, f0, agg0, w_self, w_nbr, bias):
-    def kernel(f_lent, f_rest, a_lent, a_rest, ws, wn, bias, act, slope, token):
-        token[...] = jnp.zeros_like(token)
-
+    def kernel(f_lent, f_rest, a_lent, a_rest, ws, wn, bias, act, slope):
         def work(part, first):
             f = z.flat(group_of(z, (f_lent, f_rest), part, first)[...])
             aggs = z.flat(group_of(z, (a_lent, a_rest), part, first)[...])
@@ -368,37 +378,47 @@
         kernel,
         "saved",
         [VMEM] * 7,
-        [VMEM] * 3,
-        [z.nodes(z.tiles), z.nodes(z.tiles, F32), TOKEN],
+        [VMEM] * 2,
+        [z.nodes(z.tiles), z.nodes(z.tiles, F32)],
         [],
         10,
         (*f0, *agg0, w_self, w_nbr, bias),
     )
 
 
-def spread(z, meta, start, stop, at, source, acc, shift, spare):
-    def body(i, carry):
-        for u in range(UNROLL):
-            entry = start + i * UNROLL + u
-            inside = entry < stop
-            entry = jnp.minimum(entry, z.pairs - 1)
-            target = jnp.where(inside, meta[2 * z.pairs + entry] - shift, spare)
-            pair = meta[z.pairs + entry]
-            acc[target] += dot(at[pair], source(pair // z.slots))
-        return carry
-
-    lax.fori_loop(0, (stop - start + UNROLL - 1) // UNROLL, body, 0)
-
-
-def second(z, meta, counts, f1, fw, fe, ap, at, hidden, w_self, w_nbr, bias, wt, after):
-    def kernel(meta, counts, f_lent, f_rest, fw, fe, ap, at, hidden, ws, wn, bias, wt, _after,
+def spread(z, tables, table, count, adj, source, acc, add):
+    blocks, sources, targets, counts = tables
+    x = z.index
+
+    @pl.loop(0, count, unroll=4)
+    def _(target):
+        base = (x.first[table] + target) * x.QUAD
+        lefts, rights = [], []
+        for k in range(x.QUAD):
+            block = blocks[base + k]
+            left = adj[jnp.maximum(block, 0)]
+            lefts.append(jnp.where(block >= 0, left, jnp.zeros_like(left)).T)
+            rights.append(source(sources[base + k]))
+        value = dot(jnp.concatenate(lefts, axis=1), jnp.concatenate(rights, axis=0))
+        if add:
+            acc[target] += value
+        else:
+            acc[target] = value
+
+    @pl.loop(0, counts[table])
+    def _(i):
+        at = x.more[table] + i
+        acc[targets[at]] += dot(adj[blocks[at]].T, source(sources[at]))
+
+
+def second(z, tiles, reads, tables, f1, fw, fe, adj, hidden, w_self, w_nbr, bias, wt):
+    def kernel(tiles, reads, blocks, sources, targets, counts, f_lent, f_rest, fw, fe, adj, hidden, ws, wn, bias, wt,
                agg, act, dpre, dagg, to_west, to_east, ext, acc):
         fill_extended(z, (f_lent, f_rest), fw, fe, ext)
-        acc[...] = jnp.zeros_like(acc)
 
         def work(part, first):
             here = pl.ds(first, z.group)
-            aggs = aggregate(z, meta, first, ap, ext)
+            aggs = aggregate(z, tiles, reads, first, adj, ext)
             agg[here] = z.tiled(aggs)
             pre = dot(z.flat(ext[here]), ws[1]) + dot(aggs, wn[1]) + bias[1:2, :]
             sig = sigmoid(pre)
@@ -408,19 +428,19 @@
             dagg[here] = z.tiled(dot(grad, wt[1, 1]).astype(BF16))
 
         each_group(z, work, unroll=2)
-        spread(z, meta, counts[0], z.pairs, at, lambda q: dagg[q], acc, z.tiles, z.lent)
+        spread(z, (blocks, sources, targets, counts), 1, z.lent, adj, lambda q: dagg[q], acc, False)
         to_west[...] = acc[pl.ds(0, z.edge)].astype(BF16)
         to_east[...] = acc[pl.ds(z.edge, z.edge)].astype(BF16)
 
     return call(
         kernel,
         "second",
-        [SMEM] * 2 + [VMEM] * 12,
+        [SMEM] * 6 + [VMEM] * 10,
         [VMEM] * 6,
         [z.nodes(z.tiles)] * 4 + [z.nodes(z.edge)] * 2,
-        [z.held(z.ext), z.held(z.lent + 1, F32)],
+        [z.held(z.ext), z.held(z.lent, F32)],
         12,
-        (meta, counts, *f1, fw, fe, ap, at, hidden, w_self, w_nbr, bias, wt, after),
+        (tiles, reads, *tables, *f1, fw, fe, adj, hidden, w_self, w_nbr, bias, wt),
     )
 
 
@@ -431,19 +451,23 @@
         self.sizes = (core, dom // core, phase)
         self.count = dom * phase
         place = lax.axis_index("dom")
-        self.me = jnp.stack([lax.rem(place, core), place // core, lax.axis_index("phase")]).astype(jnp.int32)
+        place = [lax.rem(place, core), place // core, lax.axis_index("phase")]
+        self.place = jnp.stack(place + [jnp.zeros_like(place[0])] * 5).astype(jnp.int32)
+        self.me = None
 
     def piece_of(self, me, steps):
         at = [lax.rem(me[i] + (steps[i] + n) % n, n) for i, n in enumerate(self.sizes)]
         return (at[0] * self.sizes[1] + at[1]) * self.sizes[2] + at[2]
 
     def passed(self, value, dim, steps):
+        return self.passed_by(value, [steps if i == dim else 0 for i in range(3)])
+
+    def passed_by(self, value, steps):
         pairs = []
         for c in range(self.sizes[0]):
             for d in range(self.sizes[1]):
                 for p in range(self.sizes[2]):
-                    to = [c, d, p]
-                    to[dim] = (to[dim] + steps) % self.sizes[dim]
+                    to = [(at + by) % n for at, by, n in zip((c, d, p), steps, self.sizes)]
                     source = (d * self.sizes[0] + c) * self.sizes[2] + p
                     target = (to[1] * self.sizes[0] + to[0]) * self.sizes[2] + to[2]
                     pairs.append((source, target))
@@ -497,7 +521,7 @@
     )
 
 
-def added(values, split=False, after=None):
+def added(values, split=False, after=(), pairs=False):
     shape = values[0].shape
     count = shape[0] if split else 1
 
@@ -505,16 +529,19 @@
         outs = refs[-count:]
         for i, out in enumerate(outs):
             parts = [ref[i] if split else ref[...] for ref in refs[: len(values)]]
-            total = parts[0].astype(F32)
+            parts = [part.astype(F32) for part in parts]
+            if pairs:
+                parts = [parts[0] + parts[1], parts[2] + parts[3]]
+            total = parts[0]
             for part in parts[1:]:
-                total = total + part.astype(F32)
+                total = total + part
             out[...] = total.astype(BF16)
 
-    args = list(values) if after is None else [*values, after]
+    args = [*values, *after]
     outs = call(
         kernel,
         "added",
-        [VMEM] * len(args),
+        [VMEM] * len(values) + [ANY] * len(after),
         [VMEM] * count,
         [jax.ShapeDtypeStruct(shape[1:] if split else shape, BF16)] * count,
         [],
@@ -524,26 +551,53 @@
     return outs if split else outs[0]
 
 
-def plane_share(plane, pieces, after=None):
+def plane_parts(plane, pieces):
     parts = added(plane.received(pieces, 0), split=True)
     parts = added(plane.received(parts, 1), split=True)
-    return added(plane.received(parts, 2), after=after)
-
-
-def share_totals(plane, share):
+    return plane.received(parts, 2)
+
+
+def line_sum(share):
     lines = lax.axis_size("feat")
-    if lines & (lines - 1) == 0:
-        step = 1
-        while step < lines:
-            other = lax.ppermute(share, "feat", [(i, i ^ step) for i in range(lines)])
-            share = added([share, other])
-            step *= 2
-    else:
-        share = lax.psum(share.astype(F32), "feat").astype(BF16)
+    if lines & (lines - 1) != 0:
+        return lax.psum(share.astype(F32), "feat").astype(BF16)
+    step = 1
+    while step < lines:
+        other = lax.ppermute(share, "feat", [(i, i ^ step) for i in range(lines)])
+        share = added([share, other])
+        step *= 2
+    return share
+
+
+def line_sum_at_once(share):
+    lines = lax.axis_size("feat")
+    if lines != 4:
+        return line_sum(share)
+    others = [lax.ppermute(share, "feat", [(i, i ^ s) for i in range(lines)]) for s in (1, 2, 3)]
+    return added([share, *others], pairs=True)
+
+
+def stacked(values):
+    def kernel(*refs):
+        for i, ref in enumerate(refs[:-1]):
+            refs[-1][i] = ref[...]
+
+    shape = (len(values),) + values[0].shape
+    out = jax.ShapeDtypeStruct(shape, values[0].dtype)
+    return call(kernel, "stacked", [VMEM] * len(values), VMEM, out, [], 4, values)
+
+
+def plane_gathered(plane, share):
     for dim in (2, 1):
         size = plane.sizes[dim]
-        share = jnp.stack([share] + [plane.passed(share, dim, i) for i in range(1, size)])
+        share = stacked([share] + [plane.passed(share, dim, i) for i in range(1, size)])
     return [share] + [plane.passed(share, 0, i) for i in range(1, plane.sizes[0])]
+
+
+def plane_gathered_at_once(plane, share):
+    core, ahead, side = plane.sizes
+    steps = [(i, j, k) for i in range(core) for j in range(ahead) for k in range(side)]
+    return [share] + [plane.passed_by(share, by) for by in steps[1:]]
 
 
 def second_out(z, bound, live, f1, act, w_out, out):
@@ -584,16 +638,16 @@
     )
 
 
-def input_grad(z, layer, meta, counts, m, dpre, dagg, at, wt):
+def input_grad(z, layer, tables, m, dpre, dagg, adj, wt):
     arrays = (m, dpre, dagg)
     flat_args = [x for a in arrays for x in (a if isinstance(a, tuple) else (a,))]
 
-    def kernel(meta, counts, *refs):
+    def kernel(blocks, sources, targets, counts, *refs):
         refs = list(refs)
         m, dpre, dagg = [
             (refs.pop(0), refs.pop(0)) if isinstance(a, tuple) else refs.pop(0) for a in arrays
         ]
-        at, wt, part_out, rest_out, token, acc = refs
+        adj, wt, part_out, rest_out, token, acc = refs
         token[...] = jnp.zeros_like(token)
 
         def direct(part, first):
@@ -610,24 +664,24 @@
             rest = dagg[1][jnp.maximum(q - z.lent, 0)]
             return jnp.where(q < z.lent, lent, rest)
 
-        spread(z, meta, 0, counts[0], at, source, acc, 0, z.tiles)
+        spread(z, (blocks, sources, targets, counts), 0, z.tiles, adj, source, acc, True)
         part_out[...] = acc[pl.ds(0, z.lent)]
         rest_out[...] = acc[pl.ds(z.lent, z.rest)].astype(BF16)
 
     return call(
         kernel,
         "input_grad%d" % layer,
-        [SMEM] * 2 + [VMEM] * (len(flat_args) + 2),
+        [SMEM] * 4 + [VMEM] * (len(flat_args) + 2),
         [VMEM] * 3,
         [z.nodes(z.lent, F32), z.nodes(z.rest), TOKEN],
-        [z.held(z.tiles + 1, F32)],
-        28,
-        [meta, counts, *flat_args, at, wt],
-    )
-
-
-def early_rest(z, meta, counts, live, upstream, slope, at, wt):
-    def kernel(meta, counts, live, g, slope, at, wt, grads, m, dpre, dagg, outer, acc, sem):
+        [z.held(z.tiles, F32)],
+        20,
+        [*tables, *flat_args, adj, wt],
+    )
+
+
+def early_rest(z, tables, live, upstream, slope, adj, wt):
+    def kernel(blocks, sources, targets, counts, live, g, slope, adj, wt, grads, m, dpre, dagg, outer, sem):
         copy = pltpu.make_async_copy(g, grads.at[1, pl.ds(z.lent, z.rest)], sem)
         copy.start()
 
@@ -641,31 +695,29 @@
             dagg[here] = z.tiled(dot(grad, wt[0, 1]).astype(BF16))
 
         each_group(z, work, (1,))
-        acc[...] = jnp.zeros_like(acc)
 
         def source(q):
             return dagg[jnp.maximum(q - z.lent, 0)]
 
-        spread(z, meta, counts[0], counts[0] + counts[1], at, source, acc, z.tiles, z.lent)
-        outer[...] = acc[pl.ds(0, z.lent)]
+        spread(z, (blocks, sources, targets, counts), 3, z.lent, adj, source, outer, False)
         copy.wait()
 
     return call(
         kernel,
         "early_rest",
-        [SMEM] * 3 + [VMEM] * 4,
+        [SMEM] * 5 + [VMEM] * 4,
         [ANY] + [VMEM] * 4,
         [jax.ShapeDtypeStruct((2, z.tiles, z.rows, z.cols), BF16)]
         + [z.nodes(z.rest)] * 3
         + [z.nodes(z.lent, F32)],
-        [z.held(z.lent + 1, F32), pltpu.SemaphoreType.DMA],
+        [pltpu.SemaphoreType.DMA],
         14,
-        (meta, counts, live, upstream, slope, at, wt),
-    )
-
-
-def early_lent(z, meta, counts, bound, part, fw, fe, slope, outer, at, wt, grads, after):
-    def kernel(meta, counts, bound, part, fw, fe, slope, outer, at, wt, _g, _ready, _late,
+        (*tables, live, upstream, slope, adj, wt),
+    )
+
+
+def early_lent(z, tables, bound, part, fw, fe, slope, outer, adj, wt, grads, after):
+    def kernel(blocks, sources, targets, counts, bound, part, fw, fe, slope, outer, adj, wt, _g, _ready, _late,
                m, dpre, dagg, grads, to_west, to_east, acc, sems):
         def work(first, got):
             here = pl.ds(first, z.group)
@@ -687,13 +739,12 @@
         ]
         for copy in copies:
             copy.start()
-        acc[pl.ds(0, z.lent)] = outer[...]
-        acc[z.lent] = jnp.zeros((z.rows, z.cols), F32)
+        acc[...] = outer[...]
 
         def source(q):
             return dagg[jnp.minimum(q, z.lent - 1)]
 
-        spread(z, meta, counts[0] + counts[1], z.pairs, at, source, acc, z.tiles, z.lent)
+        spread(z, (blocks, sources, targets, counts), 2, z.lent, adj, source, acc, True)
         to_west[...] = acc[pl.ds(0, z.edge)].astype(BF16)
         to_east[...] = acc[pl.ds(z.edge, z.edge)].astype(BF16)
         for copy in copies:
@@ -702,24 +753,18 @@
     return call(
         kernel,
         "early_lent",
-        [SMEM] * 3 + [VMEM] * 7 + [ANY, VMEM, VMEM],
+        [SMEM] * 5 + [VMEM] * 7 + [ANY, VMEM, VMEM],
         [VMEM] * 3 + [ANY] + [VMEM] * 2,
         [z.nodes(z.lent)] * 3 + [jax.ShapeDtypeStruct(grads.shape, BF16)] + [z.nodes(z.edge)] * 2,
-        [z.held(z.lent + 1, F32), pltpu.SemaphoreType.DMA((z.lent,))],
+        [z.held(z.lent, F32), pltpu.SemaphoreType.DMA((z.lent,))],
         16,
-        (meta, counts, bound, part, fw, fe, slope, outer, at, wt, grads, *after),
-        {10: 3},
-    )
-
-
-def finish(z, plane, bound, part, rest, fw, fe, early, late, grads):
-    c = z.cols
-    piece = early[0].shape[2]
-    core, ahead, side = plane.sizes
-
-    def kernel(me, bound, part, rest, fw, fe, *refs):
-        totals = refs[: 2 * core]
-        _g, grads, g_self, g_nbr, g_bias, g_out, keep, buf, sems = refs[2 * core :]
+        (*tables, bound, part, fw, fe, slope, outer, adj, wt, grads, *after),
+        {12: 3},
+    )
+
+
+def finish(z, bound, part, rest, fw, fe, grads):
+    def kernel(bound, part, rest, fw, fe, _g, grads, keep, sems):
         copies = [pltpu.make_async_copy(rest, grads.at[0, pl.ds(z.lent, z.rest)], sems.at[z.lent])]
         copies[0].start()
         for i in range(z.lent):
@@ -730,34 +775,56 @@
             )
             copy.start()
             copies.append(copy)
+        for copy in copies:
+            copy.wait()
+
+    return call(
+        kernel,
+        "finish",
+        [SMEM] + [VMEM] * 4 + [ANY],
+        ANY,
+        jax.ShapeDtypeStruct(grads.shape, BF16),
+        [z.held(z.lent), pltpu.SemaphoreType.DMA((z.lent + 1,))],
+        14,
+        (bound, part, rest, fw, fe, grads),
+        {5: 0},
+    )
+
+
+def unpack(z, plane, early, late):
+    c = z.cols
+    piece = early[0].shape[0]
+    core, ahead, side = plane.sizes
+
+    def kernel(me, *refs):
+        refs = list(refs)
+        early, late = refs[: plane.count], refs[plane.count : plane.count + core]
+        g_self, g_nbr, g_bias, g_out, buf = refs[plane.count + core :]
         for layer in range(2):
             for i in range(core):
                 for j in range(ahead):
                     for k in range(side):
                         start = pl.multiple_of(plane.piece_of(me, (-i, -j, -k)) * piece, 16)
-                        buf[pl.ds(start, piece), :] = totals[layer * core + i][j, k].astype(F32)
+                        if layer == 0:
+                            got = early[(i * ahead + j) * side + k][...]
+                        else:
+                            got = late[i][j, k]
+                        buf[pl.ds(start, piece), :] = got.astype(F32)
             g_self[layer] = buf[pl.ds(0, c), :]
             g_nbr[layer] = buf[pl.ds(c, c), :]
             g_out[layer] = buf[pl.ds(2 * c, c), :]
             g_bias[layer : layer + 1, :] = buf[pl.ds(3 * c, 1), :]
-        for copy in copies:
-            copy.wait()
 
     square = jax.ShapeDtypeStruct((2, c, c), F32)
     return call(
         kernel,
-        "finish",
-        [SMEM] * 2 + [VMEM] * (4 + 2 * core) + [ANY],
-        [ANY] + [VMEM] * 4,
-        [jax.ShapeDtypeStruct(grads.shape, BF16), square, square, jax.ShapeDtypeStruct((2, c), F32), square],
-        [
-            z.held(z.lent),
-            pltpu.VMEM((piece * plane.count, c), F32),
-            pltpu.SemaphoreType.DMA((z.lent + 1,)),
-        ],
-        14,
-        (plane.me, bound, part, rest, fw, fe, *early, *late, grads),
-        {6 + 2 * core: 0},
+        "unpack",
+        [SMEM] + [VMEM] * (plane.count + core),
+        [VMEM] * 4,
+        [square, square, jax.ShapeDtypeStruct((2, c), F32), square],
+        [pltpu.VMEM((piece * plane.count, c), F32)],
+        10,
+        (plane.me, *early, *late),
     )
 
 
@@ -773,58 +840,63 @@
     west, east = lend(z, bound_tiles, features)
     from_west = passed_along(east, 1)
     from_east = passed_along(west, -1)
-    *nodes, ap, meta, counts = arrange(z, bound_tiles, tile_nbrs, live_tiles, features, cot, adjacency)
+    *nodes, adj, tiles, reads, blocks, sources, targets, counts, plane.me = arrange(
+        z, bound_tiles, tile_nbrs, live_tiles, plane.place, features, cot, adjacency.reshape(z.pairs, r, r)
+    )
     f0, m1 = tuple(nodes[:2]), tuple(nodes[2:])
-    at, wt = turn(z, ap, w_self, w_nbr, w_out)
-
-    west, east, agg_lent = first_lent(z, meta, f0, from_west, from_east, ap, w_self, w_nbr, pre_bias, w_out)
+    tables = (blocks, sources, targets, counts)
+    wt = turn(z, w_self, w_nbr, w_out)
+
+    west, east, agg_lent = first_lent(
+        z, tiles, reads, f0, from_west, from_east, adj, w_self, w_nbr, pre_bias, w_out
+    )
     next_west = passed_along(east, 1)
     next_east = passed_along(west, -1)
     f1_lent, f1_rest, section_out, agg_rest = first_rest(
-        z, meta, bound_tiles, live_tiles, f0, from_west, from_east, ap, w_self, w_nbr, pre_bias, w_out,
+        z, tiles, reads, bound_tiles, live_tiles, f0, from_west, from_east, adj, w_self, w_nbr, pre_bias, w_out,
         west, east,
     )
     f1, agg0 = (f1_lent, f1_rest), (agg_lent, agg_rest)
     hidden = second_own(z, m1, wt)
-    act0, slope, ready = saved(z, f0, agg0, w_self, w_nbr, pre_bias)
 
     agg1, act1, dpre1, dagg1, to_west, to_east = second(
-        z, meta, counts, f1, next_west, next_east, ap, at, hidden, w_self, w_nbr, pre_bias, wt, ready
+        z, tiles, reads, tables, f1, next_west, next_east, adj, hidden, w_self, w_nbr, pre_bias, wt
     )
     back_west = passed_along(to_east, 1)
     back_east = passed_along(to_west, -1)
-    part, upstream, _ = input_grad(z, 1, meta, counts, m1, dpre1, dagg1, at, wt)
+    late = weight_grads(z, plane, f1, agg1, act1, m1, dpre1, "weight_grads1")
+    late = added(plane_parts(plane, late))
+    part, upstream, _ = input_grad(z, 1, tables, m1, dpre1, dagg1, adj, wt)
+    section_out, ready = second_out(z, bound_tiles, live_tiles, f1, act1, w_out, section_out)
+    act0, slope = saved(z, f0, agg0, w_self, w_nbr, pre_bias)
     grads, m0_rest, dpre_rest, dagg_rest, outer = early_rest(
-        z, meta, counts, live_tiles, upstream, slope, at, wt
-    )
-    late = plane_share(plane, weight_grads(z, plane, f1, agg1, act1, m1, dpre1, "weight_grads1"))
-    section_out, ready = second_out(z, bound_tiles, live_tiles, f1, act1, w_out, section_out)
+        z, tables, live_tiles, upstream, slope, adj, wt
+    )
 
     m0_lent, dpre_lent, dagg_lent, grads, to_west, to_east = early_lent(
-        z, meta, counts, bound_tiles, part, back_west, back_east, slope, outer, at, wt, grads,
-        (ready, late),
+        z, tables, bound_tiles, part, back_west, back_east, slope, outer, adj, wt, grads, (ready, late)
     )
     back_west = passed_along(to_east, 1)
     back_east = passed_along(to_west, -1)
     m0, dpre0, dagg0 = (m0_lent, m0_rest), (dpre_lent, dpre_rest), (dagg_lent, dagg_rest)
-    halves = weight_grads(z, plane, f0, agg0, act0, m0, dpre0, "weight_grads0")
-
-    def last(late, halves, m0, dpre0, dagg0, meta, counts, at, wt):
-        part, rest, done = input_grad(z, 0, meta, counts, m0, dpre0, dagg0, at, wt)
-        early = plane_share(plane, halves, done)
-        return share_totals(plane, early), share_totals(plane, late), part, rest
-
-    args = (late, halves, m0, dpre0, dagg0, meta, counts, at, wt)
-    shapes = jax.eval_shape(last, *args)
+    early = weight_grads(z, plane, f0, agg0, act0, m0, dpre0, "weight_grads0")
+
+    def meanwhile(early, late, tables, m0, dpre0, dagg0, adj, wt):
+        part, rest, _ = input_grad(z, 0, tables, m0, dpre0, dagg0, adj, wt)
+        return plane_parts(plane, early), plane_gathered(plane, line_sum(late)), part, rest
+
+    args = (early, late, tables, m0, dpre0, dagg0, adj, wt)
+    shapes = jax.eval_shape(meanwhile, *args)
     early, late, part, rest = lax.cond(
         live_tiles[0] > 0,
-        last,
+        meanwhile,
         lambda *_: jax.tree.map(lambda a: jnp.zeros(a.shape, a.dtype), shapes),
         *args,
     )
-    grads, grad_self, grad_nbr, grad_bias, grad_out = finish(
-        z, plane, bound_tiles, part, rest, back_west, back_east, early, late, grads
-    )
+    early = line_sum_at_once(added(early, after=(back_west, back_east)))
+    early = plane_gathered_at_once(plane, early)
+    grads = finish(z, bound_tiles, part, rest, back_west, back_east, grads)
+    grad_self, grad_nbr, grad_bias, grad_out = unpack(z, plane, early, late)
     return (
         section_out.reshape(2, t * r, c),
         grads.reshape(2, t * r, c),

time: 174 us -> 186 us (1.069)
  waiting for transfers between devices: 30.9 us -> 63.7 us
  local copies, waits for them, and re-layouts: 22.8 us -> 3.98 us
  starting transfers between devices: 37.8 us -> 42.6 us
  Pallas kernels: 77.8 us -> 73.4 us
    unnamed x81 -> x19, local copies, waits for them, and re-layouts: 22.8 us -> 3.89 us
    ppermute x16 -> x21, waiting for transfers between devices: 22.4 us -> 40.3 us  [the longest x2 20.3 us: line_sum(): other = lax.ppermute(share, 'feat', [(i, i ^ step) for i in range(lines)])]
    ppermute x8, waiting for transfers between devices: 8.47 us -> 23.5 us  [passed_along(): lax.ppermute(value, AXES, [(i, (i + steps) % count) for i in range(count)])]
    ppermute x16 -> x21, starting transfers between devices: 15.2 us -> 21.8 us  [the longest x16 15.9 us: passed_by(): return lax.ppermute(value, PLANE, pairs)]
    pallas_call x26 -> x28, Pallas kernels: 77.8 us -> 73.4 us  [call(): pl.pallas_call(kernel, in_specs=in_specs, out_specs=out_specs, out_shape=...]
  transfers between devices with their start and end apart: 24 -> 29, of which waited for: 14 -> 13; matrix products, arithmetic and copies ran while one was open for 1% -> 0% of each run, Pallas kernels for 30% -> 28%
where the time goes in v6:
time: 186 us; the launch traced here: 185 us
  Pallas kernels  73.4 us (39%)
  waiting for transfers between devices  63.7 us (34%)
  starting transfers between devices  42.6 us (23%)
  local copies, waits for them, and re-layouts  3.98 us (2%)
    pallas_call x28, Pallas kernels, call(): pl.pallas_call(kernel, in_specs=in_specs, out_specs=out_specs, out_shape=...  73.4 us
    ppermute x8, waiting for transfers between devices, passed_along(): lax.ppermute(value, AXES, [(i, (i + steps) % count) for i in range(count)])  23.5 us
    ppermute x8, starting transfers between devices, passed_along(): lax.ppermute(value, AXES, [(i, (i + steps) % count) for i in range(count)])  20.8 us
    ppermute x2, waiting for transfers between devices, line_sum(): other = lax.ppermute(share, 'feat', [(i, i ^ step) for i in range(lines)])  20.3 us
    ppermute x16, waiting for transfers between devices, passed_by(): return lax.ppermute(value, PLANE, pairs)  17 us
    ppermute x16, starting transfers between devices, passed_by(): return lax.ppermute(value, PLANE, pairs)  15.9 us
    ppermute x3, starting transfers between devices, line_sum_at_once(): lax.ppermute(share, 'feat', [(i, i ^ s) for i in range(lines)])  4.45 us
    unnamed x19, local copies, waits for them, and re-layouts  3.89 us
  transfers between devices with their start and end apart: 29, of which 13 were waited for; matrix products, arithmetic and copies ran while one was open for 0% of the time, Pallas kernels for 28%

profile of v6, /device:TPU:0, one launch (start us, length us, event | category | flops | bytes accessed | tf_op | source)
XLA Modules:
  0.0 185.3 jit_solution(16516469638839715298)
XLA Ops:
  6.9 3.4 %collective-permute-start.9 = (bf16[8,128,256]{2,1,0:T(8,128)(2,1)}, bf16[8,128,256]{2,1,0:T(8,128)(2,1)S(1)}, u32[]{:S(2)}, u32[]{:S(2)}) collective-permute-start(bf16[8,128,256]{2,1,0:T(8,128)(2,1)} %get-tuple-element.124), channel_id=1, source_target_pairs={{0,31},{1,0},{2,1},{3,2},{4,3},{5,4},{6,5},{7,6},{8,7},{9,8},{10,9... | collective-permute-start | bytes 1572872 | tf_op jit(solution)/shard_map/ppermute | solution.py:63
  15.0 9.4 %arrange.1 = (bf16[16,128,256]{2,1,0:T(8,128)(2,1)S(1)}, bf16[16,128,256]{2,1,0:T(8,128)(2,1)S(1)}, bf16[16,128,256]{2,1,0:T(8,128)(2,1)S(1)}, bf16[16,128,256]{...) custom-call(s32[1,2,8]{2,1,0:T(2,128)S(1)} %copy-done.6, ...), custom_call_target="tpu_custom_call" | custom-call | flops 1000 | bytes 1000 | tf_op jit(solution)/shard_map/arrange/pallas_call | solution.py:75
  24.4 7.4 %collective-permute-done.9.fe = bf16[8,128,256]{2,1,0:T(8,128)(2,1)S(1)} collective-permute-done((bf16[8,128,256]{2,1,0:T(8,128)(2,1)}, bf16[8,128,256]{2,1,0:T(8,128)(2,1)S(1)}, u32[]{:S(2)}, u32[]{:S(2)}) %collective-permute-start.9) | collective-permute-done | bytes 524320 | tf_op jit(solution)/shard_map/ppermute | solution.py:63
  31.8 3.3 %first_lent.1 = (bf16[8,128,256]{2,1,0:T(8,128)(2,1)S(1)}, bf16[8,128,256]{2,1,0:T(8,128)(2,1)S(1)}, bf16[16,128,256]{2,1,0:T(8,128)(2,1)S(1)}) custom-call(s32[32]{0:T(128)S(1)} %get-tuple-element.119.tiles, s32[128]{0:T(128)S(1)} %get-tuple-element.120.reads, bf16[16,128,256]{2,1,0:T(8,128)(2,1)S(1)} %get-tuple-element.121.f_lent.refs_0_, ...), custom_call_target="tpu_custom_call" | custom-call | flops 1000 | bytes 1000 | tf_op jit(solution)/shard_map/first_lent/pallas_call | solution.py:75
  35.1 3.5 %collective-permute-start.11 = (bf16[8,128,256]{2,1,0:T(8,128)(2,1)S(1)}, bf16[8,128,256]{2,1,0:T(8,128)(2,1)S(1)}, u32[]{:S(2)}, u32[]{:S(2)}) collective-permute-start(bf16[8,128,256]{2,1,0:T(8,128)(2,1)S(1)} %get-tuple-element.126.west), channel_id=1, source_target_pairs={{0,31},{1,0},{2,1},{3,2},{4,3},{5,4},{6,5},{7,6},{8,7},{9,8},{10,9... | collective-permute-start | bytes 1572872 | tf_op jit(solution)/shard_map/ppermute | solution.py:63
  40.7 4.7 %first_rest.1 = (bf16[16,128,256]{2,1,0:T(8,128)(2,1)S(1)}, bf16[16,128,256]{2,1,0:T(8,128)(2,1)S(1)}, bf16[2,32,128,256]{3,2,1,0:T(8,128)(2,1)}, bf16[16,128,256]{2,1,0:T(8,128)(2,1)S(1)}) custom-call(s32[32]{0:T(128)S(1)} %get-tuple-element.119.tiles, s32[128]{0:T(128)S(1)} %get-tuple-element.120.reads, s32[1,2,8]{2,1,0:T(2,128)S(1)} %copy-done.6, ...), custom_call_target="tpu_custom_call" | custom-call | flops 1000 | bytes 1000 | tf_op jit(solution)/shard_map/first_rest/pallas_call | solution.py:75
  45.4 5.6 %collective-permute-done.11.fe = bf16[8,128,256]{2,1,0:T(8,128)(2,1)S(1)} collective-permute-done((bf16[8,128,256]{2,1,0:T(8,128)(2,1)S(1)}, bf16[8,128,256]{2,1,0:T(8,128)(2,1)S(1)}, u32[]{:S(2)}, u32[]{:S(2)}) %collective-permute-start.11) | collective-permute-done | bytes 524320 | tf_op jit(solution)/shard_map/ppermute | solution.py:63
  50.9 10.5 %collective-permute-done.10.fw = bf16[8,128,256]{2,1,0:T(8,128)(2,1)S(1)} collective-permute-done((bf16[8,128,256]{2,1,0:T(8,128)(2,1)S(1)}, bf16[8,128,256]{2,1,0:T(8,128)(2,1)S(1)}, u32[]{:S(2)}, u32[]{:S(2)}) %collective-permute-start.10) | collective-permute-done | bytes 524320 | tf_op jit(solution)/shard_map/ppermute | solution.py:63
  61.4 8.3 %second.1 = (bf16[32,128,256]{2,1,0:T(8,128)(2,1)S(1)}, bf16[32,128,256]{2,1,0:T(8,128)(2,1)S(1)}, bf16[32,128,256]{2,1,0:T(8,128)(2,1)S(1)}, bf16[32,128,256]{2...) custom-call(s32[32]{0:T(128)S(1)} %get-tuple-element.119.tiles, ...), custom_call_target="tpu_custom_call" | custom-call | flops 1000 | bytes 1000 | tf_op jit(solution)/shard_map/second/pallas_call | solution.py:75
  75.1 4.1 %weight_grads1.1 = (bf16[2,2,112,256]{3,2,1,0:T(8,128)(2,1)S(1)}, bf16[2,2,112,256]{3,2,1,0:T(8,128)(2,1)S(1)}) custom-call(s32[8]{0:T(128)S(1)} %get-tuple-element.139.me, bf16[16,128,256]{2,1,0:T(8,128)(2,1)S(1)} %get-tuple-element.128.f_lent.refs_0_, bf16[16,128,256]{2,1,0:T(8,128)(2,1)S(1)} %get-tuple-element.129.f_rest.refs_1_, ...), custom_call_target="tpu_custom_call" | custom-call | flops 1000 | bytes 1000 | tf_op jit(solution)/shard_map/weight_grads1/pallas_call | solution.py:75
  83.3 3.4 %collective-permute-done.15.refs_1_ = bf16[2,112,256]{2,1,0:T(8,128)(2,1)S(1)} collective-permute-done((bf16[2,112,256]{2,1,0:T(8,128)(2,1)S(1)}, bf16[2,112,256]{2,1,0:T(8,128)(2,1)S(1)}, u32[]{:S(2)}, u32[]{:S(2)}) %collective-permute-start.15) | collective-permute-done | bytes 114720 | tf_op jit(solution)/shard_map/ppermute | solution.py:474
  91.2 3.5 %second_out.1 = (bf16[2,32,128,256]{3,2,1,0:T(8,128)(2,1)}, f32[8,128]{1,0:T(8,128)S(1)}) custom-call(s32[1,2,8]{2,1,0:T(2,128)S(1)} %copy-done.6, s32[1]{0:T(128)S(6)} %copy.35.live, bf16[16,128,256]{2,1,0:T(8,128)(2,1)S(1)} %get-tuple-element.128.f_lent.refs_0_, ...), custom_call_target="tpu_custom_call", output_to_operand_aliasing={{0}: (6, {})} | custom-call | flops 1000 | bytes 1000 | tf_op jit(solution)/shard_map/second_out/pallas_call | solution.py:75
  94.8 7.1 %input_grad1.1 = (f32[16,128,256]{2,1,0:T(8,128)S(1)}, bf16[16,128,256]{2,1,0:T(8,128)(2,1)S(1)}, f32[8,128]{1,0:T(8,128)}) custom-call(s32[968]{0:T(1024)S(1)} %get-tuple-element.130.blocks, s32[968]{0:T(1024)S(1)} %get-tuple-element.131.sources, s32[968]{0:T(1024)S(1)} %get-tuple-element.132.targets, s32[8]{0:T(128)S(1)} %get-tuple-element.133.counts, ...), custom_call_target="tpu_custom_call" | custom-call | flops 1000 | bytes 1000 | tf_op jit(solution)/shard_map/input_grad1/pallas_call | solution.py:75
  101.9 3.8 %early_rest.1 = (bf16[2,32,128,256]{3,2,1,0:T(8,128)(2,1)}, bf16[16,128,256]{2,1,0:T(8,128)(2,1)S(1)}, bf16[16,128,256]{2,1,0:T(8,128)(2,1)S(1)}, bf16[16,128,256]{2,1,0:T(8,128)(2,1)S(1)}, f32[16,128,256]{2,1,0:T(8,128)S(1)}) custom-call(s32[968]{0:T(1024)S(1)} %get-tuple-element.130.blocks, s32[968]{0:T(1024)S(1)} %get-tuple-element.131.sources, ...), custom_call_target="tpu_custom_call" | custom-call | flops 1000 | bytes 1000 | tf_op jit(solution)/shard_map/early_rest/pallas_call | solution.py:75
  105.8 3.7 %early_lent.1 = (bf16[16,128,256]{2,1,0:T(8,128)(2,1)S(1)}, bf16[16,128,256]{2,1,0:T(8,128)(2,1)S(1)}, bf16[16,128,256]{2,1,0:T(8,128)(2,1)S(1)}, bf16[2,32,128,...) custom-call(s32[968]{0:T(1024)S(1)} %get-tuple-element.130.blocks, ...), custom_call_target="tpu_custom_call", output_to_operand_aliasing={{3}: (12, {})} | custom-call | flops 1000 | bytes 1000 | tf_op jit(solution)/shard_map/early_lent/pallas_call | solution.py:75
  109.6 5.3 %collective-permute-start.18 = (bf16[8,128,256]{2,1,0:T(8,128)(2,1)S(1)}, bf16[8,128,256]{2,1,0:T(8,128)(2,1)S(1)}, u32[]{:S(2)}, u32[]{:S(2)}) collective-permute-start(bf16[8,128,256]{2,1,0:T(8,128)(2,1)S(1)} %get-tuple-element.171), channel_id=1, source_target_pairs={{0,31},{1,0},{2,1},{3,2},{4,3},{5,4},{6,5},{7,6},{8,7},{9,8},{10,9... | collective-permute-start | bytes 1572872 | tf_op jit(solution)/shard_map/ppermute | solution.py:63
  114.9 4.0 %weight_grads0.1 = (bf16[2,2,112,256]{3,2,1,0:T(8,128)(2,1)S(1)}, bf16[2,2,112,256]{3,2,1,0:T(8,128)(2,1)S(1)}) custom-call(s32[8]{0:T(128)S(1)} %get-tuple-element.139.me, bf16[16,128,256]{2,1,0:T(8,128)(2,1)S(1)} %get-tuple-element.121.f_lent.refs_0_, bf16[16,128,256]{2,1,0:T(8,128)(2,1)S(1)} %get-tuple-element.122.f_rest.refs_1_, ...), custom_call_target="tpu_custom_call" | custom-call | flops 1000 | bytes 1000 | tf_op jit(solution)/shard_map/weight_grads0/pallas_call | solution.py:75
  119.0 45.4 %conditional.1 = (bf16[112,256]{1,0:T(8,128)(2,1)S(1)}, bf16[112,256]{1,0:T(8,128)(2,1)}, bf16[2,2,112,256]{3,2,1,0:T(8,128)(2,1)}, bf16[2,2,112,256]{3,2,1,0:T(...) conditional(s32[]{:T(128)} %bitcast.7, () %tuple.16, ...), branch_computations={%region_0.1_spmd, %region_1.2_spmd} | conditional | flops 7000 | bytes 3719230 | solution.py:890
  119.1 16.4 %collective-permute-done.3.refs_1_ = bf16[112,256]{1,0:T(8,128)(2,1)S(1)} collective-permute-done((bf16[112,256]{1,0:T(8,128)(2,1)S(1)}, bf16[112,256]{1,0:T(8,128)(2,1)S(1)}, u32[]{:S(2)}, u32[]{:S(2)}) %collective-permute-start.3) | collective-permute-done | bytes 57376 | tf_op jit(solution)/shard_map/cond/branch_1_fun/ppermute | solution.py:566
  136.9 3.8 %collective-permute-done.4.refs_1_ = bf16[112,256]{1,0:T(8,128)(2,1)S(1)} collective-permute-done((bf16[112,256]{1,0:T(8,128)(2,1)S(1)}, bf16[112,256]{1,0:T(8,128)(2,1)S(1)}, u32[]{:S(2)}, u32[]{:S(2)}) %collective-permute-start.4) | collective-permute-done | bytes 57376 | tf_op jit(solution)/shard_map/cond/branch_1_fun/ppermute | solution.py:566
  141.8 3.3 %collective-permute-done.5.refs_1_ = bf16[112,256]{1,0:T(8,128)(2,1)S(1)} collective-permute-done((bf16[112,256]{1,0:T(8,128)(2,1)S(1)}, bf16[112,256]{1,0:T(8,128)(2,1)S(1)}, u32[]{:S(2)}, u32[]{:S(2)}) %collective-permute-start.5) | collective-permute-done | bytes 57376 | tf_op jit(solution)/shard_map/cond/branch_1_fun/ppermute | solution.py:474
  145.9 4.0 %collective-permute-done.6.refs_1_ = bf16[2,112,256]{2,1,0:T(8,128)(2,1)S(1)} collective-permute-done((bf16[2,112,256]{2,1,0:T(8,128)(2,1)S(1)}, bf16[2,112,256]{2,1,0:T(8,128)(2,1)S(1)}, u32[]{:S(2)}, u32[]{:S(2)}) %collective-permute-start.6) | collective-permute-done | bytes 114720 | tf_op jit(solution)/shard_map/cond/branch_1_fun/ppermute | solution.py:474
  151.5 4.8 %collective-permute-done.1.refs_1_ = bf16[2,112,256]{2,1,0:T(8,128)(2,1)S(1)} collective-permute-done((bf16[2,112,256]{2,1,0:T(8,128)(2,1)S(1)}, bf16[2,112,256]{2,1,0:T(8,128)(2,1)S(1)}, u32[]{:S(2)}, u32[]{:S(2)}) %collective-permute-start.1) | collective-permute-done | bytes 114720 | tf_op jit(solution)/shard_map/cond/branch_1_fun/ppermute | solution.py:474
  157.3 7.0 %input_grad0.1 = (f32[16,128,256]{2,1,0:T(8,128)S(1)}, bf16[16,128,256]{2,1,0:T(8,128)(2,1)S(1)}, f32[8,128]{1,0:T(8,128)}) custom-call(s32[968]{0:T(1024)S(1)} %get-tuple-element.37.blocks, s32[968]{0:T(1024)S(1)} %get-tuple-element.38.sources, s32[968]{0:T(1024)S(1)} %get-tuple-element.39.targets, s32[8]{0:T(128)S(1)} %get-tuple-element.40.counts, ...), custom_call_target="tpu_custom_call" | custom-call | flops 1000 | bytes 1000 | tf_op jit(solution)/shard_map/cond/branch_1_fun/input_grad0/pallas_call | solution.py:75
  (84 shorter events, 53.2 us)
Async XLA Ops:
  3.8 20.5 %collective-permute-start.8 = (bf16[8,128,256]{2,1,0:T(8,128)(2,1)}, bf16[8,128,256]{2,1,0:T(8,128)(2,1)S(1)}, u32[]{:S(2)}, u32[]{:S(2)}) collective-permute-start(bf16[8,128,256]{2,1,0:T(8,128)(2,1)} %get-tuple-element.123), channel_id=1, source_target_pairs={{0,1},{1,2},{2,3},{3,4},{4,5},{5,6},{6,7},{7,8},{8,9},{9,10},{10,1... | collective-permute-start | bytes 1572872 | tf_op jit(solution)/shard_map/ppermute | solution.py:63
  6.9 24.8 %collective-permute-start.9 = (bf16[8,128,256]{2,1,0:T(8,128)(2,1)}, bf16[8,128,256]{2,1,0:T(8,128)(2,1)S(1)}, u32[]{:S(2)}, u32[]{:S(2)}) collective-permute-start(bf16[8,128,256]{2,1,0:T(8,128)(2,1)} %get-tuple-element.124), channel_id=1, source_target_pairs={{0,31},{1,0},{2,1},{3,2},{4,3},{5,4},{6,5},{7,6},{8,7},{9,8},{10,9... | collective-permute-start | bytes 1572872 | tf_op jit(solution)/shard_map/ppermute | solution.py:63
  35.1 15.9 %collective-permute-start.11 = (bf16[8,128,256]{2,1,0:T(8,128)(2,1)S(1)}, bf16[8,128,256]{2,1,0:T(8,128)(2,1)S(1)}, u32[]{:S(2)}, u32[]{:S(2)}) collective-permute-start(bf16[8,128,256]{2,1,0:T(8,128)(2,1)S(1)} %get-tuple-element.126.west), channel_id=1, source_target_pairs={{0,31},{1,0},{2,1},{3,2},{4,3},{5,4},{6,5},{7,6},{8,7},{9,8},{10,9... | collective-permute-start | bytes 1572872 | tf_op jit(solution)/shard_map/ppermute | solution.py:63
  38.6 22.8 %collective-permute-start.10 = (bf16[8,128,256]{2,1,0:T(8,128)(2,1)S(1)}, bf16[8,128,256]{2,1,0:T(8,128)(2,1)S(1)}, u32[]{:S(2)}, u32[]{:S(2)}) collective-permute-start(bf16[8,128,256]{2,1,0:T(8,128)(2,1)S(1)} %get-tuple-element.127.east), channel_id=1, source_target_pairs={{0,1},{1,2},{2,3},{3,4},{4,5},{5,6},{6,7},{7,8},{8,9},{9,10},{10,1... | collective-permute-start | bytes 1572872 | tf_op jit(solution)/shard_map/ppermute | solution.py:63
  69.7 36.0 %collective-permute-start.12 = (bf16[8,128,256]{2,1,0:T(8,128)(2,1)S(1)}, bf16[8,128,256]{2,1,0:T(8,128)(2,1)S(1)}, u32[]{:S(2)}, u32[]{:S(2)}) collective-permute-start(bf16[8,128,256]{2,1,0:T(8,128)(2,1)S(1)} %get-tuple-element.146), channel_id=1, source_target_pairs={{0,1},{1,2},{2,3},{3,4},{4,5},{5,6},{6,7},{7,8},{8,9},{9,10},{10,1... | collective-permute-start | bytes 1572872 | tf_op jit(solution)/shard_map/ppermute | solution.py:63
  72.7 33.1 %collective-permute-start.13 = (bf16[8,128,256]{2,1,0:T(8,128)(2,1)S(1)}, bf16[8,128,256]{2,1,0:T(8,128)(2,1)S(1)}, u32[]{:S(2)}, u32[]{:S(2)}) collective-permute-start(bf16[8,128,256]{2,1,0:T(8,128)(2,1)S(1)} %get-tuple-element.147), channel_id=1, source_target_pairs={{0,31},{1,0},{2,1},{3,2},{4,3},{5,4},{6,5},{7,6},{8,7},{9,8},{10,9... | collective-permute-start | bytes 1572872 | tf_op jit(solution)/shard_map/ppermute | solution.py:63
  80.8 6.0 %collective-permute-start.15 = (bf16[2,112,256]{2,1,0:T(8,128)(2,1)S(1)}, bf16[2,112,256]{2,1,0:T(8,128)(2,1)S(1)}, u32[]{:S(2)}, u32[]{:S(2)}) collective-permute-start(bf16[2,112,256]{2,1,0:T(8,128)(2,1)S(1)} %get-tuple-element.157), channel_id=1, source_target_pairs={{0,16},{4,20},{16,0},{20,4},{8,24},{12,28},{24,8},{28,12},{1,17},{... | collective-permute-start | bytes 344072 | tf_op jit(solution)/shard_map/ppermute | solution.py:474
  86.8 18.9 %collective-permute-start.16 = (bf16[112,256]{1,0:T(8,128)(2,1)S(1)}, bf16[112,256]{1,0:T(8,128)(2,1)S(1)}, u32[]{:S(2)}, u32[]{:S(2)}) collective-permute-start(bf16[112,256]{1,0:T(8,128)(2,1)S(1)} %get-tuple-element.159), channel_id=1, source_target_pairs={{0,4},{4,0},{16,20},{20,16},{8,12},{12,8},{24,28},{28,24},{1,5},{5... | collective-permute-start | bytes 172040 | tf_op jit(solution)/shard_map/ppermute | solution.py:474
  109.5 54.8 %collective-permute-start.17 = (bf16[8,128,256]{2,1,0:T(8,128)(2,1)S(1)}, bf16[8,128,256]{2,1,0:T(8,128)(2,1)S(1)}, u32[]{:S(2)}, u32[]{:S(2)}) collective-permute-start(bf16[8,128,256]{2,1,0:T(8,128)(2,1)S(1)} %get-tuple-element.170), channel_id=1, source_target_pairs={{0,1},{1,2},{2,3},{3,4},{4,5},{5,6},{6,7},{7,8},{8,9},{9,10},{10,1... | collective-permute-start | bytes 1572872 | tf_op jit(solution)/shard_map/ppermute | solution.py:63
  109.6 54.8 %collective-permute-start.18 = (bf16[8,128,256]{2,1,0:T(8,128)(2,1)S(1)}, bf16[8,128,256]{2,1,0:T(8,128)(2,1)S(1)}, u32[]{:S(2)}, u32[]{:S(2)}) collective-permute-start(bf16[8,128,256]{2,1,0:T(8,128)(2,1)S(1)} %get-tuple-element.171), channel_id=1, source_target_pairs={{0,31},{1,0},{2,1},{3,2},{4,3},{5,4},{6,5},{7,6},{8,7},{9,8},{10,9... | collective-permute-start | bytes 1572872 | tf_op jit(solution)/shard_map/ppermute | solution.py:63
  119.0 16.5 %collective-permute-start.3 = (bf16[112,256]{1,0:T(8,128)(2,1)S(1)}, bf16[112,256]{1,0:T(8,128)(2,1)S(1)}, u32[]{:S(2)}, u32[]{:S(2)}) collective-permute-start(bf16[112,256]{1,0:T(8,128)(2,1)S(1)} %get-tuple-element.36.refs_0_), channel_id=1, source_target_pairs={{0,1},{1,0},{2,3},{3,2},{4,5},{5,4},{6,7},{7,6},{8,9},{9,8},{10,11... | collective-permute-start | bytes 172040 | tf_op jit(solution)/shard_map/cond/branch_1_fun/ppermute | solution.py:566
  135.5 5.2 %collective-permute-start.4 = (bf16[112,256]{1,0:T(8,128)(2,1)S(1)}, bf16[112,256]{1,0:T(8,128)(2,1)S(1)}, u32[]{:S(2)}, u32[]{:S(2)}) collective-permute-start(bf16[112,256]{1,0:T(8,128)(2,1)S(1)} %added.11.refs_0_), channel_id=1, source_target_pairs={{0,2},{1,3},{2,0},{3,1},{4,6},{5,7},{6,4},{7,5},{8,10},{9,11},{10,... | collective-permute-start | bytes 172040 | tf_op jit(solution)/shard_map/cond/branch_1_fun/ppermute | solution.py:566
  136.9 13.7 %collective-permute-start = (bf16[2,2,112,256]{3,2,1,0:T(8,128)(2,1)S(1)}, bf16[2,2,112,256]{3,2,1,0:T(8,128)(2,1)S(1)}, u32[]{:S(2)}, u32[]{:S(2)}) collective-permute-start(bf16[2,2,112,256]{3,2,1,0:T(8,128)(2,1)S(1)} %get-tuple-element.31), channel_id=1, source_target_pairs={{0,8},{4,12},{16,24},{20,28},{8,0},{12,4},{24,16},{28,20},{1,9},{5... | collective-permute-start | bytes 688136 | tf_op jit(solution)/shard_map/cond/branch_1_fun/ppermute | solution.py:474
  145.0 4.9 %collective-permute-start.6 = (bf16[2,112,256]{2,1,0:T(8,128)(2,1)S(1)}, bf16[2,112,256]{2,1,0:T(8,128)(2,1)S(1)}, u32[]{:S(2)}, u32[]{:S(2)}) collective-permute-start(bf16[2,112,256]{2,1,0:T(8,128)(2,1)S(1)} %stacked.2.refs_0_), channel_id=1, source_target_pairs={{0,16},{4,20},{16,0},{20,4},{8,24},{12,28},{24,8},{28,12},{1,17},{... | collective-permute-start | bytes 344072 | tf_op jit(solution)/shard_map/cond/branch_1_fun/ppermute | solution.py:474
  150.6 13.7 %collective-permute-start.7 = (bf16[2,2,112,256]{3,2,1,0:T(8,128)(2,1)}, bf16[2,2,112,256]{3,2,1,0:T(8,128)(2,1)}, u32[]{:S(2)}, u32[]{:S(2)}) collective-permute-start(bf16[2,2,112,256]{3,2,1,0:T(8,128)(2,1)} %stacked.3), channel_id=1, source_target_pairs={{0,8},{4,12},{16,24},{20,28},{8,0},{12,4},{24,16},{28,20},{1,9},{5... | collective-permute-start | bytes 688136 | tf_op jit(solution)/shard_map/cond/branch_1_fun/ppermute | solution.py:474
  150.7 5.6 %collective-permute-start.1 = (bf16[2,112,256]{2,1,0:T(8,128)(2,1)S(1)}, bf16[2,112,256]{2,1,0:T(8,128)(2,1)S(1)}, u32[]{:S(2)}, u32[]{:S(2)}) collective-permute-start(bf16[2,112,256]{2,1,0:T(8,128)(2,1)S(1)} %get-tuple-element.33), channel_id=1, source_target_pairs={{0,16},{4,20},{16,0},{20,4},{8,24},{12,28},{24,8},{28,12},{1,17},{... | collective-permute-start | bytes 344072 | tf_op jit(solution)/shard_map/cond/branch_1_fun/ppermute | solution.py:474
  156.3 8.0 %collective-permute-start.2 = (bf16[112,256]{1,0:T(8,128)(2,1)S(1)}, bf16[112,256]{1,0:T(8,128)(2,1)}, u32[]{:S(2)}, u32[]{:S(2)}) collective-permute-start(bf16[112,256]{1,0:T(8,128)(2,1)S(1)} %get-tuple-element.35), channel_id=1, source_target_pairs={{0,4},{4,0},{16,20},{20,16},{8,12},{12,8},{24,28},{28,24},{1,5},{5... | collective-permute-start | bytes 172040 | tf_op jit(solution)/shard_map/cond/branch_1_fun/ppermute | solution.py:474
  165.2 6.4 %collective-permute-start.21 = (bf16[112,256]{1,0:T(8,128)(2,1)S(1)}, bf16[112,256]{1,0:T(8,128)(2,1)S(1)}, u32[]{:S(2)}, u32[]{:S(2)}) collective-permute-start(bf16[112,256]{1,0:T(8,128)(2,1)S(1)} %added.16.refs_0_), channel_id=1, source_target_pairs={{0,3},{1,2},{2,1},{3,0},{4,7},{5,6},{6,5},{7,4},{8,11},{9,10},{10,... | collective-permute-start | bytes 172040 | tf_op jit(solution)/shard_map/ppermute | solution.py:576
  166.5 6.2 %collective-permute-start.20 = (bf16[112,256]{1,0:T(8,128)(2,1)S(1)}, bf16[112,256]{1,0:T(8,128)(2,1)S(1)}, u32[]{:S(2)}, u32[]{:S(2)}) collective-permute-start(bf16[112,256]{1,0:T(8,128)(2,1)S(1)} %added.16.refs_0_), channel_id=1, source_target_pairs={{0,2},{1,3},{2,0},{3,1},{4,6},{5,7},{6,4},{7,5},{8,10},{9,11},{10,... | collective-permute-start | bytes 172040 | tf_op jit(solution)/shard_map/ppermute | solution.py:576
  166.9 5.7 %collective-permute-start.19 = (bf16[112,256]{1,0:T(8,128)(2,1)S(1)}, bf16[112,256]{1,0:T(8,128)(2,1)S(1)}, u32[]{:S(2)}, u32[]{:S(2)}) collective-permute-start(bf16[112,256]{1,0:T(8,128)(2,1)S(1)} %added.16.refs_0_), channel_id=1, source_target_pairs={{0,1},{1,0},{2,3},{3,2},{4,5},{5,4},{6,7},{7,6},{8,9},{9,8},{10,11... | collective-permute-start | bytes 172040 | tf_op jit(solution)/shard_map/ppermute | solution.py:576
  172.7 5.5 %collective-permute-start.28 = (bf16[112,256]{1,0:T(8,128)(2,1)S(1)}, bf16[112,256]{1,0:T(8,128)(2,1)S(1)}, u32[]{:S(2)}, u32[]{:S(2)}) collective-permute-start(bf16[112,256]{1,0:T(8,128)(2,1)S(1)} %added.17.refs_0_), channel_id=1, source_target_pairs={{0,28},{4,24},{16,12},{20,8},{8,20},{12,16},{24,4},{28,0},{1,29},{... | collective-permute-start | bytes 172040 | tf_op jit(solution)/shard_map/ppermute | solution.py:474
  174.9 7.7 %collective-permute-start.26 = (bf16[112,256]{1,0:T(8,128)(2,1)S(1)}, bf16[112,256]{1,0:T(8,128)(2,1)S(1)}, u32[]{:S(2)}, u32[]{:S(2)}) collective-permute-start(bf16[112,256]{1,0:T(8,128)(2,1)S(1)} %added.17.refs_0_), channel_id=1, source_target_pairs={{0,12},{4,8},{16,28},{20,24},{8,4},{12,0},{24,20},{28,16},{1,13},{... | collective-permute-start | bytes 172040 | tf_op jit(solution)/shard_map/ppermute | solution.py:474
  175.4 7.1 %collective-permute-start.25 = (bf16[112,256]{1,0:T(8,128)(2,1)S(1)}, bf16[112,256]{1,0:T(8,128)(2,1)S(1)}, u32[]{:S(2)}, u32[]{:S(2)}) collective-permute-start(bf16[112,256]{1,0:T(8,128)(2,1)S(1)} %added.17.refs_0_), channel_id=1, source_target_pairs={{0,8},{4,12},{16,24},{20,28},{8,0},{12,4},{24,16},{28,20},{1,9},{5... | collective-permute-start | bytes 172040 | tf_op jit(solution)/shard_map/ppermute | solution.py:474
  176.1 6.5 %collective-permute-start.24 = (bf16[112,256]{1,0:T(8,128)(2,1)S(1)}, bf16[112,256]{1,0:T(8,128)(2,1)S(1)}, u32[]{:S(2)}, u32[]{:S(2)}) collective-permute-start(bf16[112,256]{1,0:T(8,128)(2,1)S(1)} %added.17.refs_0_), channel_id=1, source_target_pairs={{0,20},{4,16},{16,4},{20,0},{8,28},{12,24},{24,12},{28,8},{1,21},{... | collective-permute-start | bytes 172040 | tf_op jit(solution)/shard_map/ppermute | solution.py:474
  (14 other events, 121.2 us)

commit v7 on v6

--- a/solution.py
+++ b/solution.py
@@ -217,22 +217,26 @@
     )
 
 
-def turn(z, w_self, w_nbr, w_out):
-    def kernel(ws, wn, wo, wt):
+def turn(z, adj, w_self, w_nbr, w_out):
+    def kernel(adj, ws, wn, wo, at, wt):
         for layer in range(2):
             wt[layer, 0] = ws[layer].T
             wt[layer, 1] = wn[layer].T
             wt[layer, 2] = wo[layer].T
 
+        @pl.loop(0, z.pairs, unroll=4)
+        def _(i):
+            at[i] = adj[i].T
+
     return call(
         kernel,
         "turn",
-        [VMEM] * 3,
-        VMEM,
-        jax.ShapeDtypeStruct((2, 3, z.cols, z.cols), BF16),
+        [VMEM] * 4,
+        [VMEM, VMEM],
+        [jax.ShapeDtypeStruct(adj.shape, BF16), jax.ShapeDtypeStruct((2, 3, z.cols, z.cols), BF16)],
         [],
-        6,
-        (w_self, w_nbr, w_out),
+        12,
+        (adj, w_self, w_nbr, w_out),
     )
 
 
@@ -362,7 +366,9 @@
 
 
 def saved(z, f0, agg0, w_self, w_nbr, bias):
-    def kernel(f_lent, f_rest, a_lent, a_rest, ws, wn, bias, act, slope):
+    def kernel(f_lent, f_rest, a_lent, a_rest, ws, wn, bias, act, slope, token):
+        token[...] = jnp.zeros_like(token)
+
         def work(part, first):
             f = z.flat(group_of(z, (f_lent, f_rest), part, first)[...])
             aggs = z.flat(group_of(z, (a_lent, a_rest), part, first)[...])
@@ -378,15 +384,15 @@
         kernel,
         "saved",
         [VMEM] * 7,
-        [VMEM] * 2,
-        [z.nodes(z.tiles), z.nodes(z.tiles, F32)],
+        [VMEM] * 3,
+        [z.nodes(z.tiles), z.nodes(z.tiles, F32), TOKEN],
         [],
         10,
         (*f0, *agg0, w_self, w_nbr, bias),
     )
 
 
-def spread(z, tables, table, count, adj, source, acc, add):
+def spread(z, tables, table, count, at, source, acc, add):
     blocks, sources, targets, counts = tables
     x = z.index
 
@@ -396,8 +402,8 @@
         lefts, rights = [], []
         for k in range(x.QUAD):
             block = blocks[base + k]
-            left = adj[jnp.maximum(block, 0)]
-            lefts.append(jnp.where(block >= 0, left, jnp.zeros_like(left)).T)
+            left = at[jnp.maximum(block, 0)]
+            lefts.append(jnp.where(block >= 0, left, jnp.zeros_like(left)))
             rights.append(source(sources[base + k]))
         value = dot(jnp.concatenate(lefts, axis=1), jnp.concatenate(rights, axis=0))
         if add:
@@ -407,12 +413,13 @@
 
     @pl.loop(0, counts[table])
     def _(i):
-        at = x.more[table] + i
-        acc[targets[at]] += dot(adj[blocks[at]].T, source(sources[at]))
-
-
-def second(z, tiles, reads, tables, f1, fw, fe, adj, hidden, w_self, w_nbr, bias, wt):
-    def kernel(tiles, reads, blocks, sources, targets, counts, f_lent, f_rest, fw, fe, adj, hidden, ws, wn, bias, wt,
+        place = x.more[table] + i
+        acc[targets[place]] += dot(at[blocks[place]], source(sources[place]))
+
+
+def second(z, tiles, reads, tables, f1, fw, fe, adj, at, hidden, w_self, w_nbr, bias, wt, after):
+    def kernel(tiles, reads, blocks, sources, targets, counts, f_lent, f_rest, fw, fe, adj, at, hidden, ws, wn,
+               bias, wt, _after,
                agg, act, dpre, dagg, to_west, to_east, ext, acc):
         fill_extended(z, (f_lent, f_rest), fw, fe, ext)
 
@@ -428,19 +435,19 @@
             dagg[here] = z.tiled(dot(grad, wt[1, 1]).astype(BF16))
 
         each_group(z, work, unroll=2)
-        spread(z, (blocks, sources, targets, counts), 1, z.lent, adj, lambda q: dagg[q], acc, False)
+        spread(z, (blocks, sources, targets, counts), 1, z.lent, at, lambda q: dagg[q], acc, False)
         to_west[...] = acc[pl.ds(0, z.edge)].astype(BF16)
         to_east[...] = acc[pl.ds(z.edge, z.edge)].astype(BF16)
 
     return call(
         kernel,
         "second",
-        [SMEM] * 6 + [VMEM] * 10,
+        [SMEM] * 6 + [VMEM] * 12,
         [VMEM] * 6,
         [z.nodes(z.tiles)] * 4 + [z.nodes(z.edge)] * 2,
         [z.held(z.ext), z.held(z.lent, F32)],
         12,
-        (tiles, reads, *tables, *f1, fw, fe, adj, hidden, w_self, w_nbr, bias, wt),
+        (tiles, reads, *tables, *f1, fw, fe, adj, at, hidden, w_self, w_nbr, bias, wt, after),
     )
 
 
@@ -521,7 +528,7 @@
     )
 
 
-def added(values, split=False, after=(), pairs=False):
+def added(values, split=False, after=()):
     shape = values[0].shape
     count = shape[0] if split else 1
 
@@ -530,8 +537,6 @@
         for i, out in enumerate(outs):
             parts = [ref[i] if split else ref[...] for ref in refs[: len(values)]]
             parts = [part.astype(F32) for part in parts]
-            if pairs:
-                parts = [parts[0] + parts[1], parts[2] + parts[3]]
             total = parts[0]
             for part in parts[1:]:
                 total = total + part
@@ -551,10 +556,30 @@
     return outs if split else outs[0]
 
 
-def plane_parts(plane, pieces):
-    parts = added(plane.received(pieces, 0), split=True)
-    parts = added(plane.received(parts, 1), split=True)
+def plane_parts(plane, pieces, after=((), ())):
+    parts = added(plane.received(pieces, 0), split=True, after=after[0])
+    parts = added(plane.received(parts, 1), split=True, after=after[1])
     return plane.received(parts, 2)
+
+
+def joined(parts, other, after):
+    def kernel(*refs):
+        total = refs[0][...].astype(F32)
+        for ref in refs[1 : len(parts)]:
+            total = total + ref[...].astype(F32)
+        refs[-1][0] = total.astype(BF16)
+        refs[-1][1] = refs[len(parts)][...]
+
+    return call(
+        kernel,
+        "joined",
+        [VMEM] * (len(parts) + 1) + [ANY] * len(after),
+        VMEM,
+        jax.ShapeDtypeStruct((2,) + other.shape, BF16),
+        [],
+        8,
+        (*parts, other, *after),
+    )
 
 
 def line_sum(share):
@@ -569,14 +594,6 @@
     return share
 
 
-def line_sum_at_once(share):
-    lines = lax.axis_size("feat")
-    if lines != 4:
-        return line_sum(share)
-    others = [lax.ppermute(share, "feat", [(i, i ^ s) for i in range(lines)]) for s in (1, 2, 3)]
-    return added([share, *others], pairs=True)
-
-
 def stacked(values):
     def kernel(*refs):
         for i, ref in enumerate(refs[:-1]):
@@ -588,16 +605,11 @@
 
 
 def plane_gathered(plane, share):
-    for dim in (2, 1):
-        size = plane.sizes[dim]
-        share = stacked([share] + [plane.passed(share, dim, i) for i in range(1, size)])
-    return [share] + [plane.passed(share, 0, i) for i in range(1, plane.sizes[0])]
-
-
-def plane_gathered_at_once(plane, share):
     core, ahead, side = plane.sizes
-    steps = [(i, j, k) for i in range(core) for j in range(ahead) for k in range(side)]
-    return [share] + [plane.passed_by(share, by) for by in steps[1:]]
+    steps = [(0, j, k) for j in range(ahead) for k in range(side)]
+    share = stacked([share] + [plane.passed_by(share, by) for by in steps[1:]])
+    share = share.reshape(ahead, side, *share.shape[-3:])
+    return [share] + [plane.passed(share, 0, i) for i in range(1, core)]
 
 
 def second_out(z, bound, live, f1, act, w_out, out):
@@ -638,7 +650,7 @@
     )
 
 
-def input_grad(z, layer, tables, m, dpre, dagg, adj, wt):
+def input_grad(z, layer, tables, m, dpre, dagg, at, wt):
     arrays = (m, dpre, dagg)
     flat_args = [x for a in arrays for x in (a if isinstance(a, tuple) else (a,))]
 
@@ -647,7 +659,7 @@
         m, dpre, dagg = [
             (refs.pop(0), refs.pop(0)) if isinstance(a, tuple) else refs.pop(0) for a in arrays
         ]
-        adj, wt, part_out, rest_out, token, acc = refs
+        at, wt, part_out, rest_out, token, acc = refs
         token[...] = jnp.zeros_like(token)
 
         def direct(part, first):
@@ -664,7 +676,7 @@
             rest = dagg[1][jnp.maximum(q - z.lent, 0)]
             return jnp.where(q < z.lent, lent, rest)
 
-        spread(z, (blocks, sources, targets, counts), 0, z.tiles, adj, source, acc, True)
+        spread(z, (blocks, sources, targets, counts), 0, z.tiles, at, source, acc, True)
         part_out[...] = acc[pl.ds(0, z.lent)]
         rest_out[...] = acc[pl.ds(z.lent, z.rest)].astype(BF16)
 
@@ -676,12 +688,12 @@
         [z.nodes(z.lent, F32), z.nodes(z.rest), TOKEN],
         [z.held(z.tiles, F32)],
         20,
-        [*tables, *flat_args, adj, wt],
-    )
-
-
-def early_rest(z, tables, live, upstream, slope, adj, wt):
-    def kernel(blocks, sources, targets, counts, live, g, slope, adj, wt, grads, m, dpre, dagg, outer, sem):
+        [*tables, *flat_args, at, wt],
+    )
+
+
+def early_rest(z, tables, live, upstream, slope, at, wt):
+    def kernel(blocks, sources, targets, counts, live, g, slope, at, wt, grads, m, dpre, dagg, outer, sem):
         copy = pltpu.make_async_copy(g, grads.at[1, pl.ds(z.lent, z.rest)], sem)
         copy.start()
 
@@ -699,7 +711,7 @@
         def source(q):
             return dagg[jnp.maximum(q - z.lent, 0)]
 
-        spread(z, (blocks, sources, targets, counts), 3, z.lent, adj, source, outer, False)
+        spread(z, (blocks, sources, targets, counts), 3, z.lent, at, source, outer, False)
         copy.wait()
 
     return call(
@@ -712,12 +724,12 @@
         + [z.nodes(z.lent, F32)],
         [pltpu.SemaphoreType.DMA],
         14,
-        (*tables, live, upstream, slope, adj, wt),
-    )
-
-
-def early_lent(z, tables, bound, part, fw, fe, slope, outer, adj, wt, grads, after):
-    def kernel(blocks, sources, targets, counts, bound, part, fw, fe, slope, outer, adj, wt, _g, _ready, _late,
+        (*tables, live, upstream, slope, at, wt),
+    )
+
+
+def early_lent(z, tables, bound, part, fw, fe, slope, outer, at, wt, grads, after):
+    def kernel(blocks, sources, targets, counts, bound, part, fw, fe, slope, outer, at, wt, _g, _ready, _late,
                m, dpre, dagg, grads, to_west, to_east, acc, sems):
         def work(first, got):
             here = pl.ds(first, z.group)
@@ -744,7 +756,7 @@
         def source(q):
             return dagg[jnp.minimum(q, z.lent - 1)]
 
-        spread(z, (blocks, sources, targets, counts), 2, z.lent, adj, source, acc, True)
+        spread(z, (blocks, sources, targets, counts), 2, z.lent, at, source, acc, True)
         to_west[...] = acc[pl.ds(0, z.edge)].astype(BF16)
         to_east[...] = acc[pl.ds(z.edge, z.edge)].astype(BF16)
         for copy in copies:
@@ -758,7 +770,7 @@
         [z.nodes(z.lent)] * 3 + [jax.ShapeDtypeStruct(grads.shape, BF16)] + [z.nodes(z.edge)] * 2,
         [z.held(z.lent, F32), pltpu.SemaphoreType.DMA((z.lent,))],
         16,
-        (*tables, bound, part, fw, fe, slope, outer, adj, wt, grads, *after),
+        (*tables, bound, part, fw, fe, slope, outer, at, wt, grads, *after),
         {12: 3},
     )
 
@@ -791,40 +803,41 @@
     )
 
 
-def unpack(z, plane, early, late):
+def unpack(z, plane, pieces):
     c = z.cols
-    piece = early[0].shape[0]
+    piece = pieces[0].shape[3]
     core, ahead, side = plane.sizes
 
     def kernel(me, *refs):
-        refs = list(refs)
-        early, late = refs[: plane.count], refs[plane.count : plane.count + core]
-        g_self, g_nbr, g_bias, g_out, buf = refs[plane.count + core :]
+        pieces = refs[:core]
+        *outs, bias, buf, sems = refs[core:]
+        copies = []
         for layer in range(2):
             for i in range(core):
                 for j in range(ahead):
                     for k in range(side):
                         start = pl.multiple_of(plane.piece_of(me, (-i, -j, -k)) * piece, 16)
-                        if layer == 0:
-                            got = early[(i * ahead + j) * side + k][...]
-                        else:
-                            got = late[i][j, k]
-                        buf[pl.ds(start, piece), :] = got.astype(F32)
-            g_self[layer] = buf[pl.ds(0, c), :]
-            g_nbr[layer] = buf[pl.ds(c, c), :]
-            g_out[layer] = buf[pl.ds(2 * c, c), :]
-            g_bias[layer : layer + 1, :] = buf[pl.ds(3 * c, 1), :]
+                        buf[layer, pl.ds(start, piece), :] = pieces[i][j, k, layer].astype(F32)
+            for i, out in enumerate(outs):
+                copy = pltpu.make_async_copy(
+                    buf.at[layer, pl.ds(i * c, c)], out.at[layer], sems.at[3 * layer + i]
+                )
+                copy.start()
+                copies.append(copy)
+            bias[layer : layer + 1, :] = buf[layer, pl.ds(3 * c, 1), :]
+        for copy in copies:
+            copy.wait()
 
     square = jax.ShapeDtypeStruct((2, c, c), F32)
     return call(
         kernel,
         "unpack",
-        [SMEM] + [VMEM] * (plane.count + core),
-        [VMEM] * 4,
-        [square, square, jax.ShapeDtypeStruct((2, c), F32), square],
-        [pltpu.VMEM((piece * plane.count, c), F32)],
+        [SMEM] + [VMEM] * core,
+        [ANY] * 3 + [VMEM],
+        [square, square, square, jax.ShapeDtypeStruct((2, c), F32)],
+        [pltpu.VMEM((2, piece * plane.count, c), F32), pltpu.SemaphoreType.DMA((6,))],
         10,
-        (plane.me, *early, *late),
+        (plane.me, *pieces),
     )
 
 
@@ -845,7 +858,7 @@
     )
     f0, m1 = tuple(nodes[:2]), tuple(nodes[2:])
     tables = (blocks, sources, targets, counts)
-    wt = turn(z, w_self, w_nbr, w_out)
+    at, wt = turn(z, adj, w_self, w_nbr, w_out)
 
     west, east, agg_lent = first_lent(
         z, tiles, reads, f0, from_west, from_east, adj, w_self, w_nbr, pre_bias, w_out
@@ -858,45 +871,47 @@
     )
     f1, agg0 = (f1_lent, f1_rest), (agg_lent, agg_rest)
     hidden = second_own(z, m1, wt)
+    act0, slope, ready = saved(z, f0, agg0, w_self, w_nbr, pre_bias)
 
     agg1, act1, dpre1, dagg1, to_west, to_east = second(
-        z, tiles, reads, tables, f1, next_west, next_east, adj, hidden, w_self, w_nbr, pre_bias, wt
+        z, tiles, reads, tables, f1, next_west, next_east, adj, at, hidden, w_self, w_nbr, pre_bias, wt, ready
     )
     back_west = passed_along(to_east, 1)
     back_east = passed_along(to_west, -1)
     late = weight_grads(z, plane, f1, agg1, act1, m1, dpre1, "weight_grads1")
-    late = added(plane_parts(plane, late))
-    part, upstream, _ = input_grad(z, 1, tables, m1, dpre1, dagg1, adj, wt)
     section_out, ready = second_out(z, bound_tiles, live_tiles, f1, act1, w_out, section_out)
-    act0, slope = saved(z, f0, agg0, w_self, w_nbr, pre_bias)
+    part, upstream, done = input_grad(z, 1, tables, m1, dpre1, dagg1, at, wt)
+    late = plane_parts(plane, late, ((ready,), (done,)))
     grads, m0_rest, dpre_rest, dagg_rest, outer = early_rest(
-        z, tables, live_tiles, upstream, slope, adj, wt
-    )
+        z, tables, live_tiles, upstream, slope, at, wt
+    )
+    late = added(late, after=(outer,))
 
     m0_lent, dpre_lent, dagg_lent, grads, to_west, to_east = early_lent(
-        z, tables, bound_tiles, part, back_west, back_east, slope, outer, adj, wt, grads, (ready, late)
+        z, tables, bound_tiles, part, back_west, back_east, slope, outer, at, wt, grads, (ready, late)
     )
     back_west = passed_along(to_east, 1)
     back_east = passed_along(to_west, -1)
     m0, dpre0, dagg0 = (m0_lent, m0_rest), (dpre_lent, dpre_rest), (dagg_lent, dagg_rest)
     early = weight_grads(z, plane, f0, agg0, act0, m0, dpre0, "weight_grads0")
 
-    def meanwhile(early, late, tables, m0, dpre0, dagg0, adj, wt):
-        part, rest, _ = input_grad(z, 0, tables, m0, dpre0, dagg0, adj, wt)
-        return plane_parts(plane, early), plane_gathered(plane, line_sum(late)), part, rest
-
-    args = (early, late, tables, m0, dpre0, dagg0, adj, wt)
+
+    def meanwhile(early, tables, m0, dpre0, dagg0, at, wt):
+        part, rest, _ = input_grad(z, 0, tables, m0, dpre0, dagg0, at, wt)
+        return plane_parts(plane, early), part, rest
+
+    args = (early, tables, m0, dpre0, dagg0, at, wt)
     shapes = jax.eval_shape(meanwhile, *args)
-    early, late, part, rest = lax.cond(
+    early, part, rest = lax.cond(
         live_tiles[0] > 0,
         meanwhile,
         lambda *_: jax.tree.map(lambda a: jnp.zeros(a.shape, a.dtype), shapes),
         *args,
     )
-    early = line_sum_at_once(added(early, after=(back_west, back_east)))
-    early = plane_gathered_at_once(plane, early)
+    shares = line_sum(joined(early, late, (back_west, back_east)))
+    pieces = plane_gathered(plane, shares)
     grads = finish(z, bound_tiles, part, rest, back_west, back_east, grads)
-    grad_self, grad_nbr, grad_bias, grad_out = unpack(z, plane, early, late)
+    grad_self, grad_nbr, grad_out, grad_bias = unpack(z, plane, pieces)
     return (
         section_out.reshape(2, t * r, c),
         grads.reshape(2, t * r, c),

time: 186 us -> 152 us (0.82)
  waiting for transfers between devices: 63.7 us -> 34.6 us
  starting transfers between devices: 42.6 us -> 37.5 us
    ppermute x2, waiting for transfers between devices: 20.3 us -> 8.6 us  [line_sum(): other = lax.ppermute(share, 'feat', [(i, i ^ step) for i in range(lines)])]
    ppermute x8, waiting for transfers between devices: 23.5 us -> 15.4 us  [passed_along(): lax.ppermute(value, AXES, [(i, (i + steps) % count) for i in range(count)])]
    ppermute x16 -> x10, starting transfers between devices: 15.9 us -> 9.33 us  [passed_by(): return lax.ppermute(value, PLANE, pairs)]
    ppermute x16 -> x10, waiting for transfers between devices: 17 us -> 10.7 us  [passed_by(): return lax.ppermute(value, PLANE, pairs)]
    ppermute x3 -> x0, starting transfers between devices: 4.45 us -> none  [line_sum_at_once(): lax.ppermute(share, 'feat', [(i, i ^ s) for i in range(lines)])]
    ppermute x2, starting transfers between devices: 1.46 us -> 5.52 us  [line_sum(): other = lax.ppermute(share, 'feat', [(i, i ^ step) for i in range(lines)])]
    ppermute x3 -> x0, waiting for transfers between devices: 3 us -> none  [line_sum_at_once(): lax.ppermute(share, 'feat', [(i, i ^ s) for i in range(lines)])]
    ppermute x8, starting transfers between devices: 20.8 us -> 22.7 us  [passed_along(): lax.ppermute(value, AXES, [(i, (i + steps) % count) for i in range(count)])]
  transfers between devices with their start and end apart: 29 -> 20, of which waited for: 13 -> 8; matrix products, arithmetic and copies ran while one was open for 0% -> 0% of each run, Pallas kernels for 28% -> 34%
where the time goes in v7:
time: 152 us
  Pallas kernels  73.8 us (49%)
  starting transfers between devices  37.5 us (25%)
  waiting for transfers between devices  34.6 us (23%)
  local copies, waits for them, and re-layouts  3.98 us (3%)
  between operations  1.75 us (1%)
    pallas_call x26, Pallas kernels, call(): pl.pallas_call(kernel, in_specs=in_specs, out_specs=out_specs, out_shape=...  73.8 us
    ppermute x8, starting transfers between devices, passed_along(): lax.ppermute(value, AXES, [(i, (i + steps) % count) for i in range(count)])  22.7 us
    ppermute x8, waiting for transfers between devices, passed_along(): lax.ppermute(value, AXES, [(i, (i + steps) % count) for i in range(count)])  15.4 us
    ppermute x10, waiting for transfers between devices, passed_by(): return lax.ppermute(value, PLANE, pairs)  10.7 us
    ppermute x10, starting transfers between devices, passed_by(): return lax.ppermute(value, PLANE, pairs)  9.33 us
    ppermute x2, waiting for transfers between devices, line_sum(): other = lax.ppermute(share, 'feat', [(i, i ^ step) for i in range(lines)])  8.6 us
    ppermute x2, starting transfers between devices, line_sum(): other = lax.ppermute(share, 'feat', [(i, i ^ step) for i in range(lines)])  5.52 us
    unnamed x19, local copies, waits for them, and re-layouts  3.89 us
  transfers between devices with their start and end apart: 20, of which 8 were waited for; matrix products, arithmetic and copies ran while one was open for 0% of the time, Pallas kernels for 34%

profile of v7, /device:TPU:0, one launch (start us, length us, event | category | flops | bytes accessed | tf_op | source)
XLA Modules:
  0.0 151.7 jit_solution(6886323979926433866)
XLA Ops:
  0.7 3.2 %lend.1 = (bf16[8,128,256]{2,1,0:T(8,128)(2,1)}, bf16[8,128,256]{2,1,0:T(8,128)(2,1)}) custom-call(s32[1,2,8]{2,1,0:T(2,128)} %bound.11, bf16[32,128,256]{2,1,0:T(8,128)(2,1)} %bitcast.10), custom_call_target="tpu_custom_call" | custom-call | flops 1000 | bytes 1000 | tf_op jit(solution)/shard_map/lend/pallas_call | solution.py:75
  3.8 3.1 %collective-permute-start.3 = (bf16[8,128,256]{2,1,0:T(8,128)(2,1)}, bf16[8,128,256]{2,1,0:T(8,128)(2,1)S(1)}, u32[]{:S(2)}, u32[]{:S(2)}) collective-permute-start(bf16[8,128,256]{2,1,0:T(8,128)(2,1)} %get-tuple-element.122), channel_id=1, source_target_pairs={{0,1},{1,2},{2,3},{3,4},{4,5},{5,6},{6,7},{7,8},{8,9},{9,10},{10,1... | collective-permute-start | bytes 1572872 | tf_op jit(solution)/shard_map/ppermute | solution.py:63
  6.9 3.4 %collective-permute-start.4 = (bf16[8,128,256]{2,1,0:T(8,128)(2,1)}, bf16[8,128,256]{2,1,0:T(8,128)(2,1)S(1)}, u32[]{:S(2)}, u32[]{:S(2)}) collective-permute-start(bf16[8,128,256]{2,1,0:T(8,128)(2,1)} %get-tuple-element.123), channel_id=1, source_target_pairs={{0,31},{1,0},{2,1},{3,2},{4,3},{5,4},{6,5},{7,6},{8,7},{9,8},{10,9... | collective-permute-start | bytes 1572872 | tf_op jit(solution)/shard_map/ppermute | solution.py:63
  15.0 9.4 %arrange.1 = (bf16[16,128,256]{2,1,0:T(8,128)(2,1)S(1)}, bf16[16,128,256]{2,1,0:T(8,128)(2,1)S(1)}, bf16[16,128,256]{2,1,0:T(8,128)(2,1)S(1)}, bf16[16,128,256]{...) custom-call(s32[1,2,8]{2,1,0:T(2,128)S(1)} %copy-done.6, ...), custom_call_target="tpu_custom_call" | custom-call | flops 1000 | bytes 1000 | tf_op jit(solution)/shard_map/arrange/pallas_call | solution.py:75
  24.4 7.4 %collective-permute-done.4.fe = bf16[8,128,256]{2,1,0:T(8,128)(2,1)S(1)} collective-permute-done((bf16[8,128,256]{2,1,0:T(8,128)(2,1)}, bf16[8,128,256]{2,1,0:T(8,128)(2,1)S(1)}, u32[]{:S(2)}, u32[]{:S(2)}) %collective-permute-start.4) | collective-permute-done | bytes 524320 | tf_op jit(solution)/shard_map/ppermute | solution.py:63
  31.8 3.3 %first_lent.1 = (bf16[8,128,256]{2,1,0:T(8,128)(2,1)S(1)}, bf16[8,128,256]{2,1,0:T(8,128)(2,1)S(1)}, bf16[16,128,256]{2,1,0:T(8,128)(2,1)S(1)}) custom-call(s32[32]{0:T(128)S(1)} %get-tuple-element.118.tiles, s32[128]{0:T(128)S(1)} %get-tuple-element.119.reads, bf16[16,128,256]{2,1,0:T(8,128)(2,1)S(1)} %get-tuple-element.120.f_lent.refs_0_, ...), custom_call_target="tpu_custom_call" | custom-call | flops 1000 | bytes 1000 | tf_op jit(solution)/shard_map/first_lent/pallas_call | solution.py:75
  36.7 3.8 %collective-permute-start.6 = (bf16[8,128,256]{2,1,0:T(8,128)(2,1)S(1)}, bf16[8,128,256]{2,1,0:T(8,128)(2,1)S(1)}, u32[]{:S(2)}, u32[]{:S(2)}) collective-permute-start(bf16[8,128,256]{2,1,0:T(8,128)(2,1)S(1)} %get-tuple-element.125.west), channel_id=1, source_target_pairs={{0,31},{1,0},{2,1},{3,2},{4,3},{5,4},{6,5},{7,6},{8,7},{9,8},{10,9... | collective-permute-start | bytes 1572872 | tf_op jit(solution)/shard_map/ppermute | solution.py:63
  40.4 3.1 %turn.1 = (bf16[128,128,128]{2,1,0:T(8,128)(2,1)S(1)}, bf16[2,3,256,256]{3,2,1,0:T(8,128)(2,1)S(1)}) custom-call(bf16[128,128,128]{2,1,0:T(8,128)(2,1)S(1)} %get-tuple-element.124.adj, bf16[2,256,256]{2,1,0:T(8,128)(2,1)S(1)} %copy-done.1, bf16[2,256,256]{2,1,0:T(8,128)(2,1)S(1)} %copy-done.2, bf16[2,256,256]{2,1,0:T(8,128)(2,1)S(1)} %copy-done.3), custom_call_target="tpu_custom_call" | custom-call | flops 1000 | bytes 1000 | tf_op jit(solution)/shard_map/turn/pallas_call | solution.py:75
  45.3 4.6 %first_rest.1 = (bf16[16,128,256]{2,1,0:T(8,128)(2,1)S(1)}, bf16[16,128,256]{2,1,0:T(8,128)(2,1)S(1)}, bf16[2,32,128,256]{3,2,1,0:T(8,128)(2,1)}, bf16[16,128,256]{2,1,0:T(8,128)(2,1)S(1)}) custom-call(s32[32]{0:T(128)S(1)} %get-tuple-element.118.tiles, s32[128]{0:T(128)S(1)} %get-tuple-element.119.reads, s32[1,2,8]{2,1,0:T(2,128)S(1)} %copy-done.6, ...), custom_call_target="tpu_custom_call" | custom-call | flops 1000 | bytes 1000 | tf_op jit(solution)/shard_map/first_rest/pallas_call | solution.py:75
  53.0 8.0 %collective-permute-done.6.fe = bf16[8,128,256]{2,1,0:T(8,128)(2,1)S(1)} collective-permute-done((bf16[8,128,256]{2,1,0:T(8,128)(2,1)S(1)}, bf16[8,128,256]{2,1,0:T(8,128)(2,1)S(1)}, u32[]{:S(2)}, u32[]{:S(2)}) %collective-permute-start.6) | collective-permute-done | bytes 524320 | tf_op jit(solution)/shard_map/ppermute | solution.py:63
  61.0 8.7 %second.1 = (bf16[32,128,256]{2,1,0:T(8,128)(2,1)S(1)}, bf16[32,128,256]{2,1,0:T(8,128)(2,1)S(1)}, bf16[32,128,256]{2,1,0:T(8,128)(2,1)S(1)}, bf16[32,128,256]{2...) custom-call(s32[32]{0:T(128)S(1)} %get-tuple-element.118.tiles, ...), custom_call_target="tpu_custom_call" | custom-call | flops 1000 | bytes 1000 | tf_op jit(solution)/shard_map/second/pallas_call | solution.py:75
  69.7 5.3 %collective-permute-start.8 = (bf16[8,128,256]{2,1,0:T(8,128)(2,1)S(1)}, bf16[8,128,256]{2,1,0:T(8,128)(2,1)S(1)}, u32[]{:S(2)}, u32[]{:S(2)}) collective-permute-start(bf16[8,128,256]{2,1,0:T(8,128)(2,1)S(1)} %get-tuple-element.149), channel_id=1, source_target_pairs={{0,31},{1,0},{2,1},{3,2},{4,3},{5,4},{6,5},{7,6},{8,7},{9,8},{10,9... | collective-permute-start | bytes 1572872 | tf_op jit(solution)/shard_map/ppermute | solution.py:63
  75.0 4.1 %weight_grads1.1 = (bf16[2,2,112,256]{3,2,1,0:T(8,128)(2,1)S(1)}, bf16[2,2,112,256]{3,2,1,0:T(8,128)(2,1)S(1)}) custom-call(s32[8]{0:T(128)S(1)} %get-tuple-element.143.me, bf16[16,128,256]{2,1,0:T(8,128)(2,1)S(1)} %get-tuple-element.127.f_lent.refs_0_, bf16[16,128,256]{2,1,0:T(8,128)(2,1)S(1)} %get-tuple-element.128.f_rest.refs_1_, ...), custom_call_target="tpu_custom_call" | custom-call | flops 1000 | bytes 1000 | tf_op jit(solution)/shard_map/weight_grads1/pallas_call | solution.py:75
  79.2 3.6 %second_out.1 = (bf16[2,32,128,256]{3,2,1,0:T(8,128)(2,1)}, f32[8,128]{1,0:T(8,128)S(1)}) custom-call(s32[1,2,8]{2,1,0:T(2,128)S(1)} %copy-done.6, s32[1]{0:T(128)S(6)} %copy.31.live, bf16[16,128,256]{2,1,0:T(8,128)(2,1)S(1)} %get-tuple-element.127.f_lent.refs_0_, ...), custom_call_target="tpu_custom_call", output_to_operand_aliasing={{0}: (6, {})} | custom-call | flops 1000 | bytes 1000 | tf_op jit(solution)/shard_map/second_out/pallas_call | solution.py:75
  83.8 5.9 %input_grad1.1 = (f32[16,128,256]{2,1,0:T(8,128)S(1)}, bf16[16,128,256]{2,1,0:T(8,128)(2,1)S(1)}, f32[8,128]{1,0:T(8,128)S(1)}) custom-call(s32[968]{0:T(1024)S(1)} %get-tuple-element.129.blocks, s32[968]{0:T(1024)S(1)} %get-tuple-element.130.sources, s32[968]{0:T(1024)S(1)} %get-tuple-element.131.targets, s32[8]{0:T(128)S(1)} %get-tuple-element.132.counts, ...), custom_call_target="tpu_custom_call" | custom-call | flops 1000 | bytes 1000 | tf_op jit(solution)/shard_map/input_grad1/pallas_call | solution.py:75
  90.9 3.7 %early_rest.1 = (bf16[2,32,128,256]{3,2,1,0:T(8,128)(2,1)}, bf16[16,128,256]{2,1,0:T(8,128)(2,1)S(1)}, bf16[16,128,256]{2,1,0:T(8,128)(2,1)S(1)}, bf16[16,128,256]{2,1,0:T(8,128)(2,1)S(1)}, f32[16,128,256]{2,1,0:T(8,128)S(1)}) custom-call(s32[968]{0:T(1024)S(1)} %get-tuple-element.129.blocks, s32[968]{0:T(1024)S(1)} %get-tuple-element.130.sources, ...), custom_call_target="tpu_custom_call" | custom-call | flops 1000 | bytes 1000 | tf_op jit(solution)/shard_map/early_rest/pallas_call | solution.py:75
  94.6 3.5 %early_lent.1 = (bf16[16,128,256]{2,1,0:T(8,128)(2,1)S(1)}, bf16[16,128,256]{2,1,0:T(8,128)(2,1)S(1)}, bf16[16,128,256]{2,1,0:T(8,128)(2,1)S(1)}, bf16[2,32,128,...) custom-call(s32[968]{0:T(1024)S(1)} %get-tuple-element.129.blocks, ...), custom_call_target="tpu_custom_call", output_to_operand_aliasing={{3}: (12, {})} | custom-call | flops 1000 | bytes 1000 | tf_op jit(solution)/shard_map/early_lent/pallas_call | solution.py:75
  98.6 4.9 %collective-permute-start.13 = (bf16[8,128,256]{2,1,0:T(8,128)(2,1)S(1)}, bf16[8,128,256]{2,1,0:T(8,128)(2,1)S(1)}, u32[]{:S(2)}, u32[]{:S(2)}) collective-permute-start(bf16[8,128,256]{2,1,0:T(8,128)(2,1)S(1)} %get-tuple-element.174), channel_id=1, source_target_pairs={{0,31},{1,0},{2,1},{3,2},{4,3},{5,4},{6,5},{7,6},{8,7},{9,8},{10,9... | collective-permute-start | bytes 1572872 | tf_op jit(solution)/shard_map/ppermute | solution.py:63
  103.5 4.0 %weight_grads0.1 = (bf16[2,2,112,256]{3,2,1,0:T(8,128)(2,1)S(1)}, bf16[2,2,112,256]{3,2,1,0:T(8,128)(2,1)S(1)}) custom-call(s32[8]{0:T(128)S(1)} %get-tuple-element.143.me, bf16[16,128,256]{2,1,0:T(8,128)(2,1)S(1)} %get-tuple-element.120.f_lent.refs_0_, bf16[16,128,256]{2,1,0:T(8,128)(2,1)S(1)} %get-tuple-element.121.f_rest.refs_1_, ...), custom_call_target="tpu_custom_call" | custom-call | flops 1000 | bytes 1000 | tf_op jit(solution)/shard_map/weight_grads0/pallas_call | solution.py:75
  107.5 16.6 %conditional.1 = (bf16[112,256]{1,0:T(8,128)(2,1)S(1)}, bf16[112,256]{1,0:T(8,128)(2,1)}, f32[16,128,256]{2,1,0:T(8,128)S(1)}, bf16[16,128,256]{2,1,0:T(8,128)(2,1)S(1)}) conditional(s32[]{:T(128)} %bitcast.7, () %tuple.16, (bf16[2,2,112,256]{3,2,1,0:T(8,128)(2,1)S(1)}, bf16[2,2,112,256]{3,2,1,0:T(8,128)(2,1)S(1)}, s32[968]{0:T(1024)S(1)}, ...), branch_computations={%region_0.1_spmd, %region_1.2_spmd} | conditional | flops 3000 | bytes 3260458 | solution.py:905
  109.6 4.8 %collective-permute-done.1.refs_1_ = bf16[2,112,256]{2,1,0:T(8,128)(2,1)S(1)} collective-permute-done((bf16[2,112,256]{2,1,0:T(8,128)(2,1)S(1)}, bf16[2,112,256]{2,1,0:T(8,128)(2,1)S(1)}, u32[]{:S(2)}, u32[]{:S(2)}) %collective-permute-start.1) | collective-permute-done | bytes 114720 | tf_op jit(solution)/shard_map/cond/branch_1_fun/ppermute | solution.py:481
  117.5 6.6 %input_grad0.1 = (f32[16,128,256]{2,1,0:T(8,128)S(1)}, bf16[16,128,256]{2,1,0:T(8,128)(2,1)S(1)}, f32[8,128]{1,0:T(8,128)}) custom-call(s32[968]{0:T(1024)S(1)} %get-tuple-element.34.blocks, s32[968]{0:T(1024)S(1)} %get-tuple-element.35.sources, s32[968]{0:T(1024)S(1)} %get-tuple-element.36.targets, s32[8]{0:T(128)S(1)} %get-tuple-element.37.counts, ...), custom_call_target="tpu_custom_call" | custom-call | flops 1000 | bytes 1000 | tf_op jit(solution)/shard_map/cond/branch_1_fun/input_grad0/pallas_call | solution.py:75
  127.7 3.3 %collective-permute-done.14.refs_1_ = bf16[2,112,256]{2,1,0:T(8,128)(2,1)S(1)} collective-permute-done((bf16[2,112,256]{2,1,0:T(8,128)(2,1)S(1)}, bf16[2,112,256]{2,1,0:T(8,128)(2,1)S(1)}, u32[]{:S(2)}, u32[]{:S(2)}) %collective-permute-start.14) | collective-permute-done | bytes 114720 | tf_op jit(solution)/shard_map/ppermute | solution.py:591
  133.9 5.3 %collective-permute-done.15.refs_1_ = bf16[2,112,256]{2,1,0:T(8,128)(2,1)S(1)} collective-permute-done((bf16[2,112,256]{2,1,0:T(8,128)(2,1)S(1)}, bf16[2,112,256]{2,1,0:T(8,128)(2,1)S(1)}, u32[]{:S(2)}, u32[]{:S(2)}) %collective-permute-start.15) | collective-permute-done | bytes 114720 | tf_op jit(solution)/shard_map/ppermute | solution.py:591
  (64 shorter events, 37.2 us)
Async XLA Ops:
  3.8 20.5 %collective-permute-start.3 = (bf16[8,128,256]{2,1,0:T(8,128)(2,1)}, bf16[8,128,256]{2,1,0:T(8,128)(2,1)S(1)}, u32[]{:S(2)}, u32[]{:S(2)}) collective-permute-start(bf16[8,128,256]{2,1,0:T(8,128)(2,1)} %get-tuple-element.122), channel_id=1, source_target_pairs={{0,1},{1,2},{2,3},{3,4},{4,5},{5,6},{6,7},{7,8},{8,9},{9,10},{10,1... | collective-permute-start | bytes 1572872 | tf_op jit(solution)/shard_map/ppermute | solution.py:63
  6.9 24.8 %collective-permute-start.4 = (bf16[8,128,256]{2,1,0:T(8,128)(2,1)}, bf16[8,128,256]{2,1,0:T(8,128)(2,1)S(1)}, u32[]{:S(2)}, u32[]{:S(2)}) collective-permute-start(bf16[8,128,256]{2,1,0:T(8,128)(2,1)} %get-tuple-element.123), channel_id=1, source_target_pairs={{0,31},{1,0},{2,1},{3,2},{4,3},{5,4},{6,5},{7,6},{8,7},{9,8},{10,9... | collective-permute-start | bytes 1572872 | tf_op jit(solution)/shard_map/ppermute | solution.py:63
  15.0 16.8 %copy-start.1 = (bf16[2,256,256]{2,1,0:T(8,128)(2,1)S(1)}, bf16[2,256,256]{2,1,0:T(8,128)(2,1)}, u32[]{:S(2)}) copy-start(bf16[2,256,256]{2,1,0:T(8,128)(2,1)} %ws.9) | copy-start | bytes 786436
  15.0 16.8 %copy-start.2 = (bf16[2,256,256]{2,1,0:T(8,128)(2,1)S(1)}, bf16[2,256,256]{2,1,0:T(8,128)(2,1)}, u32[]{:S(2)}) copy-start(bf16[2,256,256]{2,1,0:T(8,128)(2,1)} %wn.9) | copy-start | bytes 786436
  15.0 16.8 %copy-start.3 = (bf16[2,256,256]{2,1,0:T(8,128)(2,1)S(1)}, bf16[2,256,256]{2,1,0:T(8,128)(2,1)}, u32[]{:S(2)}) copy-start(bf16[2,256,256]{2,1,0:T(8,128)(2,1)} %wo.7) | copy-start | bytes 786436
  15.0 16.8 %copy-start.7 = (f32[2,256]{1,0:T(2,128)S(1)}, f32[2,256]{1,0:T(2,128)}, u32[]{:S(2)}) copy-start(f32[2,256]{1,0:T(2,128)} %bias.7) | copy-start | bytes 6148
  35.0 17.9 %collective-permute-start.5 = (bf16[8,128,256]{2,1,0:T(8,128)(2,1)S(1)}, bf16[8,128,256]{2,1,0:T(8,128)(2,1)S(1)}, u32[]{:S(2)}, u32[]{:S(2)}) collective-permute-start(bf16[8,128,256]{2,1,0:T(8,128)(2,1)S(1)} %get-tuple-element.126.east), channel_id=1, source_target_pairs={{0,1},{1,2},{2,3},{3,4},{4,5},{5,6},{6,7},{7,8},{8,9},{9,10},{10,1... | collective-permute-start | bytes 1572872 | tf_op jit(solution)/shard_map/ppermute | solution.py:63
  36.7 24.3 %collective-permute-start.6 = (bf16[8,128,256]{2,1,0:T(8,128)(2,1)S(1)}, bf16[8,128,256]{2,1,0:T(8,128)(2,1)S(1)}, u32[]{:S(2)}, u32[]{:S(2)}) collective-permute-start(bf16[8,128,256]{2,1,0:T(8,128)(2,1)S(1)} %get-tuple-element.125.west), channel_id=1, source_target_pairs={{0,31},{1,0},{2,1},{3,2},{4,3},{5,4},{6,5},{7,6},{8,7},{9,8},{10,9... | collective-permute-start | bytes 1572872 | tf_op jit(solution)/shard_map/ppermute | solution.py:63
  69.6 25.0 %collective-permute-start.7 = (bf16[8,128,256]{2,1,0:T(8,128)(2,1)S(1)}, bf16[8,128,256]{2,1,0:T(8,128)(2,1)S(1)}, u32[]{:S(2)}, u32[]{:S(2)}) collective-permute-start(bf16[8,128,256]{2,1,0:T(8,128)(2,1)S(1)} %get-tuple-element.148), channel_id=1, source_target_pairs={{0,1},{1,2},{2,3},{3,4},{4,5},{5,6},{6,7},{7,8},{8,9},{9,10},{10,1... | collective-permute-start | bytes 1572872 | tf_op jit(solution)/shard_map/ppermute | solution.py:63
  69.7 24.9 %collective-permute-start.8 = (bf16[8,128,256]{2,1,0:T(8,128)(2,1)S(1)}, bf16[8,128,256]{2,1,0:T(8,128)(2,1)S(1)}, u32[]{:S(2)}, u32[]{:S(2)}) collective-permute-start(bf16[8,128,256]{2,1,0:T(8,128)(2,1)S(1)} %get-tuple-element.149), channel_id=1, source_target_pairs={{0,31},{1,0},{2,1},{3,2},{4,3},{5,4},{6,5},{7,6},{8,7},{9,8},{10,9... | collective-permute-start | bytes 1572872 | tf_op jit(solution)/shard_map/ppermute | solution.py:63
  79.1 3.6 %collective-permute-start.9 = (bf16[2,2,112,256]{3,2,1,0:T(8,128)(2,1)S(1)}, bf16[2,2,112,256]{3,2,1,0:T(8,128)(2,1)S(1)}, u32[]{:S(2)}, u32[]{:S(2)}) collective-permute-start(bf16[2,2,112,256]{3,2,1,0:T(8,128)(2,1)S(1)} %get-tuple-element.157), channel_id=1, source_target_pairs={{0,8},{4,12},{16,24},{20,28},{8,0},{12,4},{24,16},{28,20},{1,9},{5... | collective-permute-start | bytes 688136 | tf_op jit(solution)/shard_map/ppermute | solution.py:481
  82.8 6.8 %collective-permute-start.10 = (bf16[2,112,256]{2,1,0:T(8,128)(2,1)S(1)}, bf16[2,112,256]{2,1,0:T(8,128)(2,1)S(1)}, u32[]{:S(2)}, u32[]{:S(2)}) collective-permute-start(bf16[2,112,256]{2,1,0:T(8,128)(2,1)S(1)} %get-tuple-element.159), channel_id=1, source_target_pairs={{0,16},{4,20},{16,0},{20,4},{8,24},{12,28},{24,8},{28,12},{1,17},{... | collective-permute-start | bytes 344072 | tf_op jit(solution)/shard_map/ppermute | solution.py:481
  89.7 4.8 %collective-permute-start.11 = (bf16[112,256]{1,0:T(8,128)(2,1)S(1)}, bf16[112,256]{1,0:T(8,128)(2,1)S(1)}, u32[]{:S(2)}, u32[]{:S(2)}) collective-permute-start(bf16[112,256]{1,0:T(8,128)(2,1)S(1)} %get-tuple-element.162), channel_id=1, source_target_pairs={{0,4},{4,0},{16,20},{20,16},{8,12},{12,8},{24,28},{28,24},{1,5},{5... | collective-permute-start | bytes 172040 | tf_op jit(solution)/shard_map/ppermute | solution.py:481
  98.1 26.0 %collective-permute-start.12 = (bf16[8,128,256]{2,1,0:T(8,128)(2,1)S(1)}, bf16[8,128,256]{2,1,0:T(8,128)(2,1)S(1)}, u32[]{:S(2)}, u32[]{:S(2)}) collective-permute-start(bf16[8,128,256]{2,1,0:T(8,128)(2,1)S(1)} %get-tuple-element.173), channel_id=1, source_target_pairs={{0,1},{1,2},{2,3},{3,4},{4,5},{5,6},{6,7},{7,8},{8,9},{9,10},{10,1... | collective-permute-start | bytes 1572872 | tf_op jit(solution)/shard_map/ppermute | solution.py:63
  98.6 25.5 %collective-permute-start.13 = (bf16[8,128,256]{2,1,0:T(8,128)(2,1)S(1)}, bf16[8,128,256]{2,1,0:T(8,128)(2,1)S(1)}, u32[]{:S(2)}, u32[]{:S(2)}) collective-permute-start(bf16[8,128,256]{2,1,0:T(8,128)(2,1)S(1)} %get-tuple-element.174), channel_id=1, source_target_pairs={{0,31},{1,0},{2,1},{3,2},{4,3},{5,4},{6,5},{7,6},{8,7},{9,8},{10,9... | collective-permute-start | bytes 1572872 | tf_op jit(solution)/shard_map/ppermute | solution.py:63
  107.5 1.6 %collective-permute-start = (bf16[2,2,112,256]{3,2,1,0:T(8,128)(2,1)S(1)}, bf16[2,2,112,256]{3,2,1,0:T(8,128)(2,1)S(1)}, u32[]{:S(2)}, u32[]{:S(2)}) collective-permute-start(bf16[2,2,112,256]{3,2,1,0:T(8,128)(2,1)S(1)} %get-tuple-element.29), channel_id=1, source_target_pairs={{0,8},{4,12},{16,24},{20,28},{8,0},{12,4},{24,16},{28,20},{1,9},{5... | collective-permute-start | bytes 688136 | tf_op jit(solution)/shard_map/cond/branch_1_fun/ppermute | solution.py:481
  109.1 5.3 %collective-permute-start.1 = (bf16[2,112,256]{2,1,0:T(8,128)(2,1)S(1)}, bf16[2,112,256]{2,1,0:T(8,128)(2,1)S(1)}, u32[]{:S(2)}, u32[]{:S(2)}) collective-permute-start(bf16[2,112,256]{2,1,0:T(8,128)(2,1)S(1)} %get-tuple-element.31), channel_id=1, source_target_pairs={{0,16},{4,20},{16,0},{20,4},{8,24},{12,28},{24,8},{28,12},{1,17},{... | collective-permute-start | bytes 344072 | tf_op jit(solution)/shard_map/cond/branch_1_fun/ppermute | solution.py:481
  114.4 9.7 %collective-permute-start.2 = (bf16[112,256]{1,0:T(8,128)(2,1)S(1)}, bf16[112,256]{1,0:T(8,128)(2,1)}, u32[]{:S(2)}, u32[]{:S(2)}) collective-permute-start(bf16[112,256]{1,0:T(8,128)(2,1)S(1)} %get-tuple-element.33), channel_id=1, source_target_pairs={{0,4},{4,0},{16,20},{20,16},{8,12},{12,8},{24,28},{28,24},{1,5},{5... | collective-permute-start | bytes 172040 | tf_op jit(solution)/shard_map/cond/branch_1_fun/ppermute | solution.py:481
  125.0 6.0 %collective-permute-start.14 = (bf16[2,112,256]{2,1,0:T(8,128)(2,1)S(1)}, bf16[2,112,256]{2,1,0:T(8,128)(2,1)S(1)}, u32[]{:S(2)}, u32[]{:S(2)}) collective-permute-start(bf16[2,112,256]{2,1,0:T(8,128)(2,1)S(1)} %joined.1.refs_0_), channel_id=1, source_target_pairs={{0,1},{1,0},{2,3},{3,2},{4,5},{5,4},{6,7},{7,6},{8,9},{9,8},{10,11... | collective-permute-start | bytes 344072 | tf_op jit(solution)/shard_map/ppermute | solution.py:591
  131.0 8.1 %collective-permute-start.15 = (bf16[2,112,256]{2,1,0:T(8,128)(2,1)S(1)}, bf16[2,112,256]{2,1,0:T(8,128)(2,1)S(1)}, u32[]{:S(2)}, u32[]{:S(2)}) collective-permute-start(bf16[2,112,256]{2,1,0:T(8,128)(2,1)S(1)} %added.12.refs_0_), channel_id=1, source_target_pairs={{0,2},{1,3},{2,0},{3,1},{4,6},{5,7},{6,4},{7,5},{8,10},{9,11},{10,... | collective-permute-start | bytes 344072 | tf_op jit(solution)/shard_map/ppermute | solution.py:591
  139.1 6.1 %collective-permute-start.16 = (bf16[2,112,256]{2,1,0:T(8,128)(2,1)S(1)}, bf16[2,112,256]{2,1,0:T(8,128)(2,1)S(1)}, u32[]{:S(2)}, u32[]{:S(2)}) collective-permute-start(bf16[2,112,256]{2,1,0:T(8,128)(2,1)S(1)} %added.13.refs_0_), channel_id=1, source_target_pairs={{0,4},{4,0},{16,20},{20,16},{8,12},{12,8},{24,28},{28,24},{1,5},{5... | collective-permute-start | bytes 344072 | tf_op jit(solution)/shard_map/ppermute | solution.py:481
  139.3 5.9 %collective-permute-start.17 = (bf16[2,112,256]{2,1,0:T(8,128)(2,1)S(1)}, bf16[2,112,256]{2,1,0:T(8,128)(2,1)S(1)}, u32[]{:S(2)}, u32[]{:S(2)}) collective-permute-start(bf16[2,112,256]{2,1,0:T(8,128)(2,1)S(1)} %added.13.refs_0_), channel_id=1, source_target_pairs={{0,16},{4,20},{16,0},{20,4},{8,24},{12,28},{24,8},{28,12},{1,17},{... | collective-permute-start | bytes 344072 | tf_op jit(solution)/shard_map/ppermute | solution.py:481
  139.6 7.4 %collective-permute-start.18 = (bf16[2,112,256]{2,1,0:T(8,128)(2,1)S(1)}, bf16[2,112,256]{2,1,0:T(8,128)(2,1)S(1)}, u32[]{:S(2)}, u32[]{:S(2)}) collective-permute-start(bf16[2,112,256]{2,1,0:T(8,128)(2,1)S(1)} %added.13.refs_0_), channel_id=1, source_target_pairs={{0,20},{4,16},{16,4},{20,0},{8,28},{12,24},{24,12},{28,8},{1,21},{... | collective-permute-start | bytes 344072 | tf_op jit(solution)/shard_map/ppermute | solution.py:481
  147.1 2.1 %collective-permute-start.19 = (bf16[2,2,2,112,256]{4,3,2,1,0:T(8,128)(2,1)S(1)}, bf16[2,2,2,112,256]{4,3,2,1,0:T(8,128)(2,1)S(1)}, u32[]{:S(2)}, u32[]{:S(2)}) collective-permute-start(bf16[2,2,2,112,256]{4,3,2,1,0:T(8,128)(2,1)S(1)} %bitcast.14), channel_id=1, source_target_pairs={{0,8},{4,12},{16,24},{20,28},{8,0},{12,4},{24,16},{28,20},{1,9},{5... | collective-permute-start | bytes 1376264 | tf_op jit(solution)/shard_map/ppermute | solution.py:481
  (5 other events, 35.2 us)

commit v8 on v7

--- a/solution.py
+++ b/solution.py
@@ -345,23 +345,26 @@
     )
 
 
-def second_own(z, m1, wt):
-    def kernel(m_lent, m_rest, wt, hidden):
+def second_own(z, f1, m1, w_self, bias, wt):
+    def kernel(f_lent, f_rest, m_lent, m_rest, ws, bias, wt, own, hidden):
         def work(part, first):
+            f = z.flat(group_of(z, (f_lent, f_rest), part, first)[...])
             m = z.flat(group_of(z, (m_lent, m_rest), part, first)[...])
-            hidden[pl.ds(first, z.group)] = z.tiled(dot(m, wt[1, 2]))
+            here = pl.ds(first, z.group)
+            own[here] = z.tiled(dot(f, ws[1]) + bias[1:2, :])
+            hidden[here] = z.tiled(dot(m, wt[1, 2]))
 
         each_group(z, work)
 
     return call(
         kernel,
         "second_own",
-        [VMEM] * 3,
-        VMEM,
-        z.nodes(z.tiles, F32),
+        [VMEM] * 7,
+        [VMEM] * 2,
+        [z.nodes(z.tiles, F32)] * 2,
         [],
-        8,
-        (*m1, wt),
+        12,
+        (*f1, *m1, w_self, bias, wt),
     )
 
 
@@ -417,24 +420,36 @@
         acc[targets[place]] += dot(at[blocks[place]], source(sources[place]))
 
 
-def second(z, tiles, reads, tables, f1, fw, fe, adj, at, hidden, w_self, w_nbr, bias, wt, after):
-    def kernel(tiles, reads, blocks, sources, targets, counts, f_lent, f_rest, fw, fe, adj, at, hidden, ws, wn,
-               bias, wt, _after,
-               agg, act, dpre, dagg, to_west, to_east, ext, acc):
+def second(z, tiles, reads, tables, f1, fw, fe, adj, at, own, hidden, w_nbr, wt, after):
+    groups = z.tiles // z.group
+
+    def kernel(tiles, reads, blocks, sources, targets, counts, f_lent, f_rest, fw, fe, adj, at, own, hidden, wn,
+               wt, _after, agg, act, dpre, dagg, to_west, to_east, ext, acc):
         fill_extended(z, (f_lent, f_rest), fw, fe, ext)
 
-        def work(part, first):
-            here = pl.ds(first, z.group)
-            aggs = aggregate(z, tiles, reads, first, adj, ext)
-            agg[here] = z.tiled(aggs)
-            pre = dot(z.flat(ext[here]), ws[1]) + dot(aggs, wn[1]) + bias[1:2, :]
+        def gather(s):
+            agg[pl.ds(s * z.group, z.group)] = z.tiled(aggregate(z, tiles, reads, s * z.group, adj, ext))
+
+        def middle(s):
+            here = pl.ds(s * z.group, z.group)
+            pre = z.flat(own[here]) + dot(z.flat(agg[here]), wn[1])
             sig = sigmoid(pre)
             act[here] = z.tiled((pre * sig).astype(BF16))
-            grad = (z.flat(hidden[here]) * (sig * (1.0 + pre * (1.0 - sig)))).astype(BF16)
-            dpre[here] = z.tiled(grad)
-            dagg[here] = z.tiled(dot(grad, wt[1, 1]).astype(BF16))
-
-        each_group(z, work, unroll=2)
+            slope = sig * (1.0 + pre * (1.0 - sig))
+            dpre[here] = z.tiled((z.flat(hidden[here]) * slope).astype(BF16))
+
+        def last(s):
+            here = pl.ds(s * z.group, z.group)
+            dagg[here] = z.tiled(dot(z.flat(dpre[here]), wt[1, 1]).astype(BF16))
+
+        for s in range(groups + 2):
+            if s < groups:
+                gather(s)
+            if 0 <= s - 1 < groups:
+                middle(s - 1)
+            if s >= 2:
+                last(s - 2)
+
         spread(z, (blocks, sources, targets, counts), 1, z.lent, at, lambda q: dagg[q], acc, False)
         to_west[...] = acc[pl.ds(0, z.edge)].astype(BF16)
         to_east[...] = acc[pl.ds(z.edge, z.edge)].astype(BF16)
@@ -442,12 +457,12 @@
     return call(
         kernel,
         "second",
-        [SMEM] * 6 + [VMEM] * 12,
+        [SMEM] * 6 + [VMEM] * 11,
         [VMEM] * 6,
         [z.nodes(z.tiles)] * 4 + [z.nodes(z.edge)] * 2,
         [z.held(z.ext), z.held(z.lent, F32)],
         12,
-        (tiles, reads, *tables, *f1, fw, fe, adj, at, hidden, w_self, w_nbr, bias, wt, after),
+        (tiles, reads, *tables, *f1, fw, fe, adj, at, own, hidden, w_nbr, wt, after),
     )
 
 
@@ -496,20 +511,24 @@
         f, agg, act, m, dpre = [
             (refs.pop(0), refs.pop(0)) if isinstance(a, tuple) else refs.pop(0) for a in arrays
         ]
-        outs, acc = refs[:-1], refs[-1]
+        *outs, acc, sums = refs
         acc[...] = jnp.zeros_like(acc)
+        sums[...] = jnp.zeros_like(sums)
 
         def work(part, first):
             def rows(array):
                 return z.flat(group_of(z, array, part, first)[...])
 
             grad = rows(dpre)
-            acc[pl.ds(0, c), :] += dot_rows(rows(f), grad)
-            acc[pl.ds(c, c), :] += dot_rows(rows(agg), grad)
-            acc[pl.ds(2 * c, c), :] += dot_rows(rows(act), rows(m))
+            turned = grad.T
+            sums[0] += dot(turned, rows(f))
+            sums[1] += dot(turned, rows(agg))
+            sums[2] += dot(rows(m).T, rows(act))
             acc[pl.ds(3 * c, 1), :] += jnp.sum(grad.astype(F32), axis=0, keepdims=True)
 
         each_group(z, work)
+        for i in range(3):
+            acc[pl.ds(i * c, c), :] = sums[i].T
         for i, out in enumerate(outs):
             for j in range(ahead):
                 for k in range(side):
@@ -522,7 +541,7 @@
         [SMEM] + [VMEM] * len(flat_args),
         [VMEM] * core,
         [jax.ShapeDtypeStruct((ahead, side, piece, c), BF16)] * core,
-        [pltpu.VMEM((piece * plane.count, c), F32)],
+        [pltpu.VMEM((piece * plane.count, c), F32), pltpu.VMEM((3, c, c), F32)],
         14,
         (plane.me, *flat_args),
     )
@@ -562,7 +581,7 @@
     return plane.received(parts, 2)
 
 
-def joined(parts, other, after):
+def joined(parts, other):
     def kernel(*refs):
         total = refs[0][...].astype(F32)
         for ref in refs[1 : len(parts)]:
@@ -573,23 +592,23 @@
     return call(
         kernel,
         "joined",
-        [VMEM] * (len(parts) + 1) + [ANY] * len(after),
+        [VMEM] * (len(parts) + 1),
         VMEM,
         jax.ShapeDtypeStruct((2,) + other.shape, BF16),
         [],
         8,
-        (*parts, other, *after),
-    )
-
-
-def line_sum(share):
+        (*parts, other),
+    )
+
+
+def line_sum(share, after):
     lines = lax.axis_size("feat")
     if lines & (lines - 1) != 0:
         return lax.psum(share.astype(F32), "feat").astype(BF16)
     step = 1
     while step < lines:
         other = lax.ppermute(share, "feat", [(i, i ^ step) for i in range(lines)])
-        share = added([share, other])
+        share = added([share, other], after=after if step == 1 else ())
         step *= 2
     return share
 
@@ -661,13 +680,7 @@
         ]
         at, wt, part_out, rest_out, token, acc = refs
         token[...] = jnp.zeros_like(token)
-
-        def direct(part, first):
-            mine = z.flat(group_of(z, m, part, first)[...]).astype(F32)
-            res = mine + dot(z.flat(group_of(z, dpre, part, first)[...]), wt[layer, 0])
-            acc[pl.ds(first, z.group)] = z.tiled(res)
-
-        each_group(z, direct)
+        x = z.index
 
         def source(q):
             if not isinstance(dagg, tuple):
@@ -676,7 +689,27 @@
             rest = dagg[1][jnp.maximum(q - z.lent, 0)]
             return jnp.where(q < z.lent, lent, rest)
 
-        spread(z, (blocks, sources, targets, counts), 0, z.tiles, at, source, acc, True)
+        def tile_of(array, part, base, i):
+            return array[part][i] if isinstance(array, tuple) else array[base + i]
+
+        for part, base, count in z.parts:
+
+            @pl.loop(0, count, unroll=4)
+            def _(i):
+                lefts, rights = [tile_of(dpre, part, base, i)], [wt[layer, 0]]
+                for k in range(x.QUAD):
+                    block = blocks[(base + i) * x.QUAD + k]
+                    left = at[jnp.maximum(block, 0)]
+                    lefts.append(jnp.where(block >= 0, left, jnp.zeros_like(left)))
+                    rights.append(source(sources[(base + i) * x.QUAD + k]))
+                value = dot(jnp.concatenate(lefts, axis=1), jnp.concatenate(rights, axis=0))
+                acc[base + i] = value + tile_of(m, part, base, i).astype(F32)
+
+        @pl.loop(0, counts[0])
+        def _(i):
+            place = x.more[0] + i
+            acc[targets[place]] += dot(at[blocks[place]], source(sources[place]))
+
         part_out[...] = acc[pl.ds(0, z.lent)]
         rest_out[...] = acc[pl.ds(z.lent, z.rest)].astype(BF16)
 
@@ -870,11 +903,11 @@
         west, east,
     )
     f1, agg0 = (f1_lent, f1_rest), (agg_lent, agg_rest)
-    hidden = second_own(z, m1, wt)
+    own, hidden = second_own(z, f1, m1, w_self, pre_bias, wt)
     act0, slope, ready = saved(z, f0, agg0, w_self, w_nbr, pre_bias)
 
     agg1, act1, dpre1, dagg1, to_west, to_east = second(
-        z, tiles, reads, tables, f1, next_west, next_east, adj, at, hidden, w_self, w_nbr, pre_bias, wt, ready
+        z, tiles, reads, tables, f1, next_west, next_east, adj, at, own, hidden, w_nbr, wt, ready
     )
     back_west = passed_along(to_east, 1)
     back_east = passed_along(to_west, -1)
@@ -908,7 +941,7 @@
         lambda *_: jax.tree.map(lambda a: jnp.zeros(a.shape, a.dtype), shapes),
         *args,
     )
-    shares = line_sum(joined(early, late, (back_west, back_east)))
+    shares = line_sum(joined(early, late), (back_west, back_east))
     pieces = plane_gathered(plane, shares)
     grads = finish(z, bound_tiles, part, rest, back_west, back_east, grads)
     grad_self, grad_nbr, grad_out, grad_bias = unpack(z, plane, pieces)

time: 152 us -> 150 us (0.987)
  Pallas kernels: 73.8 us -> 69.1 us
    pallas_call x26, Pallas kernels: 73.8 us -> 69.1 us  [call(): pl.pallas_call(kernel, in_specs=in_specs, out_specs=out_specs, out_shape=...]
    ppermute x2, waiting for transfers between devices: 8.6 us -> 10.2 us  [line_sum(): other = lax.ppermute(share, 'feat', [(i, i ^ step) for i in range(lines)])]
    ppermute x10, starting transfers between devices: 9.33 us -> 10.9 us  [passed_by(): return lax.ppermute(value, PLANE, pairs)]
  transfers between devices with their start and end apart: 20 -> 20, of which waited for: 8 -> 9; matrix products, arithmetic and copies ran while one was open for 0% -> 0% of each run, Pallas kernels for 34% -> 34%
where the time goes in v8:
time: 150 us; the launch traced here: 149 us
  Pallas kernels  69.1 us (46%)
  starting transfers between devices  38.6 us (26%)
  waiting for transfers between devices  35.4 us (24%)
  local copies, waits for them, and re-layouts  3.98 us (3%)
  between operations  1.75 us (1%)
    pallas_call x26, Pallas kernels, call(): pl.pallas_call(kernel, in_specs=in_specs, out_specs=out_specs, out_shape=...  69.1 us
    ppermute x8, starting transfers between devices, passed_along(): lax.ppermute(value, AXES, [(i, (i + steps) % count) for i in range(count)])  22.7 us
    ppermute x8, waiting for transfers between devices, passed_along(): lax.ppermute(value, AXES, [(i, (i + steps) % count) for i in range(count)])  15.1 us
    ppermute x10, starting transfers between devices, passed_by(): return lax.ppermute(value, PLANE, pairs)  10.9 us
    ppermute x2, waiting for transfers between devices, line_sum(): other = lax.ppermute(share, 'feat', [(i, i ^ step) for i in range(lines)])  10.2 us
    ppermute x10, waiting for transfers between devices, passed_by(): return lax.ppermute(value, PLANE, pairs)  10.1 us
    ppermute x2, starting transfers between devices, line_sum(): other = lax.ppermute(share, 'feat', [(i, i ^ step) for i in range(lines)])  5.09 us
    unnamed x19, local copies, waits for them, and re-layouts  3.89 us
  transfers between devices with their start and end apart: 20, of which 9 were waited for; matrix products, arithmetic and copies ran while one was open for 0% of the time, Pallas kernels for 34%

profile of v8, /device:TPU:0, one launch (start us, length us, event | category | flops | bytes accessed | tf_op | source)
XLA Modules:
  0.0 148.9 jit_solution(3362376855079666491)
XLA Ops:
  0.7 3.2 %lend.1 = (bf16[8,128,256]{2,1,0:T(8,128)(2,1)}, bf16[8,128,256]{2,1,0:T(8,128)(2,1)}) custom-call(s32[1,2,8]{2,1,0:T(2,128)} %bound.11, bf16[32,128,256]{2,1,0:T(8,128)(2,1)} %bitcast.10), custom_call_target="tpu_custom_call" | custom-call | flops 1000 | bytes 1000 | tf_op jit(solution)/shard_map/lend/pallas_call | solution.py:75
  3.8 3.1 %collective-permute-start.3 = (bf16[8,128,256]{2,1,0:T(8,128)(2,1)}, bf16[8,128,256]{2,1,0:T(8,128)(2,1)S(1)}, u32[]{:S(2)}, u32[]{:S(2)}) collective-permute-start(bf16[8,128,256]{2,1,0:T(8,128)(2,1)} %get-tuple-element.124), channel_id=1, source_target_pairs={{0,1},{1,2},{2,3},{3,4},{4,5},{5,6},{6,7},{7,8},{8,9},{9,10},{10,1... | collective-permute-start | bytes 1572872 | tf_op jit(solution)/shard_map/ppermute | solution.py:63
  6.9 3.4 %collective-permute-start.4 = (bf16[8,128,256]{2,1,0:T(8,128)(2,1)}, bf16[8,128,256]{2,1,0:T(8,128)(2,1)S(1)}, u32[]{:S(2)}, u32[]{:S(2)}) collective-permute-start(bf16[8,128,256]{2,1,0:T(8,128)(2,1)} %get-tuple-element.125), channel_id=1, source_target_pairs={{0,31},{1,0},{2,1},{3,2},{4,3},{5,4},{6,5},{7,6},{8,7},{9,8},{10,9... | collective-permute-start | bytes 1572872 | tf_op jit(solution)/shard_map/ppermute | solution.py:63
  15.0 9.4 %arrange.1 = (bf16[16,128,256]{2,1,0:T(8,128)(2,1)S(1)}, bf16[16,128,256]{2,1,0:T(8,128)(2,1)S(1)}, bf16[16,128,256]{2,1,0:T(8,128)(2,1)S(1)}, bf16[16,128,256]{...) custom-call(s32[1,2,8]{2,1,0:T(2,128)S(1)} %copy-done.6, ...), custom_call_target="tpu_custom_call" | custom-call | flops 1000 | bytes 1000 | tf_op jit(solution)/shard_map/arrange/pallas_call | solution.py:75
  24.4 7.4 %collective-permute-done.4.fe = bf16[8,128,256]{2,1,0:T(8,128)(2,1)S(1)} collective-permute-done((bf16[8,128,256]{2,1,0:T(8,128)(2,1)}, bf16[8,128,256]{2,1,0:T(8,128)(2,1)S(1)}, u32[]{:S(2)}, u32[]{:S(2)}) %collective-permute-start.4) | collective-permute-done | bytes 524320 | tf_op jit(solution)/shard_map/ppermute | solution.py:63
  31.8 3.3 %first_lent.1 = (bf16[8,128,256]{2,1,0:T(8,128)(2,1)S(1)}, bf16[8,128,256]{2,1,0:T(8,128)(2,1)S(1)}, bf16[16,128,256]{2,1,0:T(8,128)(2,1)S(1)}) custom-call(s32[32]{0:T(128)S(1)} %get-tuple-element.120.tiles, s32[128]{0:T(128)S(1)} %get-tuple-element.121.reads, bf16[16,128,256]{2,1,0:T(8,128)(2,1)S(1)} %get-tuple-element.122.f_lent.refs_0_, ...), custom_call_target="tpu_custom_call" | custom-call | flops 1000 | bytes 1000 | tf_op jit(solution)/shard_map/first_lent/pallas_call | solution.py:75
  36.7 3.8 %collective-permute-start.6 = (bf16[8,128,256]{2,1,0:T(8,128)(2,1)S(1)}, bf16[8,128,256]{2,1,0:T(8,128)(2,1)S(1)}, u32[]{:S(2)}, u32[]{:S(2)}) collective-permute-start(bf16[8,128,256]{2,1,0:T(8,128)(2,1)S(1)} %get-tuple-element.127.west), channel_id=1, source_target_pairs={{0,31},{1,0},{2,1},{3,2},{4,3},{5,4},{6,5},{7,6},{8,7},{9,8},{10,9... | collective-permute-start | bytes 1572872 | tf_op jit(solution)/shard_map/ppermute | solution.py:63
  43.6 4.7 %first_rest.1 = (bf16[16,128,256]{2,1,0:T(8,128)(2,1)S(1)}, bf16[16,128,256]{2,1,0:T(8,128)(2,1)S(1)}, bf16[2,32,128,256]{3,2,1,0:T(8,128)(2,1)}, bf16[16,128,256]{2,1,0:T(8,128)(2,1)S(1)}) custom-call(s32[32]{0:T(128)S(1)} %get-tuple-element.120.tiles, s32[128]{0:T(128)S(1)} %get-tuple-element.121.reads, s32[1,2,8]{2,1,0:T(2,128)S(1)} %copy-done.6, ...), custom_call_target="tpu_custom_call" | custom-call | flops 1000 | bytes 1000 | tf_op jit(solution)/shard_map/first_rest/pallas_call | solution.py:75
  53.6 7.4 %collective-permute-done.6.fe = bf16[8,128,256]{2,1,0:T(8,128)(2,1)S(1)} collective-permute-done((bf16[8,128,256]{2,1,0:T(8,128)(2,1)S(1)}, bf16[8,128,256]{2,1,0:T(8,128)(2,1)S(1)}, u32[]{:S(2)}, u32[]{:S(2)}) %collective-permute-start.6) | collective-permute-done | bytes 524320 | tf_op jit(solution)/shard_map/ppermute | solution.py:63
  61.0 5.5 %second.1 = (bf16[32,128,256]{2,1,0:T(8,128)(2,1)S(1)}, bf16[32,128,256]{2,1,0:T(8,128)(2,1)S(1)}, bf16[32,128,256]{2,1,0:T(8,128)(2,1)S(1)}, bf16[32,128,256]{2...) custom-call(s32[32]{0:T(128)S(1)} %get-tuple-element.120.tiles, ...), custom_call_target="tpu_custom_call" | custom-call | flops 1000 | bytes 1000 | tf_op jit(solution)/shard_map/second/pallas_call | solution.py:75
  67.4 4.5 %collective-permute-start.8 = (bf16[8,128,256]{2,1,0:T(8,128)(2,1)S(1)}, bf16[8,128,256]{2,1,0:T(8,128)(2,1)S(1)}, u32[]{:S(2)}, u32[]{:S(2)}) collective-permute-start(bf16[8,128,256]{2,1,0:T(8,128)(2,1)S(1)} %get-tuple-element.153), channel_id=1, source_target_pairs={{0,31},{1,0},{2,1},{3,2},{4,3},{5,4},{6,5},{7,6},{8,7},{9,8},{10,9... | collective-permute-start | bytes 1572872 | tf_op jit(solution)/shard_map/ppermute | solution.py:63
  71.9 4.3 %weight_grads1.1 = (bf16[2,2,112,256]{3,2,1,0:T(8,128)(2,1)S(1)}, bf16[2,2,112,256]{3,2,1,0:T(8,128)(2,1)S(1)}) custom-call(s32[8]{0:T(128)S(1)} %get-tuple-element.147.me, bf16[16,128,256]{2,1,0:T(8,128)(2,1)S(1)} %get-tuple-element.129.f_lent.refs_0_, bf16[16,128,256]{2,1,0:T(8,128)(2,1)S(1)} %get-tuple-element.130.f_rest.refs_1_, ...), custom_call_target="tpu_custom_call" | custom-call | flops 1000 | bytes 1000 | tf_op jit(solution)/shard_map/weight_grads1/pallas_call | solution.py:75
  76.4 3.6 %second_out.1 = (bf16[2,32,128,256]{3,2,1,0:T(8,128)(2,1)}, f32[8,128]{1,0:T(8,128)S(1)}) custom-call(s32[1,2,8]{2,1,0:T(2,128)S(1)} %copy-done.6, s32[1]{0:T(128)S(6)} %copy.31.live, bf16[16,128,256]{2,1,0:T(8,128)(2,1)S(1)} %get-tuple-element.129.f_lent.refs_0_, ...), custom_call_target="tpu_custom_call", output_to_operand_aliasing={{0}: (6, {})} | custom-call | flops 1000 | bytes 1000 | tf_op jit(solution)/shard_map/second_out/pallas_call | solution.py:75
  81.8 4.4 %input_grad1.1 = (f32[16,128,256]{2,1,0:T(8,128)S(1)}, bf16[16,128,256]{2,1,0:T(8,128)(2,1)S(1)}, f32[8,128]{1,0:T(8,128)S(1)}) custom-call(s32[968]{0:T(1024)S(1)} %get-tuple-element.131.blocks, s32[968]{0:T(1024)S(1)} %get-tuple-element.132.sources, s32[968]{0:T(1024)S(1)} %get-tuple-element.133.targets, s32[8]{0:T(128)S(1)} %get-tuple-element.134.counts, ...), custom_call_target="tpu_custom_call" | custom-call | flops 1000 | bytes 1000 | tf_op jit(solution)/shard_map/input_grad1/pallas_call | solution.py:75
  87.5 3.8 %early_rest.1 = (bf16[2,32,128,256]{3,2,1,0:T(8,128)(2,1)}, bf16[16,128,256]{2,1,0:T(8,128)(2,1)S(1)}, bf16[16,128,256]{2,1,0:T(8,128)(2,1)S(1)}, bf16[16,128,256]{2,1,0:T(8,128)(2,1)S(1)}, f32[16,128,256]{2,1,0:T(8,128)S(1)}) custom-call(s32[968]{0:T(1024)S(1)} %get-tuple-element.131.blocks, s32[968]{0:T(1024)S(1)} %get-tuple-element.132.sources, ...), custom_call_target="tpu_custom_call" | custom-call | flops 1000 | bytes 1000 | tf_op jit(solution)/shard_map/early_rest/pallas_call | solution.py:75
  91.7 3.6 %early_lent.1 = (bf16[16,128,256]{2,1,0:T(8,128)(2,1)S(1)}, bf16[16,128,256]{2,1,0:T(8,128)(2,1)S(1)}, bf16[16,128,256]{2,1,0:T(8,128)(2,1)S(1)}, bf16[2,32,128,...) custom-call(s32[968]{0:T(1024)S(1)} %get-tuple-element.131.blocks, ...), custom_call_target="tpu_custom_call", output_to_operand_aliasing={{3}: (12, {})} | custom-call | flops 1000 | bytes 1000 | tf_op jit(solution)/shard_map/early_lent/pallas_call | solution.py:75
  96.4 4.3 %collective-permute-start.13 = (bf16[8,128,256]{2,1,0:T(8,128)(2,1)S(1)}, bf16[8,128,256]{2,1,0:T(8,128)(2,1)S(1)}, u32[]{:S(2)}, u32[]{:S(2)}) collective-permute-start(bf16[8,128,256]{2,1,0:T(8,128)(2,1)S(1)} %get-tuple-element.178), channel_id=1, source_target_pairs={{0,31},{1,0},{2,1},{3,2},{4,3},{5,4},{6,5},{7,6},{8,7},{9,8},{10,9... | collective-permute-start | bytes 1572872 | tf_op jit(solution)/shard_map/ppermute | solution.py:63
  100.7 4.3 %weight_grads0.1 = (bf16[2,2,112,256]{3,2,1,0:T(8,128)(2,1)S(1)}, bf16[2,2,112,256]{3,2,1,0:T(8,128)(2,1)S(1)}) custom-call(s32[8]{0:T(128)S(1)} %get-tuple-element.147.me, bf16[16,128,256]{2,1,0:T(8,128)(2,1)S(1)} %get-tuple-element.122.f_lent.refs_0_, bf16[16,128,256]{2,1,0:T(8,128)(2,1)S(1)} %get-tuple-element.123.f_rest.refs_1_, ...), custom_call_target="tpu_custom_call" | custom-call | flops 1000 | bytes 1000 | tf_op jit(solution)/shard_map/weight_grads0/pallas_call | solution.py:75
  105.0 15.1 %conditional.1 = (bf16[112,256]{1,0:T(8,128)(2,1)S(1)}, bf16[112,256]{1,0:T(8,128)(2,1)}, f32[16,128,256]{2,1,0:T(8,128)S(1)}, bf16[16,128,256]{2,1,0:T(8,128)(2,1)S(1)}) conditional(s32[]{:T(128)} %bitcast.7, () %tuple.16, (bf16[2,2,112,256]{3,2,1,0:T(8,128)(2,1)S(1)}, bf16[2,2,112,256]{3,2,1,0:T(8,128)(2,1)S(1)}, s32[968]{0:T(1024)S(1)}, ...), branch_computations={%region_0.1_spmd, %region_1.2_spmd} | conditional | flops 3000 | bytes 3260458 | solution.py:938
  107.7 4.2 %collective-permute-done.1.refs_1_ = bf16[2,112,256]{2,1,0:T(8,128)(2,1)S(1)} collective-permute-done((bf16[2,112,256]{2,1,0:T(8,128)(2,1)S(1)}, bf16[2,112,256]{2,1,0:T(8,128)(2,1)S(1)}, u32[]{:S(2)}, u32[]{:S(2)}) %collective-permute-start.1) | collective-permute-done | bytes 114720 | tf_op jit(solution)/shard_map/cond/branch_1_fun/ppermute | solution.py:496
  115.0 5.1 %input_grad0.1 = (f32[16,128,256]{2,1,0:T(8,128)S(1)}, bf16[16,128,256]{2,1,0:T(8,128)(2,1)S(1)}, f32[8,128]{1,0:T(8,128)}) custom-call(s32[968]{0:T(1024)S(1)} %get-tuple-element.34.blocks, s32[968]{0:T(1024)S(1)} %get-tuple-element.35.sources, s32[968]{0:T(1024)S(1)} %get-tuple-element.36.targets, s32[8]{0:T(128)S(1)} %get-tuple-element.37.counts, ...), custom_call_target="tpu_custom_call" | custom-call | flops 1000 | bytes 1000 | tf_op jit(solution)/shard_map/cond/branch_1_fun/input_grad0/pallas_call | solution.py:75
  121.1 4.9 %collective-permute-done.14.refs_1_ = bf16[2,112,256]{2,1,0:T(8,128)(2,1)S(1)} collective-permute-done((bf16[2,112,256]{2,1,0:T(8,128)(2,1)S(1)}, bf16[2,112,256]{2,1,0:T(8,128)(2,1)S(1)}, u32[]{:S(2)}, u32[]{:S(2)}) %collective-permute-start.14) | collective-permute-done | bytes 114720 | tf_op jit(solution)/shard_map/ppermute | solution.py:610
  126.0 5.0 %collective-permute-start.15 = (bf16[2,112,256]{2,1,0:T(8,128)(2,1)S(1)}, bf16[2,112,256]{2,1,0:T(8,128)(2,1)S(1)}, u32[]{:S(2)}, u32[]{:S(2)}) collective-permute-start(bf16[2,112,256]{2,1,0:T(8,128)(2,1)S(1)} %added.12.refs_0_), channel_id=1, source_target_pairs={{0,2},{1,3},{2,0},{3,1},{4,6},{5,7},{6,4},{7,5},{8,10},{9,11},{10,... | collective-permute-start | bytes 344072 | tf_op jit(solution)/shard_map/ppermute | solution.py:610
  131.1 5.3 %collective-permute-done.15.refs_1_ = bf16[2,112,256]{2,1,0:T(8,128)(2,1)S(1)} collective-permute-done((bf16[2,112,256]{2,1,0:T(8,128)(2,1)S(1)}, bf16[2,112,256]{2,1,0:T(8,128)(2,1)S(1)}, u32[]{:S(2)}, u32[]{:S(2)}) %collective-permute-start.15) | collective-permute-done | bytes 114720 | tf_op jit(solution)/shard_map/ppermute | solution.py:610
  (64 shorter events, 38.7 us)
Async XLA Ops:
  3.8 20.5 %collective-permute-start.3 = (bf16[8,128,256]{2,1,0:T(8,128)(2,1)}, bf16[8,128,256]{2,1,0:T(8,128)(2,1)S(1)}, u32[]{:S(2)}, u32[]{:S(2)}) collective-permute-start(bf16[8,128,256]{2,1,0:T(8,128)(2,1)} %get-tuple-element.124), channel_id=1, source_target_pairs={{0,1},{1,2},{2,3},{3,4},{4,5},{5,6},{6,7},{7,8},{8,9},{9,10},{10,1... | collective-permute-start | bytes 1572872 | tf_op jit(solution)/shard_map/ppermute | solution.py:63
  6.9 24.8 %collective-permute-start.4 = (bf16[8,128,256]{2,1,0:T(8,128)(2,1)}, bf16[8,128,256]{2,1,0:T(8,128)(2,1)S(1)}, u32[]{:S(2)}, u32[]{:S(2)}) collective-permute-start(bf16[8,128,256]{2,1,0:T(8,128)(2,1)} %get-tuple-element.125), channel_id=1, source_target_pairs={{0,31},{1,0},{2,1},{3,2},{4,3},{5,4},{6,5},{7,6},{8,7},{9,8},{10,9... | collective-permute-start | bytes 1572872 | tf_op jit(solution)/shard_map/ppermute | solution.py:63
  15.0 16.8 %copy-start.1 = (bf16[2,256,256]{2,1,0:T(8,128)(2,1)S(1)}, bf16[2,256,256]{2,1,0:T(8,128)(2,1)}, u32[]{:S(2)}) copy-start(bf16[2,256,256]{2,1,0:T(8,128)(2,1)} %wn.9) | copy-start | bytes 786436
  15.0 16.8 %copy-start.2 = (bf16[2,256,256]{2,1,0:T(8,128)(2,1)S(1)}, bf16[2,256,256]{2,1,0:T(8,128)(2,1)}, u32[]{:S(2)}) copy-start(bf16[2,256,256]{2,1,0:T(8,128)(2,1)} %ws.9) | copy-start | bytes 786436
  15.0 16.8 %copy-start.3 = (bf16[2,256,256]{2,1,0:T(8,128)(2,1)S(1)}, bf16[2,256,256]{2,1,0:T(8,128)(2,1)}, u32[]{:S(2)}) copy-start(bf16[2,256,256]{2,1,0:T(8,128)(2,1)} %wo.7) | copy-start | bytes 786436
  15.0 16.8 %copy-start.7 = (f32[2,256]{1,0:T(2,128)S(1)}, f32[2,256]{1,0:T(2,128)}, u32[]{:S(2)}) copy-start(f32[2,256]{1,0:T(2,128)} %bias.7) | copy-start | bytes 6148
  35.1 18.6 %collective-permute-start.5 = (bf16[8,128,256]{2,1,0:T(8,128)(2,1)S(1)}, bf16[8,128,256]{2,1,0:T(8,128)(2,1)S(1)}, u32[]{:S(2)}, u32[]{:S(2)}) collective-permute-start(bf16[8,128,256]{2,1,0:T(8,128)(2,1)S(1)} %get-tuple-element.128.east), channel_id=1, source_target_pairs={{0,1},{1,2},{2,3},{3,4},{4,5},{5,6},{6,7},{7,8},{8,9},{9,10},{10,1... | collective-permute-start | bytes 1572872 | tf_op jit(solution)/shard_map/ppermute | solution.py:63
  36.7 24.3 %collective-permute-start.6 = (bf16[8,128,256]{2,1,0:T(8,128)(2,1)S(1)}, bf16[8,128,256]{2,1,0:T(8,128)(2,1)S(1)}, u32[]{:S(2)}, u32[]{:S(2)}) collective-permute-start(bf16[8,128,256]{2,1,0:T(8,128)(2,1)S(1)} %get-tuple-element.127.west), channel_id=1, source_target_pairs={{0,31},{1,0},{2,1},{3,2},{4,3},{5,4},{6,5},{7,6},{8,7},{9,8},{10,9... | collective-permute-start | bytes 1572872 | tf_op jit(solution)/shard_map/ppermute | solution.py:63
  66.5 24.8 %collective-permute-start.7 = (bf16[8,128,256]{2,1,0:T(8,128)(2,1)S(1)}, bf16[8,128,256]{2,1,0:T(8,128)(2,1)S(1)}, u32[]{:S(2)}, u32[]{:S(2)}) collective-permute-start(bf16[8,128,256]{2,1,0:T(8,128)(2,1)S(1)} %get-tuple-element.152), channel_id=1, source_target_pairs={{0,1},{1,2},{2,3},{3,4},{4,5},{5,6},{6,7},{7,8},{8,9},{9,10},{10,1... | collective-permute-start | bytes 1572872 | tf_op jit(solution)/shard_map/ppermute | solution.py:63
  67.4 24.3 %collective-permute-start.8 = (bf16[8,128,256]{2,1,0:T(8,128)(2,1)S(1)}, bf16[8,128,256]{2,1,0:T(8,128)(2,1)S(1)}, u32[]{:S(2)}, u32[]{:S(2)}) collective-permute-start(bf16[8,128,256]{2,1,0:T(8,128)(2,1)S(1)} %get-tuple-element.153), channel_id=1, source_target_pairs={{0,31},{1,0},{2,1},{3,2},{4,3},{5,4},{6,5},{7,6},{8,7},{9,8},{10,9... | collective-permute-start | bytes 1572872 | tf_op jit(solution)/shard_map/ppermute | solution.py:63
  76.3 3.6 %collective-permute-start.9 = (bf16[2,2,112,256]{3,2,1,0:T(8,128)(2,1)S(1)}, bf16[2,2,112,256]{3,2,1,0:T(8,128)(2,1)S(1)}, u32[]{:S(2)}, u32[]{:S(2)}) collective-permute-start(bf16[2,2,112,256]{3,2,1,0:T(8,128)(2,1)S(1)} %get-tuple-element.161), channel_id=1, source_target_pairs={{0,8},{4,12},{16,24},{20,28},{8,0},{12,4},{24,16},{28,20},{1,9},{5... | collective-permute-start | bytes 688136 | tf_op jit(solution)/shard_map/ppermute | solution.py:496
  80.0 6.2 %collective-permute-start.10 = (bf16[2,112,256]{2,1,0:T(8,128)(2,1)S(1)}, bf16[2,112,256]{2,1,0:T(8,128)(2,1)S(1)}, u32[]{:S(2)}, u32[]{:S(2)}) collective-permute-start(bf16[2,112,256]{2,1,0:T(8,128)(2,1)S(1)} %get-tuple-element.163), channel_id=1, source_target_pairs={{0,16},{4,20},{16,0},{20,4},{8,24},{12,28},{24,8},{28,12},{1,17},{... | collective-permute-start | bytes 344072 | tf_op jit(solution)/shard_map/ppermute | solution.py:496
  86.3 5.0 %collective-permute-start.11 = (bf16[112,256]{1,0:T(8,128)(2,1)S(1)}, bf16[112,256]{1,0:T(8,128)(2,1)S(1)}, u32[]{:S(2)}, u32[]{:S(2)}) collective-permute-start(bf16[112,256]{1,0:T(8,128)(2,1)S(1)} %get-tuple-element.166), channel_id=1, source_target_pairs={{0,4},{4,0},{16,20},{20,16},{8,12},{12,8},{24,28},{28,24},{1,5},{5... | collective-permute-start | bytes 172040 | tf_op jit(solution)/shard_map/ppermute | solution.py:496
  95.3 30.7 %collective-permute-start.12 = (bf16[8,128,256]{2,1,0:T(8,128)(2,1)S(1)}, bf16[8,128,256]{2,1,0:T(8,128)(2,1)S(1)}, u32[]{:S(2)}, u32[]{:S(2)}) collective-permute-start(bf16[8,128,256]{2,1,0:T(8,128)(2,1)S(1)} %get-tuple-element.177), channel_id=1, source_target_pairs={{0,1},{1,2},{2,3},{3,4},{4,5},{5,6},{6,7},{7,8},{8,9},{9,10},{10,1... | collective-permute-start | bytes 1572872 | tf_op jit(solution)/shard_map/ppermute | solution.py:63
  96.4 29.6 %collective-permute-start.13 = (bf16[8,128,256]{2,1,0:T(8,128)(2,1)S(1)}, bf16[8,128,256]{2,1,0:T(8,128)(2,1)S(1)}, u32[]{:S(2)}, u32[]{:S(2)}) collective-permute-start(bf16[8,128,256]{2,1,0:T(8,128)(2,1)S(1)} %get-tuple-element.178), channel_id=1, source_target_pairs={{0,31},{1,0},{2,1},{3,2},{4,3},{5,4},{6,5},{7,6},{8,7},{9,8},{10,9... | collective-permute-start | bytes 1572872 | tf_op jit(solution)/shard_map/ppermute | solution.py:63
  105.1 1.6 %collective-permute-start = (bf16[2,2,112,256]{3,2,1,0:T(8,128)(2,1)S(1)}, bf16[2,2,112,256]{3,2,1,0:T(8,128)(2,1)S(1)}, u32[]{:S(2)}, u32[]{:S(2)}) collective-permute-start(bf16[2,2,112,256]{3,2,1,0:T(8,128)(2,1)S(1)} %get-tuple-element.29), channel_id=1, source_target_pairs={{0,8},{4,12},{16,24},{20,28},{8,0},{12,4},{24,16},{28,20},{1,9},{5... | collective-permute-start | bytes 688136 | tf_op jit(solution)/shard_map/cond/branch_1_fun/ppermute | solution.py:496
  106.7 5.3 %collective-permute-start.1 = (bf16[2,112,256]{2,1,0:T(8,128)(2,1)S(1)}, bf16[2,112,256]{2,1,0:T(8,128)(2,1)S(1)}, u32[]{:S(2)}, u32[]{:S(2)}) collective-permute-start(bf16[2,112,256]{2,1,0:T(8,128)(2,1)S(1)} %get-tuple-element.31), channel_id=1, source_target_pairs={{0,16},{4,20},{16,0},{20,4},{8,24},{12,28},{24,8},{28,12},{1,17},{... | collective-permute-start | bytes 344072 | tf_op jit(solution)/shard_map/cond/branch_1_fun/ppermute | solution.py:496
  112.0 8.2 %collective-permute-start.2 = (bf16[112,256]{1,0:T(8,128)(2,1)S(1)}, bf16[112,256]{1,0:T(8,128)(2,1)}, u32[]{:S(2)}, u32[]{:S(2)}) collective-permute-start(bf16[112,256]{1,0:T(8,128)(2,1)S(1)} %get-tuple-element.33), channel_id=1, source_target_pairs={{0,4},{4,0},{16,20},{20,16},{8,12},{12,8},{24,28},{28,24},{1,5},{5... | collective-permute-start | bytes 172040 | tf_op jit(solution)/shard_map/cond/branch_1_fun/ppermute | solution.py:496
  121.0 5.0 %collective-permute-start.14 = (bf16[2,112,256]{2,1,0:T(8,128)(2,1)S(1)}, bf16[2,112,256]{2,1,0:T(8,128)(2,1)S(1)}, u32[]{:S(2)}, u32[]{:S(2)}) collective-permute-start(bf16[2,112,256]{2,1,0:T(8,128)(2,1)S(1)} %joined.1.refs_0_), channel_id=1, source_target_pairs={{0,1},{1,0},{2,3},{3,2},{4,5},{5,4},{6,7},{7,6},{8,9},{9,8},{10,11... | collective-permute-start | bytes 344072 | tf_op jit(solution)/shard_map/ppermute | solution.py:610
  126.0 10.3 %collective-permute-start.15 = (bf16[2,112,256]{2,1,0:T(8,128)(2,1)S(1)}, bf16[2,112,256]{2,1,0:T(8,128)(2,1)S(1)}, u32[]{:S(2)}, u32[]{:S(2)}) collective-permute-start(bf16[2,112,256]{2,1,0:T(8,128)(2,1)S(1)} %added.12.refs_0_), channel_id=1, source_target_pairs={{0,2},{1,3},{2,0},{3,1},{4,6},{5,7},{6,4},{7,5},{8,10},{9,11},{10,... | collective-permute-start | bytes 344072 | tf_op jit(solution)/shard_map/ppermute | solution.py:610
  136.3 6.1 %collective-permute-start.16 = (bf16[2,112,256]{2,1,0:T(8,128)(2,1)S(1)}, bf16[2,112,256]{2,1,0:T(8,128)(2,1)S(1)}, u32[]{:S(2)}, u32[]{:S(2)}) collective-permute-start(bf16[2,112,256]{2,1,0:T(8,128)(2,1)S(1)} %added.13.refs_0_), channel_id=1, source_target_pairs={{0,4},{4,0},{16,20},{20,16},{8,12},{12,8},{24,28},{28,24},{1,5},{5... | collective-permute-start | bytes 344072 | tf_op jit(solution)/shard_map/ppermute | solution.py:496
  136.4 6.0 %collective-permute-start.17 = (bf16[2,112,256]{2,1,0:T(8,128)(2,1)S(1)}, bf16[2,112,256]{2,1,0:T(8,128)(2,1)S(1)}, u32[]{:S(2)}, u32[]{:S(2)}) collective-permute-start(bf16[2,112,256]{2,1,0:T(8,128)(2,1)S(1)} %added.13.refs_0_), channel_id=1, source_target_pairs={{0,16},{4,20},{16,0},{20,4},{8,24},{12,28},{24,8},{28,12},{1,17},{... | collective-permute-start | bytes 344072 | tf_op jit(solution)/shard_map/ppermute | solution.py:496
  137.2 7.1 %collective-permute-start.18 = (bf16[2,112,256]{2,1,0:T(8,128)(2,1)S(1)}, bf16[2,112,256]{2,1,0:T(8,128)(2,1)S(1)}, u32[]{:S(2)}, u32[]{:S(2)}) collective-permute-start(bf16[2,112,256]{2,1,0:T(8,128)(2,1)S(1)} %added.13.refs_0_), channel_id=1, source_target_pairs={{0,20},{4,16},{16,4},{20,0},{8,28},{12,24},{24,12},{28,8},{1,21},{... | collective-permute-start | bytes 344072 | tf_op jit(solution)/shard_map/ppermute | solution.py:496
  144.3 2.1 %collective-permute-start.19 = (bf16[2,2,2,112,256]{4,3,2,1,0:T(8,128)(2,1)S(1)}, bf16[2,2,2,112,256]{4,3,2,1,0:T(8,128)(2,1)S(1)}, u32[]{:S(2)}, u32[]{:S(2)}) collective-permute-start(bf16[2,2,2,112,256]{4,3,2,1,0:T(8,128)(2,1)S(1)} %bitcast.14), channel_id=1, source_target_pairs={{0,8},{4,12},{16,24},{20,28},{8,0},{12,4},{24,16},{28,20},{1,9},{5... | collective-permute-start | bytes 1376264 | tf_op jit(solution)/shard_map/ppermute | solution.py:496
  (5 other events, 35.2 us)

commit v9 on v8

--- a/solution.py
+++ b/solution.py
@@ -58,6 +58,13 @@
                 body(part, base + s * z.group)
 
 
+def staged(count, *stages):
+    for s in range(count + len(stages) - 1):
+        for i, stage in enumerate(stages):
+            if 0 <= s - i < count:
+                stage(s - i)
+
+
 def passed_along(value, steps):
     count = lax.axis_size(AXES)
     return lax.ppermute(value, AXES, [(i, (i + steps) % count) for i in range(count)])
@@ -90,17 +97,13 @@
 
 
 def lend(z, bound, features):
-    def kernel(bound, feats, west, east, sems):
-        copies = []
+    def kernel(bound, feats, west, east, buf, sem):
+        copy = pltpu.make_async_copy(feats.at[pl.ds(0, z.lent)], buf, sem)
+        copy.start()
+        copy.wait()
         for i in range(z.edge):
-            for side, target in ((0, west), (1, east)):
-                copy = pltpu.make_async_copy(
-                    feats.at[bound[0, side, i]], target.at[i], sems.at[side * z.edge + i]
-                )
-                copy.start()
-                copies.append(copy)
-        for copy in copies:
-            copy.wait()
+            west[i] = buf[bound[0, 0, i]]
+            east[i] = buf[bound[0, 1, i]]
 
     return call(
         kernel,
@@ -108,7 +111,7 @@
         [SMEM, ANY],
         [VMEM, VMEM],
         [z.nodes(z.edge), z.nodes(z.edge)],
-        [pltpu.SemaphoreType.DMA((z.lent,))],
+        [z.held(z.lent), pltpu.SemaphoreType.DMA],
         56,
         (bound, features),
     )
@@ -267,22 +270,26 @@
 
 
 def first_lent(z, tiles, reads, f0, fw, fe, adj, w_self, w_nbr, bias, w_out):
-    def kernel(tiles, reads, f_lent, f_rest, fw, fe, adj, ws, wn, bias, wo, west, east, agg, ext):
+    def kernel(tiles, reads, f_lent, f_rest, fw, fe, adj, ws, wn, bias, wo, west, east, agg, ext, acts):
         fill_extended(z, (f_lent, f_rest), fw, fe, ext)
 
-        def work(first, target, offset):
-            here = pl.ds(first, z.group)
+        def gather(s):
+            agg[pl.ds(s * z.group, z.group)] = z.tiled(aggregate(z, tiles, reads, s * z.group, adj, ext))
+
+        def middle(s):
+            here = pl.ds(s * z.group, z.group)
             f = z.flat(ext[here])
-            aggs = aggregate(z, tiles, reads, first, adj, ext)
-            agg[here] = z.tiled(aggs)
-            pre = dot(f, ws[0]) + dot(aggs, wn[0]) + bias[0:1, :]
-            act = (pre * sigmoid(pre)).astype(BF16)
-            target[pl.ds(offset, z.group)] = z.tiled((f.astype(F32) + dot(act, wo[0])).astype(BF16))
-
-        @pl.loop(0, z.edge // z.group)
-        def _(s):
-            work(s * z.group, west, s * z.group)
-            work(z.edge + s * z.group, east, s * z.group)
+            pre = dot(f, ws[0]) + dot(z.flat(agg[here]), wn[0]) + bias[0:1, :]
+            acts[here] = z.tiled((pre * sigmoid(pre)).astype(BF16))
+
+        def last(s):
+            here = pl.ds(s * z.group, z.group)
+            out = z.flat(ext[here]).astype(F32) + dot(z.flat(acts[here]), wo[0])
+            half = z.edge // z.group
+            target = west if s < half else east
+            target[pl.ds(s % half * z.group, z.group)] = z.tiled(out.astype(BF16))
+
+        staged(z.lent // z.group, gather, middle, last)
 
     return call(
         kernel,
@@ -290,7 +297,7 @@
         [SMEM] * 2 + [VMEM] * 9,
         [VMEM] * 3,
         [z.nodes(z.edge), z.nodes(z.edge), z.nodes(z.lent)],
-        [z.held(z.ext)],
+        [z.held(z.ext), z.held(z.lent)],
         12,
         (tiles, reads, *f0, fw, fe, adj, w_self, w_nbr, bias, w_out),
     )
@@ -442,14 +449,7 @@
             here = pl.ds(s * z.group, z.group)
             dagg[here] = z.tiled(dot(z.flat(dpre[here]), wt[1, 1]).astype(BF16))
 
-        for s in range(groups + 2):
-            if s < groups:
-                gather(s)
-            if 0 <= s - 1 < groups:
-                middle(s - 1)
-            if s >= 2:
-                last(s - 2)
-
+        staged(groups, gather, middle, last)
         spread(z, (blocks, sources, targets, counts), 1, z.lent, at, lambda q: dagg[q], acc, False)
         to_west[...] = acc[pl.ds(0, z.edge)].astype(BF16)
         to_east[...] = acc[pl.ds(z.edge, z.edge)].astype(BF16)
@@ -547,15 +547,16 @@
     )
 
 
-def added(values, split=False, after=()):
+def added(values, split=False, after=(), pairs=False):
     shape = values[0].shape
     count = shape[0] if split else 1
 
     def kernel(*refs):
         outs = refs[-count:]
         for i, out in enumerate(outs):
-            parts = [ref[i] if split else ref[...] for ref in refs[: len(values)]]
-            parts = [part.astype(F32) for part in parts]
+            parts = [(ref[i] if split else ref[...]).astype(F32) for ref in refs[: len(values)]]
+            if pairs:
+                parts = [parts[0] + parts[1], parts[2] + parts[3]]
             total = parts[0]
             for part in parts[1:]:
                 total = total + part
@@ -605,10 +606,16 @@
     lines = lax.axis_size("feat")
     if lines & (lines - 1) != 0:
         return lax.psum(share.astype(F32), "feat").astype(BF16)
+
+    def from_line(value, step):
+        return lax.ppermute(value, "feat", [(i, i ^ step) for i in range(lines)])
+
+    if lines == 4:
+        others = [from_line(share, step) for step in (1, 2, 3)]
+        return added([share, *others], after=after, pairs=True)
     step = 1
     while step < lines:
-        other = lax.ppermute(share, "feat", [(i, i ^ step) for i in range(lines)])
-        share = added([share, other], after=after if step == 1 else ())
+        share = added([share, from_line(share, step)], after=after if step == 1 else ())
         step *= 2
     return share
 
@@ -764,20 +771,23 @@
 def early_lent(z, tables, bound, part, fw, fe, slope, outer, at, wt, grads, after):
     def kernel(blocks, sources, targets, counts, bound, part, fw, fe, slope, outer, at, wt, _g, _ready, _late,
                m, dpre, dagg, grads, to_west, to_east, acc, sems):
-        def work(first, got):
-            here = pl.ds(first, z.group)
-            g = z.flat((part[here] + got.astype(F32)).astype(BF16))
-            m[here] = z.tiled(g)
-            grad = (dot(g, wt[0, 2]) * z.flat(slope[here])).astype(BF16)
-            dpre[here] = z.tiled(grad)
-            dagg[here] = z.tiled(dot(grad, wt[0, 1]).astype(BF16))
-
-        @pl.loop(0, z.edge // z.group)
-        def _(s):
+        half = z.edge // z.group
+
+        def collect(s):
             here = pl.ds(s * z.group, z.group)
-            work(s * z.group, fw[here])
-            work(z.edge + s * z.group, fe[here])
-
+            got = (fw if s < half else fe)[pl.ds(s % half * z.group, z.group)]
+            m[here] = (part[here] + got.astype(F32)).astype(BF16)
+
+        def middle(s):
+            here = pl.ds(s * z.group, z.group)
+            grad = dot(z.flat(m[here]), wt[0, 2]) * z.flat(slope[here])
+            dpre[here] = z.tiled(grad.astype(BF16))
+
+        def last(s):
+            here = pl.ds(s * z.group, z.group)
+            dagg[here] = z.tiled(dot(z.flat(dpre[here]), wt[0, 1]).astype(BF16))
+
+        staged(2 * half, collect, middle, last)
         copies = [
             pltpu.make_async_copy(m.at[i], grads.at[1, bound[0, i // z.edge, i % z.edge]], sems.at[i])
             for i in range(z.lent)

time: 150 us -> 148 us (0.987)
  waiting for transfers between devices: 35.4 us -> 33.3 us
    ppermute x2 -> x3, waiting for transfers between devices: 10.2 us -> 8.9 us  [from_line(): return lax.ppermute(value, 'feat', [(i, i ^ step) for i in range(lines)])]
    ppermute x2 -> x3, starting transfers between devices: 5.09 us -> 5.89 us  [from_line(): return lax.ppermute(value, 'feat', [(i, i ^ step) for i in range(lines)])]
    pallas_call x26 -> x25, Pallas kernels: 69.1 us -> 69 us  [call(): pl.pallas_call(kernel, in_specs=in_specs, out_specs=out_specs, out_shape=...]
  transfers between devices with their start and end apart: 20 -> 21, of which waited for: 9 -> 7; matrix products, arithmetic and copies ran while one was open for 0% -> 0% of each run, Pallas kernels for 34% -> 35%
where the time goes in v9:
time: 148 us
  Pallas kernels  69 us (47%)
  starting transfers between devices  39.4 us (27%)
  waiting for transfers between devices  33.3 us (22%)
  local copies, waits for them, and re-layouts  3.98 us (3%)
  between operations  1.76 us (1%)
    pallas_call x25, Pallas kernels, call(): pl.pallas_call(kernel, in_specs=in_specs, out_specs=out_specs, out_shape=...  69 us
    ppermute x8, starting transfers between devices, passed_along(): lax.ppermute(value, AXES, [(i, (i + steps) % count) for i in range(count)])  22.7 us
    ppermute x8, waiting for transfers between devices, passed_along(): lax.ppermute(value, AXES, [(i, (i + steps) % count) for i in range(count)])  14.8 us
    ppermute x10, starting transfers between devices, passed_by(): return lax.ppermute(value, PLANE, pairs)  10.8 us
    ppermute x10, waiting for transfers between devices, passed_by(): return lax.ppermute(value, PLANE, pairs)  9.68 us
    ppermute x3, waiting for transfers between devices, from_line(): return lax.ppermute(value, 'feat', [(i, i ^ step) for i in range(lines)])  8.9 us
    ppermute x3, starting transfers between devices, from_line(): return lax.ppermute(value, 'feat', [(i, i ^ step) for i in range(lines)])  5.89 us
    unnamed x19, local copies, waits for them, and re-layouts  3.89 us
  transfers between devices with their start and end apart: 21, of which 7 were waited for; matrix products, arithmetic and copies ran while one was open for 0% of the time, Pallas kernels for 35%

profile of v9, /device:TPU:0, one launch (start us, length us, event | category | flops | bytes accessed | tf_op | source)
XLA Modules:
  0.0 147.5 jit_solution(164232214799148285)
XLA Ops:
  0.7 3.1 %lend.1 = (bf16[8,128,256]{2,1,0:T(8,128)(2,1)}, bf16[8,128,256]{2,1,0:T(8,128)(2,1)}) custom-call(s32[1,2,8]{2,1,0:T(2,128)} %bound.11, bf16[32,128,256]{2,1,0:T(8,128)(2,1)} %bitcast.10), custom_call_target="tpu_custom_call" | custom-call | flops 1000 | bytes 1000 | tf_op jit(solution)/shard_map/lend/pallas_call | solution.py:82
  3.8 3.1 %collective-permute-start.3 = (bf16[8,128,256]{2,1,0:T(8,128)(2,1)}, bf16[8,128,256]{2,1,0:T(8,128)(2,1)S(1)}, u32[]{:S(2)}, u32[]{:S(2)}) collective-permute-start(bf16[8,128,256]{2,1,0:T(8,128)(2,1)} %get-tuple-element.124), channel_id=1, source_target_pairs={{0,1},{1,2},{2,3},{3,4},{4,5},{5,6},{6,7},{7,8},{8,9},{9,10},{10,1... | collective-permute-start | bytes 1572872 | tf_op jit(solution)/shard_map/ppermute | solution.py:70
  6.8 3.4 %collective-permute-start.4 = (bf16[8,128,256]{2,1,0:T(8,128)(2,1)}, bf16[8,128,256]{2,1,0:T(8,128)(2,1)S(1)}, u32[]{:S(2)}, u32[]{:S(2)}) collective-permute-start(bf16[8,128,256]{2,1,0:T(8,128)(2,1)} %get-tuple-element.125), channel_id=1, source_target_pairs={{0,31},{1,0},{2,1},{3,2},{4,3},{5,4},{6,5},{7,6},{8,7},{9,8},{10,9... | collective-permute-start | bytes 1572872 | tf_op jit(solution)/shard_map/ppermute | solution.py:70
  14.9 9.4 %arrange.1 = (bf16[16,128,256]{2,1,0:T(8,128)(2,1)S(1)}, bf16[16,128,256]{2,1,0:T(8,128)(2,1)S(1)}, bf16[16,128,256]{2,1,0:T(8,128)(2,1)S(1)}, bf16[16,128,256]{...) custom-call(s32[1,2,8]{2,1,0:T(2,128)S(1)} %copy-done.6, ...), custom_call_target="tpu_custom_call" | custom-call | flops 1000 | bytes 1000 | tf_op jit(solution)/shard_map/arrange/pallas_call | solution.py:82
  24.3 7.4 %collective-permute-done.4.fe = bf16[8,128,256]{2,1,0:T(8,128)(2,1)S(1)} collective-permute-done((bf16[8,128,256]{2,1,0:T(8,128)(2,1)}, bf16[8,128,256]{2,1,0:T(8,128)(2,1)S(1)}, u32[]{:S(2)}, u32[]{:S(2)}) %collective-permute-start.4) | collective-permute-done | bytes 524320 | tf_op jit(solution)/shard_map/ppermute | solution.py:70
  35.8 3.8 %collective-permute-start.6 = (bf16[8,128,256]{2,1,0:T(8,128)(2,1)S(1)}, bf16[8,128,256]{2,1,0:T(8,128)(2,1)S(1)}, u32[]{:S(2)}, u32[]{:S(2)}) collective-permute-start(bf16[8,128,256]{2,1,0:T(8,128)(2,1)S(1)} %get-tuple-element.127.west), channel_id=1, source_target_pairs={{0,31},{1,0},{2,1},{3,2},{4,3},{5,4},{6,5},{7,6},{8,7},{9,8},{10,9... | collective-permute-start | bytes 1572872 | tf_op jit(solution)/shard_map/ppermute | solution.py:70
  39.6 3.1 %turn.1 = (bf16[128,128,128]{2,1,0:T(8,128)(2,1)S(1)}, bf16[2,3,256,256]{3,2,1,0:T(8,128)(2,1)S(1)}) custom-call(bf16[128,128,128]{2,1,0:T(8,128)(2,1)S(1)} %get-tuple-element.126.adj, bf16[2,256,256]{2,1,0:T(8,128)(2,1)S(1)} %copy-done.2, bf16[2,256,256]{2,1,0:T(8,128)(2,1)S(1)} %copy-done.1, bf16[2,256,256]{2,1,0:T(8,128)(2,1)S(1)} %copy-done.3), custom_call_target="tpu_custom_call" | custom-call | flops 1000 | bytes 1000 | tf_op jit(solution)/shard_map/turn/pallas_call | solution.py:82
  42.7 4.7 %first_rest.1 = (bf16[16,128,256]{2,1,0:T(8,128)(2,1)S(1)}, bf16[16,128,256]{2,1,0:T(8,128)(2,1)S(1)}, bf16[2,32,128,256]{3,2,1,0:T(8,128)(2,1)}, bf16[16,128,256]{2,1,0:T(8,128)(2,1)S(1)}) custom-call(s32[32]{0:T(128)S(1)} %get-tuple-element.120.tiles, s32[128]{0:T(128)S(1)} %get-tuple-element.121.reads, s32[1,2,8]{2,1,0:T(2,128)S(1)} %copy-done.6, ...), custom_call_target="tpu_custom_call" | custom-call | flops 1000 | bytes 1000 | tf_op jit(solution)/shard_map/first_rest/pallas_call | solution.py:82
  47.3 3.0 %saved.1 = (bf16[32,128,256]{2,1,0:T(8,128)(2,1)S(1)}, f32[32,128,256]{2,1,0:T(8,128)S(1)}, f32[8,128]{1,0:T(8,128)S(1)}) custom-call(bf16[16,128,256]{2,1,0:T(8,128)(2,1)S(1)} %get-tuple-element.122.f_lent.refs_0_, bf16[16,128,256]{2,1,0:T(8,128)(2,1)S(1)} %get-tuple-element.123.f_rest.refs_1_, bf16[16,128,256]{2,1,0:T(8,128)(2,1)S(1)} %get-tuple-element.141.a_lent.refs_2_, ...), custom_call_target="tpu_custom_call" | custom-call | flops 1000 | bytes 1000 | tf_op jit(solution)/shard_map/saved/pallas_call | solution.py:82
  52.8 7.4 %collective-permute-done.6.fe = bf16[8,128,256]{2,1,0:T(8,128)(2,1)S(1)} collective-permute-done((bf16[8,128,256]{2,1,0:T(8,128)(2,1)S(1)}, bf16[8,128,256]{2,1,0:T(8,128)(2,1)S(1)}, u32[]{:S(2)}, u32[]{:S(2)}) %collective-permute-start.6) | collective-permute-done | bytes 524320 | tf_op jit(solution)/shard_map/ppermute | solution.py:70
  60.1 5.7 %second.1 = (bf16[32,128,256]{2,1,0:T(8,128)(2,1)S(1)}, bf16[32,128,256]{2,1,0:T(8,128)(2,1)S(1)}, bf16[32,128,256]{2,1,0:T(8,128)(2,1)S(1)}, bf16[32,128,256]{2...) custom-call(s32[32]{0:T(128)S(1)} %get-tuple-element.120.tiles, ...), custom_call_target="tpu_custom_call" | custom-call | flops 1000 | bytes 1000 | tf_op jit(solution)/shard_map/second/pallas_call | solution.py:82
  66.5 4.7 %collective-permute-start.8 = (bf16[8,128,256]{2,1,0:T(8,128)(2,1)S(1)}, bf16[8,128,256]{2,1,0:T(8,128)(2,1)S(1)}, u32[]{:S(2)}, u32[]{:S(2)}) collective-permute-start(bf16[8,128,256]{2,1,0:T(8,128)(2,1)S(1)} %get-tuple-element.153), channel_id=1, source_target_pairs={{0,31},{1,0},{2,1},{3,2},{4,3},{5,4},{6,5},{7,6},{8,7},{9,8},{10,9... | collective-permute-start | bytes 1572872 | tf_op jit(solution)/shard_map/ppermute | solution.py:70
  71.2 4.3 %weight_grads1.1 = (bf16[2,2,112,256]{3,2,1,0:T(8,128)(2,1)S(1)}, bf16[2,2,112,256]{3,2,1,0:T(8,128)(2,1)S(1)}) custom-call(s32[8]{0:T(128)S(1)} %get-tuple-element.147.me, bf16[16,128,256]{2,1,0:T(8,128)(2,1)S(1)} %get-tuple-element.129.f_lent.refs_0_, bf16[16,128,256]{2,1,0:T(8,128)(2,1)S(1)} %get-tuple-element.130.f_rest.refs_1_, ...), custom_call_target="tpu_custom_call" | custom-call | flops 1000 | bytes 1000 | tf_op jit(solution)/shard_map/weight_grads1/pallas_call | solution.py:82
  75.6 3.5 %second_out.1 = (bf16[2,32,128,256]{3,2,1,0:T(8,128)(2,1)}, f32[8,128]{1,0:T(8,128)S(1)}) custom-call(s32[1,2,8]{2,1,0:T(2,128)S(1)} %copy-done.6, s32[1]{0:T(128)S(6)} %copy.31.live, bf16[16,128,256]{2,1,0:T(8,128)(2,1)S(1)} %get-tuple-element.129.f_lent.refs_0_, ...), custom_call_target="tpu_custom_call", output_to_operand_aliasing={{0}: (6, {})} | custom-call | flops 1000 | bytes 1000 | tf_op jit(solution)/shard_map/second_out/pallas_call | solution.py:82
  81.4 5.0 %input_grad1.1 = (f32[16,128,256]{2,1,0:T(8,128)S(1)}, bf16[16,128,256]{2,1,0:T(8,128)(2,1)S(1)}, f32[8,128]{1,0:T(8,128)S(1)}) custom-call(s32[968]{0:T(1024)S(1)} %get-tuple-element.131.blocks, s32[968]{0:T(1024)S(1)} %get-tuple-element.132.sources, s32[968]{0:T(1024)S(1)} %get-tuple-element.133.targets, s32[8]{0:T(128)S(1)} %get-tuple-element.134.counts, ...), custom_call_target="tpu_custom_call" | custom-call | flops 1000 | bytes 1000 | tf_op jit(solution)/shard_map/input_grad1/pallas_call | solution.py:82
  87.3 3.7 %early_rest.1 = (bf16[2,32,128,256]{3,2,1,0:T(8,128)(2,1)}, bf16[16,128,256]{2,1,0:T(8,128)(2,1)S(1)}, bf16[16,128,256]{2,1,0:T(8,128)(2,1)S(1)}, bf16[16,128,256]{2,1,0:T(8,128)(2,1)S(1)}, f32[16,128,256]{2,1,0:T(8,128)S(1)}) custom-call(s32[968]{0:T(1024)S(1)} %get-tuple-element.131.blocks, s32[968]{0:T(1024)S(1)} %get-tuple-element.132.sources, ...), custom_call_target="tpu_custom_call" | custom-call | flops 1000 | bytes 1000 | tf_op jit(solution)/shard_map/early_rest/pallas_call | solution.py:82
  91.1 3.2 %early_lent.1 = (bf16[16,128,256]{2,1,0:T(8,128)(2,1)S(1)}, bf16[16,128,256]{2,1,0:T(8,128)(2,1)S(1)}, bf16[16,128,256]{2,1,0:T(8,128)(2,1)S(1)}, bf16[2,32,128,...) custom-call(s32[968]{0:T(1024)S(1)} %get-tuple-element.131.blocks, ...), custom_call_target="tpu_custom_call", output_to_operand_aliasing={{3}: (12, {})} | custom-call | flops 1000 | bytes 1000 | tf_op jit(solution)/shard_map/early_lent/pallas_call | solution.py:82
  95.2 4.6 %collective-permute-start.13 = (bf16[8,128,256]{2,1,0:T(8,128)(2,1)S(1)}, bf16[8,128,256]{2,1,0:T(8,128)(2,1)S(1)}, u32[]{:S(2)}, u32[]{:S(2)}) collective-permute-start(bf16[8,128,256]{2,1,0:T(8,128)(2,1)S(1)} %get-tuple-element.178), channel_id=1, source_target_pairs={{0,31},{1,0},{2,1},{3,2},{4,3},{5,4},{6,5},{7,6},{8,7},{9,8},{10,9... | collective-permute-start | bytes 1572872 | tf_op jit(solution)/shard_map/ppermute | solution.py:70
  99.7 4.3 %weight_grads0.1 = (bf16[2,2,112,256]{3,2,1,0:T(8,128)(2,1)S(1)}, bf16[2,2,112,256]{3,2,1,0:T(8,128)(2,1)S(1)}) custom-call(s32[8]{0:T(128)S(1)} %get-tuple-element.147.me, bf16[16,128,256]{2,1,0:T(8,128)(2,1)S(1)} %get-tuple-element.122.f_lent.refs_0_, bf16[16,128,256]{2,1,0:T(8,128)(2,1)S(1)} %get-tuple-element.123.f_rest.refs_1_, ...), custom_call_target="tpu_custom_call" | custom-call | flops 1000 | bytes 1000 | tf_op jit(solution)/shard_map/weight_grads0/pallas_call | solution.py:82
  104.1 15.5 %conditional.1 = (bf16[112,256]{1,0:T(8,128)(2,1)S(1)}, bf16[112,256]{1,0:T(8,128)(2,1)}, f32[16,128,256]{2,1,0:T(8,128)S(1)}, bf16[16,128,256]{2,1,0:T(8,128)(2,1)S(1)}) conditional(s32[]{:T(128)} %bitcast.7, () %tuple.16, (bf16[2,2,112,256]{3,2,1,0:T(8,128)(2,1)S(1)}, bf16[2,2,112,256]{3,2,1,0:T(8,128)(2,1)S(1)}, s32[968]{0:T(1024)S(1)}, ...), branch_computations={%region_0.1_spmd, %region_1.2_spmd} | conditional | flops 3000 | bytes 3260458 | solution.py:948
  106.8 4.2 %collective-permute-done.1.refs_1_ = bf16[2,112,256]{2,1,0:T(8,128)(2,1)S(1)} collective-permute-done((bf16[2,112,256]{2,1,0:T(8,128)(2,1)S(1)}, bf16[2,112,256]{2,1,0:T(8,128)(2,1)S(1)}, u32[]{:S(2)}, u32[]{:S(2)}) %collective-permute-start.1) | collective-permute-done | bytes 114720 | tf_op jit(solution)/shard_map/cond/branch_1_fun/ppermute | solution.py:496
  114.0 5.6 %input_grad0.1 = (f32[16,128,256]{2,1,0:T(8,128)S(1)}, bf16[16,128,256]{2,1,0:T(8,128)(2,1)S(1)}, f32[8,128]{1,0:T(8,128)}) custom-call(s32[968]{0:T(1024)S(1)} %get-tuple-element.34.blocks, s32[968]{0:T(1024)S(1)} %get-tuple-element.35.sources, s32[968]{0:T(1024)S(1)} %get-tuple-element.36.targets, s32[8]{0:T(128)S(1)} %get-tuple-element.37.counts, ...), custom_call_target="tpu_custom_call" | custom-call | flops 1000 | bytes 1000 | tf_op jit(solution)/shard_map/cond/branch_1_fun/input_grad0/pallas_call | solution.py:82
  120.5 5.8 %collective-permute-start.15 = (bf16[2,112,256]{2,1,0:T(8,128)(2,1)S(1)}, bf16[2,112,256]{2,1,0:T(8,128)(2,1)S(1)}, u32[]{:S(2)}, u32[]{:S(2)}) collective-permute-start(bf16[2,112,256]{2,1,0:T(8,128)(2,1)S(1)} %joined.1.refs_0_), channel_id=1, source_target_pairs={{0,2},{1,3},{2,0},{3,1},{4,6},{5,7},{6,4},{7,5},{8,10},{9,11},{10,... | collective-permute-start | bytes 344072 | tf_op jit(solution)/shard_map/ppermute | solution.py:611
  126.3 8.9 %collective-permute-done.15.refs_2_ = bf16[2,112,256]{2,1,0:T(8,128)(2,1)S(1)} collective-permute-done((bf16[2,112,256]{2,1,0:T(8,128)(2,1)S(1)}, bf16[2,112,256]{2,1,0:T(8,128)(2,1)S(1)}, u32[]{:S(2)}, u32[]{:S(2)}) %collective-permute-start.15) | collective-permute-done | bytes 114720 | tf_op jit(solution)/shard_map/ppermute | solution.py:611
  (65 shorter events, 34.0 us)
Async XLA Ops:
  3.8 20.5 %collective-permute-start.3 = (bf16[8,128,256]{2,1,0:T(8,128)(2,1)}, bf16[8,128,256]{2,1,0:T(8,128)(2,1)S(1)}, u32[]{:S(2)}, u32[]{:S(2)}) collective-permute-start(bf16[8,128,256]{2,1,0:T(8,128)(2,1)} %get-tuple-element.124), channel_id=1, source_target_pairs={{0,1},{1,2},{2,3},{3,4},{4,5},{5,6},{6,7},{7,8},{8,9},{9,10},{10,1... | collective-permute-start | bytes 1572872 | tf_op jit(solution)/shard_map/ppermute | solution.py:70
  6.8 24.8 %collective-permute-start.4 = (bf16[8,128,256]{2,1,0:T(8,128)(2,1)}, bf16[8,128,256]{2,1,0:T(8,128)(2,1)S(1)}, u32[]{:S(2)}, u32[]{:S(2)}) collective-permute-start(bf16[8,128,256]{2,1,0:T(8,128)(2,1)} %get-tuple-element.125), channel_id=1, source_target_pairs={{0,31},{1,0},{2,1},{3,2},{4,3},{5,4},{6,5},{7,6},{8,7},{9,8},{10,9... | collective-permute-start | bytes 1572872 | tf_op jit(solution)/shard_map/ppermute | solution.py:70
  14.9 16.8 %copy-start.2 = (bf16[2,256,256]{2,1,0:T(8,128)(2,1)S(1)}, bf16[2,256,256]{2,1,0:T(8,128)(2,1)}, u32[]{:S(2)}) copy-start(bf16[2,256,256]{2,1,0:T(8,128)(2,1)} %ws.9) | copy-start | bytes 786436
  14.9 16.8 %copy-start.3 = (bf16[2,256,256]{2,1,0:T(8,128)(2,1)S(1)}, bf16[2,256,256]{2,1,0:T(8,128)(2,1)}, u32[]{:S(2)}) copy-start(bf16[2,256,256]{2,1,0:T(8,128)(2,1)} %wo.7) | copy-start | bytes 786436
  14.9 16.8 %copy-start.7 = (f32[2,256]{1,0:T(2,128)S(1)}, f32[2,256]{1,0:T(2,128)}, u32[]{:S(2)}) copy-start(f32[2,256]{1,0:T(2,128)} %bias.7) | copy-start | bytes 6148
  34.2 18.6 %collective-permute-start.5 = (bf16[8,128,256]{2,1,0:T(8,128)(2,1)S(1)}, bf16[8,128,256]{2,1,0:T(8,128)(2,1)S(1)}, u32[]{:S(2)}, u32[]{:S(2)}) collective-permute-start(bf16[8,128,256]{2,1,0:T(8,128)(2,1)S(1)} %get-tuple-element.128.east), channel_id=1, source_target_pairs={{0,1},{1,2},{2,3},{3,4},{4,5},{5,6},{6,7},{7,8},{8,9},{9,10},{10,1... | collective-permute-start | bytes 1572872 | tf_op jit(solution)/shard_map/ppermute | solution.py:70
  35.8 24.3 %collective-permute-start.6 = (bf16[8,128,256]{2,1,0:T(8,128)(2,1)S(1)}, bf16[8,128,256]{2,1,0:T(8,128)(2,1)S(1)}, u32[]{:S(2)}, u32[]{:S(2)}) collective-permute-start(bf16[8,128,256]{2,1,0:T(8,128)(2,1)S(1)} %get-tuple-element.127.west), channel_id=1, source_target_pairs={{0,31},{1,0},{2,1},{3,2},{4,3},{5,4},{6,5},{7,6},{8,7},{9,8},{10,9... | collective-permute-start | bytes 1572872 | tf_op jit(solution)/shard_map/ppermute | solution.py:70
  65.8 25.3 %collective-permute-start.7 = (bf16[8,128,256]{2,1,0:T(8,128)(2,1)S(1)}, bf16[8,128,256]{2,1,0:T(8,128)(2,1)S(1)}, u32[]{:S(2)}, u32[]{:S(2)}) collective-permute-start(bf16[8,128,256]{2,1,0:T(8,128)(2,1)S(1)} %get-tuple-element.152), channel_id=1, source_target_pairs={{0,1},{1,2},{2,3},{3,4},{4,5},{5,6},{6,7},{7,8},{8,9},{9,10},{10,1... | collective-permute-start | bytes 1572872 | tf_op jit(solution)/shard_map/ppermute | solution.py:70
  66.5 24.6 %collective-permute-start.8 = (bf16[8,128,256]{2,1,0:T(8,128)(2,1)S(1)}, bf16[8,128,256]{2,1,0:T(8,128)(2,1)S(1)}, u32[]{:S(2)}, u32[]{:S(2)}) collective-permute-start(bf16[8,128,256]{2,1,0:T(8,128)(2,1)S(1)} %get-tuple-element.153), channel_id=1, source_target_pairs={{0,31},{1,0},{2,1},{3,2},{4,3},{5,4},{6,5},{7,6},{8,7},{9,8},{10,9... | collective-permute-start | bytes 1572872 | tf_op jit(solution)/shard_map/ppermute | solution.py:70
  75.5 3.6 %collective-permute-start.9 = (bf16[2,2,112,256]{3,2,1,0:T(8,128)(2,1)S(1)}, bf16[2,2,112,256]{3,2,1,0:T(8,128)(2,1)S(1)}, u32[]{:S(2)}, u32[]{:S(2)}) collective-permute-start(bf16[2,2,112,256]{3,2,1,0:T(8,128)(2,1)S(1)} %get-tuple-element.161), channel_id=1, source_target_pairs={{0,8},{4,12},{16,24},{20,28},{8,0},{12,4},{24,16},{28,20},{1,9},{5... | collective-permute-start | bytes 688136 | tf_op jit(solution)/shard_map/ppermute | solution.py:496
  79.2 7.2 %collective-permute-start.10 = (bf16[2,112,256]{2,1,0:T(8,128)(2,1)S(1)}, bf16[2,112,256]{2,1,0:T(8,128)(2,1)S(1)}, u32[]{:S(2)}, u32[]{:S(2)}) collective-permute-start(bf16[2,112,256]{2,1,0:T(8,128)(2,1)S(1)} %get-tuple-element.163), channel_id=1, source_target_pairs={{0,16},{4,20},{16,0},{20,4},{8,24},{12,28},{24,8},{28,12},{1,17},{... | collective-permute-start | bytes 344072 | tf_op jit(solution)/shard_map/ppermute | solution.py:496
  86.5 4.6 %collective-permute-start.11 = (bf16[112,256]{1,0:T(8,128)(2,1)S(1)}, bf16[112,256]{1,0:T(8,128)(2,1)S(1)}, u32[]{:S(2)}, u32[]{:S(2)}) collective-permute-start(bf16[112,256]{1,0:T(8,128)(2,1)S(1)} %get-tuple-element.166), channel_id=1, source_target_pairs={{0,4},{4,0},{16,20},{20,16},{8,12},{12,8},{24,28},{28,24},{1,5},{5... | collective-permute-start | bytes 172040 | tf_op jit(solution)/shard_map/ppermute | solution.py:496
  94.3 40.9 %collective-permute-start.12 = (bf16[8,128,256]{2,1,0:T(8,128)(2,1)S(1)}, bf16[8,128,256]{2,1,0:T(8,128)(2,1)S(1)}, u32[]{:S(2)}, u32[]{:S(2)}) collective-permute-start(bf16[8,128,256]{2,1,0:T(8,128)(2,1)S(1)} %get-tuple-element.177), channel_id=1, source_target_pairs={{0,1},{1,2},{2,3},{3,4},{4,5},{5,6},{6,7},{7,8},{8,9},{9,10},{10,1... | collective-permute-start | bytes 1572872 | tf_op jit(solution)/shard_map/ppermute | solution.py:70
  95.2 40.1 %collective-permute-start.13 = (bf16[8,128,256]{2,1,0:T(8,128)(2,1)S(1)}, bf16[8,128,256]{2,1,0:T(8,128)(2,1)S(1)}, u32[]{:S(2)}, u32[]{:S(2)}) collective-permute-start(bf16[8,128,256]{2,1,0:T(8,128)(2,1)S(1)} %get-tuple-element.178), channel_id=1, source_target_pairs={{0,31},{1,0},{2,1},{3,2},{4,3},{5,4},{6,5},{7,6},{8,7},{9,8},{10,9... | collective-permute-start | bytes 1572872 | tf_op jit(solution)/shard_map/ppermute | solution.py:70
  104.1 1.6 %collective-permute-start = (bf16[2,2,112,256]{3,2,1,0:T(8,128)(2,1)S(1)}, bf16[2,2,112,256]{3,2,1,0:T(8,128)(2,1)S(1)}, u32[]{:S(2)}, u32[]{:S(2)}) collective-permute-start(bf16[2,2,112,256]{3,2,1,0:T(8,128)(2,1)S(1)} %get-tuple-element.29), channel_id=1, source_target_pairs={{0,8},{4,12},{16,24},{20,28},{8,0},{12,4},{24,16},{28,20},{1,9},{5... | collective-permute-start | bytes 688136 | tf_op jit(solution)/shard_map/cond/branch_1_fun/ppermute | solution.py:496
  105.7 5.3 %collective-permute-start.1 = (bf16[2,112,256]{2,1,0:T(8,128)(2,1)S(1)}, bf16[2,112,256]{2,1,0:T(8,128)(2,1)S(1)}, u32[]{:S(2)}, u32[]{:S(2)}) collective-permute-start(bf16[2,112,256]{2,1,0:T(8,128)(2,1)S(1)} %get-tuple-element.31), channel_id=1, source_target_pairs={{0,16},{4,20},{16,0},{20,4},{8,24},{12,28},{24,8},{28,12},{1,17},{... | collective-permute-start | bytes 344072 | tf_op jit(solution)/shard_map/cond/branch_1_fun/ppermute | solution.py:496
  111.0 8.6 %collective-permute-start.2 = (bf16[112,256]{1,0:T(8,128)(2,1)S(1)}, bf16[112,256]{1,0:T(8,128)(2,1)}, u32[]{:S(2)}, u32[]{:S(2)}) collective-permute-start(bf16[112,256]{1,0:T(8,128)(2,1)S(1)} %get-tuple-element.33), channel_id=1, source_target_pairs={{0,4},{4,0},{16,20},{20,16},{8,12},{12,8},{24,28},{28,24},{1,5},{5... | collective-permute-start | bytes 172040 | tf_op jit(solution)/shard_map/cond/branch_1_fun/ppermute | solution.py:496
  120.4 5.9 %collective-permute-start.14 = (bf16[2,112,256]{2,1,0:T(8,128)(2,1)S(1)}, bf16[2,112,256]{2,1,0:T(8,128)(2,1)S(1)}, u32[]{:S(2)}, u32[]{:S(2)}) collective-permute-start(bf16[2,112,256]{2,1,0:T(8,128)(2,1)S(1)} %joined.1.refs_0_), channel_id=1, source_target_pairs={{0,1},{1,0},{2,3},{3,2},{4,5},{5,4},{6,7},{7,6},{8,9},{9,8},{10,11... | collective-permute-start | bytes 344072 | tf_op jit(solution)/shard_map/ppermute | solution.py:611
  120.5 14.7 %collective-permute-start.15 = (bf16[2,112,256]{2,1,0:T(8,128)(2,1)S(1)}, bf16[2,112,256]{2,1,0:T(8,128)(2,1)S(1)}, u32[]{:S(2)}, u32[]{:S(2)}) collective-permute-start(bf16[2,112,256]{2,1,0:T(8,128)(2,1)S(1)} %joined.1.refs_0_), channel_id=1, source_target_pairs={{0,2},{1,3},{2,0},{3,1},{4,6},{5,7},{6,4},{7,5},{8,10},{9,11},{10,... | collective-permute-start | bytes 344072 | tf_op jit(solution)/shard_map/ppermute | solution.py:611
  126.3 8.9 %collective-permute-start.16 = (bf16[2,112,256]{2,1,0:T(8,128)(2,1)S(1)}, bf16[2,112,256]{2,1,0:T(8,128)(2,1)S(1)}, u32[]{:S(2)}, u32[]{:S(2)}) collective-permute-start(bf16[2,112,256]{2,1,0:T(8,128)(2,1)S(1)} %joined.1.refs_0_), channel_id=1, source_target_pairs={{0,3},{1,2},{2,1},{3,0},{4,7},{5,6},{6,5},{7,4},{8,11},{9,10},{10,... | collective-permute-start | bytes 344072 | tf_op jit(solution)/shard_map/ppermute | solution.py:611
  135.3 5.8 %collective-permute-start.17 = (bf16[2,112,256]{2,1,0:T(8,128)(2,1)S(1)}, bf16[2,112,256]{2,1,0:T(8,128)(2,1)S(1)}, u32[]{:S(2)}, u32[]{:S(2)}) collective-permute-start(bf16[2,112,256]{2,1,0:T(8,128)(2,1)S(1)} %added.11.refs_0_), channel_id=1, source_target_pairs={{0,4},{4,0},{16,20},{20,16},{8,12},{12,8},{24,28},{28,24},{1,5},{5... | collective-permute-start | bytes 344072 | tf_op jit(solution)/shard_map/ppermute | solution.py:496
  135.4 5.8 %collective-permute-start.18 = (bf16[2,112,256]{2,1,0:T(8,128)(2,1)S(1)}, bf16[2,112,256]{2,1,0:T(8,128)(2,1)S(1)}, u32[]{:S(2)}, u32[]{:S(2)}) collective-permute-start(bf16[2,112,256]{2,1,0:T(8,128)(2,1)S(1)} %added.11.refs_0_), channel_id=1, source_target_pairs={{0,16},{4,20},{16,0},{20,4},{8,24},{12,28},{24,8},{28,12},{1,17},{... | collective-permute-start | bytes 344072 | tf_op jit(solution)/shard_map/ppermute | solution.py:496
  136.8 6.0 %collective-permute-start.19 = (bf16[2,112,256]{2,1,0:T(8,128)(2,1)S(1)}, bf16[2,112,256]{2,1,0:T(8,128)(2,1)S(1)}, u32[]{:S(2)}, u32[]{:S(2)}) collective-permute-start(bf16[2,112,256]{2,1,0:T(8,128)(2,1)S(1)} %added.11.refs_0_), channel_id=1, source_target_pairs={{0,20},{4,16},{16,4},{20,0},{8,28},{12,24},{24,12},{28,8},{1,21},{... | collective-permute-start | bytes 344072 | tf_op jit(solution)/shard_map/ppermute | solution.py:496
  142.9 2.1 %collective-permute-start.20 = (bf16[2,2,2,112,256]{4,3,2,1,0:T(8,128)(2,1)S(1)}, bf16[2,2,2,112,256]{4,3,2,1,0:T(8,128)(2,1)S(1)}, u32[]{:S(2)}, u32[]{:S(2)}) collective-permute-start(bf16[2,2,2,112,256]{4,3,2,1,0:T(8,128)(2,1)S(1)} %bitcast.14), channel_id=1, source_target_pairs={{0,8},{4,12},{16,24},{20,28},{8,0},{12,4},{24,16},{28,20},{1,9},{5... | collective-permute-start | bytes 1376264 | tf_op jit(solution)/shard_map/ppermute | solution.py:496
  (6 other events, 51.7 us)

commit v10 on v9

--- a/solution.py
+++ b/solution.py
@@ -97,21 +97,26 @@
 
 
 def lend(z, bound, features):
-    def kernel(bound, feats, west, east, buf, sem):
-        copy = pltpu.make_async_copy(feats.at[pl.ds(0, z.lent)], buf, sem)
-        copy.start()
-        copy.wait()
+    def kernel(bound, feats, west, east, buf, index, sems):
+        copies = [
+            pltpu.make_async_copy(feats.at[pl.ds(0, z.lent)], buf, sems.at[0]),
+            pltpu.make_async_copy(bound, index, sems.at[1]),
+        ]
+        for copy in copies:
+            copy.start()
+        for copy in copies:
+            copy.wait()
         for i in range(z.edge):
-            west[i] = buf[bound[0, 0, i]]
-            east[i] = buf[bound[0, 1, i]]
+            west[i] = buf[index[0, 0, i]]
+            east[i] = buf[index[0, 1, i]]
 
     return call(
         kernel,
         "lend",
-        [SMEM, ANY],
+        [ANY, ANY],
         [VMEM, VMEM],
         [z.nodes(z.edge), z.nodes(z.edge)],
-        [z.held(z.lent), pltpu.SemaphoreType.DMA],
+        [z.held(z.lent), pltpu.SMEM(bound.shape, jnp.int32), pltpu.SemaphoreType.DMA((2,))],
         56,
         (bound, features),
     )
@@ -499,7 +504,7 @@
         return [parts[0]] + [self.passed(parts[i], dim, i) for i in range(1, self.sizes[dim])]
 
 
-def weight_grads(z, plane, f, agg, act, m, dpre, name):
+def weight_grads(z, plane, f, agg, act, m, dpre, name, after=()):
     c = z.cols
     piece = -(-(3 * c + 1) // (plane.count * 16)) * 16
     core, ahead, side = plane.sizes
@@ -511,7 +516,7 @@
         f, agg, act, m, dpre = [
             (refs.pop(0), refs.pop(0)) if isinstance(a, tuple) else refs.pop(0) for a in arrays
         ]
-        *outs, acc, sums = refs
+        *outs, acc, sums = refs[len(after) :]
         acc[...] = jnp.zeros_like(acc)
         sums[...] = jnp.zeros_like(sums)
 
@@ -538,16 +543,16 @@
     return call(
         kernel,
         name,
-        [SMEM] + [VMEM] * len(flat_args),
+        [SMEM] + [VMEM] * (len(flat_args) + len(after)),
         [VMEM] * core,
         [jax.ShapeDtypeStruct((ahead, side, piece, c), BF16)] * core,
         [pltpu.VMEM((piece * plane.count, c), F32), pltpu.VMEM((3, c, c), F32)],
         14,
-        (plane.me, *flat_args),
-    )
-
-
-def added(values, split=False, after=(), pairs=False):
+        (plane.me, *flat_args, *after),
+    )
+
+
+def added(values, split=False, after=()):
     shape = values[0].shape
     count = shape[0] if split else 1
 
@@ -555,8 +560,6 @@
         outs = refs[-count:]
         for i, out in enumerate(outs):
             parts = [(ref[i] if split else ref[...]).astype(F32) for ref in refs[: len(values)]]
-            if pairs:
-                parts = [parts[0] + parts[1], parts[2] + parts[3]]
             total = parts[0]
             for part in parts[1:]:
                 total = total + part
@@ -582,40 +585,46 @@
     return plane.received(parts, 2)
 
 
-def joined(parts, other):
-    def kernel(*refs):
-        total = refs[0][...].astype(F32)
-        for ref in refs[1 : len(parts)]:
-            total = total + ref[...].astype(F32)
-        refs[-1][0] = total.astype(BF16)
-        refs[-1][1] = refs[len(parts)][...]
-
-    return call(
-        kernel,
-        "joined",
-        [VMEM] * (len(parts) + 1),
+def from_line(value, step):
+    lines = lax.axis_size("feat")
+    return lax.ppermute(value, "feat", [(i, i ^ step) for i in range(lines)])
+
+
+def joined(early, late):
+    def kernel(early, late, out):
+        out[0] = early[...]
+        out[1] = late[...]
+
+    out = jax.ShapeDtypeStruct((2,) + late.shape, BF16)
+    return call(kernel, "joined", [VMEM] * 2, VMEM, out, [], 4, (early, late))
+
+
+def line_sum_of_four(both, near, early, late, after):
+    def kernel(both, near, early0, early1, late0, late1, *rest):
+        out = rest[-1]
+        for layer, (first, second) in enumerate(((early0, early1), (late0, late1))):
+            pair = both[layer].astype(F32) + near[layer].astype(F32)
+            out[layer] = (pair + (first[...].astype(F32) + second[...].astype(F32))).astype(BF16)
+
+    return call(
+        kernel,
+        "line_sum",
+        [VMEM] * 6 + [ANY] * len(after),
         VMEM,
-        jax.ShapeDtypeStruct((2,) + other.shape, BF16),
+        jax.ShapeDtypeStruct(both.shape, BF16),
         [],
-        8,
-        (*parts, other),
-    )
-
-
-def line_sum(share, after):
+        6,
+        (both, near, *early, *late, *after),
+    )
+
+
+def line_sum(share):
     lines = lax.axis_size("feat")
     if lines & (lines - 1) != 0:
         return lax.psum(share.astype(F32), "feat").astype(BF16)
-
-    def from_line(value, step):
-        return lax.ppermute(value, "feat", [(i, i ^ step) for i in range(lines)])
-
-    if lines == 4:
-        others = [from_line(share, step) for step in (1, 2, 3)]
-        return added([share, *others], after=after, pairs=True)
     step = 1
     while step < lines:
-        share = added([share, from_line(share, step)], after=after if step == 1 else ())
+        share = added([share, from_line(share, step)])
         step *= 2
     return share
 
@@ -768,9 +777,9 @@
     )
 
 
-def early_lent(z, tables, bound, part, fw, fe, slope, outer, at, wt, grads, after):
-    def kernel(blocks, sources, targets, counts, bound, part, fw, fe, slope, outer, at, wt, _g, _ready, _late,
-               m, dpre, dagg, grads, to_west, to_east, acc, sems):
+def early_lent(z, tables, part, fw, fe, slope, outer, at, wt, after):
+    def kernel(blocks, sources, targets, counts, part, fw, fe, slope, outer, at, wt, _ready, _late,
+               m, dpre, dagg, to_west, to_east, acc):
         half = z.edge // z.group
 
         def collect(s):
@@ -788,33 +797,49 @@
             dagg[here] = z.tiled(dot(z.flat(dpre[here]), wt[0, 1]).astype(BF16))
 
         staged(2 * half, collect, middle, last)
+        acc[...] = outer[...]
+
+        def source(q):
+            return dagg[jnp.minimum(q, z.lent - 1)]
+
+        spread(z, (blocks, sources, targets, counts), 2, z.lent, at, source, acc, True)
+        to_west[...] = acc[pl.ds(0, z.edge)].astype(BF16)
+        to_east[...] = acc[pl.ds(z.edge, z.edge)].astype(BF16)
+
+    return call(
+        kernel,
+        "early_lent",
+        [SMEM] * 4 + [VMEM] * 9,
+        [VMEM] * 5,
+        [z.nodes(z.lent)] * 3 + [z.nodes(z.edge)] * 2,
+        [z.held(z.lent, F32)],
+        16,
+        (*tables, part, fw, fe, slope, outer, at, wt, *after),
+    )
+
+
+def place_lent(z, bound, m, grads):
+    def kernel(bound, m, _g, grads, token, sems):
+        token[...] = jnp.zeros_like(token)
         copies = [
             pltpu.make_async_copy(m.at[i], grads.at[1, bound[0, i // z.edge, i % z.edge]], sems.at[i])
             for i in range(z.lent)
         ]
         for copy in copies:
             copy.start()
-        acc[...] = outer[...]
-
-        def source(q):
-            return dagg[jnp.minimum(q, z.lent - 1)]
-
-        spread(z, (blocks, sources, targets, counts), 2, z.lent, at, source, acc, True)
-        to_west[...] = acc[pl.ds(0, z.edge)].astype(BF16)
-        to_east[...] = acc[pl.ds(z.edge, z.edge)].astype(BF16)
         for copy in copies:
             copy.wait()
 
     return call(
         kernel,
-        "early_lent",
-        [SMEM] * 5 + [VMEM] * 7 + [ANY, VMEM, VMEM],
-        [VMEM] * 3 + [ANY] + [VMEM] * 2,
-        [z.nodes(z.lent)] * 3 + [jax.ShapeDtypeStruct(grads.shape, BF16)] + [z.nodes(z.edge)] * 2,
-        [z.held(z.lent, F32), pltpu.SemaphoreType.DMA((z.lent,))],
-        16,
-        (*tables, bound, part, fw, fe, slope, outer, at, wt, grads, *after),
-        {12: 3},
+        "place_lent",
+        [SMEM, VMEM, ANY],
+        [ANY, VMEM],
+        [jax.ShapeDtypeStruct(grads.shape, BF16), TOKEN],
+        [pltpu.SemaphoreType.DMA((z.lent,))],
+        6,
+        (bound, m, grads),
+        {2: 0},
     )
 
 
@@ -930,18 +955,21 @@
     )
     late = added(late, after=(outer,))
 
-    m0_lent, dpre_lent, dagg_lent, grads, to_west, to_east = early_lent(
-        z, tables, bound_tiles, part, back_west, back_east, slope, outer, at, wt, grads, (ready, late)
+    m0_lent, dpre_lent, dagg_lent, to_west, to_east = early_lent(
+        z, tables, part, back_west, back_east, slope, outer, at, wt, (ready, late)
     )
     back_west = passed_along(to_east, 1)
     back_east = passed_along(to_west, -1)
     m0, dpre0, dagg0 = (m0_lent, m0_rest), (dpre_lent, dpre_rest), (dagg_lent, dagg_rest)
-    early = weight_grads(z, plane, f0, agg0, act0, m0, dpre0, "weight_grads0")
-
+    grads, ready = place_lent(z, bound_tiles, m0_lent, grads)
+    early = weight_grads(z, plane, f0, agg0, act0, m0, dpre0, "weight_grads0", (ready,))
+
+
+    late_far = [from_line(late, step) for step in (2, 3)] if lax.axis_size("feat") == 4 else []
 
     def meanwhile(early, tables, m0, dpre0, dagg0, at, wt):
         part, rest, _ = input_grad(z, 0, tables, m0, dpre0, dagg0, at, wt)
-        return plane_parts(plane, early), part, rest
+        return added(plane_parts(plane, early)), part, rest
 
     args = (early, tables, m0, dpre0, dagg0, at, wt)
     shapes = jax.eval_shape(meanwhile, *args)
@@ -951,7 +979,13 @@
         lambda *_: jax.tree.map(lambda a: jnp.zeros(a.shape, a.dtype), shapes),
         *args,
     )
-    shares = line_sum(joined(early, late), (back_west, back_east))
+    both = joined(early, late)
+    if lax.axis_size("feat") == 4:
+        near = from_line(both, 1)
+        far = [from_line(early, step) for step in (2, 3)]
+        shares = line_sum_of_four(both, near, far, late_far, (back_west, back_east))
+    else:
+        shares = line_sum(both)
     pieces = plane_gathered(plane, shares)
     grads = finish(z, bound_tiles, part, rest, back_west, back_east, grads)
     grad_self, grad_nbr, grad_out, grad_bias = unpack(z, plane, pieces)

time: 148 us -> 145 us (0.980)
  starting transfers between devices: 39.4 us -> 36.8 us
    ppermute x10, starting transfers between devices: 10.8 us -> 7.57 us  [passed_by(): return lax.ppermute(value, PLANE, pairs)]
    pallas_call x25 -> x27, Pallas kernels: 69 us -> 67.7 us  [call(): pl.pallas_call(kernel, in_specs=in_specs, out_specs=out_specs, out_shape=...]
    ppermute x3 -> x5, starting transfers between devices: 5.89 us -> 6.54 us  [from_line(): return lax.ppermute(value, 'feat', [(i, i ^ step) for i in range(lines)])]
    ppermute x3 -> x5, waiting for transfers between devices: 8.9 us -> 8.92 us  [from_line(): return lax.ppermute(value, 'feat', [(i, i ^ step) for i in range(lines)])]
  transfers between devices with their start and end apart: 21 -> 23, of which waited for: 7 -> 8; matrix products, arithmetic and copies ran while one was open for 0% -> 0% of each run, Pallas kernels for 35% -> 36%
where the time goes in v10:
time: 145 us
  Pallas kernels  67.7 us (47%)
  starting transfers between devices  36.8 us (25%)
  waiting for transfers between devices  34.2 us (24%)
  local copies, waits for them, and re-layouts  3.98 us (3%)
  between operations  1.77 us (1%)
    pallas_call x27, Pallas kernels, call(): pl.pallas_call(kernel, in_specs=in_specs, out_specs=out_specs, out_shape=...  67.7 us
    ppermute x8, starting transfers between devices, passed_along(): lax.ppermute(value, AXES, [(i, (i + steps) % count) for i in range(count)])  22.7 us
    ppermute x8, waiting for transfers between devices, passed_along(): lax.ppermute(value, AXES, [(i, (i + steps) % count) for i in range(count)])  14.8 us
    ppermute x10, waiting for transfers between devices, passed_by(): return lax.ppermute(value, PLANE, pairs)  10.6 us
    ppermute x5, waiting for transfers between devices, from_line(): return lax.ppermute(value, 'feat', [(i, i ^ step) for i in range(lines)])  8.92 us
    ppermute x10, starting transfers between devices, passed_by(): return lax.ppermute(value, PLANE, pairs)  7.57 us
    ppermute x5, starting transfers between devices, from_line(): return lax.ppermute(value, 'feat', [(i, i ^ step) for i in range(lines)])  6.54 us
    unnamed x19, local copies, waits for them, and re-layouts  3.89 us
  transfers between devices with their start and end apart: 23, of which 8 were waited for; matrix products, arithmetic and copies ran while one was open for 0% of the time, Pallas kernels for 36%

profile of v10, /device:TPU:0, one launch (start us, length us, event | category | flops | bytes accessed | tf_op | source)
XLA Modules:
  0.0 144.5 jit_solution(13782884165839056599)
XLA Ops:
  3.1 3.1 %collective-permute-start.3 = (bf16[8,128,256]{2,1,0:T(8,128)(2,1)}, bf16[8,128,256]{2,1,0:T(8,128)(2,1)S(1)}, u32[]{:S(2)}, u32[]{:S(2)}) collective-permute-start(bf16[8,128,256]{2,1,0:T(8,128)(2,1)} %get-tuple-element.124), channel_id=1, source_target_pairs={{0,1},{1,2},{2,3},{3,4},{4,5},{5,6},{6,7},{7,8},{8,9},{9,10},{10,1... | collective-permute-start | bytes 1572872 | tf_op jit(solution)/shard_map/ppermute | solution.py:70
  6.2 3.4 %collective-permute-start.4 = (bf16[8,128,256]{2,1,0:T(8,128)(2,1)}, bf16[8,128,256]{2,1,0:T(8,128)(2,1)S(1)}, u32[]{:S(2)}, u32[]{:S(2)}) collective-permute-start(bf16[8,128,256]{2,1,0:T(8,128)(2,1)} %get-tuple-element.125), channel_id=1, source_target_pairs={{0,31},{1,0},{2,1},{3,2},{4,3},{5,4},{6,5},{7,6},{8,7},{9,8},{10,9... | collective-permute-start | bytes 1572872 | tf_op jit(solution)/shard_map/ppermute | solution.py:70
  14.2 9.4 %arrange.1 = (bf16[16,128,256]{2,1,0:T(8,128)(2,1)S(1)}, bf16[16,128,256]{2,1,0:T(8,128)(2,1)S(1)}, bf16[16,128,256]{2,1,0:T(8,128)(2,1)S(1)}, bf16[16,128,256]{...) custom-call(s32[1,2,8]{2,1,0:T(2,128)S(1)} %copy-done.6, ...), custom_call_target="tpu_custom_call" | custom-call | flops 1000 | bytes 1000 | tf_op jit(solution)/shard_map/arrange/pallas_call | solution.py:82
  23.6 7.4 %collective-permute-done.4.fe = bf16[8,128,256]{2,1,0:T(8,128)(2,1)S(1)} collective-permute-done((bf16[8,128,256]{2,1,0:T(8,128)(2,1)}, bf16[8,128,256]{2,1,0:T(8,128)(2,1)S(1)}, u32[]{:S(2)}, u32[]{:S(2)}) %collective-permute-start.4) | collective-permute-done | bytes 524320 | tf_op jit(solution)/shard_map/ppermute | solution.py:70
  35.2 3.8 %collective-permute-start.6 = (bf16[8,128,256]{2,1,0:T(8,128)(2,1)S(1)}, bf16[8,128,256]{2,1,0:T(8,128)(2,1)S(1)}, u32[]{:S(2)}, u32[]{:S(2)}) collective-permute-start(bf16[8,128,256]{2,1,0:T(8,128)(2,1)S(1)} %get-tuple-element.127.west), channel_id=1, source_target_pairs={{0,31},{1,0},{2,1},{3,2},{4,3},{5,4},{6,5},{7,6},{8,7},{9,8},{10,9... | collective-permute-start | bytes 1572872 | tf_op jit(solution)/shard_map/ppermute | solution.py:70
  38.9 3.1 %turn.1 = (bf16[128,128,128]{2,1,0:T(8,128)(2,1)S(1)}, bf16[2,3,256,256]{3,2,1,0:T(8,128)(2,1)S(1)}) custom-call(bf16[128,128,128]{2,1,0:T(8,128)(2,1)S(1)} %get-tuple-element.126.adj, bf16[2,256,256]{2,1,0:T(8,128)(2,1)S(1)} %copy-done.2, bf16[2,256,256]{2,1,0:T(8,128)(2,1)S(1)} %copy-done.1, bf16[2,256,256]{2,1,0:T(8,128)(2,1)S(1)} %copy-done.3), custom_call_target="tpu_custom_call" | custom-call | flops 1000 | bytes 1000 | tf_op jit(solution)/shard_map/turn/pallas_call | solution.py:82
  42.0 4.7 %first_rest.1 = (bf16[16,128,256]{2,1,0:T(8,128)(2,1)S(1)}, bf16[16,128,256]{2,1,0:T(8,128)(2,1)S(1)}, bf16[2,32,128,256]{3,2,1,0:T(8,128)(2,1)}, bf16[16,128,256]{2,1,0:T(8,128)(2,1)S(1)}) custom-call(s32[32]{0:T(128)S(1)} %get-tuple-element.120.tiles, s32[128]{0:T(128)S(1)} %get-tuple-element.121.reads, s32[1,2,8]{2,1,0:T(2,128)S(1)} %copy-done.6, ...), custom_call_target="tpu_custom_call" | custom-call | flops 1000 | bytes 1000 | tf_op jit(solution)/shard_map/first_rest/pallas_call | solution.py:82
  46.7 3.0 %saved.1 = (bf16[32,128,256]{2,1,0:T(8,128)(2,1)S(1)}, f32[32,128,256]{2,1,0:T(8,128)S(1)}, f32[8,128]{1,0:T(8,128)S(1)}) custom-call(bf16[16,128,256]{2,1,0:T(8,128)(2,1)S(1)} %get-tuple-element.122.f_lent.refs_0_, bf16[16,128,256]{2,1,0:T(8,128)(2,1)S(1)} %get-tuple-element.123.f_rest.refs_1_, bf16[16,128,256]{2,1,0:T(8,128)(2,1)S(1)} %get-tuple-element.141.a_lent.refs_2_, ...), custom_call_target="tpu_custom_call" | custom-call | flops 1000 | bytes 1000 | tf_op jit(solution)/shard_map/saved/pallas_call | solution.py:82
  52.1 7.4 %collective-permute-done.6.fe = bf16[8,128,256]{2,1,0:T(8,128)(2,1)S(1)} collective-permute-done((bf16[8,128,256]{2,1,0:T(8,128)(2,1)S(1)}, bf16[8,128,256]{2,1,0:T(8,128)(2,1)S(1)}, u32[]{:S(2)}, u32[]{:S(2)}) %collective-permute-start.6) | collective-permute-done | bytes 524320 | tf_op jit(solution)/shard_map/ppermute | solution.py:70
  59.5 5.5 %second.1 = (bf16[32,128,256]{2,1,0:T(8,128)(2,1)S(1)}, bf16[32,128,256]{2,1,0:T(8,128)(2,1)S(1)}, bf16[32,128,256]{2,1,0:T(8,128)(2,1)S(1)}, bf16[32,128,256]{2...) custom-call(s32[32]{0:T(128)S(1)} %get-tuple-element.120.tiles, ...), custom_call_target="tpu_custom_call" | custom-call | flops 1000 | bytes 1000 | tf_op jit(solution)/shard_map/second/pallas_call | solution.py:82
  65.6 4.8 %collective-permute-start.8 = (bf16[8,128,256]{2,1,0:T(8,128)(2,1)S(1)}, bf16[8,128,256]{2,1,0:T(8,128)(2,1)S(1)}, u32[]{:S(2)}, u32[]{:S(2)}) collective-permute-start(bf16[8,128,256]{2,1,0:T(8,128)(2,1)S(1)} %get-tuple-element.153), channel_id=1, source_target_pairs={{0,31},{1,0},{2,1},{3,2},{4,3},{5,4},{6,5},{7,6},{8,7},{9,8},{10,9... | collective-permute-start | bytes 1572872 | tf_op jit(solution)/shard_map/ppermute | solution.py:70
  70.4 4.3 %weight_grads1.1 = (bf16[2,2,112,256]{3,2,1,0:T(8,128)(2,1)S(1)}, bf16[2,2,112,256]{3,2,1,0:T(8,128)(2,1)S(1)}) custom-call(s32[8]{0:T(128)S(1)} %get-tuple-element.147.me, bf16[16,128,256]{2,1,0:T(8,128)(2,1)S(1)} %get-tuple-element.129.f_lent.refs_0_, bf16[16,128,256]{2,1,0:T(8,128)(2,1)S(1)} %get-tuple-element.130.f_rest.refs_1_, ...), custom_call_target="tpu_custom_call" | custom-call | flops 1000 | bytes 1000 | tf_op jit(solution)/shard_map/weight_grads1/pallas_call | solution.py:82
  74.8 3.6 %second_out.1 = (bf16[2,32,128,256]{3,2,1,0:T(8,128)(2,1)}, f32[8,128]{1,0:T(8,128)S(1)}) custom-call(s32[1,2,8]{2,1,0:T(2,128)S(1)} %copy-done.6, s32[1]{0:T(128)S(6)} %copy.29.live, bf16[16,128,256]{2,1,0:T(8,128)(2,1)S(1)} %get-tuple-element.129.f_lent.refs_0_, ...), custom_call_target="tpu_custom_call", output_to_operand_aliasing={{0}: (6, {})} | custom-call | flops 1000 | bytes 1000 | tf_op jit(solution)/shard_map/second_out/pallas_call | solution.py:82
  80.0 4.4 %input_grad1.1 = (f32[16,128,256]{2,1,0:T(8,128)S(1)}, bf16[16,128,256]{2,1,0:T(8,128)(2,1)S(1)}, f32[8,128]{1,0:T(8,128)S(1)}) custom-call(s32[968]{0:T(1024)S(1)} %get-tuple-element.131.blocks, s32[968]{0:T(1024)S(1)} %get-tuple-element.132.sources, s32[968]{0:T(1024)S(1)} %get-tuple-element.133.targets, s32[8]{0:T(128)S(1)} %get-tuple-element.134.counts, ...), custom_call_target="tpu_custom_call" | custom-call | flops 1000 | bytes 1000 | tf_op jit(solution)/shard_map/input_grad1/pallas_call | solution.py:82
  86.1 3.7 %early_rest.1 = (bf16[2,32,128,256]{3,2,1,0:T(8,128)(2,1)}, bf16[16,128,256]{2,1,0:T(8,128)(2,1)S(1)}, bf16[16,128,256]{2,1,0:T(8,128)(2,1)S(1)}, bf16[16,128,256]{2,1,0:T(8,128)(2,1)S(1)}, f32[16,128,256]{2,1,0:T(8,128)S(1)}) custom-call(s32[968]{0:T(1024)S(1)} %get-tuple-element.131.blocks, s32[968]{0:T(1024)S(1)} %get-tuple-element.132.sources, ...), custom_call_target="tpu_custom_call" | custom-call | flops 1000 | bytes 1000 | tf_op jit(solution)/shard_map/early_rest/pallas_call | solution.py:82
  89.8 3.0 %early_lent.1 = (bf16[16,128,256]{2,1,0:T(8,128)(2,1)S(1)}, bf16[16,128,256]{2,1,0:T(8,128)(2,1)S(1)}, bf16[16,128,256]{2,1,0:T(8,128)(2,1)S(1)}, bf16[8,128,256...) custom-call(s32[968]{0:T(1024)S(1)} %get-tuple-element.131.blocks, s32[968]{0:T(1024)S(1)} %get-tuple-element.132.sources, ...), custom_call_target="tpu_custom_call" | custom-call | flops 1000 | bytes 1000 | tf_op jit(solution)/shard_map/early_lent/pallas_call | solution.py:82
  94.0 4.2 %collective-permute-start.13 = (bf16[8,128,256]{2,1,0:T(8,128)(2,1)S(1)}, bf16[8,128,256]{2,1,0:T(8,128)(2,1)S(1)}, u32[]{:S(2)}, u32[]{:S(2)}) collective-permute-start(bf16[8,128,256]{2,1,0:T(8,128)(2,1)S(1)} %get-tuple-element.179), channel_id=1, source_target_pairs={{0,31},{1,0},{2,1},{3,2},{4,3},{5,4},{6,5},{7,6},{8,7},{9,8},{10,9... | collective-permute-start | bytes 1572872 | tf_op jit(solution)/shard_map/ppermute | solution.py:70
  102.2 4.3 %weight_grads0.1 = (bf16[2,2,112,256]{3,2,1,0:T(8,128)(2,1)S(1)}, bf16[2,2,112,256]{3,2,1,0:T(8,128)(2,1)S(1)}) custom-call(s32[8]{0:T(128)S(1)} %get-tuple-element.147.me, bf16[16,128,256]{2,1,0:T(8,128)(2,1)S(1)} %get-tuple-element.122.f_lent.refs_0_, bf16[16,128,256]{2,1,0:T(8,128)(2,1)S(1)} %get-tuple-element.123.f_rest.refs_1_, ...), custom_call_target="tpu_custom_call" | custom-call | flops 1000 | bytes 1000 | tf_op jit(solution)/shard_map/weight_grads0/pallas_call | solution.py:82
  106.6 12.5 %conditional.1 = (bf16[112,256]{1,0:T(8,128)(2,1)S(1)}, f32[16,128,256]{2,1,0:T(8,128)S(1)}, bf16[16,128,256]{2,1,0:T(8,128)(2,1)S(1)}) conditional(s32[]{:T(128)} %bitcast.7, () %tuple.16, (bf16[2,2,112,256]{3,2,1,0:T(8,128)(2,1)S(1)}, bf16[2,2,112,256]{3,2,1,0:T(8,128)(2,1)S(1)}, s32[968]{0:T(1024)S(1)}, s32[968]{0:T(1024)S(1)}, s32[968]{0:T(1024)S(1)}, ...), branch_computations={%region_0.1_spmd, %region_1.2_spmd} | conditional | flops 4000 | bytes 3203104 | solution.py:976
  108.4 5.1 %collective-permute-done.1.refs_1_ = bf16[2,112,256]{2,1,0:T(8,128)(2,1)S(1)} collective-permute-done((bf16[2,112,256]{2,1,0:T(8,128)(2,1)S(1)}, bf16[2,112,256]{2,1,0:T(8,128)(2,1)S(1)}, u32[]{:S(2)}, u32[]{:S(2)}) %collective-permute-start.1) | collective-permute-done | bytes 114720 | tf_op jit(solution)/shard_map/cond/branch_1_fun/ppermute | solution.py:501
  114.0 5.1 %input_grad0.1 = (f32[16,128,256]{2,1,0:T(8,128)S(1)}, bf16[16,128,256]{2,1,0:T(8,128)(2,1)S(1)}, f32[8,128]{1,0:T(8,128)}) custom-call(s32[968]{0:T(1024)S(1)} %get-tuple-element.34.blocks, s32[968]{0:T(1024)S(1)} %get-tuple-element.35.sources, s32[968]{0:T(1024)S(1)} %get-tuple-element.36.targets, s32[8]{0:T(128)S(1)} %get-tuple-element.37.counts, ...), custom_call_target="tpu_custom_call" | custom-call | flops 1000 | bytes 1000 | tf_op jit(solution)/shard_map/cond/branch_1_fun/input_grad0/pallas_call | solution.py:82
  119.1 3.1 %collective-permute-start.14 = (bf16[2,112,256]{2,1,0:T(8,128)(2,1)S(1)}, bf16[2,112,256]{2,1,0:T(8,128)(2,1)S(1)}, u32[]{:S(2)}, u32[]{:S(2)}) collective-permute-start(bf16[2,112,256]{2,1,0:T(8,128)(2,1)S(1)} %joined.1.both), channel_id=1, source_target_pairs={{0,1},{1,0},{2,3},{3,2},{4,5},{5,4},{6,7},{7,6},{8,9},{9,8},{10,11... | collective-permute-start | bytes 344072 | tf_op jit(solution)/shard_map/ppermute | solution.py:590
  122.2 3.5 %collective-permute-done.17.late0 = bf16[112,256]{1,0:T(8,128)(2,1)S(1)} collective-permute-done((bf16[112,256]{1,0:T(8,128)(2,1)S(1)}, bf16[112,256]{1,0:T(8,128)(2,1)S(1)}, u32[]{:S(2)}, u32[]{:S(2)}) %collective-permute-start.17) | collective-permute-done | bytes 57376 | tf_op jit(solution)/shard_map/ppermute | solution.py:590
  126.8 5.4 %collective-permute-done.15.early0 = bf16[112,256]{1,0:T(8,128)(2,1)S(1)} collective-permute-done((bf16[112,256]{1,0:T(8,128)(2,1)S(1)}, bf16[112,256]{1,0:T(8,128)(2,1)S(1)}, u32[]{:S(2)}, u32[]{:S(2)}) %collective-permute-start.15) | collective-permute-done | bytes 57376 | tf_op jit(solution)/shard_map/ppermute | solution.py:590
  (71 shorter events, 37.6 us)
Async XLA Ops:
  3.1 20.5 %collective-permute-start.3 = (bf16[8,128,256]{2,1,0:T(8,128)(2,1)}, bf16[8,128,256]{2,1,0:T(8,128)(2,1)S(1)}, u32[]{:S(2)}, u32[]{:S(2)}) collective-permute-start(bf16[8,128,256]{2,1,0:T(8,128)(2,1)} %get-tuple-element.124), channel_id=1, source_target_pairs={{0,1},{1,2},{2,3},{3,4},{4,5},{5,6},{6,7},{7,8},{8,9},{9,10},{10,1... | collective-permute-start | bytes 1572872 | tf_op jit(solution)/shard_map/ppermute | solution.py:70
  6.2 24.8 %collective-permute-start.4 = (bf16[8,128,256]{2,1,0:T(8,128)(2,1)}, bf16[8,128,256]{2,1,0:T(8,128)(2,1)S(1)}, u32[]{:S(2)}, u32[]{:S(2)}) collective-permute-start(bf16[8,128,256]{2,1,0:T(8,128)(2,1)} %get-tuple-element.125), channel_id=1, source_target_pairs={{0,31},{1,0},{2,1},{3,2},{4,3},{5,4},{6,5},{7,6},{8,7},{9,8},{10,9... | collective-permute-start | bytes 1572872 | tf_op jit(solution)/shard_map/ppermute | solution.py:70
  14.2 16.8 %copy-start.7 = (f32[2,256]{1,0:T(2,128)S(1)}, f32[2,256]{1,0:T(2,128)}, u32[]{:S(2)}) copy-start(f32[2,256]{1,0:T(2,128)} %bias.7) | copy-start | bytes 6148
  33.5 18.5 %collective-permute-start.5 = (bf16[8,128,256]{2,1,0:T(8,128)(2,1)S(1)}, bf16[8,128,256]{2,1,0:T(8,128)(2,1)S(1)}, u32[]{:S(2)}, u32[]{:S(2)}) collective-permute-start(bf16[8,128,256]{2,1,0:T(8,128)(2,1)S(1)} %get-tuple-element.128.east), channel_id=1, source_target_pairs={{0,1},{1,2},{2,3},{3,4},{4,5},{5,6},{6,7},{7,8},{8,9},{9,10},{10,1... | collective-permute-start | bytes 1572872 | tf_op jit(solution)/shard_map/ppermute | solution.py:70
  35.2 24.3 %collective-permute-start.6 = (bf16[8,128,256]{2,1,0:T(8,128)(2,1)S(1)}, bf16[8,128,256]{2,1,0:T(8,128)(2,1)S(1)}, u32[]{:S(2)}, u32[]{:S(2)}) collective-permute-start(bf16[8,128,256]{2,1,0:T(8,128)(2,1)S(1)} %get-tuple-element.127.west), channel_id=1, source_target_pairs={{0,31},{1,0},{2,1},{3,2},{4,3},{5,4},{6,5},{7,6},{8,7},{9,8},{10,9... | collective-permute-start | bytes 1572872 | tf_op jit(solution)/shard_map/ppermute | solution.py:70
  65.0 24.8 %collective-permute-start.7 = (bf16[8,128,256]{2,1,0:T(8,128)(2,1)S(1)}, bf16[8,128,256]{2,1,0:T(8,128)(2,1)S(1)}, u32[]{:S(2)}, u32[]{:S(2)}) collective-permute-start(bf16[8,128,256]{2,1,0:T(8,128)(2,1)S(1)} %get-tuple-element.152), channel_id=1, source_target_pairs={{0,1},{1,2},{2,3},{3,4},{4,5},{5,6},{6,7},{7,8},{8,9},{9,10},{10,1... | collective-permute-start | bytes 1572872 | tf_op jit(solution)/shard_map/ppermute | solution.py:70
  65.6 24.2 %collective-permute-start.8 = (bf16[8,128,256]{2,1,0:T(8,128)(2,1)S(1)}, bf16[8,128,256]{2,1,0:T(8,128)(2,1)S(1)}, u32[]{:S(2)}, u32[]{:S(2)}) collective-permute-start(bf16[8,128,256]{2,1,0:T(8,128)(2,1)S(1)} %get-tuple-element.153), channel_id=1, source_target_pairs={{0,31},{1,0},{2,1},{3,2},{4,3},{5,4},{6,5},{7,6},{8,7},{9,8},{10,9... | collective-permute-start | bytes 1572872 | tf_op jit(solution)/shard_map/ppermute | solution.py:70
  74.7 3.7 %collective-permute-start.9 = (bf16[2,2,112,256]{3,2,1,0:T(8,128)(2,1)S(1)}, bf16[2,2,112,256]{3,2,1,0:T(8,128)(2,1)S(1)}, u32[]{:S(2)}, u32[]{:S(2)}) collective-permute-start(bf16[2,2,112,256]{3,2,1,0:T(8,128)(2,1)S(1)} %get-tuple-element.160), channel_id=1, source_target_pairs={{0,8},{4,12},{16,24},{20,28},{8,0},{12,4},{24,16},{28,20},{1,9},{5... | collective-permute-start | bytes 688136 | tf_op jit(solution)/shard_map/ppermute | solution.py:501
  78.5 6.0 %collective-permute-start.10 = (bf16[2,112,256]{2,1,0:T(8,128)(2,1)S(1)}, bf16[2,112,256]{2,1,0:T(8,128)(2,1)S(1)}, u32[]{:S(2)}, u32[]{:S(2)}) collective-permute-start(bf16[2,112,256]{2,1,0:T(8,128)(2,1)S(1)} %get-tuple-element.162), channel_id=1, source_target_pairs={{0,16},{4,20},{16,0},{20,4},{8,24},{12,28},{24,8},{28,12},{1,17},{... | collective-permute-start | bytes 344072 | tf_op jit(solution)/shard_map/ppermute | solution.py:501
  84.5 5.3 %collective-permute-start.11 = (bf16[112,256]{1,0:T(8,128)(2,1)S(1)}, bf16[112,256]{1,0:T(8,128)(2,1)S(1)}, u32[]{:S(2)}, u32[]{:S(2)}) collective-permute-start(bf16[112,256]{1,0:T(8,128)(2,1)S(1)} %get-tuple-element.165), channel_id=1, source_target_pairs={{0,4},{4,0},{16,20},{20,16},{8,12},{12,8},{24,28},{28,24},{1,5},{5... | collective-permute-start | bytes 172040 | tf_op jit(solution)/shard_map/ppermute | solution.py:501
  92.8 39.4 %collective-permute-start.12 = (bf16[8,128,256]{2,1,0:T(8,128)(2,1)S(1)}, bf16[8,128,256]{2,1,0:T(8,128)(2,1)S(1)}, u32[]{:S(2)}, u32[]{:S(2)}) collective-permute-start(bf16[8,128,256]{2,1,0:T(8,128)(2,1)S(1)} %get-tuple-element.178), channel_id=1, source_target_pairs={{0,1},{1,2},{2,3},{3,4},{4,5},{5,6},{6,7},{7,8},{8,9},{9,10},{10,1... | collective-permute-start | bytes 1572872 | tf_op jit(solution)/shard_map/ppermute | solution.py:70
  94.0 38.2 %collective-permute-start.13 = (bf16[8,128,256]{2,1,0:T(8,128)(2,1)S(1)}, bf16[8,128,256]{2,1,0:T(8,128)(2,1)S(1)}, u32[]{:S(2)}, u32[]{:S(2)}) collective-permute-start(bf16[8,128,256]{2,1,0:T(8,128)(2,1)S(1)} %get-tuple-element.179), channel_id=1, source_target_pairs={{0,31},{1,0},{2,1},{3,2},{4,3},{5,4},{6,5},{7,6},{8,7},{9,8},{10,9... | collective-permute-start | bytes 1572872 | tf_op jit(solution)/shard_map/ppermute | solution.py:70
  98.2 27.5 %collective-permute-start.17 = (bf16[112,256]{1,0:T(8,128)(2,1)S(1)}, bf16[112,256]{1,0:T(8,128)(2,1)S(1)}, u32[]{:S(2)}, u32[]{:S(2)}) collective-permute-start(bf16[112,256]{1,0:T(8,128)(2,1)S(1)} %added.11._late.late), channel_id=1, source_target_pairs={{0,2},{1,3},{2,0},{3,1},{4,6},{5,7},{6,4},{7,5},{8,10},{9,11},{10,... | collective-permute-start | bytes 172040 | tf_op jit(solution)/shard_map/ppermute | solution.py:590
  99.1 26.6 %collective-permute-start.18 = (bf16[112,256]{1,0:T(8,128)(2,1)S(1)}, bf16[112,256]{1,0:T(8,128)(2,1)S(1)}, u32[]{:S(2)}, u32[]{:S(2)}) collective-permute-start(bf16[112,256]{1,0:T(8,128)(2,1)S(1)} %added.11._late.late), channel_id=1, source_target_pairs={{0,3},{1,2},{2,1},{3,0},{4,7},{5,6},{6,5},{7,4},{8,11},{9,10},{10,... | collective-permute-start | bytes 172040 | tf_op jit(solution)/shard_map/ppermute | solution.py:590
  106.6 1.6 %collective-permute-start = (bf16[2,2,112,256]{3,2,1,0:T(8,128)(2,1)S(1)}, bf16[2,2,112,256]{3,2,1,0:T(8,128)(2,1)S(1)}, u32[]{:S(2)}, u32[]{:S(2)}) collective-permute-start(bf16[2,2,112,256]{3,2,1,0:T(8,128)(2,1)S(1)} %get-tuple-element.29), channel_id=1, source_target_pairs={{0,8},{4,12},{16,24},{20,28},{8,0},{12,4},{24,16},{28,20},{1,9},{5... | collective-permute-start | bytes 688136 | tf_op jit(solution)/shard_map/cond/branch_1_fun/ppermute | solution.py:501
  108.2 5.3 %collective-permute-start.1 = (bf16[2,112,256]{2,1,0:T(8,128)(2,1)S(1)}, bf16[2,112,256]{2,1,0:T(8,128)(2,1)S(1)}, u32[]{:S(2)}, u32[]{:S(2)}) collective-permute-start(bf16[2,112,256]{2,1,0:T(8,128)(2,1)S(1)} %get-tuple-element.31), channel_id=1, source_target_pairs={{0,16},{4,20},{16,0},{20,4},{8,24},{12,28},{24,8},{28,12},{1,17},{... | collective-permute-start | bytes 344072 | tf_op jit(solution)/shard_map/cond/branch_1_fun/ppermute | solution.py:501
  113.5 5.6 %collective-permute-start.2 = (bf16[112,256]{1,0:T(8,128)(2,1)S(1)}, bf16[112,256]{1,0:T(8,128)(2,1)S(1)}, u32[]{:S(2)}, u32[]{:S(2)}) collective-permute-start(bf16[112,256]{1,0:T(8,128)(2,1)S(1)} %get-tuple-element.33), channel_id=1, source_target_pairs={{0,4},{4,0},{16,20},{20,16},{8,12},{12,8},{24,28},{28,24},{1,5},{5... | collective-permute-start | bytes 172040 | tf_op jit(solution)/shard_map/cond/branch_1_fun/ppermute | solution.py:501
  119.1 13.1 %collective-permute-start.14 = (bf16[2,112,256]{2,1,0:T(8,128)(2,1)S(1)}, bf16[2,112,256]{2,1,0:T(8,128)(2,1)S(1)}, u32[]{:S(2)}, u32[]{:S(2)}) collective-permute-start(bf16[2,112,256]{2,1,0:T(8,128)(2,1)S(1)} %joined.1.both), channel_id=1, source_target_pairs={{0,1},{1,0},{2,3},{3,2},{4,5},{5,4},{6,7},{7,6},{8,9},{9,8},{10,11... | collective-permute-start | bytes 344072 | tf_op jit(solution)/shard_map/ppermute | solution.py:590
  125.7 6.5 %collective-permute-start.15 = (bf16[112,256]{1,0:T(8,128)(2,1)S(1)}, bf16[112,256]{1,0:T(8,128)(2,1)S(1)}, u32[]{:S(2)}, u32[]{:S(2)}) collective-permute-start(bf16[112,256]{1,0:T(8,128)(2,1)S(1)} %get-tuple-element.181.early), channel_id=1, source_target_pairs={{0,2},{1,3},{2,0},{3,1},{4,6},{5,7},{6,4},{7,5},{8,10},{9,11},{10,... | collective-permute-start | bytes 172040 | tf_op jit(solution)/shard_map/ppermute | solution.py:590
  125.7 6.5 %collective-permute-start.16 = (bf16[112,256]{1,0:T(8,128)(2,1)S(1)}, bf16[112,256]{1,0:T(8,128)(2,1)S(1)}, u32[]{:S(2)}, u32[]{:S(2)}) collective-permute-start(bf16[112,256]{1,0:T(8,128)(2,1)S(1)} %get-tuple-element.181.early), channel_id=1, source_target_pairs={{0,3},{1,2},{2,1},{3,0},{4,7},{5,6},{6,5},{7,4},{8,11},{9,10},{10,... | collective-permute-start | bytes 172040 | tf_op jit(solution)/shard_map/ppermute | solution.py:590
  132.3 5.9 %collective-permute-start.19 = (bf16[2,112,256]{2,1,0:T(8,128)(2,1)S(1)}, bf16[2,112,256]{2,1,0:T(8,128)(2,1)S(1)}, u32[]{:S(2)}, u32[]{:S(2)}) collective-permute-start(bf16[2,112,256]{2,1,0:T(8,128)(2,1)S(1)} %line_sum.1.refs_0_), channel_id=1, source_target_pairs={{0,4},{4,0},{16,20},{20,16},{8,12},{12,8},{24,28},{28,24},{1,5},{5... | collective-permute-start | bytes 344072 | tf_op jit(solution)/shard_map/ppermute | solution.py:501
  132.7 5.6 %collective-permute-start.20 = (bf16[2,112,256]{2,1,0:T(8,128)(2,1)S(1)}, bf16[2,112,256]{2,1,0:T(8,128)(2,1)S(1)}, u32[]{:S(2)}, u32[]{:S(2)}) collective-permute-start(bf16[2,112,256]{2,1,0:T(8,128)(2,1)S(1)} %line_sum.1.refs_0_), channel_id=1, source_target_pairs={{0,16},{4,20},{16,0},{20,4},{8,24},{12,28},{24,8},{28,12},{1,17},{... | collective-permute-start | bytes 344072 | tf_op jit(solution)/shard_map/ppermute | solution.py:501
  133.8 6.1 %collective-permute-start.21 = (bf16[2,112,256]{2,1,0:T(8,128)(2,1)S(1)}, bf16[2,112,256]{2,1,0:T(8,128)(2,1)S(1)}, u32[]{:S(2)}, u32[]{:S(2)}) collective-permute-start(bf16[2,112,256]{2,1,0:T(8,128)(2,1)S(1)} %line_sum.1.refs_0_), channel_id=1, source_target_pairs={{0,20},{4,16},{16,4},{20,0},{8,28},{12,24},{24,12},{28,8},{1,21},{... | collective-permute-start | bytes 344072 | tf_op jit(solution)/shard_map/ppermute | solution.py:501
  139.9 2.1 %collective-permute-start.22 = (bf16[2,2,2,112,256]{4,3,2,1,0:T(8,128)(2,1)S(1)}, bf16[2,2,2,112,256]{4,3,2,1,0:T(8,128)(2,1)S(1)}, u32[]{:S(2)}, u32[]{:S(2)}) collective-permute-start(bf16[2,2,2,112,256]{4,3,2,1,0:T(8,128)(2,1)S(1)} %bitcast.14), channel_id=1, source_target_pairs={{0,8},{4,12},{16,24},{20,28},{8,0},{12,4},{24,16},{28,20},{1,9},{5... | collective-permute-start | bytes 1376264 | tf_op jit(solution)/shard_map/ppermute | solution.py:501
  (8 other events, 83.4 us)

commit v11 on v10

--- a/solution.py
+++ b/solution.py
@@ -137,7 +137,7 @@
     s4 = z.slots
     x = z.index
 
-    def kernel(bound, nbrs, live, place, feats, cot, adj, f_lent, f_rest, m_lent, m_rest, adj_out,
+    def kernel(bound, nbrs, live, place, feats, cot, adj, f_lent, f_rest, m_lent, m_rest, adj_out, ext,
                tiles, reads, blocks, sources, targets, counts, me, inverse, used, sems):
         copies = []
         for i in range(8):
@@ -150,12 +150,14 @@
 
         tail = pl.ds(z.lent, z.rest)
         start(feats.at[tail], f_rest)
+        start(feats.at[tail], ext.at[tail])
         start(cot.at[tail], m_rest)
         start(adj, adj_out)
         for i in range(z.lent):
             tile = bound[0, i // z.edge, i % z.edge]
             inverse[tile] = i
             start(feats.at[tile], f_lent.at[i])
+            start(feats.at[tile], ext.at[i])
             start(cot.at[tile], m_lent.at[i])
 
         @pl.loop(0, x.targets)
@@ -211,16 +213,16 @@
         kernel,
         "arrange",
         [SMEM] * 4 + [ANY] * 3,
-        [VMEM] * 5 + [SMEM] * 7,
+        [VMEM] * 6 + [SMEM] * 7,
         [z.nodes(z.lent), z.nodes(z.rest), z.nodes(z.lent), z.nodes(z.rest)]
-        + [jax.ShapeDtypeStruct(adjacency.shape, BF16)]
+        + [jax.ShapeDtypeStruct(adjacency.shape, BF16), z.nodes(z.ext)]
         + [jax.ShapeDtypeStruct((n,), jnp.int32) for n in (z.tiles, z.pairs, x.size, x.size, x.size, 8, 8)],
         [
             pltpu.SMEM((z.lent,), jnp.int32),
             pltpu.SMEM((x.targets,), jnp.int32),
-            pltpu.SemaphoreType.DMA((2 * z.lent + 3,)),
+            pltpu.SemaphoreType.DMA((3 * z.lent + 4,)),
         ],
-        12,
+        14,
         (bound, nbrs, live, place, features, cot, adjacency),
     )
 
@@ -248,11 +250,15 @@
     )
 
 
+def fill_borrowed(z, fw, fe, ext):
+    ext[pl.ds(z.tiles, z.edge)] = fw[...]
+    ext[pl.ds(z.tiles + z.edge, z.edge)] = fe[...]
+
+
 def fill_extended(z, own, fw, fe, ext):
     ext[pl.ds(0, z.lent)] = own[0][...]
     ext[pl.ds(z.lent, z.rest)] = own[1][...]
-    ext[pl.ds(z.tiles, z.edge)] = fw[...]
-    ext[pl.ds(z.tiles + z.edge, z.edge)] = fe[...]
+    fill_borrowed(z, fw, fe, ext)
 
 
 def aggregate(z, tiles, reads, first, adj, ext):
@@ -274,9 +280,9 @@
     return jnp.concatenate(parts, axis=0)
 
 
-def first_lent(z, tiles, reads, f0, fw, fe, adj, w_self, w_nbr, bias, w_out):
-    def kernel(tiles, reads, f_lent, f_rest, fw, fe, adj, ws, wn, bias, wo, west, east, agg, ext, acts):
-        fill_extended(z, (f_lent, f_rest), fw, fe, ext)
+def first_lent(z, tiles, reads, ext, fw, fe, adj, w_self, w_nbr, bias, w_out):
+    def kernel(tiles, reads, _ext, fw, fe, adj, ws, wn, bias, wo, west, east, agg, ext, acts):
+        fill_borrowed(z, fw, fe, ext)
 
         def gather(s):
             agg[pl.ds(s * z.group, z.group)] = z.tiled(aggregate(z, tiles, reads, s * z.group, adj, ext))
@@ -299,12 +305,13 @@
     return call(
         kernel,
         "first_lent",
-        [SMEM] * 2 + [VMEM] * 9,
-        [VMEM] * 3,
-        [z.nodes(z.edge), z.nodes(z.edge), z.nodes(z.lent)],
-        [z.held(z.ext), z.held(z.lent)],
+        [SMEM] * 2 + [VMEM] * 8,
+        [VMEM] * 4,
+        [z.nodes(z.edge), z.nodes(z.edge), z.nodes(z.lent), z.nodes(z.ext)],
+        [z.held(z.lent)],
         12,
-        (tiles, reads, *f0, fw, fe, adj, w_self, w_nbr, bias, w_out),
+        (tiles, reads, ext, fw, fe, adj, w_self, w_nbr, bias, w_out),
+        {2: 3},
     )
 
 
@@ -358,7 +365,10 @@
 
 
 def second_own(z, f1, m1, w_self, bias, wt):
-    def kernel(f_lent, f_rest, m_lent, m_rest, ws, bias, wt, own, hidden):
+    def kernel(f_lent, f_rest, m_lent, m_rest, ws, bias, wt, own, hidden, ext):
+        ext[pl.ds(0, z.lent)] = f_lent[...]
+        ext[pl.ds(z.lent, z.rest)] = f_rest[...]
+
         def work(part, first):
             f = z.flat(group_of(z, (f_lent, f_rest), part, first)[...])
             m = z.flat(group_of(z, (m_lent, m_rest), part, first)[...])
@@ -372,8 +382,8 @@
         kernel,
         "second_own",
         [VMEM] * 7,
-        [VMEM] * 2,
-        [z.nodes(z.tiles, F32)] * 2,
+        [VMEM] * 3,
+        [z.nodes(z.tiles, F32)] * 2 + [z.nodes(z.ext)],
         [],
         12,
         (*f1, *m1, w_self, bias, wt),
@@ -432,12 +442,12 @@
         acc[targets[place]] += dot(at[blocks[place]], source(sources[place]))
 
 
-def second(z, tiles, reads, tables, f1, fw, fe, adj, at, own, hidden, w_nbr, wt, after):
+def second(z, tiles, reads, tables, ext, fw, fe, adj, at, own, hidden, w_nbr, wt, after):
     groups = z.tiles // z.group
 
-    def kernel(tiles, reads, blocks, sources, targets, counts, f_lent, f_rest, fw, fe, adj, at, own, hidden, wn,
+    def kernel(tiles, reads, blocks, sources, targets, counts, _ext, fw, fe, adj, at, own, hidden, wn,
                wt, _after, agg, act, dpre, dagg, to_west, to_east, ext, acc):
-        fill_extended(z, (f_lent, f_rest), fw, fe, ext)
+        fill_borrowed(z, fw, fe, ext)
 
         def gather(s):
             agg[pl.ds(s * z.group, z.group)] = z.tiled(aggregate(z, tiles, reads, s * z.group, adj, ext))
@@ -462,12 +472,13 @@
     return call(
         kernel,
         "second",
-        [SMEM] * 6 + [VMEM] * 11,
-        [VMEM] * 6,
-        [z.nodes(z.tiles)] * 4 + [z.nodes(z.edge)] * 2,
-        [z.held(z.ext), z.held(z.lent, F32)],
+        [SMEM] * 6 + [VMEM] * 10,
+        [VMEM] * 7,
+        [z.nodes(z.tiles)] * 4 + [z.nodes(z.edge)] * 2 + [z.nodes(z.ext)],
+        [z.held(z.lent, F32)],
         12,
-        (tiles, reads, *tables, *f1, fw, fe, adj, at, own, hidden, w_nbr, wt, after),
+        (tiles, reads, *tables, ext, fw, fe, adj, at, own, hidden, w_nbr, wt, after),
+        {6: 6},
     )
 
 
@@ -504,7 +515,7 @@
         return [parts[0]] + [self.passed(parts[i], dim, i) for i in range(1, self.sizes[dim])]
 
 
-def weight_grads(z, plane, f, agg, act, m, dpre, name, after=()):
+def weight_grads(z, plane, f, agg, act, m, dpre, name, place=()):
     c = z.cols
     piece = -(-(3 * c + 1) // (plane.count * 16)) * 16
     core, ahead, side = plane.sizes
@@ -516,7 +527,16 @@
         f, agg, act, m, dpre = [
             (refs.pop(0), refs.pop(0)) if isinstance(a, tuple) else refs.pop(0) for a in arrays
         ]
-        *outs, acc, sums = refs[len(after) :]
+        copies = []
+        if place:
+            bound, _, *refs = refs
+            *outs, grads, acc, sums, sems = refs
+            for i in range(z.lent):
+                target = grads.at[1, bound[0, i // z.edge, i % z.edge]]
+                copies.append(pltpu.make_async_copy(m[0].at[i], target, sems.at[i]))
+                copies[-1].start()
+        else:
+            *outs, acc, sums = refs
         acc[...] = jnp.zeros_like(acc)
         sums[...] = jnp.zeros_like(sums)
 
@@ -539,16 +559,21 @@
                 for k in range(side):
                     owner = pl.multiple_of(plane.piece_of(me, (i, j, k)) * piece, 16)
                     out[j, k] = acc[pl.ds(owner, piece), :].astype(BF16)
+        for copy in copies:
+            copy.wait()
 
     return call(
         kernel,
         name,
-        [SMEM] + [VMEM] * (len(flat_args) + len(after)),
-        [VMEM] * core,
-        [jax.ShapeDtypeStruct((ahead, side, piece, c), BF16)] * core,
-        [pltpu.VMEM((piece * plane.count, c), F32), pltpu.VMEM((3, c, c), F32)],
+        [SMEM] + [VMEM] * len(flat_args) + ([SMEM, ANY] if place else []),
+        [VMEM] * core + ([ANY] if place else []),
+        [jax.ShapeDtypeStruct((ahead, side, piece, c), BF16)] * core
+        + ([jax.ShapeDtypeStruct(place[1].shape, BF16)] if place else []),
+        [pltpu.VMEM((piece * plane.count, c), F32), pltpu.VMEM((3, c, c), F32)]
+        + ([pltpu.SemaphoreType.DMA((z.lent,))] if place else []),
         14,
-        (plane.me, *flat_args, *after),
+        (plane.me, *flat_args, *place),
+        {2 + len(flat_args): core} if place else None,
     )
 
 
@@ -815,31 +840,6 @@
         [z.held(z.lent, F32)],
         16,
         (*tables, part, fw, fe, slope, outer, at, wt, *after),
-    )
-
-
-def place_lent(z, bound, m, grads):
-    def kernel(bound, m, _g, grads, token, sems):
-        token[...] = jnp.zeros_like(token)
-        copies = [
-            pltpu.make_async_copy(m.at[i], grads.at[1, bound[0, i // z.edge, i % z.edge]], sems.at[i])
-            for i in range(z.lent)
-        ]
-        for copy in copies:
-            copy.start()
-        for copy in copies:
-            copy.wait()
-
-    return call(
-        kernel,
-        "place_lent",
-        [SMEM, VMEM, ANY],
-        [ANY, VMEM],
-        [jax.ShapeDtypeStruct(grads.shape, BF16), TOKEN],
-        [pltpu.SemaphoreType.DMA((z.lent,))],
-        6,
-        (bound, m, grads),
-        {2: 0},
     )
 
 
@@ -921,15 +921,15 @@
     west, east = lend(z, bound_tiles, features)
     from_west = passed_along(east, 1)
     from_east = passed_along(west, -1)
-    *nodes, adj, tiles, reads, blocks, sources, targets, counts, plane.me = arrange(
+    *nodes, adj, ext, tiles, reads, blocks, sources, targets, counts, plane.me = arrange(
         z, bound_tiles, tile_nbrs, live_tiles, plane.place, features, cot, adjacency.reshape(z.pairs, r, r)
     )
     f0, m1 = tuple(nodes[:2]), tuple(nodes[2:])
     tables = (blocks, sources, targets, counts)
     at, wt = turn(z, adj, w_self, w_nbr, w_out)
 
-    west, east, agg_lent = first_lent(
-        z, tiles, reads, f0, from_west, from_east, adj, w_self, w_nbr, pre_bias, w_out
+    west, east, agg_lent, _ = first_lent(
+        z, tiles, reads, ext, from_west, from_east, adj, w_self, w_nbr, pre_bias, w_out
     )
     next_west = passed_along(east, 1)
     next_east = passed_along(west, -1)
@@ -938,11 +938,11 @@
         west, east,
     )
     f1, agg0 = (f1_lent, f1_rest), (agg_lent, agg_rest)
-    own, hidden = second_own(z, f1, m1, w_self, pre_bias, wt)
+    own, hidden, ext = second_own(z, f1, m1, w_self, pre_bias, wt)
     act0, slope, ready = saved(z, f0, agg0, w_self, w_nbr, pre_bias)
 
-    agg1, act1, dpre1, dagg1, to_west, to_east = second(
-        z, tiles, reads, tables, f1, next_west, next_east, adj, at, own, hidden, w_nbr, wt, ready
+    agg1, act1, dpre1, dagg1, to_west, to_east, _ = second(
+        z, tiles, reads, tables, ext, next_west, next_east, adj, at, own, hidden, w_nbr, wt, ready
     )
     back_west = passed_along(to_east, 1)
     back_east = passed_along(to_west, -1)
@@ -961,8 +961,7 @@
     back_west = passed_along(to_east, 1)
     back_east = passed_along(to_west, -1)
     m0, dpre0, dagg0 = (m0_lent, m0_rest), (dpre_lent, dpre_rest), (dagg_lent, dagg_rest)
-    grads, ready = place_lent(z, bound_tiles, m0_lent, grads)
-    early = weight_grads(z, plane, f0, agg0, act0, m0, dpre0, "weight_grads0", (ready,))
+    *early, grads = weight_grads(z, plane, f0, agg0, act0, m0, dpre0, "weight_grads0", (bound_tiles, grads))
 
 
     late_far = [from_line(late, step) for step in (2, 3)] if lax.axis_size("feat") == 4 else []

time: 145 us -> 144 us (level)
  waiting for transfers between devices: 34.2 us -> 31.8 us
    ppermute x8, waiting for transfers between devices: 14.8 us -> 11.6 us  [passed_along(): lax.ppermute(value, AXES, [(i, (i + steps) % count) for i in range(count)])]
    ppermute x10, starting transfers between devices: 7.57 us -> 9.48 us  [passed_by(): return lax.ppermute(value, PLANE, pairs)]
    pallas_call x27 -> x26, Pallas kernels: 67.7 us -> 67.7 us  [call(): pl.pallas_call(kernel, in_specs=in_specs, out_specs=out_specs, out_shape=...]
  transfers between devices with their start and end apart: 23 -> 23, of which waited for: 8 -> 8; matrix products, arithmetic and copies ran while one was open for 0% -> 1% of each run, Pallas kernels for 36% -> 36%
where the time goes in v11:
time: 144 us
  Pallas kernels  67.7 us (47%)
  starting transfers between devices  37.3 us (26%)
  waiting for transfers between devices  31.8 us (22%)
  local copies, waits for them, and re-layouts  5.33 us (4%)
  between operations  1.74 us (1%)
    pallas_call x26, Pallas kernels, call(): pl.pallas_call(kernel, in_specs=in_specs, out_specs=out_specs, out_shape=...  67.7 us
    ppermute x8, starting transfers between devices, passed_along(): lax.ppermute(value, AXES, [(i, (i + steps) % count) for i in range(count)])  22.7 us
    ppermute x8, waiting for transfers between devices, passed_along(): lax.ppermute(value, AXES, [(i, (i + steps) % count) for i in range(count)])  11.6 us
    ppermute x10, waiting for transfers between devices, passed_by(): return lax.ppermute(value, PLANE, pairs)  10.2 us
    ppermute x5, waiting for transfers between devices, from_line(): return lax.ppermute(value, 'feat', [(i, i ^ step) for i in range(lines)])  10 us
    ppermute x10, starting transfers between devices, passed_by(): return lax.ppermute(value, PLANE, pairs)  9.48 us
    unnamed x19, local copies, waits for them, and re-layouts  5.25 us
    ppermute x5, starting transfers between devices, from_line(): return lax.ppermute(value, 'feat', [(i, i ^ step) for i in range(lines)])  5.12 us
  transfers between devices with their start and end apart: 23, of which 8 were waited for; matrix products, arithmetic and copies ran while one was open for 1% of the time, Pallas kernels for 36%

profile of v11, /device:TPU:0, one launch (start us, length us, event | category | flops | bytes accessed | tf_op | source)
XLA Modules:
  0.0 144.0 jit_solution(12794863763325361556)
XLA Ops:
  3.1 3.1 %collective-permute-start.3 = (bf16[8,128,256]{2,1,0:T(8,128)(2,1)}, bf16[8,128,256]{2,1,0:T(8,128)(2,1)S(1)}, u32[]{:S(2)}, u32[]{:S(2)}) collective-permute-start(bf16[8,128,256]{2,1,0:T(8,128)(2,1)} %get-tuple-element.125), channel_id=1, source_target_pairs={{0,1},{1,2},{2,3},{3,4},{4,5},{5,6},{6,7},{7,8},{8,9},{9,10},{10,1... | collective-permute-start | bytes 1572872 | tf_op jit(solution)/shard_map/ppermute | solution.py:70
  6.2 3.4 %collective-permute-start.4 = (bf16[8,128,256]{2,1,0:T(8,128)(2,1)}, bf16[8,128,256]{2,1,0:T(8,128)(2,1)S(1)}, u32[]{:S(2)}, u32[]{:S(2)}) collective-permute-start(bf16[8,128,256]{2,1,0:T(8,128)(2,1)} %get-tuple-element.126), channel_id=1, source_target_pairs={{0,31},{1,0},{2,1},{3,2},{4,3},{5,4},{6,5},{7,6},{8,7},{9,8},{10,9... | collective-permute-start | bytes 1572872 | tf_op jit(solution)/shard_map/ppermute | solution.py:70
  15.6 11.0 %arrange.1 = (bf16[16,128,256]{2,1,0:T(8,128)(2,1)S(1)}, bf16[16,128,256]{2,1,0:T(8,128)(2,1)S(1)}, bf16[16,128,256]{2,1,0:T(8,128)(2,1)S(1)}, bf16[16,128,256]{...) custom-call(s32[1,2,8]{2,1,0:T(2,128)S(1)} %copy-done.6, ...), custom_call_target="tpu_custom_call" | custom-call | flops 1000 | bytes 1000 | tf_op jit(solution)/shard_map/arrange/pallas_call | solution.py:82
  26.6 4.4 %collective-permute-done.4.fe = bf16[8,128,256]{2,1,0:T(8,128)(2,1)S(1)} collective-permute-done((bf16[8,128,256]{2,1,0:T(8,128)(2,1)}, bf16[8,128,256]{2,1,0:T(8,128)(2,1)S(1)}, u32[]{:S(2)}, u32[]{:S(2)}) %collective-permute-start.4) | collective-permute-done | bytes 524320 | tf_op jit(solution)/shard_map/ppermute | solution.py:70
  35.1 3.8 %collective-permute-start.6 = (bf16[8,128,256]{2,1,0:T(8,128)(2,1)S(1)}, bf16[8,128,256]{2,1,0:T(8,128)(2,1)S(1)}, u32[]{:S(2)}, u32[]{:S(2)}) collective-permute-start(bf16[8,128,256]{2,1,0:T(8,128)(2,1)S(1)} %get-tuple-element.129.west), channel_id=1, source_target_pairs={{0,31},{1,0},{2,1},{3,2},{4,3},{5,4},{6,5},{7,6},{8,7},{9,8},{10,9... | collective-permute-start | bytes 1572872 | tf_op jit(solution)/shard_map/ppermute | solution.py:70
  38.9 3.1 %turn.1 = (bf16[128,128,128]{2,1,0:T(8,128)(2,1)S(1)}, bf16[2,3,256,256]{3,2,1,0:T(8,128)(2,1)S(1)}) custom-call(bf16[128,128,128]{2,1,0:T(8,128)(2,1)S(1)} %get-tuple-element.127.adj, bf16[2,256,256]{2,1,0:T(8,128)(2,1)S(1)} %copy-done.2, bf16[2,256,256]{2,1,0:T(8,128)(2,1)S(1)} %copy-done.1, bf16[2,256,256]{2,1,0:T(8,128)(2,1)S(1)} %copy-done.3), custom_call_target="tpu_custom_call" | custom-call | flops 1000 | bytes 1000 | tf_op jit(solution)/shard_map/turn/pallas_call | solution.py:82
  41.9 4.7 %first_rest.1 = (bf16[16,128,256]{2,1,0:T(8,128)(2,1)S(1)}, bf16[16,128,256]{2,1,0:T(8,128)(2,1)S(1)}, bf16[2,32,128,256]{3,2,1,0:T(8,128)(2,1)}, bf16[16,128,256]{2,1,0:T(8,128)(2,1)S(1)}) custom-call(s32[32]{0:T(128)S(1)} %get-tuple-element.121.tiles, s32[128]{0:T(128)S(1)} %get-tuple-element.122.reads, s32[1,2,8]{2,1,0:T(2,128)S(1)} %copy-done.6, ...), custom_call_target="tpu_custom_call" | custom-call | flops 1000 | bytes 1000 | tf_op jit(solution)/shard_map/first_rest/pallas_call | solution.py:82
  46.6 3.0 %saved.1 = (bf16[32,128,256]{2,1,0:T(8,128)(2,1)S(1)}, f32[32,128,256]{2,1,0:T(8,128)S(1)}, f32[8,128]{1,0:T(8,128)S(1)}) custom-call(bf16[16,128,256]{2,1,0:T(8,128)(2,1)S(1)} %get-tuple-element.123.f_lent.refs_0_, bf16[16,128,256]{2,1,0:T(8,128)(2,1)S(1)} %get-tuple-element.124.f_rest.refs_1_, bf16[16,128,256]{2,1,0:T(8,128)(2,1)S(1)} %get-tuple-element.144.a_lent.refs_2_, ...), custom_call_target="tpu_custom_call" | custom-call | flops 1000 | bytes 1000 | tf_op jit(solution)/shard_map/saved/pallas_call | solution.py:82
  52.2 7.2 %collective-permute-done.6.fe = bf16[8,128,256]{2,1,0:T(8,128)(2,1)S(1)} collective-permute-done((bf16[8,128,256]{2,1,0:T(8,128)(2,1)S(1)}, bf16[8,128,256]{2,1,0:T(8,128)(2,1)S(1)}, u32[]{:S(2)}, u32[]{:S(2)}) %collective-permute-start.6) | collective-permute-done | bytes 524320 | tf_op jit(solution)/shard_map/ppermute | solution.py:70
  59.4 5.4 %second.1 = (bf16[32,128,256]{2,1,0:T(8,128)(2,1)S(1)}, bf16[32,128,256]{2,1,0:T(8,128)(2,1)S(1)}, bf16[32,128,256]{2,1,0:T(8,128)(2,1)S(1)}, bf16[32,128,256]{2...) custom-call(s32[32]{0:T(128)S(1)} %get-tuple-element.121.tiles, ...), custom_call_target="tpu_custom_call", output_to_operand_aliasing={{6}: (6, {})} | custom-call | flops 1000 | bytes 1000 | tf_op jit(solution)/shard_map/second/pallas_call | solution.py:82
  65.4 4.8 %collective-permute-start.8 = (bf16[8,128,256]{2,1,0:T(8,128)(2,1)S(1)}, bf16[8,128,256]{2,1,0:T(8,128)(2,1)S(1)}, u32[]{:S(2)}, u32[]{:S(2)}) collective-permute-start(bf16[8,128,256]{2,1,0:T(8,128)(2,1)S(1)} %get-tuple-element.156), channel_id=1, source_target_pairs={{0,31},{1,0},{2,1},{3,2},{4,3},{5,4},{6,5},{7,6},{8,7},{9,8},{10,9... | collective-permute-start | bytes 1572872 | tf_op jit(solution)/shard_map/ppermute | solution.py:70
  70.2 4.3 %weight_grads1.1 = (bf16[2,2,112,256]{3,2,1,0:T(8,128)(2,1)S(1)}, bf16[2,2,112,256]{3,2,1,0:T(8,128)(2,1)S(1)}) custom-call(s32[8]{0:T(128)S(1)} %get-tuple-element.150.me, bf16[16,128,256]{2,1,0:T(8,128)(2,1)S(1)} %get-tuple-element.131.f_lent.refs_0_, bf16[16,128,256]{2,1,0:T(8,128)(2,1)S(1)} %get-tuple-element.132.f_rest.refs_1_, ...), custom_call_target="tpu_custom_call" | custom-call | flops 1000 | bytes 1000 | tf_op jit(solution)/shard_map/weight_grads1/pallas_call | solution.py:82
  74.6 3.6 %second_out.1 = (bf16[2,32,128,256]{3,2,1,0:T(8,128)(2,1)}, f32[8,128]{1,0:T(8,128)S(1)}) custom-call(s32[1,2,8]{2,1,0:T(2,128)S(1)} %copy-done.7, s32[1]{0:T(128)S(6)} %copy.33.live, bf16[16,128,256]{2,1,0:T(8,128)(2,1)S(1)} %get-tuple-element.131.f_lent.refs_0_, ...), custom_call_target="tpu_custom_call", output_to_operand_aliasing={{0}: (6, {})} | custom-call | flops 1000 | bytes 1000 | tf_op jit(solution)/shard_map/second_out/pallas_call | solution.py:82
  79.8 4.4 %input_grad1.1 = (f32[16,128,256]{2,1,0:T(8,128)S(1)}, bf16[16,128,256]{2,1,0:T(8,128)(2,1)S(1)}, f32[8,128]{1,0:T(8,128)S(1)}) custom-call(s32[968]{0:T(1024)S(1)} %get-tuple-element.133.blocks, s32[968]{0:T(1024)S(1)} %get-tuple-element.134.sources, s32[968]{0:T(1024)S(1)} %get-tuple-element.135.targets, s32[8]{0:T(128)S(1)} %get-tuple-element.136.counts, ...), custom_call_target="tpu_custom_call" | custom-call | flops 1000 | bytes 1000 | tf_op jit(solution)/shard_map/input_grad1/pallas_call | solution.py:82
  86.2 3.7 %early_rest.1 = (bf16[2,32,128,256]{3,2,1,0:T(8,128)(2,1)}, bf16[16,128,256]{2,1,0:T(8,128)(2,1)S(1)}, bf16[16,128,256]{2,1,0:T(8,128)(2,1)S(1)}, bf16[16,128,256]{2,1,0:T(8,128)(2,1)S(1)}, f32[16,128,256]{2,1,0:T(8,128)S(1)}) custom-call(s32[968]{0:T(1024)S(1)} %get-tuple-element.133.blocks, s32[968]{0:T(1024)S(1)} %get-tuple-element.134.sources, ...), custom_call_target="tpu_custom_call" | custom-call | flops 1000 | bytes 1000 | tf_op jit(solution)/shard_map/early_rest/pallas_call | solution.py:82
  89.9 3.0 %early_lent.1 = (bf16[16,128,256]{2,1,0:T(8,128)(2,1)S(1)}, bf16[16,128,256]{2,1,0:T(8,128)(2,1)S(1)}, bf16[16,128,256]{2,1,0:T(8,128)(2,1)S(1)}, bf16[8,128,256...) custom-call(s32[968]{0:T(1024)S(1)} %get-tuple-element.133.blocks, s32[968]{0:T(1024)S(1)} %get-tuple-element.134.sources, ...), custom_call_target="tpu_custom_call" | custom-call | flops 1000 | bytes 1000 | tf_op jit(solution)/shard_map/early_lent/pallas_call | solution.py:82
  93.7 4.6 %collective-permute-start.13 = (bf16[8,128,256]{2,1,0:T(8,128)(2,1)S(1)}, bf16[8,128,256]{2,1,0:T(8,128)(2,1)S(1)}, u32[]{:S(2)}, u32[]{:S(2)}) collective-permute-start(bf16[8,128,256]{2,1,0:T(8,128)(2,1)S(1)} %get-tuple-element.181), channel_id=1, source_target_pairs={{0,31},{1,0},{2,1},{3,2},{4,3},{5,4},{6,5},{7,6},{8,7},{9,8},{10,9... | collective-permute-start | bytes 1572872 | tf_op jit(solution)/shard_map/ppermute | solution.py:70
  100.0 4.5 %weight_grads0.1 = (bf16[2,2,112,256]{3,2,1,0:T(8,128)(2,1)S(1)}, bf16[2,2,112,256]{3,2,1,0:T(8,128)(2,1)S(1)}, bf16[2,32,128,256]{3,2,1,0:T(8,128)(2,1)}) custom-call(s32[8]{0:T(128)S(1)} %get-tuple-element.150.me, bf16[16,128,256]{2,1,0:T(8,128)(2,1)S(1)} %get-tuple-element.123.f_lent.refs_0_, ...), custom_call_target="tpu_custom_call", output_to_operand_aliasing={{2}: (11, {})} | custom-call | flops 1000 | bytes 1000 | tf_op jit(solution)/shard_map/weight_grads0/pallas_call | solution.py:82
  104.5 13.7 %conditional.1 = (bf16[112,256]{1,0:T(8,128)(2,1)S(1)}, f32[16,128,256]{2,1,0:T(8,128)S(1)}, bf16[16,128,256]{2,1,0:T(8,128)(2,1)S(1)}) conditional(s32[]{:T(128)} %bitcast.7, () %tuple.16, (bf16[2,2,112,256]{3,2,1,0:T(8,128)(2,1)S(1)}, bf16[2,2,112,256]{3,2,1,0:T(8,128)(2,1)S(1)}, s32[968]{0:T(1024)S(1)}, s32[968]{0:T(1024)S(1)}, s32[968]{0:T(1024)S(1)}, ...), branch_computations={%region_0.1_spmd, %region_1.2_spmd} | conditional | flops 4000 | bytes 3203104 | solution.py:975
  106.7 4.7 %collective-permute-done.1.refs_1_ = bf16[2,112,256]{2,1,0:T(8,128)(2,1)S(1)} collective-permute-done((bf16[2,112,256]{2,1,0:T(8,128)(2,1)S(1)}, bf16[2,112,256]{2,1,0:T(8,128)(2,1)S(1)}, u32[]{:S(2)}, u32[]{:S(2)}) %collective-permute-start.1) | collective-permute-done | bytes 114720 | tf_op jit(solution)/shard_map/cond/branch_1_fun/ppermute | solution.py:512
  113.1 5.1 %input_grad0.1 = (f32[16,128,256]{2,1,0:T(8,128)S(1)}, bf16[16,128,256]{2,1,0:T(8,128)(2,1)S(1)}, f32[8,128]{1,0:T(8,128)}) custom-call(s32[968]{0:T(1024)S(1)} %get-tuple-element.34.blocks, s32[968]{0:T(1024)S(1)} %get-tuple-element.35.sources, s32[968]{0:T(1024)S(1)} %get-tuple-element.36.targets, s32[8]{0:T(128)S(1)} %get-tuple-element.37.counts, ...), custom_call_target="tpu_custom_call" | custom-call | flops 1000 | bytes 1000 | tf_op jit(solution)/shard_map/cond/branch_1_fun/input_grad0/pallas_call | solution.py:82
  120.6 4.6 %collective-permute-done.17.late0 = bf16[112,256]{1,0:T(8,128)(2,1)S(1)} collective-permute-done((bf16[112,256]{1,0:T(8,128)(2,1)S(1)}, bf16[112,256]{1,0:T(8,128)(2,1)S(1)}, u32[]{:S(2)}, u32[]{:S(2)}) %collective-permute-start.17) | collective-permute-done | bytes 57376 | tf_op jit(solution)/shard_map/ppermute | solution.py:615
  126.3 5.4 %collective-permute-done.15.early0 = bf16[112,256]{1,0:T(8,128)(2,1)S(1)} collective-permute-done((bf16[112,256]{1,0:T(8,128)(2,1)S(1)}, bf16[112,256]{1,0:T(8,128)(2,1)S(1)}, u32[]{:S(2)}, u32[]{:S(2)}) %collective-permute-start.15) | collective-permute-done | bytes 57376 | tf_op jit(solution)/shard_map/ppermute | solution.py:615
  132.5 2.8 %collective-permute-start.21 = (bf16[2,112,256]{2,1,0:T(8,128)(2,1)S(1)}, bf16[2,112,256]{2,1,0:T(8,128)(2,1)S(1)}, u32[]{:S(2)}, u32[]{:S(2)}) collective-permute-start(bf16[2,112,256]{2,1,0:T(8,128)(2,1)S(1)} %line_sum.1.refs_0_), channel_id=1, source_target_pairs={{0,20},{4,16},{16,4},{20,0},{8,28},{12,24},{24,12},{28,8},{1,21},{... | collective-permute-start | bytes 344072 | tf_op jit(solution)/shard_map/ppermute | solution.py:512
  (70 shorter events, 37.7 us)
Async XLA Ops:
  3.1 23.5 %collective-permute-start.3 = (bf16[8,128,256]{2,1,0:T(8,128)(2,1)}, bf16[8,128,256]{2,1,0:T(8,128)(2,1)S(1)}, u32[]{:S(2)}, u32[]{:S(2)}) collective-permute-start(bf16[8,128,256]{2,1,0:T(8,128)(2,1)} %get-tuple-element.125), channel_id=1, source_target_pairs={{0,1},{1,2},{2,3},{3,4},{4,5},{5,6},{6,7},{7,8},{8,9},{9,10},{10,1... | collective-permute-start | bytes 1572872 | tf_op jit(solution)/shard_map/ppermute | solution.py:70
  6.2 24.8 %collective-permute-start.4 = (bf16[8,128,256]{2,1,0:T(8,128)(2,1)}, bf16[8,128,256]{2,1,0:T(8,128)(2,1)S(1)}, u32[]{:S(2)}, u32[]{:S(2)}) collective-permute-start(bf16[8,128,256]{2,1,0:T(8,128)(2,1)} %get-tuple-element.126), channel_id=1, source_target_pairs={{0,31},{1,0},{2,1},{3,2},{4,3},{5,4},{6,5},{7,6},{8,7},{9,8},{10,9... | collective-permute-start | bytes 1572872 | tf_op jit(solution)/shard_map/ppermute | solution.py:70
  15.6 15.5 %copy-start.8 = (f32[2,256]{1,0:T(2,128)S(1)}, f32[2,256]{1,0:T(2,128)}, u32[]{:S(2)}) copy-start(f32[2,256]{1,0:T(2,128)} %bias.7) | copy-start | bytes 6148
  33.5 18.7 %collective-permute-start.5 = (bf16[8,128,256]{2,1,0:T(8,128)(2,1)S(1)}, bf16[8,128,256]{2,1,0:T(8,128)(2,1)S(1)}, u32[]{:S(2)}, u32[]{:S(2)}) collective-permute-start(bf16[8,128,256]{2,1,0:T(8,128)(2,1)S(1)} %get-tuple-element.130.east), channel_id=1, source_target_pairs={{0,1},{1,2},{2,3},{3,4},{4,5},{5,6},{6,7},{7,8},{8,9},{9,10},{10,1... | collective-permute-start | bytes 1572872 | tf_op jit(solution)/shard_map/ppermute | solution.py:70
  35.1 24.3 %collective-permute-start.6 = (bf16[8,128,256]{2,1,0:T(8,128)(2,1)S(1)}, bf16[8,128,256]{2,1,0:T(8,128)(2,1)S(1)}, u32[]{:S(2)}, u32[]{:S(2)}) collective-permute-start(bf16[8,128,256]{2,1,0:T(8,128)(2,1)S(1)} %get-tuple-element.129.west), channel_id=1, source_target_pairs={{0,31},{1,0},{2,1},{3,2},{4,3},{5,4},{6,5},{7,6},{8,7},{9,8},{10,9... | collective-permute-start | bytes 1572872 | tf_op jit(solution)/shard_map/ppermute | solution.py:70
  64.8 25.1 %collective-permute-start.7 = (bf16[8,128,256]{2,1,0:T(8,128)(2,1)S(1)}, bf16[8,128,256]{2,1,0:T(8,128)(2,1)S(1)}, u32[]{:S(2)}, u32[]{:S(2)}) collective-permute-start(bf16[8,128,256]{2,1,0:T(8,128)(2,1)S(1)} %get-tuple-element.155), channel_id=1, source_target_pairs={{0,1},{1,2},{2,3},{3,4},{4,5},{5,6},{6,7},{7,8},{8,9},{9,10},{10,1... | collective-permute-start | bytes 1572872 | tf_op jit(solution)/shard_map/ppermute | solution.py:70
  65.4 24.6 %collective-permute-start.8 = (bf16[8,128,256]{2,1,0:T(8,128)(2,1)S(1)}, bf16[8,128,256]{2,1,0:T(8,128)(2,1)S(1)}, u32[]{:S(2)}, u32[]{:S(2)}) collective-permute-start(bf16[8,128,256]{2,1,0:T(8,128)(2,1)S(1)} %get-tuple-element.156), channel_id=1, source_target_pairs={{0,31},{1,0},{2,1},{3,2},{4,3},{5,4},{6,5},{7,6},{8,7},{9,8},{10,9... | collective-permute-start | bytes 1572872 | tf_op jit(solution)/shard_map/ppermute | solution.py:70
  74.5 3.7 %collective-permute-start.9 = (bf16[2,2,112,256]{3,2,1,0:T(8,128)(2,1)S(1)}, bf16[2,2,112,256]{3,2,1,0:T(8,128)(2,1)S(1)}, u32[]{:S(2)}, u32[]{:S(2)}) collective-permute-start(bf16[2,2,112,256]{3,2,1,0:T(8,128)(2,1)S(1)} %get-tuple-element.163), channel_id=1, source_target_pairs={{0,8},{4,12},{16,24},{20,28},{8,0},{12,4},{24,16},{28,20},{1,9},{5... | collective-permute-start | bytes 688136 | tf_op jit(solution)/shard_map/ppermute | solution.py:512
  78.2 5.9 %collective-permute-start.10 = (bf16[2,112,256]{2,1,0:T(8,128)(2,1)S(1)}, bf16[2,112,256]{2,1,0:T(8,128)(2,1)S(1)}, u32[]{:S(2)}, u32[]{:S(2)}) collective-permute-start(bf16[2,112,256]{2,1,0:T(8,128)(2,1)S(1)} %get-tuple-element.165), channel_id=1, source_target_pairs={{0,16},{4,20},{16,0},{20,4},{8,24},{12,28},{24,8},{28,12},{1,17},{... | collective-permute-start | bytes 344072 | tf_op jit(solution)/shard_map/ppermute | solution.py:512
  84.2 5.6 %collective-permute-start.11 = (bf16[112,256]{1,0:T(8,128)(2,1)S(1)}, bf16[112,256]{1,0:T(8,128)(2,1)S(1)}, u32[]{:S(2)}, u32[]{:S(2)}) collective-permute-start(bf16[112,256]{1,0:T(8,128)(2,1)S(1)} %get-tuple-element.168), channel_id=1, source_target_pairs={{0,4},{4,0},{16,20},{20,16},{8,12},{12,8},{24,28},{28,24},{1,5},{5... | collective-permute-start | bytes 172040 | tf_op jit(solution)/shard_map/ppermute | solution.py:512
  92.9 38.8 %collective-permute-start.12 = (bf16[8,128,256]{2,1,0:T(8,128)(2,1)S(1)}, bf16[8,128,256]{2,1,0:T(8,128)(2,1)S(1)}, u32[]{:S(2)}, u32[]{:S(2)}) collective-permute-start(bf16[8,128,256]{2,1,0:T(8,128)(2,1)S(1)} %get-tuple-element.180), channel_id=1, source_target_pairs={{0,1},{1,2},{2,3},{3,4},{4,5},{5,6},{6,7},{7,8},{8,9},{9,10},{10,1... | collective-permute-start | bytes 1572872 | tf_op jit(solution)/shard_map/ppermute | solution.py:70
  93.7 38.0 %collective-permute-start.13 = (bf16[8,128,256]{2,1,0:T(8,128)(2,1)S(1)}, bf16[8,128,256]{2,1,0:T(8,128)(2,1)S(1)}, u32[]{:S(2)}, u32[]{:S(2)}) collective-permute-start(bf16[8,128,256]{2,1,0:T(8,128)(2,1)S(1)} %get-tuple-element.181), channel_id=1, source_target_pairs={{0,31},{1,0},{2,1},{3,2},{4,3},{5,4},{6,5},{7,6},{8,7},{9,8},{10,9... | collective-permute-start | bytes 1572872 | tf_op jit(solution)/shard_map/ppermute | solution.py:70
  98.3 26.9 %collective-permute-start.17 = (bf16[112,256]{1,0:T(8,128)(2,1)S(1)}, bf16[112,256]{1,0:T(8,128)(2,1)S(1)}, u32[]{:S(2)}, u32[]{:S(2)}) collective-permute-start(bf16[112,256]{1,0:T(8,128)(2,1)S(1)} %added.11._late.late), channel_id=1, source_target_pairs={{0,2},{1,3},{2,0},{3,1},{4,6},{5,7},{6,4},{7,5},{8,10},{9,11},{10,... | collective-permute-start | bytes 172040 | tf_op jit(solution)/shard_map/ppermute | solution.py:615
  98.5 26.6 %collective-permute-start.18 = (bf16[112,256]{1,0:T(8,128)(2,1)S(1)}, bf16[112,256]{1,0:T(8,128)(2,1)S(1)}, u32[]{:S(2)}, u32[]{:S(2)}) collective-permute-start(bf16[112,256]{1,0:T(8,128)(2,1)S(1)} %added.11._late.late), channel_id=1, source_target_pairs={{0,3},{1,2},{2,1},{3,0},{4,7},{5,6},{6,5},{7,4},{8,11},{9,10},{10,... | collective-permute-start | bytes 172040 | tf_op jit(solution)/shard_map/ppermute | solution.py:615
  104.5 1.6 %collective-permute-start = (bf16[2,2,112,256]{3,2,1,0:T(8,128)(2,1)S(1)}, bf16[2,2,112,256]{3,2,1,0:T(8,128)(2,1)S(1)}, u32[]{:S(2)}, u32[]{:S(2)}) collective-permute-start(bf16[2,2,112,256]{3,2,1,0:T(8,128)(2,1)S(1)} %get-tuple-element.29), channel_id=1, source_target_pairs={{0,8},{4,12},{16,24},{20,28},{8,0},{12,4},{24,16},{28,20},{1,9},{5... | collective-permute-start | bytes 688136 | tf_op jit(solution)/shard_map/cond/branch_1_fun/ppermute | solution.py:512
  106.1 5.3 %collective-permute-start.1 = (bf16[2,112,256]{2,1,0:T(8,128)(2,1)S(1)}, bf16[2,112,256]{2,1,0:T(8,128)(2,1)S(1)}, u32[]{:S(2)}, u32[]{:S(2)}) collective-permute-start(bf16[2,112,256]{2,1,0:T(8,128)(2,1)S(1)} %get-tuple-element.31), channel_id=1, source_target_pairs={{0,16},{4,20},{16,0},{20,4},{8,24},{12,28},{24,8},{28,12},{1,17},{... | collective-permute-start | bytes 344072 | tf_op jit(solution)/shard_map/cond/branch_1_fun/ppermute | solution.py:512
  111.4 6.8 %collective-permute-start.2 = (bf16[112,256]{1,0:T(8,128)(2,1)S(1)}, bf16[112,256]{1,0:T(8,128)(2,1)S(1)}, u32[]{:S(2)}, u32[]{:S(2)}) collective-permute-start(bf16[112,256]{1,0:T(8,128)(2,1)S(1)} %get-tuple-element.33), channel_id=1, source_target_pairs={{0,4},{4,0},{16,20},{20,16},{8,12},{12,8},{24,28},{28,24},{1,5},{5... | collective-permute-start | bytes 172040 | tf_op jit(solution)/shard_map/cond/branch_1_fun/ppermute | solution.py:512
  118.2 13.4 %collective-permute-start.14 = (bf16[2,112,256]{2,1,0:T(8,128)(2,1)S(1)}, bf16[2,112,256]{2,1,0:T(8,128)(2,1)S(1)}, u32[]{:S(2)}, u32[]{:S(2)}) collective-permute-start(bf16[2,112,256]{2,1,0:T(8,128)(2,1)S(1)} %joined.1.both), channel_id=1, source_target_pairs={{0,1},{1,0},{2,3},{3,2},{4,5},{5,4},{6,7},{7,6},{8,9},{9,8},{10,11... | collective-permute-start | bytes 344072 | tf_op jit(solution)/shard_map/ppermute | solution.py:615
  125.2 6.5 %collective-permute-start.15 = (bf16[112,256]{1,0:T(8,128)(2,1)S(1)}, bf16[112,256]{1,0:T(8,128)(2,1)S(1)}, u32[]{:S(2)}, u32[]{:S(2)}) collective-permute-start(bf16[112,256]{1,0:T(8,128)(2,1)S(1)} %get-tuple-element.183.early), channel_id=1, source_target_pairs={{0,2},{1,3},{2,0},{3,1},{4,6},{5,7},{6,4},{7,5},{8,10},{9,11},{10,... | collective-permute-start | bytes 172040 | tf_op jit(solution)/shard_map/ppermute | solution.py:615
  125.2 6.5 %collective-permute-start.16 = (bf16[112,256]{1,0:T(8,128)(2,1)S(1)}, bf16[112,256]{1,0:T(8,128)(2,1)S(1)}, u32[]{:S(2)}, u32[]{:S(2)}) collective-permute-start(bf16[112,256]{1,0:T(8,128)(2,1)S(1)} %get-tuple-element.183.early), channel_id=1, source_target_pairs={{0,3},{1,2},{2,1},{3,0},{4,7},{5,6},{6,5},{7,4},{8,11},{9,10},{10,... | collective-permute-start | bytes 172040 | tf_op jit(solution)/shard_map/ppermute | solution.py:615
  131.8 5.9 %collective-permute-start.19 = (bf16[2,112,256]{2,1,0:T(8,128)(2,1)S(1)}, bf16[2,112,256]{2,1,0:T(8,128)(2,1)S(1)}, u32[]{:S(2)}, u32[]{:S(2)}) collective-permute-start(bf16[2,112,256]{2,1,0:T(8,128)(2,1)S(1)} %line_sum.1.refs_0_), channel_id=1, source_target_pairs={{0,4},{4,0},{16,20},{20,16},{8,12},{12,8},{24,28},{28,24},{1,5},{5... | collective-permute-start | bytes 344072 | tf_op jit(solution)/shard_map/ppermute | solution.py:512
  131.9 5.7 %collective-permute-start.20 = (bf16[2,112,256]{2,1,0:T(8,128)(2,1)S(1)}, bf16[2,112,256]{2,1,0:T(8,128)(2,1)S(1)}, u32[]{:S(2)}, u32[]{:S(2)}) collective-permute-start(bf16[2,112,256]{2,1,0:T(8,128)(2,1)S(1)} %line_sum.1.refs_0_), channel_id=1, source_target_pairs={{0,16},{4,20},{16,0},{20,4},{8,24},{12,28},{24,8},{28,12},{1,17},{... | collective-permute-start | bytes 344072 | tf_op jit(solution)/shard_map/ppermute | solution.py:512
  132.5 6.8 %collective-permute-start.21 = (bf16[2,112,256]{2,1,0:T(8,128)(2,1)S(1)}, bf16[2,112,256]{2,1,0:T(8,128)(2,1)S(1)}, u32[]{:S(2)}, u32[]{:S(2)}) collective-permute-start(bf16[2,112,256]{2,1,0:T(8,128)(2,1)S(1)} %line_sum.1.refs_0_), channel_id=1, source_target_pairs={{0,20},{4,16},{16,4},{20,0},{8,28},{12,24},{24,12},{28,8},{1,21},{... | collective-permute-start | bytes 344072 | tf_op jit(solution)/shard_map/ppermute | solution.py:512
  139.4 2.1 %collective-permute-start.22 = (bf16[2,2,2,112,256]{4,3,2,1,0:T(8,128)(2,1)S(1)}, bf16[2,2,2,112,256]{4,3,2,1,0:T(8,128)(2,1)S(1)}, u32[]{:S(2)}, u32[]{:S(2)}) collective-permute-start(bf16[2,2,2,112,256]{4,3,2,1,0:T(8,128)(2,1)S(1)} %bitcast.14), channel_id=1, source_target_pairs={{0,8},{4,12},{16,24},{20,28},{8,0},{12,4},{24,16},{28,20},{1,9},{5... | collective-permute-start | bytes 1376264 | tf_op jit(solution)/shard_map/ppermute | solution.py:512
  (8 other events, 65.7 us)

commit v12 on v11

--- a/solution.py
+++ b/solution.py
@@ -654,20 +654,21 @@
     return share
 
 
-def stacked(values):
+def stacked(values, after):
     def kernel(*refs):
-        for i, ref in enumerate(refs[:-1]):
+        for i, ref in enumerate(refs[: len(values)]):
             refs[-1][i] = ref[...]
 
     shape = (len(values),) + values[0].shape
     out = jax.ShapeDtypeStruct(shape, values[0].dtype)
-    return call(kernel, "stacked", [VMEM] * len(values), VMEM, out, [], 4, values)
-
-
-def plane_gathered(plane, share):
+    args = (*values, *after)
+    return call(kernel, "stacked", [VMEM] * len(args), VMEM, out, [], 4, args)
+
+
+def plane_gathered(plane, share, after):
     core, ahead, side = plane.sizes
     steps = [(0, j, k) for j in range(ahead) for k in range(side)]
-    share = stacked([share] + [plane.passed_by(share, by) for by in steps[1:]])
+    share = stacked([share] + [plane.passed_by(share, by) for by in steps[1:]], after)
     share = share.reshape(ahead, side, *share.shape[-3:])
     return [share] + [plane.passed(share, 0, i) for i in range(1, core)]
 
@@ -844,7 +845,8 @@
 
 
 def finish(z, bound, part, rest, fw, fe, grads):
-    def kernel(bound, part, rest, fw, fe, _g, grads, keep, sems):
+    def kernel(bound, part, rest, fw, fe, _g, grads, token, keep, sems):
+        token[...] = jnp.zeros_like(token)
         copies = [pltpu.make_async_copy(rest, grads.at[0, pl.ds(z.lent, z.rest)], sems.at[z.lent])]
         copies[0].start()
         for i in range(z.lent):
@@ -862,8 +864,8 @@
         kernel,
         "finish",
         [SMEM] + [VMEM] * 4 + [ANY],
-        ANY,
-        jax.ShapeDtypeStruct(grads.shape, BF16),
+        [ANY, VMEM],
+        [jax.ShapeDtypeStruct(grads.shape, BF16), TOKEN],
         [z.held(z.lent), pltpu.SemaphoreType.DMA((z.lent + 1,))],
         14,
         (bound, part, rest, fw, fe, grads),
@@ -985,8 +987,8 @@
         shares = line_sum_of_four(both, near, far, late_far, (back_west, back_east))
     else:
         shares = line_sum(both)
-    pieces = plane_gathered(plane, shares)
-    grads = finish(z, bound_tiles, part, rest, back_west, back_east, grads)
+    grads, done = finish(z, bound_tiles, part, rest, back_west, back_east, grads)
+    pieces = plane_gathered(plane, shares, (done,))
     grad_self, grad_nbr, grad_out, grad_bias = unpack(z, plane, pieces)
     return (
         section_out.reshape(2, t * r, c),

time: 144 us -> 144 us (level)
  transfers between devices with their start and end apart: 23 -> 23, of which waited for: 8 -> 9; matrix products, arithmetic and copies ran while one was open for 1% -> 1% of each run, Pallas kernels for 36% -> 37%
where the time goes in v12:
time: 144 us
  Pallas kernels  68.7 us (48%)
  starting transfers between devices  36.2 us (25%)
  waiting for transfers between devices  31.9 us (22%)
  local copies, waits for them, and re-layouts  5.33 us (4%)
  between operations  1.74 us (1%)
    pallas_call x26, Pallas kernels, call(): pl.pallas_call(kernel, in_specs=in_specs, out_specs=out_specs, out_shape=...  68.7 us
    ppermute x8, starting transfers between devices, passed_along(): lax.ppermute(value, AXES, [(i, (i + steps) % count) for i in range(count)])  22.7 us
    ppermute x8, waiting for transfers between devices, passed_along(): lax.ppermute(value, AXES, [(i, (i + steps) % count) for i in range(count)])  11.6 us
    ppermute x5, waiting for transfers between devices, from_line(): return lax.ppermute(value, 'feat', [(i, i ^ step) for i in range(lines)])  10.2 us
    ppermute x10, waiting for transfers between devices, passed_by(): return lax.ppermute(value, PLANE, pairs)  10.1 us
    ppermute x10, starting transfers between devices, passed_by(): return lax.ppermute(value, PLANE, pairs)  8.7 us
    unnamed x19, local copies, waits for them, and re-layouts  5.25 us
    ppermute x5, starting transfers between devices, from_line(): return lax.ppermute(value, 'feat', [(i, i ^ step) for i in range(lines)])  4.8 us
  transfers between devices with their start and end apart: 23, of which 9 were waited for; matrix products, arithmetic and copies ran while one was open for 1% of the time, Pallas kernels for 37%

profile of v12, /device:TPU:0, one launch (start us, length us, event | category | flops | bytes accessed | tf_op | source)
XLA Modules:
  0.0 143.9 jit_solution(12057341328926859405)
XLA Ops:
  3.1 3.1 %collective-permute-start.3 = (bf16[8,128,256]{2,1,0:T(8,128)(2,1)}, bf16[8,128,256]{2,1,0:T(8,128)(2,1)S(1)}, u32[]{:S(2)}, u32[]{:S(2)}) collective-permute-start(bf16[8,128,256]{2,1,0:T(8,128)(2,1)} %get-tuple-element.127), channel_id=1, source_target_pairs={{0,1},{1,2},{2,3},{3,4},{4,5},{5,6},{6,7},{7,8},{8,9},{9,10},{10,1... | collective-permute-start | bytes 1572872 | tf_op jit(solution)/shard_map/ppermute | solution.py:70
  6.2 3.4 %collective-permute-start.4 = (bf16[8,128,256]{2,1,0:T(8,128)(2,1)}, bf16[8,128,256]{2,1,0:T(8,128)(2,1)S(1)}, u32[]{:S(2)}, u32[]{:S(2)}) collective-permute-start(bf16[8,128,256]{2,1,0:T(8,128)(2,1)} %get-tuple-element.128), channel_id=1, source_target_pairs={{0,31},{1,0},{2,1},{3,2},{4,3},{5,4},{6,5},{7,6},{8,7},{9,8},{10,9... | collective-permute-start | bytes 1572872 | tf_op jit(solution)/shard_map/ppermute | solution.py:70
  15.6 11.0 %arrange.1 = (bf16[16,128,256]{2,1,0:T(8,128)(2,1)S(1)}, bf16[16,128,256]{2,1,0:T(8,128)(2,1)S(1)}, bf16[16,128,256]{2,1,0:T(8,128)(2,1)S(1)}, bf16[16,128,256]{...) custom-call(s32[1,2,8]{2,1,0:T(2,128)S(1)} %copy-done.6, ...), custom_call_target="tpu_custom_call" | custom-call | flops 1000 | bytes 1000 | tf_op jit(solution)/shard_map/arrange/pallas_call | solution.py:82
  26.6 4.4 %collective-permute-done.4.fe = bf16[8,128,256]{2,1,0:T(8,128)(2,1)S(1)} collective-permute-done((bf16[8,128,256]{2,1,0:T(8,128)(2,1)}, bf16[8,128,256]{2,1,0:T(8,128)(2,1)S(1)}, u32[]{:S(2)}, u32[]{:S(2)}) %collective-permute-start.4) | collective-permute-done | bytes 524320 | tf_op jit(solution)/shard_map/ppermute | solution.py:70
  35.1 3.8 %collective-permute-start.6 = (bf16[8,128,256]{2,1,0:T(8,128)(2,1)S(1)}, bf16[8,128,256]{2,1,0:T(8,128)(2,1)S(1)}, u32[]{:S(2)}, u32[]{:S(2)}) collective-permute-start(bf16[8,128,256]{2,1,0:T(8,128)(2,1)S(1)} %get-tuple-element.131.west), channel_id=1, source_target_pairs={{0,31},{1,0},{2,1},{3,2},{4,3},{5,4},{6,5},{7,6},{8,7},{9,8},{10,9... | collective-permute-start | bytes 1572872 | tf_op jit(solution)/shard_map/ppermute | solution.py:70
  38.9 3.1 %turn.1 = (bf16[128,128,128]{2,1,0:T(8,128)(2,1)S(1)}, bf16[2,3,256,256]{3,2,1,0:T(8,128)(2,1)S(1)}) custom-call(bf16[128,128,128]{2,1,0:T(8,128)(2,1)S(1)} %get-tuple-element.129.adj, bf16[2,256,256]{2,1,0:T(8,128)(2,1)S(1)} %copy-done.2, bf16[2,256,256]{2,1,0:T(8,128)(2,1)S(1)} %copy-done.1, bf16[2,256,256]{2,1,0:T(8,128)(2,1)S(1)} %copy-done.3), custom_call_target="tpu_custom_call" | custom-call | flops 1000 | bytes 1000 | tf_op jit(solution)/shard_map/turn/pallas_call | solution.py:82
  41.9 4.7 %first_rest.1 = (bf16[16,128,256]{2,1,0:T(8,128)(2,1)S(1)}, bf16[16,128,256]{2,1,0:T(8,128)(2,1)S(1)}, bf16[2,32,128,256]{3,2,1,0:T(8,128)(2,1)}, bf16[16,128,256]{2,1,0:T(8,128)(2,1)S(1)}) custom-call(s32[32]{0:T(128)S(1)} %get-tuple-element.123.tiles, s32[128]{0:T(128)S(1)} %get-tuple-element.124.reads, s32[1,2,8]{2,1,0:T(2,128)S(1)} %copy-done.6, ...), custom_call_target="tpu_custom_call" | custom-call | flops 1000 | bytes 1000 | tf_op jit(solution)/shard_map/first_rest/pallas_call | solution.py:82
  46.6 3.0 %saved.1 = (bf16[32,128,256]{2,1,0:T(8,128)(2,1)S(1)}, f32[32,128,256]{2,1,0:T(8,128)S(1)}, f32[8,128]{1,0:T(8,128)S(1)}) custom-call(bf16[16,128,256]{2,1,0:T(8,128)(2,1)S(1)} %get-tuple-element.125.f_lent.refs_0_, bf16[16,128,256]{2,1,0:T(8,128)(2,1)S(1)} %get-tuple-element.126.f_rest.refs_1_, bf16[16,128,256]{2,1,0:T(8,128)(2,1)S(1)} %get-tuple-element.146.a_lent.refs_2_, ...), custom_call_target="tpu_custom_call" | custom-call | flops 1000 | bytes 1000 | tf_op jit(solution)/shard_map/saved/pallas_call | solution.py:82
  52.2 7.2 %collective-permute-done.6.fe = bf16[8,128,256]{2,1,0:T(8,128)(2,1)S(1)} collective-permute-done((bf16[8,128,256]{2,1,0:T(8,128)(2,1)S(1)}, bf16[8,128,256]{2,1,0:T(8,128)(2,1)S(1)}, u32[]{:S(2)}, u32[]{:S(2)}) %collective-permute-start.6) | collective-permute-done | bytes 524320 | tf_op jit(solution)/shard_map/ppermute | solution.py:70
  59.4 5.4 %second.1 = (bf16[32,128,256]{2,1,0:T(8,128)(2,1)S(1)}, bf16[32,128,256]{2,1,0:T(8,128)(2,1)S(1)}, bf16[32,128,256]{2,1,0:T(8,128)(2,1)S(1)}, bf16[32,128,256]{2...) custom-call(s32[32]{0:T(128)S(1)} %get-tuple-element.123.tiles, ...), custom_call_target="tpu_custom_call", output_to_operand_aliasing={{6}: (6, {})} | custom-call | flops 1000 | bytes 1000 | tf_op jit(solution)/shard_map/second/pallas_call | solution.py:82
  65.4 4.8 %collective-permute-start.8 = (bf16[8,128,256]{2,1,0:T(8,128)(2,1)S(1)}, bf16[8,128,256]{2,1,0:T(8,128)(2,1)S(1)}, u32[]{:S(2)}, u32[]{:S(2)}) collective-permute-start(bf16[8,128,256]{2,1,0:T(8,128)(2,1)S(1)} %get-tuple-element.158), channel_id=1, source_target_pairs={{0,31},{1,0},{2,1},{3,2},{4,3},{5,4},{6,5},{7,6},{8,7},{9,8},{10,9... | collective-permute-start | bytes 1572872 | tf_op jit(solution)/shard_map/ppermute | solution.py:70
  70.2 4.3 %weight_grads1.1 = (bf16[2,2,112,256]{3,2,1,0:T(8,128)(2,1)S(1)}, bf16[2,2,112,256]{3,2,1,0:T(8,128)(2,1)S(1)}) custom-call(s32[8]{0:T(128)S(1)} %get-tuple-element.152.me, bf16[16,128,256]{2,1,0:T(8,128)(2,1)S(1)} %get-tuple-element.133.f_lent.refs_0_, bf16[16,128,256]{2,1,0:T(8,128)(2,1)S(1)} %get-tuple-element.134.f_rest.refs_1_, ...), custom_call_target="tpu_custom_call" | custom-call | flops 1000 | bytes 1000 | tf_op jit(solution)/shard_map/weight_grads1/pallas_call | solution.py:82
  74.6 3.6 %second_out.1 = (bf16[2,32,128,256]{3,2,1,0:T(8,128)(2,1)}, f32[8,128]{1,0:T(8,128)S(1)}) custom-call(s32[1,2,8]{2,1,0:T(2,128)S(1)} %copy-done.7, s32[1]{0:T(128)S(6)} %copy.33.live, bf16[16,128,256]{2,1,0:T(8,128)(2,1)S(1)} %get-tuple-element.133.f_lent.refs_0_, ...), custom_call_target="tpu_custom_call", output_to_operand_aliasing={{0}: (6, {})} | custom-call | flops 1000 | bytes 1000 | tf_op jit(solution)/shard_map/second_out/pallas_call | solution.py:82
  80.2 4.9 %input_grad1.1 = (f32[16,128,256]{2,1,0:T(8,128)S(1)}, bf16[16,128,256]{2,1,0:T(8,128)(2,1)S(1)}, f32[8,128]{1,0:T(8,128)S(1)}) custom-call(s32[968]{0:T(1024)S(1)} %get-tuple-element.135.blocks, s32[968]{0:T(1024)S(1)} %get-tuple-element.136.sources, s32[968]{0:T(1024)S(1)} %get-tuple-element.137.targets, s32[8]{0:T(128)S(1)} %get-tuple-element.138.counts, ...), custom_call_target="tpu_custom_call" | custom-call | flops 1000 | bytes 1000 | tf_op jit(solution)/shard_map/input_grad1/pallas_call | solution.py:82
  86.2 3.7 %early_rest.1 = (bf16[2,32,128,256]{3,2,1,0:T(8,128)(2,1)}, bf16[16,128,256]{2,1,0:T(8,128)(2,1)S(1)}, bf16[16,128,256]{2,1,0:T(8,128)(2,1)S(1)}, bf16[16,128,256]{2,1,0:T(8,128)(2,1)S(1)}, f32[16,128,256]{2,1,0:T(8,128)S(1)}) custom-call(s32[968]{0:T(1024)S(1)} %get-tuple-element.135.blocks, s32[968]{0:T(1024)S(1)} %get-tuple-element.136.sources, ...), custom_call_target="tpu_custom_call" | custom-call | flops 1000 | bytes 1000 | tf_op jit(solution)/shard_map/early_rest/pallas_call | solution.py:82
  89.9 3.0 %early_lent.1 = (bf16[16,128,256]{2,1,0:T(8,128)(2,1)S(1)}, bf16[16,128,256]{2,1,0:T(8,128)(2,1)S(1)}, bf16[16,128,256]{2,1,0:T(8,128)(2,1)S(1)}, bf16[8,128,256...) custom-call(s32[968]{0:T(1024)S(1)} %get-tuple-element.135.blocks, s32[968]{0:T(1024)S(1)} %get-tuple-element.136.sources, ...), custom_call_target="tpu_custom_call" | custom-call | flops 1000 | bytes 1000 | tf_op jit(solution)/shard_map/early_lent/pallas_call | solution.py:82
  93.7 4.6 %collective-permute-start.13 = (bf16[8,128,256]{2,1,0:T(8,128)(2,1)S(1)}, bf16[8,128,256]{2,1,0:T(8,128)(2,1)S(1)}, u32[]{:S(2)}, u32[]{:S(2)}) collective-permute-start(bf16[8,128,256]{2,1,0:T(8,128)(2,1)S(1)} %get-tuple-element.183), channel_id=1, source_target_pairs={{0,31},{1,0},{2,1},{3,2},{4,3},{5,4},{6,5},{7,6},{8,7},{9,8},{10,9... | collective-permute-start | bytes 1572872 | tf_op jit(solution)/shard_map/ppermute | solution.py:70
  100.1 4.5 %weight_grads0.1 = (bf16[2,2,112,256]{3,2,1,0:T(8,128)(2,1)S(1)}, bf16[2,2,112,256]{3,2,1,0:T(8,128)(2,1)S(1)}, bf16[2,32,128,256]{3,2,1,0:T(8,128)(2,1)}) custom-call(s32[8]{0:T(128)S(1)} %get-tuple-element.152.me, bf16[16,128,256]{2,1,0:T(8,128)(2,1)S(1)} %get-tuple-element.125.f_lent.refs_0_, ...), custom_call_target="tpu_custom_call", output_to_operand_aliasing={{2}: (11, {})} | custom-call | flops 1000 | bytes 1000 | tf_op jit(solution)/shard_map/weight_grads0/pallas_call | solution.py:82
  104.6 14.0 %conditional.1 = (bf16[112,256]{1,0:T(8,128)(2,1)S(1)}, f32[16,128,256]{2,1,0:T(8,128)S(1)}, bf16[16,128,256]{2,1,0:T(8,128)(2,1)S(1)}) conditional(s32[]{:T(128)} %bitcast.7, () %tuple.16, (bf16[2,2,112,256]{3,2,1,0:T(8,128)(2,1)S(1)}, bf16[2,2,112,256]{3,2,1,0:T(8,128)(2,1)S(1)}, s32[968]{0:T(1024)S(1)}, s32[968]{0:T(1024)S(1)}, s32[968]{0:T(1024)S(1)}, ...), branch_computations={%region_0.1_spmd, %region_1.2_spmd} | conditional | flops 4000 | bytes 3203104 | solution.py:977
  106.7 4.8 %collective-permute-done.1.refs_1_ = bf16[2,112,256]{2,1,0:T(8,128)(2,1)S(1)} collective-permute-done((bf16[2,112,256]{2,1,0:T(8,128)(2,1)S(1)}, bf16[2,112,256]{2,1,0:T(8,128)(2,1)S(1)}, u32[]{:S(2)}, u32[]{:S(2)}) %collective-permute-start.1) | collective-permute-done | bytes 114720 | tf_op jit(solution)/shard_map/cond/branch_1_fun/ppermute | solution.py:512
  113.1 5.6 %input_grad0.1 = (f32[16,128,256]{2,1,0:T(8,128)S(1)}, bf16[16,128,256]{2,1,0:T(8,128)(2,1)S(1)}, f32[8,128]{1,0:T(8,128)}) custom-call(s32[968]{0:T(1024)S(1)} %get-tuple-element.34.blocks, s32[968]{0:T(1024)S(1)} %get-tuple-element.35.sources, s32[968]{0:T(1024)S(1)} %get-tuple-element.36.targets, s32[8]{0:T(128)S(1)} %get-tuple-element.37.counts, ...), custom_call_target="tpu_custom_call" | custom-call | flops 1000 | bytes 1000 | tf_op jit(solution)/shard_map/cond/branch_1_fun/input_grad0/pallas_call | solution.py:82
  120.6 4.7 %collective-permute-done.17.late0 = bf16[112,256]{1,0:T(8,128)(2,1)S(1)} collective-permute-done((bf16[112,256]{1,0:T(8,128)(2,1)S(1)}, bf16[112,256]{1,0:T(8,128)(2,1)S(1)}, u32[]{:S(2)}, u32[]{:S(2)}) %collective-permute-start.17) | collective-permute-done | bytes 57376 | tf_op jit(solution)/shard_map/ppermute | solution.py:615
  126.4 5.4 %collective-permute-done.15.early0 = bf16[112,256]{1,0:T(8,128)(2,1)S(1)} collective-permute-done((bf16[112,256]{1,0:T(8,128)(2,1)S(1)}, bf16[112,256]{1,0:T(8,128)(2,1)S(1)}, u32[]{:S(2)}, u32[]{:S(2)}) %collective-permute-start.15) | collective-permute-done | bytes 57376 | tf_op jit(solution)/shard_map/ppermute | solution.py:615
  132.5 2.9 %collective-permute-start.21 = (bf16[2,112,256]{2,1,0:T(8,128)(2,1)S(1)}, bf16[2,112,256]{2,1,0:T(8,128)(2,1)S(1)}, u32[]{:S(2)}, u32[]{:S(2)}) collective-permute-start(bf16[2,112,256]{2,1,0:T(8,128)(2,1)S(1)} %line_sum.1.refs_0_), channel_id=1, source_target_pairs={{0,20},{4,16},{16,4},{20,0},{8,28},{12,24},{24,12},{28,8},{1,21},{... | collective-permute-start | bytes 344072 | tf_op jit(solution)/shard_map/ppermute | solution.py:512
  (70 shorter events, 36.3 us)
Async XLA Ops:
  3.1 23.5 %collective-permute-start.3 = (bf16[8,128,256]{2,1,0:T(8,128)(2,1)}, bf16[8,128,256]{2,1,0:T(8,128)(2,1)S(1)}, u32[]{:S(2)}, u32[]{:S(2)}) collective-permute-start(bf16[8,128,256]{2,1,0:T(8,128)(2,1)} %get-tuple-element.127), channel_id=1, source_target_pairs={{0,1},{1,2},{2,3},{3,4},{4,5},{5,6},{6,7},{7,8},{8,9},{9,10},{10,1... | collective-permute-start | bytes 1572872 | tf_op jit(solution)/shard_map/ppermute | solution.py:70
  6.2 24.8 %collective-permute-start.4 = (bf16[8,128,256]{2,1,0:T(8,128)(2,1)}, bf16[8,128,256]{2,1,0:T(8,128)(2,1)S(1)}, u32[]{:S(2)}, u32[]{:S(2)}) collective-permute-start(bf16[8,128,256]{2,1,0:T(8,128)(2,1)} %get-tuple-element.128), channel_id=1, source_target_pairs={{0,31},{1,0},{2,1},{3,2},{4,3},{5,4},{6,5},{7,6},{8,7},{9,8},{10,9... | collective-permute-start | bytes 1572872 | tf_op jit(solution)/shard_map/ppermute | solution.py:70
  15.6 15.5 %copy-start.8 = (f32[2,256]{1,0:T(2,128)S(1)}, f32[2,256]{1,0:T(2,128)}, u32[]{:S(2)}) copy-start(f32[2,256]{1,0:T(2,128)} %bias.7) | copy-start | bytes 6148
  33.5 18.7 %collective-permute-start.5 = (bf16[8,128,256]{2,1,0:T(8,128)(2,1)S(1)}, bf16[8,128,256]{2,1,0:T(8,128)(2,1)S(1)}, u32[]{:S(2)}, u32[]{:S(2)}) collective-permute-start(bf16[8,128,256]{2,1,0:T(8,128)(2,1)S(1)} %get-tuple-element.132.east), channel_id=1, source_target_pairs={{0,1},{1,2},{2,3},{3,4},{4,5},{5,6},{6,7},{7,8},{8,9},{9,10},{10,1... | collective-permute-start | bytes 1572872 | tf_op jit(solution)/shard_map/ppermute | solution.py:70
  35.1 24.3 %collective-permute-start.6 = (bf16[8,128,256]{2,1,0:T(8,128)(2,1)S(1)}, bf16[8,128,256]{2,1,0:T(8,128)(2,1)S(1)}, u32[]{:S(2)}, u32[]{:S(2)}) collective-permute-start(bf16[8,128,256]{2,1,0:T(8,128)(2,1)S(1)} %get-tuple-element.131.west), channel_id=1, source_target_pairs={{0,31},{1,0},{2,1},{3,2},{4,3},{5,4},{6,5},{7,6},{8,7},{9,8},{10,9... | collective-permute-start | bytes 1572872 | tf_op jit(solution)/shard_map/ppermute | solution.py:70
  64.8 25.2 %collective-permute-start.7 = (bf16[8,128,256]{2,1,0:T(8,128)(2,1)S(1)}, bf16[8,128,256]{2,1,0:T(8,128)(2,1)S(1)}, u32[]{:S(2)}, u32[]{:S(2)}) collective-permute-start(bf16[8,128,256]{2,1,0:T(8,128)(2,1)S(1)} %get-tuple-element.157), channel_id=1, source_target_pairs={{0,1},{1,2},{2,3},{3,4},{4,5},{5,6},{6,7},{7,8},{8,9},{9,10},{10,1... | collective-permute-start | bytes 1572872 | tf_op jit(solution)/shard_map/ppermute | solution.py:70
  65.4 24.6 %collective-permute-start.8 = (bf16[8,128,256]{2,1,0:T(8,128)(2,1)S(1)}, bf16[8,128,256]{2,1,0:T(8,128)(2,1)S(1)}, u32[]{:S(2)}, u32[]{:S(2)}) collective-permute-start(bf16[8,128,256]{2,1,0:T(8,128)(2,1)S(1)} %get-tuple-element.158), channel_id=1, source_target_pairs={{0,31},{1,0},{2,1},{3,2},{4,3},{5,4},{6,5},{7,6},{8,7},{9,8},{10,9... | collective-permute-start | bytes 1572872 | tf_op jit(solution)/shard_map/ppermute | solution.py:70
  74.5 3.7 %collective-permute-start.9 = (bf16[2,2,112,256]{3,2,1,0:T(8,128)(2,1)S(1)}, bf16[2,2,112,256]{3,2,1,0:T(8,128)(2,1)S(1)}, u32[]{:S(2)}, u32[]{:S(2)}) collective-permute-start(bf16[2,2,112,256]{3,2,1,0:T(8,128)(2,1)S(1)} %get-tuple-element.165), channel_id=1, source_target_pairs={{0,8},{4,12},{16,24},{20,28},{8,0},{12,4},{24,16},{28,20},{1,9},{5... | collective-permute-start | bytes 688136 | tf_op jit(solution)/shard_map/ppermute | solution.py:512
  78.2 6.9 %collective-permute-start.10 = (bf16[2,112,256]{2,1,0:T(8,128)(2,1)S(1)}, bf16[2,112,256]{2,1,0:T(8,128)(2,1)S(1)}, u32[]{:S(2)}, u32[]{:S(2)}) collective-permute-start(bf16[2,112,256]{2,1,0:T(8,128)(2,1)S(1)} %get-tuple-element.167), channel_id=1, source_target_pairs={{0,16},{4,20},{16,0},{20,4},{8,24},{12,28},{24,8},{28,12},{1,17},{... | collective-permute-start | bytes 344072 | tf_op jit(solution)/shard_map/ppermute | solution.py:512
  85.1 4.7 %collective-permute-start.11 = (bf16[112,256]{1,0:T(8,128)(2,1)S(1)}, bf16[112,256]{1,0:T(8,128)(2,1)S(1)}, u32[]{:S(2)}, u32[]{:S(2)}) collective-permute-start(bf16[112,256]{1,0:T(8,128)(2,1)S(1)} %get-tuple-element.170), channel_id=1, source_target_pairs={{0,4},{4,0},{16,20},{20,16},{8,12},{12,8},{24,28},{28,24},{1,5},{5... | collective-permute-start | bytes 172040 | tf_op jit(solution)/shard_map/ppermute | solution.py:512
  92.9 38.9 %collective-permute-start.12 = (bf16[8,128,256]{2,1,0:T(8,128)(2,1)S(1)}, bf16[8,128,256]{2,1,0:T(8,128)(2,1)S(1)}, u32[]{:S(2)}, u32[]{:S(2)}) collective-permute-start(bf16[8,128,256]{2,1,0:T(8,128)(2,1)S(1)} %get-tuple-element.182), channel_id=1, source_target_pairs={{0,1},{1,2},{2,3},{3,4},{4,5},{5,6},{6,7},{7,8},{8,9},{9,10},{10,1... | collective-permute-start | bytes 1572872 | tf_op jit(solution)/shard_map/ppermute | solution.py:70
  93.7 38.2 %collective-permute-start.13 = (bf16[8,128,256]{2,1,0:T(8,128)(2,1)S(1)}, bf16[8,128,256]{2,1,0:T(8,128)(2,1)S(1)}, u32[]{:S(2)}, u32[]{:S(2)}) collective-permute-start(bf16[8,128,256]{2,1,0:T(8,128)(2,1)S(1)} %get-tuple-element.183), channel_id=1, source_target_pairs={{0,31},{1,0},{2,1},{3,2},{4,3},{5,4},{6,5},{7,6},{8,7},{9,8},{10,9... | collective-permute-start | bytes 1572872 | tf_op jit(solution)/shard_map/ppermute | solution.py:70
  98.3 27.0 %collective-permute-start.17 = (bf16[112,256]{1,0:T(8,128)(2,1)S(1)}, bf16[112,256]{1,0:T(8,128)(2,1)S(1)}, u32[]{:S(2)}, u32[]{:S(2)}) collective-permute-start(bf16[112,256]{1,0:T(8,128)(2,1)S(1)} %added.11._late.late), channel_id=1, source_target_pairs={{0,2},{1,3},{2,0},{3,1},{4,6},{5,7},{6,4},{7,5},{8,10},{9,11},{10,... | collective-permute-start | bytes 172040 | tf_op jit(solution)/shard_map/ppermute | solution.py:615
  98.7 26.6 %collective-permute-start.18 = (bf16[112,256]{1,0:T(8,128)(2,1)S(1)}, bf16[112,256]{1,0:T(8,128)(2,1)S(1)}, u32[]{:S(2)}, u32[]{:S(2)}) collective-permute-start(bf16[112,256]{1,0:T(8,128)(2,1)S(1)} %added.11._late.late), channel_id=1, source_target_pairs={{0,3},{1,2},{2,1},{3,0},{4,7},{5,6},{6,5},{7,4},{8,11},{9,10},{10,... | collective-permute-start | bytes 172040 | tf_op jit(solution)/shard_map/ppermute | solution.py:615
  104.7 1.6 %collective-permute-start = (bf16[2,2,112,256]{3,2,1,0:T(8,128)(2,1)S(1)}, bf16[2,2,112,256]{3,2,1,0:T(8,128)(2,1)S(1)}, u32[]{:S(2)}, u32[]{:S(2)}) collective-permute-start(bf16[2,2,112,256]{3,2,1,0:T(8,128)(2,1)S(1)} %get-tuple-element.29), channel_id=1, source_target_pairs={{0,8},{4,12},{16,24},{20,28},{8,0},{12,4},{24,16},{28,20},{1,9},{5... | collective-permute-start | bytes 688136 | tf_op jit(solution)/shard_map/cond/branch_1_fun/ppermute | solution.py:512
  106.3 5.3 %collective-permute-start.1 = (bf16[2,112,256]{2,1,0:T(8,128)(2,1)S(1)}, bf16[2,112,256]{2,1,0:T(8,128)(2,1)S(1)}, u32[]{:S(2)}, u32[]{:S(2)}) collective-permute-start(bf16[2,112,256]{2,1,0:T(8,128)(2,1)S(1)} %get-tuple-element.31), channel_id=1, source_target_pairs={{0,16},{4,20},{16,0},{20,4},{8,24},{12,28},{24,8},{28,12},{1,17},{... | collective-permute-start | bytes 344072 | tf_op jit(solution)/shard_map/cond/branch_1_fun/ppermute | solution.py:512
  111.6 7.1 %collective-permute-start.2 = (bf16[112,256]{1,0:T(8,128)(2,1)S(1)}, bf16[112,256]{1,0:T(8,128)(2,1)S(1)}, u32[]{:S(2)}, u32[]{:S(2)}) collective-permute-start(bf16[112,256]{1,0:T(8,128)(2,1)S(1)} %get-tuple-element.33), channel_id=1, source_target_pairs={{0,4},{4,0},{16,20},{20,16},{8,12},{12,8},{24,28},{28,24},{1,5},{5... | collective-permute-start | bytes 172040 | tf_op jit(solution)/shard_map/cond/branch_1_fun/ppermute | solution.py:512
  118.7 13.1 %collective-permute-start.14 = (bf16[2,112,256]{2,1,0:T(8,128)(2,1)S(1)}, bf16[2,112,256]{2,1,0:T(8,128)(2,1)S(1)}, u32[]{:S(2)}, u32[]{:S(2)}) collective-permute-start(bf16[2,112,256]{2,1,0:T(8,128)(2,1)S(1)} %joined.1.both), channel_id=1, source_target_pairs={{0,1},{1,0},{2,3},{3,2},{4,5},{5,4},{6,7},{7,6},{8,9},{9,8},{10,11... | collective-permute-start | bytes 344072 | tf_op jit(solution)/shard_map/ppermute | solution.py:615
  125.3 6.5 %collective-permute-start.15 = (bf16[112,256]{1,0:T(8,128)(2,1)S(1)}, bf16[112,256]{1,0:T(8,128)(2,1)S(1)}, u32[]{:S(2)}, u32[]{:S(2)}) collective-permute-start(bf16[112,256]{1,0:T(8,128)(2,1)S(1)} %get-tuple-element.186.early), channel_id=1, source_target_pairs={{0,2},{1,3},{2,0},{3,1},{4,6},{5,7},{6,4},{7,5},{8,10},{9,11},{10,... | collective-permute-start | bytes 172040 | tf_op jit(solution)/shard_map/ppermute | solution.py:615
  125.3 6.5 %collective-permute-start.16 = (bf16[112,256]{1,0:T(8,128)(2,1)S(1)}, bf16[112,256]{1,0:T(8,128)(2,1)S(1)}, u32[]{:S(2)}, u32[]{:S(2)}) collective-permute-start(bf16[112,256]{1,0:T(8,128)(2,1)S(1)} %get-tuple-element.186.early), channel_id=1, source_target_pairs={{0,3},{1,2},{2,1},{3,0},{4,7},{5,6},{6,5},{7,4},{8,11},{9,10},{10,... | collective-permute-start | bytes 172040 | tf_op jit(solution)/shard_map/ppermute | solution.py:615
  131.9 5.9 %collective-permute-start.19 = (bf16[2,112,256]{2,1,0:T(8,128)(2,1)S(1)}, bf16[2,112,256]{2,1,0:T(8,128)(2,1)S(1)}, u32[]{:S(2)}, u32[]{:S(2)}) collective-permute-start(bf16[2,112,256]{2,1,0:T(8,128)(2,1)S(1)} %line_sum.1.refs_0_), channel_id=1, source_target_pairs={{0,4},{4,0},{16,20},{20,16},{8,12},{12,8},{24,28},{28,24},{1,5},{5... | collective-permute-start | bytes 344072 | tf_op jit(solution)/shard_map/ppermute | solution.py:512
  132.0 5.8 %collective-permute-start.20 = (bf16[2,112,256]{2,1,0:T(8,128)(2,1)S(1)}, bf16[2,112,256]{2,1,0:T(8,128)(2,1)S(1)}, u32[]{:S(2)}, u32[]{:S(2)}) collective-permute-start(bf16[2,112,256]{2,1,0:T(8,128)(2,1)S(1)} %line_sum.1.refs_0_), channel_id=1, source_target_pairs={{0,16},{4,20},{16,0},{20,4},{8,24},{12,28},{24,8},{28,12},{1,17},{... | collective-permute-start | bytes 344072 | tf_op jit(solution)/shard_map/ppermute | solution.py:512
  132.5 6.9 %collective-permute-start.21 = (bf16[2,112,256]{2,1,0:T(8,128)(2,1)S(1)}, bf16[2,112,256]{2,1,0:T(8,128)(2,1)S(1)}, u32[]{:S(2)}, u32[]{:S(2)}) collective-permute-start(bf16[2,112,256]{2,1,0:T(8,128)(2,1)S(1)} %line_sum.1.refs_0_), channel_id=1, source_target_pairs={{0,20},{4,16},{16,4},{20,0},{8,28},{12,24},{24,12},{28,8},{1,21},{... | collective-permute-start | bytes 344072 | tf_op jit(solution)/shard_map/ppermute | solution.py:512
  139.5 1.9 %collective-permute-start.22 = (bf16[2,2,2,112,256]{4,3,2,1,0:T(8,128)(2,1)S(1)}, bf16[2,2,2,112,256]{4,3,2,1,0:T(8,128)(2,1)S(1)}, u32[]{:S(2)}, u32[]{:S(2)}) collective-permute-start(bf16[2,2,2,112,256]{4,3,2,1,0:T(8,128)(2,1)S(1)} %bitcast.14), channel_id=1, source_target_pairs={{0,8},{4,12},{16,24},{20,28},{8,0},{12,4},{24,16},{28,20},{1,9},{5... | collective-permute-start | bytes 1376264 | tf_op jit(solution)/shard_map/ppermute | solution.py:512
  (8 other events, 65.7 us)
